TPU v7x, 128 devices: a whole 4x4x4 slice. The times are simulated.
128 devices in a mesh: blk: 16 (over z, y_lo, core), mp: 8 (over x, y_hi).
Axes of the slice: x: 4, y: 4 (y_hi: 2, y_lo: 2; y = y_hi * 2 + y_lo), z: 4, core: 2. Of those that a mesh axis runs over, the one named last changes fastest.
Arguments:
- img_feat: bfloat16 [16384, 6144], P('blk', 'mp'), may hold values from -60 to 60
- txt_feat: bfloat16 [16384, 4096], P('blk', 'mp'), may hold values from -60 to 60
- img_weight: bfloat16 [6144, 1024], P('mp'), may hold values from -0.5 to 2
- txt_weight: bfloat16 [4096, 1024], P('mp'), may hold values from -0.5 to 2
- natural_exponent_multiplier: float32 [1], replicated, may hold values from 2.3 to 3
- bias: float32 [1], replicated, may hold values from -3 to -1
Outputs:
- img_feat_grad: bfloat16 [16384, 6144], P('blk', 'mp')
- txt_feat_grad: bfloat16 [16384, 4096], P('blk', 'mp')
- img_weight_grad: float32 [6144, 1024], P('mp', 'blk')
- txt_weight_grad: float32 [4096, 1024], P('mp', 'blk')
All inputs are finite; a program needn't handle non-finite values.
Results may differ from a plain program's by a relative error of at most 0.019.
Values may be sent and summed in bfloat16 or wider, within the bound.
No kernel may reach another device: no remote copies, remote signals or barrier semaphores. Data moves between devices by JAX's collectives and lax.ppermute only.
A program may use at most 128 MiB of HBM per device.

v0:
```python
import jax
import jax.numpy as jnp
from jax import lax
from jax.sharding import PartitionSpec as P

EPS = 1e-06


def shifted(value, axis, steps):
    count = lax.axis_size(axis)
    pairs = [(source, (source + steps) % count) for source in range(count)]
    return lax.ppermute(value, axis, pairs)


def unit_rows(embedded):
    inverse = lax.rsqrt(jnp.sum(embedded * embedded, axis=1, keepdims=True) + EPS)
    return (embedded * inverse, inverse)


def norm_back(unit_grad, unit_full, inverse):
    return inverse * (unit_grad - unit_full * jnp.sum(unit_full * unit_grad, axis=1, keepdims=True))


def cross_contributions(
    picture_sample_group, caption_submatrix, matching_targets, sharpness_multiplier, additive_offset
):
    cosine_affinities = lax.dot_general(
        caption_submatrix,
        picture_sample_group,
        (((1,), (1,)), ((), ())),
        preferred_element_type=jnp.float32,
    )
    matching_affinities = sharpness_multiplier * cosine_affinities + additive_offset
    derivative_multiplier = (
        -matching_targets
        * jax.nn.sigmoid(-matching_targets * matching_affinities)
        * sharpness_multiplier
    ).astype(jnp.bfloat16)
    picture_portion = lax.dot_general(
        derivative_multiplier,
        caption_submatrix,
        (((0,), (0,)), ((), ())),
        preferred_element_type=jnp.float32,
    )
    caption_portion = jnp.dot(
        derivative_multiplier, picture_sample_group, preferred_element_type=jnp.float32
    )
    return (picture_portion, caption_portion)


def local(img_feat, txt_feat, img_weight, txt_weight, natural_exponent_multiplier, bias):
    sharpness_multiplier = jnp.exp(natural_exponent_multiplier[0])
    additive_offset = bias[0]
    group_rows = img_feat.shape[0]
    embed_width = img_weight.shape[1]
    blk_count = lax.axis_size("blk")
    mp_count = lax.axis_size("mp")
    own_rows = group_rows // mp_count
    embedded = lax.psum_scatter(
        jnp.concatenate(
            [
                jnp.dot(img_feat, img_weight, preferred_element_type=jnp.float32),
                jnp.dot(txt_feat, txt_weight, preferred_element_type=jnp.float32),
            ],
            axis=1,
        ),
        "mp",
        scatter_dimension=0,
        tiled=True,
    )
    img_unit, img_inv = unit_rows(embedded[:, :embed_width])
    txt_unit, txt_inv = unit_rows(embedded[:, embed_width:])
    text_own = txt_unit.astype(jnp.bfloat16)
    picture_sample_group = lax.all_gather(img_unit.astype(jnp.bfloat16), "mp", axis=0, tiled=True)
    column = lax.axis_index("mp")
    image_ids = lax.broadcasted_iota(jnp.int32, (1, group_rows), 1)
    text_local = column * own_rows + lax.broadcasted_iota(jnp.int32, (own_rows, 1), 0)
    img_zeros = jnp.zeros((group_rows, embed_width), jnp.float32)
    first_labels = jnp.where(text_local == image_ids, 1.0, -1.0).astype(jnp.float32)

    def cycle_turn(turn_index, state):
        caption_submatrix, carried, img_total = state
        matching_targets = jnp.where(turn_index == 0, first_labels, -1.0)
        picture_portion, caption_portion = cross_contributions(
            picture_sample_group,
            caption_submatrix,
            matching_targets,
            sharpness_multiplier,
            additive_offset,
        )
        caption_submatrix = shifted(caption_submatrix, "blk", 1)
        carried = shifted(carried + caption_portion, "blk", 1)
        return (caption_submatrix, carried, img_total + picture_portion)

    start_state = (text_own, jnp.zeros((own_rows, embed_width), jnp.float32), img_zeros)
    final_block, txt_ugrad, img_total = lax.fori_loop(0, blk_count, cycle_turn, start_state)
    img_ugrad = lax.psum_scatter(
        img_total.astype(jnp.bfloat16), "mp", scatter_dimension=0, tiled=True
    ).astype(jnp.float32)
    img_egrad = norm_back(img_ugrad, img_unit, img_inv).astype(jnp.bfloat16)
    txt_egrad = norm_back(txt_ugrad, txt_unit, txt_inv).astype(jnp.bfloat16)
    img_all, txt_all = (
        lax.all_gather(img_egrad, "mp", axis=0, tiled=True),
        lax.all_gather(txt_egrad, "mp", axis=0, tiled=True),
    )
    img_feat_grad = lax.dot_general(
        img_all, img_weight, (((1,), (1,)), ((), ())), preferred_element_type=jnp.float32
    ).astype(jnp.bfloat16)
    txt_feat_grad = lax.dot_general(
        txt_all, txt_weight, (((1,), (1,)), ((), ())), preferred_element_type=jnp.float32
    ).astype(jnp.bfloat16)
    img_wpart = lax.dot_general(
        img_feat, img_all, (((0,), (0,)), ((), ())), preferred_element_type=jnp.float32
    )
    txt_wpart = lax.dot_general(
        txt_feat, txt_all, (((0,), (0,)), ((), ())), preferred_element_type=jnp.float32
    )
    img_weight_grad, txt_weight_grad = (
        lax.psum_scatter(
            img_wpart.astype(jnp.bfloat16), "blk", scatter_dimension=1, tiled=True
        ).astype(jnp.float32),
        lax.psum_scatter(
            txt_wpart.astype(jnp.bfloat16), "blk", scatter_dimension=1, tiled=True
        ).astype(jnp.float32),
    )
    return (img_feat_grad, txt_feat_grad, img_weight_grad, txt_weight_grad)


def solution(mesh):
    return jax.shard_map(
        local,
        mesh=mesh,
        in_specs=(P("blk", "mp"), P("blk", "mp"), P("mp", None), P("mp", None), P(), P()),
        out_specs=(P("blk", "mp"), P("blk", "mp"), P("mp", "blk"), P("mp", "blk")),
        check_vma=False,
    )
```

profile of v0, /device:TPU:8, one launch (start us, length us, event | category | flops | bytes accessed | tf_op | source)
XLA Modules:
  0.0 806.4 jit_solution(12313407878027466303)
XLA Ops:
  17.4 116.0 %reduce-scatter.7.cloned.1.call-done = f32[128,2048]{0,1:T(8,128)} async-done(((f32[1024,2048]{0,1:T(8,128)}), f32[128,2048]{0,1:T(8,128)}) %reduce-scatter.7.cloned.1.call-update) | async-done | bytes 1048592 | tf_op jit(solution)/shard_map/reduce_scatter | solution.py:59
  137.7 54.6 %all-gather.4.cloned.1.call-done = bf16[1024,1024]{0,1:T(8,128)(2,1)} async-done(((bf16[128,1024]{0,1:T(8,128)(2,1)}), bf16[1024,1024]{0,1:T(8,128)(2,1)}) %all-gather.4.cloned.1.call-update) | async-done | bytes 2097168 | tf_op jit(solution)/shard_map/all_gather | solution.py:74
  196.3 265.6 %while.18 = (s32[]{:T(128)}, bf16[128,1024]{1,0:T(8,128)(2,1)S(1)}, f32[128,1024]{1,0:T(8,128)S(1)}, f32[1024,1024]{1,0:T(8,128)}, f32[]{:T(128)}, /*index=5*/bf...) while((s32[]{:T(128)}, bf16[128,1024]{1,0:T(8,128)(2,1)S(1)}, ...), condition=%wide.region_4.5_spmd.clone, body=%wide.region_3.4_spmd.clone.sunk | while | flops 809238528 | bytes 27001572 | solution.py:96
  205.5 6.2 collective-permute-done
  219.1 4.9 select_add_fusion.2
  235.3 4.9 select_add_fusion.2
  251.6 4.9 select_add_fusion.2
  267.9 4.9 select_add_fusion.2
  284.1 4.9 select_add_fusion.2
  300.4 4.9 select_add_fusion.2
  316.6 4.9 select_add_fusion.2
  332.9 4.9 select_add_fusion.2
  349.2 4.9 select_add_fusion.2
  365.4 4.9 select_add_fusion.2
  370.3 4.2 collective-permute-done
  381.7 4.9 select_add_fusion.2
  386.6 5.4 collective-permute-done
  397.9 4.9 select_add_fusion.2
  402.8 6.6 collective-permute-done
  414.2 4.9 select_add_fusion.2
  419.1 7.8 collective-permute-done
  431.0 4.9 select_add_fusion.2
  435.8 8.6 %collective-permute-done = bf16[128,1024]{1,0:T(8,128)(2,1)S(1)} collective-permute-done((bf16[128,1024]{1,0:T(8,128)(2,1)S(1)}, bf16[128,1024]{1,0:T(8,128)(2,1)S(1)}, u32[]{:S(2)}, u32[]{:S(2)}) %collective-permute-start) | collective-permute-done | bytes 262176 | tf_op jit(solution)/shard_map/while/body/eval_jaxpr/ppermute | solution.py:12
  448.4 4.9 select_add_fusion.2
  453.3 8.6 %collective-permute-done = bf16[128,1024]{1,0:T(8,128)(2,1)S(1)} collective-permute-done((bf16[128,1024]{1,0:T(8,128)(2,1)S(1)}, bf16[128,1024]{1,0:T(8,128)(2,1)S(1)}, u32[]{:S(2)}, u32[]{:S(2)}) %collective-permute-start) | collective-permute-done | bytes 262176 | tf_op jit(solution)/shard_map/while/body/eval_jaxpr/ppermute | solution.py:12
  461.9 4.6 copy.17
  471.5 84.2 %reduce-scatter.13.cloned.1.call-done = bf16[128,1024]{1,0:T(8,128)(2,1)} async-done(((bf16[1024,1024]{1,0:T(8,128)(2,1)}), bf16[128,1024]{1,0:T(8,128)(2,1)}) %reduce-scatter.13.cloned.1.call-update) | async-done | bytes 262160
  559.7 55.8 %all-gather.8.cloned.1.call-done = bf16[1024,1024]{0,1:T(8,128)(2,1)} async-done(((bf16[128,1024]{0,1:T(8,128)(2,1)}), bf16[1024,1024]{0,1:T(8,128)(2,1)}) %all-gather.8.cloned.1.call-update) | async-done | bytes 2097168 | tf_op jit(solution)/shard_map/all_gather | solution.py:104
  619.8 54.8 %all-gather.6.cloned.1.call-done = bf16[1024,1024]{0,1:T(8,128)(2,1)} async-done(((bf16[128,1024]{0,1:T(8,128)(2,1)}), bf16[1024,1024]{0,1:T(8,128)(2,1)}) %all-gather.6.cloned.1.call-update) | async-done | bytes 2097168 | tf_op jit(solution)/shard_map/all_gather | solution.py:103
  674.6 4.6 fusion.12
  686.3 48.3 %reduce-scatter.11.cloned.1.call-done = bf16[512,64]{0,1:T(8,128)(2,1)} async-done(((bf16[512,1024]{0,1:T(8,128)(2,1)}), bf16[512,64]{0,1:T(8,128)(2,1)}) %reduce-scatter.11.cloned.1.call-update) | async-done | bytes 65552 | tf_op jit(solution)/shard_map/reduce_scatter | solution.py:122
  736.1 61.9 %reduce-scatter.9.cloned.1.call-done = bf16[768,64]{0,1:T(8,128)(2,1)} async-done(((bf16[768,1024]{0,1:T(8,128)(2,1)}), bf16[768,64]{0,1:T(8,128)(2,1)}) %reduce-scatter.9.cloned.1.call-update) | async-done | bytes 98320 | tf_op jit(solution)/shard_map/reduce_scatter | solution.py:119
  (189 shorter events, 185.6 us)
Async XLA Ops:
  7.2 126.2 %reduce-scatter.7.cloned.1.call-start = ((), (), s32[]{:S(2)}) async-start(), calls=%async_computation.4 | async-start | bytes 9437184 | tf_op jit(solution)/shard_map/reduce_scatter | solution.py:59
  17.3 175.0 %all-gather.4.cloned.1.call-start = ((), (), s32[]{:S(2)}) async-start(), calls=%async_computation.5 | async-start | bytes 2359296 | tf_op jit(solution)/shard_map/all_gather | solution.py:74
  136.8 418.9 %reduce-scatter.13.cloned.1.call-start = ((), (), s32[]{:S(2)}) async-start(), calls=%async_computation.10 | async-start | bytes 2359296
  200.2 11.5 %collective-permute-start.1 = (f32[128,1024]{1,0:T(8,128)S(1)}, f32[128,1024]{1,0:T(8,128)S(1)}, u32[]{:S(2)}, u32[]{:S(2)}) collective-permute-start(f32[128,1024]{1,0:T(8,128)S(1)} %convolution_add_fusion.2), channel_id=1, source_target_pairs={{0,8},{8,16},{16,24},{24,32},{32,40},{40,48},{48,56},{56,64},{64,7... | collective-permute-start | bytes 1572872 | tf_op jit(solution)/shard_map/while/body/eval_jaxpr/ppermute | solution.py:12
  200.3 11.4 %collective-permute-start = (bf16[128,1024]{1,0:T(8,128)(2,1)S(1)}, bf16[128,1024]{1,0:T(8,128)(2,1)S(1)}, u32[]{:S(2)}, u32[]{:S(2)}) collective-permute-start(bf16[128,1024]{1,0:T(8,128)(2,1)S(1)} %copy.27), channel_id=1, source_target_pairs={{0,8},{8,16},{16,24},{24,32},{32,40},{40,48},{48,56},{56,64},{64,7... | collective-permute-start | bytes 786440 | tf_op jit(solution)/shard_map/while/body/eval_jaxpr/ppermute | solution.py:12
  215.6 11.5 %collective-permute-start.1 = (f32[128,1024]{1,0:T(8,128)S(1)}, f32[128,1024]{1,0:T(8,128)S(1)}, u32[]{:S(2)}, u32[]{:S(2)}) collective-permute-start(f32[128,1024]{1,0:T(8,128)S(1)} %convolution_add_fusion.2), channel_id=1, source_target_pairs={{0,8},{8,16},{16,24},{24,32},{32,40},{40,48},{48,56},{56,64},{64,7... | collective-permute-start | bytes 1572872 | tf_op jit(solution)/shard_map/while/body/eval_jaxpr/ppermute | solution.py:12
  215.7 11.4 %collective-permute-start = (bf16[128,1024]{1,0:T(8,128)(2,1)S(1)}, bf16[128,1024]{1,0:T(8,128)(2,1)S(1)}, u32[]{:S(2)}, u32[]{:S(2)}) collective-permute-start(bf16[128,1024]{1,0:T(8,128)(2,1)S(1)} %copy.27), channel_id=1, source_target_pairs={{0,8},{8,16},{16,24},{24,32},{32,40},{40,48},{48,56},{56,64},{64,7... | collective-permute-start | bytes 786440 | tf_op jit(solution)/shard_map/while/body/eval_jaxpr/ppermute | solution.py:12
  230.9 11.5 %collective-permute-start.1 = (f32[128,1024]{1,0:T(8,128)S(1)}, f32[128,1024]{1,0:T(8,128)S(1)}, u32[]{:S(2)}, u32[]{:S(2)}) collective-permute-start(f32[128,1024]{1,0:T(8,128)S(1)} %convolution_add_fusion.2), channel_id=1, source_target_pairs={{0,8},{8,16},{16,24},{24,32},{32,40},{40,48},{48,56},{56,64},{64,7... | collective-permute-start | bytes 1572872 | tf_op jit(solution)/shard_map/while/body/eval_jaxpr/ppermute | solution.py:12
  246.3 11.5 %collective-permute-start.1 = (f32[128,1024]{1,0:T(8,128)S(1)}, f32[128,1024]{1,0:T(8,128)S(1)}, u32[]{:S(2)}, u32[]{:S(2)}) collective-permute-start(f32[128,1024]{1,0:T(8,128)S(1)} %convolution_add_fusion.2), channel_id=1, source_target_pairs={{0,8},{8,16},{16,24},{24,32},{32,40},{40,48},{48,56},{56,64},{64,7... | collective-permute-start | bytes 1572872 | tf_op jit(solution)/shard_map/while/body/eval_jaxpr/ppermute | solution.py:12
  261.7 11.5 %collective-permute-start.1 = (f32[128,1024]{1,0:T(8,128)S(1)}, f32[128,1024]{1,0:T(8,128)S(1)}, u32[]{:S(2)}, u32[]{:S(2)}) collective-permute-start(f32[128,1024]{1,0:T(8,128)S(1)} %convolution_add_fusion.2), channel_id=1, source_target_pairs={{0,8},{8,16},{16,24},{24,32},{32,40},{40,48},{48,56},{56,64},{64,7... | collective-permute-start | bytes 1572872 | tf_op jit(solution)/shard_map/while/body/eval_jaxpr/ppermute | solution.py:12
  277.0 11.9 %collective-permute-start.1 = (f32[128,1024]{1,0:T(8,128)S(1)}, f32[128,1024]{1,0:T(8,128)S(1)}, u32[]{:S(2)}, u32[]{:S(2)}) collective-permute-start(f32[128,1024]{1,0:T(8,128)S(1)} %convolution_add_fusion.2), channel_id=1, source_target_pairs={{0,8},{8,16},{16,24},{24,32},{32,40},{40,48},{48,56},{56,64},{64,7... | collective-permute-start | bytes 1572872 | tf_op jit(solution)/shard_map/while/body/eval_jaxpr/ppermute | solution.py:12
  292.9 12.4 %collective-permute-start.1 = (f32[128,1024]{1,0:T(8,128)S(1)}, f32[128,1024]{1,0:T(8,128)S(1)}, u32[]{:S(2)}, u32[]{:S(2)}) collective-permute-start(f32[128,1024]{1,0:T(8,128)S(1)} %convolution_add_fusion.2), channel_id=1, source_target_pairs={{0,8},{8,16},{16,24},{24,32},{32,40},{40,48},{48,56},{56,64},{64,7... | collective-permute-start | bytes 1572872 | tf_op jit(solution)/shard_map/while/body/eval_jaxpr/ppermute | solution.py:12
  309.1 12.9 %collective-permute-start.1 = (f32[128,1024]{1,0:T(8,128)S(1)}, f32[128,1024]{1,0:T(8,128)S(1)}, u32[]{:S(2)}, u32[]{:S(2)}) collective-permute-start(f32[128,1024]{1,0:T(8,128)S(1)} %convolution_add_fusion.2), channel_id=1, source_target_pairs={{0,8},{8,16},{16,24},{24,32},{32,40},{40,48},{48,56},{56,64},{64,7... | collective-permute-start | bytes 1572872 | tf_op jit(solution)/shard_map/while/body/eval_jaxpr/ppermute | solution.py:12
  326.0 13.6 %collective-permute-start.1 = (f32[128,1024]{1,0:T(8,128)S(1)}, f32[128,1024]{1,0:T(8,128)S(1)}, u32[]{:S(2)}, u32[]{:S(2)}) collective-permute-start(f32[128,1024]{1,0:T(8,128)S(1)} %convolution_add_fusion.2), channel_id=1, source_target_pairs={{0,8},{8,16},{16,24},{24,32},{32,40},{40,48},{48,56},{56,64},{64,7... | collective-permute-start | bytes 1572872 | tf_op jit(solution)/shard_map/while/body/eval_jaxpr/ppermute | solution.py:12
  343.4 13.6 %collective-permute-start.1 = (f32[128,1024]{1,0:T(8,128)S(1)}, f32[128,1024]{1,0:T(8,128)S(1)}, u32[]{:S(2)}, u32[]{:S(2)}) collective-permute-start(f32[128,1024]{1,0:T(8,128)S(1)} %convolution_add_fusion.2), channel_id=1, source_target_pairs={{0,8},{8,16},{16,24},{24,32},{32,40},{40,48},{48,56},{56,64},{64,7... | collective-permute-start | bytes 1572872 | tf_op jit(solution)/shard_map/while/body/eval_jaxpr/ppermute | solution.py:12
  345.8 11.2 %collective-permute-start = (bf16[128,1024]{1,0:T(8,128)(2,1)S(1)}, bf16[128,1024]{1,0:T(8,128)(2,1)S(1)}, u32[]{:S(2)}, u32[]{:S(2)}) collective-permute-start(bf16[128,1024]{1,0:T(8,128)(2,1)S(1)} %copy.27), channel_id=1, source_target_pairs={{0,8},{8,16},{16,24},{24,32},{32,40},{40,48},{48,56},{56,64},{64,7... | collective-permute-start | bytes 786440 | tf_op jit(solution)/shard_map/while/body/eval_jaxpr/ppermute | solution.py:12
  360.9 13.6 %collective-permute-start.1 = (f32[128,1024]{1,0:T(8,128)S(1)}, f32[128,1024]{1,0:T(8,128)S(1)}, u32[]{:S(2)}, u32[]{:S(2)}) collective-permute-start(f32[128,1024]{1,0:T(8,128)S(1)} %convolution_add_fusion.2), channel_id=1, source_target_pairs={{0,8},{8,16},{16,24},{24,32},{32,40},{40,48},{48,56},{56,64},{64,7... | collective-permute-start | bytes 1572872 | tf_op jit(solution)/shard_map/while/body/eval_jaxpr/ppermute | solution.py:12
  362.1 12.4 %collective-permute-start = (bf16[128,1024]{1,0:T(8,128)(2,1)S(1)}, bf16[128,1024]{1,0:T(8,128)(2,1)S(1)}, u32[]{:S(2)}, u32[]{:S(2)}) collective-permute-start(bf16[128,1024]{1,0:T(8,128)(2,1)S(1)} %copy.27), channel_id=1, source_target_pairs={{0,8},{8,16},{16,24},{24,32},{32,40},{40,48},{48,56},{56,64},{64,7... | collective-permute-start | bytes 786440 | tf_op jit(solution)/shard_map/while/body/eval_jaxpr/ppermute | solution.py:12
  378.4 13.6 %collective-permute-start.1 = (f32[128,1024]{1,0:T(8,128)S(1)}, f32[128,1024]{1,0:T(8,128)S(1)}, u32[]{:S(2)}, u32[]{:S(2)}) collective-permute-start(f32[128,1024]{1,0:T(8,128)S(1)} %convolution_add_fusion.2), channel_id=1, source_target_pairs={{0,8},{8,16},{16,24},{24,32},{32,40},{40,48},{48,56},{56,64},{64,7... | collective-permute-start | bytes 1572872 | tf_op jit(solution)/shard_map/while/body/eval_jaxpr/ppermute | solution.py:12
  378.5 13.5 %collective-permute-start = (bf16[128,1024]{1,0:T(8,128)(2,1)S(1)}, bf16[128,1024]{1,0:T(8,128)(2,1)S(1)}, u32[]{:S(2)}, u32[]{:S(2)}) collective-permute-start(bf16[128,1024]{1,0:T(8,128)(2,1)S(1)} %copy.27), channel_id=1, source_target_pairs={{0,8},{8,16},{16,24},{24,32},{32,40},{40,48},{48,56},{56,64},{64,7... | collective-permute-start | bytes 786440 | tf_op jit(solution)/shard_map/while/body/eval_jaxpr/ppermute | solution.py:12
  395.8 13.6 %collective-permute-start.1 = (f32[128,1024]{1,0:T(8,128)S(1)}, f32[128,1024]{1,0:T(8,128)S(1)}, u32[]{:S(2)}, u32[]{:S(2)}) collective-permute-start(f32[128,1024]{1,0:T(8,128)S(1)} %convolution_add_fusion.2), channel_id=1, source_target_pairs={{0,8},{8,16},{16,24},{24,32},{32,40},{40,48},{48,56},{56,64},{64,7... | collective-permute-start | bytes 1572872 | tf_op jit(solution)/shard_map/while/body/eval_jaxpr/ppermute | solution.py:12
  395.9 13.5 %collective-permute-start = (bf16[128,1024]{1,0:T(8,128)(2,1)S(1)}, bf16[128,1024]{1,0:T(8,128)(2,1)S(1)}, u32[]{:S(2)}, u32[]{:S(2)}) collective-permute-start(bf16[128,1024]{1,0:T(8,128)(2,1)S(1)} %copy.27), channel_id=1, source_target_pairs={{0,8},{8,16},{16,24},{24,32},{32,40},{40,48},{48,56},{56,64},{64,7... | collective-permute-start | bytes 786440 | tf_op jit(solution)/shard_map/while/body/eval_jaxpr/ppermute | solution.py:12
  413.3 13.6 %collective-permute-start.1 = (f32[128,1024]{1,0:T(8,128)S(1)}, f32[128,1024]{1,0:T(8,128)S(1)}, u32[]{:S(2)}, u32[]{:S(2)}) collective-permute-start(f32[128,1024]{1,0:T(8,128)S(1)} %convolution_add_fusion.2), channel_id=1, source_target_pairs={{0,8},{8,16},{16,24},{24,32},{32,40},{40,48},{48,56},{56,64},{64,7... | collective-permute-start | bytes 1572872 | tf_op jit(solution)/shard_map/while/body/eval_jaxpr/ppermute | solution.py:12
  413.4 13.5 %collective-permute-start = (bf16[128,1024]{1,0:T(8,128)(2,1)S(1)}, bf16[128,1024]{1,0:T(8,128)(2,1)S(1)}, u32[]{:S(2)}, u32[]{:S(2)}) collective-permute-start(bf16[128,1024]{1,0:T(8,128)(2,1)S(1)} %copy.27), channel_id=1, source_target_pairs={{0,8},{8,16},{16,24},{24,32},{32,40},{40,48},{48,56},{56,64},{64,7... | collective-permute-start | bytes 786440 | tf_op jit(solution)/shard_map/while/body/eval_jaxpr/ppermute | solution.py:12
  430.8 13.6 %collective-permute-start.1 = (f32[128,1024]{1,0:T(8,128)S(1)}, f32[128,1024]{1,0:T(8,128)S(1)}, u32[]{:S(2)}, u32[]{:S(2)}) collective-permute-start(f32[128,1024]{1,0:T(8,128)S(1)} %convolution_add_fusion.2), channel_id=1, source_target_pairs={{0,8},{8,16},{16,24},{24,32},{32,40},{40,48},{48,56},{56,64},{64,7... | collective-permute-start | bytes 1572872 | tf_op jit(solution)/shard_map/while/body/eval_jaxpr/ppermute | solution.py:12
  430.9 13.5 %collective-permute-start = (bf16[128,1024]{1,0:T(8,128)(2,1)S(1)}, bf16[128,1024]{1,0:T(8,128)(2,1)S(1)}, u32[]{:S(2)}, u32[]{:S(2)}) collective-permute-start(bf16[128,1024]{1,0:T(8,128)(2,1)S(1)} %copy.27), channel_id=1, source_target_pairs={{0,8},{8,16},{16,24},{24,32},{32,40},{40,48},{48,56},{56,64},{64,7... | collective-permute-start | bytes 786440 | tf_op jit(solution)/shard_map/while/body/eval_jaxpr/ppermute | solution.py:12
  448.3 13.6 %collective-permute-start.1 = (f32[128,1024]{1,0:T(8,128)S(1)}, f32[128,1024]{1,0:T(8,128)S(1)}, u32[]{:S(2)}, u32[]{:S(2)}) collective-permute-start(f32[128,1024]{1,0:T(8,128)S(1)} %convolution_add_fusion.2), channel_id=1, source_target_pairs={{0,8},{8,16},{16,24},{24,32},{32,40},{40,48},{48,56},{56,64},{64,7... | collective-permute-start | bytes 1572872 | tf_op jit(solution)/shard_map/while/body/eval_jaxpr/ppermute | solution.py:12
  448.3 13.5 %collective-permute-start = (bf16[128,1024]{1,0:T(8,128)(2,1)S(1)}, bf16[128,1024]{1,0:T(8,128)(2,1)S(1)}, u32[]{:S(2)}, u32[]{:S(2)}) collective-permute-start(bf16[128,1024]{1,0:T(8,128)(2,1)S(1)} %copy.27), channel_id=1, source_target_pairs={{0,8},{8,16},{16,24},{24,32},{32,40},{40,48},{48,56},{56,64},{64,7... | collective-permute-start | bytes 786440 | tf_op jit(solution)/shard_map/while/body/eval_jaxpr/ppermute | solution.py:12
  470.4 145.0 %all-gather.8.cloned.1.call-start = ((), (), s32[]{:S(2)}) async-start(), calls=%async_computation.7 | async-start | bytes 2359296 | tf_op jit(solution)/shard_map/all_gather | solution.py:104
  559.0 115.6 %all-gather.6.cloned.1.call-start = ((), (), s32[]{:S(2)}) async-start(), calls=%async_computation.6 | async-start | bytes 2359296 | tf_op jit(solution)/shard_map/all_gather | solution.py:103
  559.6 175.0 %reduce-scatter.11.cloned.1.call-start = ((), (), s32[]{:S(2)}) async-start(), calls=%async_computation.9 | async-start | bytes 1114112 | tf_op jit(solution)/shard_map/reduce_scatter | solution.py:122
  619.6 178.4 %reduce-scatter.9.cloned.1.call-start = ((), (), s32[]{:S(2)}) async-start(), calls=%async_computation.8 | async-start | bytes 1671168 | tf_op jit(solution)/shard_map/reduce_scatter | solution.py:119
  (31 other events, 368.2 us)
Sparse Core Ops, SparseCore 0:
  17.5 115.9 reduce-scatter.6
  136.9 55.3 all-gather.3
  470.6 85.0 reduce-scatter.12
  559.2 56.2 all-gather.7
  618.3 56.2 all-gather.5
  677.0 57.5 reduce-scatter.10
  737.0 60.9 reduce-scatter.8
where the time goes:
time: 812 us; the launch traced here: 806 us
  waiting for transfers between devices  536 us (66%)
  matrix products  157 us (19%)
  starting transfers between devices  68.4 us (8%)
  local copies, waits for them, and re-layouts  16.5 us (2%)
  between operations  15 us (2%)
  other arithmetic  12.7 us (2%)
    reduce_scatter x1, waiting for transfers between devices, local(): lax.psum_scatter(jnp.concatenate([jnp.dot(img_feat, img_weight, preferred...  116 us
    unnamed x8, waiting for transfers between devices  84.8 us
    dot_general x16, matrix products, cross_contributions(): lax.dot_general(derivative_multiplier, caption_submatrix, (((0,), (0,)),...  75.6 us
    ppermute x32, starting transfers between devices, shifted(): return lax.ppermute(value, axis, pairs)  67.9 us
    reduce_scatter x1, waiting for transfers between devices, local(): lax.psum_scatter(img_wpart.astype(jnp.bfloat16), 'blk', scatter_dimension...  61.9 us
    ppermute x32, waiting for transfers between devices, shifted(): return lax.ppermute(value, axis, pairs)  59.8 us
    all_gather x1, waiting for transfers between devices, local(): lax.all_gather(txt_egrad, 'mp', axis=0, tiled=True)  55.8 us
    all_gather x1, waiting for transfers between devices, local(): lax.all_gather(img_egrad, 'mp', axis=0, tiled=True)  54.8 us
  transfers between devices with their start and end apart: 39, of which 21 were waited for; matrix products, arithmetic and copies ran while one was open for 12% of the time, Pallas kernels for 0%

commit v1 on v0

v1 whole, which is shorter than its diff:
```python
import jax
import jax.numpy as jnp
from jax import lax
from jax.experimental import pallas as pl
from jax.experimental.pallas import tpu as pltpu
from jax.sharding import PartitionSpec as P

EPS = 1e-06
BF16 = jnp.bfloat16
F32 = jnp.float32
VMEM_LIMIT = 48 * 1024 * 1024


def swap(value, axis, offset):
    count = lax.axis_size(axis)
    return lax.ppermute(value, axis, [(i, i ^ offset) for i in range(count)])


def shape(*dims, dtype=BF16):
    return jax.ShapeDtypeStruct(dims, dtype)


def call(name, body, outs, ins, flops=0, grid_spec=None, scratch=()):
    if grid_spec is None:
        layout = dict(scratch_shapes=list(scratch))
    else:
        layout = dict(grid_spec=grid_spec)
    moved = sum(a.size * a.dtype.itemsize for a in list(ins) + list(outs))
    return pl.pallas_call(
        body,
        out_shape=outs,
        compiler_params=pltpu.CompilerParams(vmem_limit_bytes=VMEM_LIMIT),
        cost_estimate=pl.CostEstimate(flops=flops, bytes_accessed=moved, transcendentals=0),
        name=name,
        **layout,
    )(*ins)


def wide(ref, block=None):
    return (ref[...] if block is None else ref[block]).astype(F32)


def embed(name, feat, weight, column, blocks, tile=256):
    rows, width = feat.shape
    columns = weight.shape[1]
    own = rows // blocks

    def body(column_ref, feat_ref, weight_ref, p01, p23, p67, p4, p5, product):
        product[...] = jnp.dot(feat_ref[...], weight_ref[...], preferred_element_type=F32).astype(BF16)

        def part(k):
            return product[pl.ds(pl.multiple_of((column_ref[0] ^ k) * own, own), own)]

        for k in range(2):
            p01[k] = part(k)
            p23[k] = part(2 + k)
            p67[k] = part(6 + k)
        p4[...] = part(4)
        p5[...] = part(5)

    pair = pl.BlockSpec((2, own, tile), lambda i, c: (0, 0, i))
    single = pl.BlockSpec((own, tile), lambda i, c: (0, i))
    grid_spec = pltpu.PrefetchScalarGridSpec(
        num_scalar_prefetch=1,
        grid=(columns // tile,),
        in_specs=[
            pl.BlockSpec((rows, width), lambda i, c: (0, 0)),
            pl.BlockSpec((width, tile), lambda i, c: (0, i)),
        ],
        out_specs=[pair, pair, pair, single, single],
        scratch_shapes=[pltpu.VMEM((rows, tile), BF16)],
    )
    outs = [shape(2, own, columns)] * 3 + [shape(own, columns)] * 2
    return call(name, body, outs, (column, feat, weight), 2 * rows * width * columns, grid_spec)


def relay_add(p23, p67, r4, r5, out23, out67):
    out23[0] = (wide(p23, 0) + wide(r4)).astype(BF16)
    out23[1] = p23[1]
    out67[0] = p67[0]
    out67[1] = (wide(p67, 1) + wide(r5)).astype(BF16)


def unit_of(embedded):
    inverse = lax.rsqrt(jnp.sum(embedded * embedded, axis=1, keepdims=True) + EPS)
    return embedded * inverse, inverse


def norm_back(unit_grad, embedded):
    unit, inverse = unit_of(embedded)
    return inverse * (unit_grad - unit * jnp.sum(unit * unit_grad, axis=1, keepdims=True))


def flat(ref):
    return ref[...].reshape(-1, ref.shape[-1])


def rows_of(*refs):
    return jnp.concatenate([flat(ref) for ref in refs], axis=0)


def factors(scale, bias, txt, img):
    affinity = lax.dot_general(txt, img, (((1,), (1,)), ((), ())), preferred_element_type=F32)
    logits = scale * affinity + bias
    return logits, (scale / (1.0 + jnp.exp(-logits))).astype(BF16)


def product(first, second):
    return jnp.dot(first, second, preferred_element_type=F32)


def pair_call(name, body, outs, scale, bias, arrays, flops):
    smem = pl.BlockSpec(memory_space=pltpu.SMEM)
    vmem = pl.BlockSpec(memory_space=pltpu.VMEM)
    moved = sum(a.size * a.dtype.itemsize for a in list(arrays) + outs)
    return pl.pallas_call(
        body,
        in_specs=[smem, smem] + [vmem] * len(arrays),
        out_shape=outs,
        compiler_params=pltpu.CompilerParams(vmem_limit_bytes=VMEM_LIMIT),
        cost_estimate=pl.CostEstimate(flops=flops, bytes_accessed=moved, transcendentals=0),
        name=name,
    )(scale, bias, *arrays)


def pairs_near(scale, bias, even, odd, near):
    own, width = even.shape[-2:]
    texts, images = 12 * own, 6 * own

    def body(scale_ref, bias_ref, even, odd, u01, u23, u67, out, flipped):
        scale, bias = scale_ref[0], bias_ref[0]
        for t, txt_ref in enumerate((even, odd)):
            rows = slice(t * 6 * own, (t + 1) * 6 * own)
            for i, img_ref in enumerate((u01, u23, u67)):
                columns = slice(i * 2 * own, (i + 1) * 2 * own)
                logits, factor = factors(scale, bias, flat(txt_ref), flat(img_ref))
                if t == 0 and i == 0:
                    row = lax.broadcasted_iota(jnp.int32, logits.shape, 0)
                    column = lax.broadcasted_iota(jnp.int32, logits.shape, 1)
                    pull = (-scale / (1.0 + jnp.exp(logits))).astype(BF16)
                    factor = jnp.where((row == column) & (row < own), pull, factor)
                out[rows, columns] = factor
                flipped[columns, rows] = factor.T

    outs = [shape(texts, images), shape(images, texts)]
    return pair_call("pairs_near", body, outs, scale, bias, (even, odd, *near), 2 * texts * images * width)


def pairs_far(scale, bias, even, odd, far, near, u4, u5):
    own, width = u4.shape
    texts, images = 12 * own, 6 * own

    def body(scale_ref, bias_ref, even, odd, a8, a10, a9, a11, u01, u23, u67, u4, u5, near_far, far_near, far_flip, far_far, g4, g5):
        scale, bias = scale_ref[0], bias_ref[0]
        far_images = rows_of(u4, u5)
        far_texts = rows_of(a8, a10, a9, a11)
        total = jnp.zeros((2 * own, width), F32)
        for t, txt_ref in enumerate((even, odd)):
            factor = factors(scale, bias, flat(txt_ref), far_images)[1]
            near_far[t * 6 * own : (t + 1) * 6 * own] = factor
            total = total + product(factor.T, flat(txt_ref))
        factor = factors(scale, bias, far_texts, far_images)[1]
        far_far[...] = factor
        total = total + product(factor.T, far_texts)
        g4[...] = total[:own].astype(BF16)
        g5[...] = total[own:].astype(BF16)
        for i, img_ref in enumerate((u01, u23, u67)):
            columns = slice(i * 2 * own, (i + 1) * 2 * own)
            factor = factors(scale, bias, far_texts, flat(img_ref))[1]
            far_near[:, columns] = factor
            far_flip[columns] = factor.T

    outs = [
        shape(texts, 2 * own),
        shape(4 * own, images),
        shape(images, 4 * own),
        shape(4 * own, 2 * own),
        shape(own, width),
        shape(own, width),
    ]
    flops = 2 * width * own * own * (16 * 2 * 2 + 4 * 6)
    return pair_call("pairs_far", body, outs, scale, bias, (even, odd, *far, *near, u4, u5), flops)


def text_grads(out, start, far_start, near_near, near_far, far_near, far_far, image_refs, own):
    width = out.shape[-1]
    near_rows = jnp.concatenate(
        [near_near[start : start + 6 * own], near_far[start : start + 6 * own]], axis=1
    )
    far_rows = jnp.concatenate(
        [far_near[far_start : far_start + 2 * own], far_far[far_start : far_start + 2 * own]], axis=1
    )
    all_rows = jnp.concatenate([near_rows, far_rows], axis=0)
    for at in range(0, width, 256):
        images = jnp.concatenate(
            [ref[:, :, at : at + 256].reshape(-1, 256) for ref in image_refs[:3]]
            + [ref[:, at : at + 256] for ref in image_refs[3:]],
            axis=0,
        )
        out[:, :, at : at + 256] = product(all_rows, images).astype(BF16).reshape(8, own, 256)


def pairs_odd(scale, bias, near_near, near_far, far_near, far_far, images):
    own, width = images[-1].shape

    def body(scale_ref, bias_ref, near_near, near_far, far_near, far_far, u01, u23, u67, u4, u5, out):
        text_grads(out, 6 * own, 2 * own, near_near, near_far, far_near, far_far, (u01, u23, u67, u4, u5), own)

    flops = 2 * 8 * 8 * own * own * width
    arrays = (near_near, near_far, far_near, far_far, *images)
    return pair_call("pairs_odd", body, [shape(8, own, width)], scale, bias, arrays, flops)[0]


def pairs_rest(scale, bias, near_near, near_far, far_near, far_far, images, near_flip, far_flip, even, odd, far):
    own, width = images[-1].shape

    def body(*refs):
        near_near, near_far, far_near, far_far = refs[2:6]
        image_refs, (near_flip, far_flip, even, odd), far = refs[6:11], refs[11:15], refs[15:19]
        g01, g23, g67, out = refs[19:]
        text_grads(out, 0, 0, near_near, near_far, far_near, far_far, image_refs, own)
        for at in range(0, width, 256):
            columns = slice(at, at + 256)
            texts = [ref[:, :, columns].reshape(-1, 256) for ref in (even, odd)]
            far_texts = jnp.concatenate([ref[:, columns] for ref in far], axis=0)
            total = product(near_flip[:, : 6 * own], texts[0])
            total = total + product(near_flip[:, 6 * own :], texts[1])
            total = total + product(far_flip[...], far_texts)
            total = total.astype(BF16).reshape(3, 2, own, 256)
            g01[:, :, columns] = total[0]
            g23[:, :, columns] = total[1]
            g67[:, :, columns] = total[2]

    flops = 2 * own * own * width * (8 * 8 + 6 * 16)
    arrays = (near_near, near_far, far_near, far_far, *images, near_flip, far_flip, even, odd, *far)
    outs = [shape(2, own, width)] * 3 + [shape(8, own, width)]
    return pair_call("pairs_rest", body, outs, scale, bias, arrays, flops)


def in_index_order(e01, e23, e67, e4, e5):
    return [e01.at[0], e01.at[1], e23.at[0], e23.at[1], e4, e5, e67.at[0], e67.at[1]]


def weight_part(name, column, place, pieces, feat):
    own, width = pieces[-1].shape
    rows, features = feat.shape
    strip = width // 16
    tile = 256

    def body(column_ref, place_ref, e01, e23, e67, e4, e5, feat_ref, same, other, flipped, moved, result):
        @pl.when(pl.program_id(0) == 0)
        def _():
            for k, block in enumerate(in_index_order(e01, e23, e67, e4, e5)):
                flipped[:, k * own : (k + 1) * own] = block[...].T

        for k in range(rows // own):
            start = pl.multiple_of((column_ref[0] ^ k) * own, own)
            moved[k * own : (k + 1) * own] = feat_ref[pl.ds(start, own)]
        result[...] = product(flipped[...], moved[...]).astype(BF16)
        core = place_ref[0] & 1
        for j in range(8):
            mine = pl.multiple_of((2 * j + core) * strip, strip)
            theirs = pl.multiple_of((2 * j + 1 - core) * strip, strip)
            same[j] = result[pl.ds(mine, strip)]
            other[j] = result[pl.ds(theirs, strip)]

    def whole(array):
        zeros = (0,) * array.ndim
        return pl.BlockSpec(array.shape, lambda i, c, p: zeros)

    strips = pl.BlockSpec((8, strip, tile), lambda i, c, p: (0, 0, i))
    grid_spec = pltpu.PrefetchScalarGridSpec(
        num_scalar_prefetch=2,
        grid=(features // tile,),
        in_specs=[whole(piece) for piece in pieces] + [pl.BlockSpec((rows, tile), lambda i, c, p: (0, i))],
        out_specs=[strips, strips],
        scratch_shapes=[
            pltpu.VMEM((width, rows), BF16),
            pltpu.VMEM((rows, tile), BF16),
            pltpu.VMEM((width, tile), BF16),
        ],
    )
    outs = [shape(8, strip, features)] * 2
    return call(name, body, outs, (column, place, *pieces, feat), 2 * rows * width * features, grid_spec)


def feature_grad(name, column, pieces, weight):
    own, width = pieces[-1].shape
    features = weight.shape[0]
    rows = 8 * own
    tile = 256

    def body(column_ref, e01, e23, e67, e4, e5, weight_ref, out):
        egrad = rows_of(e01, e23, e4, e5, e67)
        result = lax.dot_general(
            egrad, weight_ref[...], (((1,), (1,)), ((), ())), preferred_element_type=F32
        ).astype(BF16)
        for k in range(rows // own):
            start = pl.multiple_of((column_ref[0] ^ k) * own, own)
            out[pl.ds(start, own)] = result[k * own : (k + 1) * own]

    def whole(array):
        zeros = (0,) * array.ndim
        return pl.BlockSpec(array.shape, lambda i, c: zeros)

    grid_spec = pltpu.PrefetchScalarGridSpec(
        num_scalar_prefetch=1,
        grid=(features // tile,),
        in_specs=[whole(piece) for piece in pieces] + [pl.BlockSpec((tile, width), lambda i, c: (i, 0))],
        out_specs=[pl.BlockSpec((rows, tile), lambda i, c: (0, i))],
    )
    outs = shape(rows, features)
    moved = (column, *pieces, weight)
    return call(name, body, [outs], moved, 2 * rows * width * features, grid_spec)[0]


def sum_weight(same, other):
    def body(same_ref, got_ref, out):
        out[...] = (wide(same_ref) + wide(got_ref)).astype(BF16)

    got = swap(other, "blk", 1)
    (chip,) = call("weight_chip", body, [shape(*same.shape)], (same, got))
    groups = [list(range(core, 16, 2)) for core in range(2)]
    parts = lax.all_to_all(chip, "blk", 0, 0, axis_index_groups=groups, tiled=True)
    return jnp.sum(parts.astype(F32), axis=0).T


def local(img_feat, txt_feat, img_weight, txt_weight, natural_exponent_multiplier, bias):
    scale = jnp.exp(natural_exponent_multiplier)
    blocks = lax.axis_size("mp")
    column = lax.axis_index("mp").astype(jnp.int32)[None]
    place = lax.axis_index("blk").astype(jnp.int32)[None]
    own = img_feat.shape[0] // blocks
    width = img_weight.shape[1]
    one, two = (own, width), (2, own, width)

    t01, t23, t67, t4, t5 = embed("embed_text", txt_feat, txt_weight, column, blocks)
    t4, t5 = swap(t4, "mp", 6), swap(t5, "mp", 2)
    i01, i23, i67, i4, i5 = embed("embed_image", img_feat, img_weight, column, blocks)
    t23, t67 = call("relay_text", relay_add, [shape(*two)] * 2, (t23, t67, t4, t5))
    t23, t67 = swap(t23, "mp", 2), swap(t67, "mp", 6)
    i4, i5 = swap(i4, "mp", 6), swap(i5, "mp", 2)

    def second(t01, t23, t67, i23, i67, i4, i5, t0_out, t1_out, i23_out, i67_out):
        t0_out[...] = wide(t01, 0) + wide(t23, 0) + wide(t67, 0)
        t1_out[...] = (wide(t01, 1) + wide(t23, 1) + wide(t67, 1)).astype(BF16)
        relay_add(i23, i67, i4, i5, i23_out, i67_out)

    t0, t1, i23, i67 = call(
        "sums_second",
        second,
        [shape(*one, dtype=F32), shape(*one), shape(*two), shape(*two)],
        (t01, t23, t67, i23, i67, i4, i5),
    )
    t1 = swap(t1, "mp", 1)
    i23, i67 = swap(i23, "mp", 2), swap(i67, "mp", 6)

    def third(t0, t1, i01, i23, i67, text_out, unit_out, i01_out):
        embedded = t0[...] + wide(t1)
        text_out[...] = embedded
        unit_out[...] = unit_of(embedded)[0].astype(BF16)
        for k in range(2):
            i01_out[k] = (wide(i01, k) + wide(i23, k) + wide(i67, k)).astype(BF16)

    txt_emb, a0, i01 = call(
        "sums_third",
        third,
        [shape(*one, dtype=F32), shape(*one), shape(*two)],
        (t0, t1, i01, i23, i67),
    )
    a2 = swap(a0, "blk", 2)
    got01 = swap(i01, "mp", 1)

    def fourth(a0, a2, i01, got01, a02_out, emb_out, unit_out):
        a02_out[0] = a0[...]
        a02_out[1] = a2[...]
        for k in range(2):
            embedded = wide(i01, k) + wide(got01, 1 - k)
            emb_out[k] = embedded
            unit_out[k] = unit_of(embedded)[0].astype(BF16)

    a02, img_emb, u01 = call(
        "sums_fourth",
        fourth,
        [shape(*two), shape(*two, dtype=F32), shape(*two)],
        (a0, a2, i01, got01),
    )

    a46, a1214 = swap(a02, "blk", 4), swap(a02, "blk", 12)
    u23, u67 = swap(u01, "mp", 2), swap(u01, "mp", 6)

    def joined(a02, a46, a1214, u23, u67, even_out, a4_out, a14_out, u2_out, u7_out):
        even_out[0:2] = a02[...]
        even_out[2:4] = a46[...]
        even_out[4:6] = a1214[...]
        a4_out[...] = a46[0]
        a14_out[...] = a1214[1]
        u2_out[...] = u23[0]
        u7_out[...] = u67[1]

    even, a8, a10, u4, u5 = call(
        "join", joined, [shape(6, *one)] + [shape(*one)] * 4, (a02, a46, a1214, u23, u67)
    )
    odd = swap(even, "blk", 1)
    a8, a10 = swap(a8, "blk", 12), swap(a10, "blk", 4)
    u4, u5 = swap(u4, "mp", 6), swap(u5, "mp", 2)
    a9, a11 = swap(a8, "blk", 1), swap(a10, "blk", 1)
    near, far, images = (u01, u23, u67), (a8, a10, a9, a11), (u01, u23, u67, u4, u5)
    near_near, near_flip = pairs_near(scale, bias, even, odd, near)
    near_far, far_near, far_flip, far_far, g4, g5 = pairs_far(scale, bias, even, odd, far, near, u4, u5)
    g4, g5 = swap(g4, "mp", 6), swap(g5, "mp", 2)
    factor_parts = (near_near, near_far, far_near, far_far)
    odd_sum = pairs_odd(scale, bias, *factor_parts, images)
    odd_got = swap(odd_sum, "blk", 1)
    g01, g23, g67, even_sum = pairs_rest(
        scale, bias, *factor_parts, images, near_flip, far_flip, even, odd, far
    )

    def fifth(even, got, g23, g67, g4, g5, p8, p10, g23_out, g67_out):
        p8[...] = (wide(even, 6) + wide(got, 6)).astype(BF16)
        p10[...] = (wide(even, 7) + wide(got, 7)).astype(BF16)
        relay_add(g23, g67, g4, g5, g23_out, g67_out)

    p8, p10, g23, g67 = call(
        "sums_fifth",
        fifth,
        [shape(*one), shape(*one), shape(*two), shape(*two)],
        (even_sum, odd_got, g23, g67, g4, g5),
    )
    g23, g67 = swap(g23, "mp", 2), swap(g67, "mp", 6)
    p8, p10 = swap(p8, "blk", 12), swap(p10, "blk", 4)

    def sixth(even, got, p8, p10, g01, g23, g67, p02, p46, p1214, g01_out):
        for k in range(2):
            p02[k] = (wide(even, k) + wide(got, k)).astype(BF16)
            g01_out[k] = (wide(g01, k) + wide(g23, k) + wide(g67, k)).astype(BF16)
        p46[0] = (wide(even, 2) + wide(got, 2) + wide(p8)).astype(BF16)
        p46[1] = (wide(even, 3) + wide(got, 3)).astype(BF16)
        p1214[0] = (wide(even, 4) + wide(got, 4)).astype(BF16)
        p1214[1] = (wide(even, 5) + wide(got, 5) + wide(p10)).astype(BF16)

    p02, p46, p1214, g01 = call(
        "sums_sixth", sixth, [shape(*two)] * 4, (even_sum, odd_got, p8, p10, g01, g23, g67)
    )
    g01_got = swap(g01, "mp", 1)
    p46, p1214 = swap(p46, "blk", 4), swap(p1214, "blk", 12)

    def seventh(p02, p46, p1214, g01, g01_got, img_emb, p0_out, p2_out, e01_out):
        p0_out[...] = wide(p02, 0) + wide(p46, 0) + wide(p1214, 0)
        p2_out[...] = (wide(p02, 1) + wide(p46, 1) + wide(p1214, 1)).astype(BF16)
        for k in range(2):
            unit_grad = wide(g01, k) + wide(g01_got, 1 - k)
            e01_out[k] = norm_back(unit_grad, img_emb[k]).astype(BF16)

    p0, p2, e01 = call(
        "sums_seventh",
        seventh,
        [shape(*one, dtype=F32), shape(*one), shape(*two)],
        (p02, p46, p1214, g01, g01_got, img_emb),
    )
    p2 = swap(p2, "blk", 2)
    e23, e67 = swap(e01, "mp", 2), swap(e01, "mp", 6)

    def eighth(p0, p2, txt_emb, out):
        out[...] = norm_back(p0[...] + wide(p2), txt_emb[...]).astype(BF16)

    (d0,) = call("sums_eighth", eighth, [shape(*one)], (p0, p2, txt_emb))
    d1 = swap(d0, "mp", 1)

    def ninth(d0, d1, e23, e67, d01_out, e2_out, e7_out):
        d01_out[0] = d0[...]
        d01_out[1] = d1[...]
        e2_out[...] = e23[0]
        e7_out[...] = e67[1]

    d01, e4, e5 = call("join_ninth", ninth, [shape(*two), shape(*one), shape(*one)], (d0, d1, e23, e67))
    e4, e5 = swap(e4, "mp", 6), swap(e5, "mp", 2)
    d23, d67 = swap(d01, "mp", 2), swap(d01, "mp", 6)
    e_all = (e01, e23, e67, e4, e5)
    img_weight_grad = sum_weight(*weight_part("weight_image", column, place, e_all, img_feat))
    d4, d5 = swap(d23[0], "mp", 6), swap(d67[1], "mp", 2)
    d_all = (d01, d23, d67, d4, d5)
    txt_weight_grad = sum_weight(*weight_part("weight_text", column, place, d_all, txt_feat))
    return (
        feature_grad("feature_image", column, e_all, img_weight),
        feature_grad("feature_text", column, d_all, txt_weight),
        img_weight_grad,
        txt_weight_grad,
    )


def solution(mesh):
    return jax.shard_map(
        local,
        mesh=mesh,
        in_specs=(P("blk", "mp"), P("blk", "mp"), P("mp", None), P("mp", None), P(), P()),
        out_specs=(P("blk", "mp"), P("blk", "mp"), P("mp", "blk"), P("mp", "blk")),
        check_vma=False,
    )
```

time: 812 us -> 236 us (0.29)
  waiting for transfers between devices: 536 us -> 106 us
  matrix products: 157 us -> 0 us
  Pallas kernels: 0 us -> 55.6 us
  between operations: 15 us -> 2.26 us
  starting transfers between devices: 68.4 us -> 56.5 us
  other arithmetic: 12.7 us -> 3.71 us
    reduce_scatter x3 -> x0, waiting for transfers between devices: 226 us -> none  [the longest x1 116 us: local(): lax.psum_scatter(jnp.concatenate([jnp.dot(img_feat, img_weight, preferred...]
    all_gather x3 -> x0, waiting for transfers between devices: 165 us -> none  [the longest x1 55.8 us: local(): lax.all_gather(txt_egrad, 'mp', axis=0, tiled=True)]
    dot_general x54 -> x0, matrix products: 157 us -> none  [the longest x16 75.6 us: cross_contributions(): lax.dot_general(derivative_multiplier, caption_submatrix, (((0,), (0,)),...]
    unnamed x8 -> x0, waiting for transfers between devices: 84.8 us -> none
    pallas_call x0 -> x22, Pallas kernels: none -> 55.6 us  [the longest x18 28.2 us: call(): pl.pallas_call(body, out_shape=outs, compiler_params=pltpu.CompilerParams...]
    ppermute x32 -> x44, waiting for transfers between devices: 59.8 us -> 103 us  [swap(): return lax.ppermute(value, axis, [(i, i ^ offset) for i in range(count)])]
    ppermute x32 -> x44, starting transfers between devices: 67.9 us -> 46.4 us  [swap(): return lax.ppermute(value, axis, [(i, i ^ offset) for i in range(count)])]
    all_to_all x0 -> x2, starting transfers between devices: none -> 10.2 us  [sum_weight(): lax.all_to_all(chip, 'blk', 0, 0, axis_index_groups=groups, tiled=True)]
  transfers between devices with their start and end apart: 39 -> 46, of which waited for: 21 -> 26; matrix products, arithmetic and copies ran while one was open for 12% -> 1% of each run, Pallas kernels for 0% -> 15%
where the time goes in v1:
time: 236 us
  waiting for transfers between devices  106 us (45%)
  starting transfers between devices  56.5 us (24%)
  Pallas kernels  55.6 us (24%)
  local copies, waits for them, and re-layouts  11.9 us (5%)
  other arithmetic  3.71 us (2%)
    ppermute x44, waiting for transfers between devices, swap(): return lax.ppermute(value, axis, [(i, i ^ offset) for i in range(count)])  103 us
    ppermute x44, starting transfers between devices, swap(): return lax.ppermute(value, axis, [(i, i ^ offset) for i in range(count)])  46.4 us
    pallas_call x18, Pallas kernels, call(): pl.pallas_call(body, out_shape=outs, compiler_params=pltpu.CompilerParams...  28.2 us
    pallas_call x4, Pallas kernels, pair_call(): pl.pallas_call(body, in_specs=[smem, smem] + [vmem] * len(arrays), out_sh...  27.4 us
    unnamed x30, local copies, waits for them, and re-layouts  10.5 us
    all_to_all x2, starting transfers between devices, sum_weight(): lax.all_to_all(chip, 'blk', 0, 0, axis_index_groups=groups, tiled=True)  10.2 us
  transfers between devices with their start and end apart: 46, of which 26 were waited for; matrix products, arithmetic and copies ran while one was open for 1% of the time, Pallas kernels for 15%

profile of v1, /device:TPU:8, one launch (start us, length us, event | category | flops | bytes accessed | tf_op | source)
XLA Modules:
  0.0 235.7 jit_solution(5022833662152143221)
XLA Ops:
  3.1 2.4 embed_text.1
  5.5 2.8 %collective-permute-start = (bf16[128,1024]{1,0:T(8,128)(2,1)S(1)}, bf16[128,1024]{1,0:T(8,128)(2,1)S(1)}, u32[]{:S(2)}, u32[]{:S(2)}) collective-permute-start(bf16[128,1024]{1,0:T(8,128)(2,1)S(1)} %get-tuple-element.64), channel_id=1, source_target_pairs={{0,6},{1,7},{2,4},{3,5},{4,2},{5,3},{6,0},{7,1},{8,14},{9,15},{10,... | collective-permute-start | bytes 786440 | tf_op jit(solution)/shard_map/ppermute | solution.py:16
  8.5 6.3 %collective-permute-done.r4 = bf16[128,1024]{1,0:T(8,128)(2,1)S(1)} collective-permute-done((bf16[128,1024]{1,0:T(8,128)(2,1)S(1)}, bf16[128,1024]{1,0:T(8,128)(2,1)S(1)}, u32[]{:S(2)}, u32[]{:S(2)}) %collective-permute-start) | collective-permute-done | bytes 262176 | tf_op jit(solution)/shard_map/ppermute | solution.py:16
  17.9 3.0 %embed_image.1 = (bf16[2,128,1024]{2,1,0:T(8,128)(2,1)S(1)}, bf16[2,128,1024]{2,1,0:T(8,128)(2,1)S(1)}, bf16[2,128,1024]{2,1,0:T(8,128)(2,1)S(1)}, bf16[128,1024]{1,0:T(8,128)(2,1)S(1)}, bf16[128,1024]{1,0:T(8,128)(2,1)S(1)}) custom-call(s32[1]{0:T(128)} %bitcast.column_ref, bf16[1024,768]{1,0:T(8,128)(2,1)S(1)} %copy-done.4, bf16[768,1024]{1,0:T(8,128)(2,1)S(1)} %copy-done.6), custom_call_target="tpu_custom_call" | custom-call | flops 1610612736 | bytes 5242884 | tf_op jit(solution)/shard_map/embed_image/pallas_call | solution.py:29
  23.4 12.2 %collective-permute-done.4.i4 = bf16[128,1024]{1,0:T(8,128)(2,1)S(1)} collective-permute-done((bf16[128,1024]{1,0:T(8,128)(2,1)S(1)}, bf16[128,1024]{1,0:T(8,128)(2,1)S(1)}, u32[]{:S(2)}, u32[]{:S(2)}) %collective-permute-start.4) | collective-permute-done | bytes 262176 | tf_op jit(solution)/shard_map/ppermute | solution.py:16
  38.3 2.3 collective-permute-start.6
  40.6 5.6 %collective-permute-done.6.t1 = bf16[128,1024]{1,0:T(8,128)(2,1)S(1)} collective-permute-done((bf16[128,1024]{1,0:T(8,128)(2,1)S(1)}, bf16[128,1024]{1,0:T(8,128)(2,1)S(1)}, u32[]{:S(2)}, u32[]{:S(2)}) %collective-permute-start.6) | collective-permute-done | bytes 262176 | tf_op jit(solution)/shard_map/ppermute | solution.py:16
  49.2 2.4 %collective-permute-start.10 = (bf16[2,128,1024]{2,1,0:T(8,128)(2,1)S(1)}, bf16[2,128,1024]{2,1,0:T(8,128)(2,1)S(1)}, u32[]{:S(2)}, u32[]{:S(2)}) collective-permute-start(bf16[2,128,1024]{2,1,0:T(8,128)(2,1)S(1)} %get-tuple-element.78.i01), channel_id=1, source_target_pairs={{0,1},{1,0},{2,3},{3,2},{4,5},{5,4},{6,7},{7,6},{8,9},{9,8},{10,11... | collective-permute-start | bytes 1572872 | tf_op jit(solution)/shard_map/ppermute | solution.py:16
  52.9 13.7 %collective-permute-done.9.a2 = bf16[128,1024]{1,0:T(8,128)(2,1)S(1)} collective-permute-done((bf16[128,1024]{1,0:T(8,128)(2,1)S(1)}, bf16[128,1024]{1,0:T(8,128)(2,1)S(1)}, u32[]{:S(2)}, u32[]{:S(2)}) %collective-permute-start.9) | collective-permute-done | bytes 262176 | tf_op jit(solution)/shard_map/ppermute | solution.py:16
  66.9 4.1 %collective-permute-start.12 = (bf16[2,128,1024]{2,1,0:T(8,128)(2,1)S(1)}, bf16[2,128,1024]{2,1,0:T(8,128)(2,1)S(1)}, u32[]{:S(2)}, u32[]{:S(2)}) collective-permute-start(bf16[2,128,1024]{2,1,0:T(8,128)(2,1)S(1)} %get-tuple-element.79.a02), channel_id=1, source_target_pairs={{0,96},{8,104},{16,112},{24,120},{32,64},{40,72},{48,80},{56,88},{... | collective-permute-start | bytes 1572872 | tf_op jit(solution)/shard_map/ppermute | solution.py:16
  71.0 2.8 %collective-permute-start.14 = (bf16[2,128,1024]{2,1,0:T(8,128)(2,1)S(1)}, bf16[2,128,1024]{2,1,0:T(8,128)(2,1)S(1)}, u32[]{:S(2)}, u32[]{:S(2)}) collective-permute-start(bf16[2,128,1024]{2,1,0:T(8,128)(2,1)S(1)} %get-tuple-element.80.u01.refs_6_), channel_id=1, source_target_pairs={{0,6},{1,7},{2,4},{3,5},{4,2},{5,3},{6,0},{7,1},{8,14},{9,15},{10,... | collective-permute-start | bytes 1572872 | tf_op jit(solution)/shard_map/ppermute | solution.py:16
  73.8 4.6 %collective-permute-done.12.a1214 = bf16[2,128,1024]{2,1,0:T(8,128)(2,1)S(1)} collective-permute-done((bf16[2,128,1024]{2,1,0:T(8,128)(2,1)S(1)}, bf16[2,128,1024]{2,1,0:T(8,128)(2,1)S(1)}, u32[]{:S(2)}, u32[]{:S(2)}) %collective-permute-start.12) | collective-permute-done | bytes 524320 | tf_op jit(solution)/shard_map/ppermute | solution.py:16
  86.7 6.5 %collective-permute-done.16.a8.refs_15_ = bf16[128,1024]{1,0:T(8,128)(2,1)S(1)} collective-permute-done((bf16[128,1024]{1,0:T(8,128)(2,1)S(1)}, bf16[128,1024]{1,0:T(8,128)(2,1)S(1)}, u32[]{:S(2)}, u32[]{:S(2)}) %collective-permute-start.16) | collective-permute-done | bytes 262176 | tf_op jit(solution)/shard_map/ppermute | solution.py:16
  95.1 5.9 %pairs_near.1 = (bf16[1536,768]{1,0:T(8,128)(2,1)}, bf16[768,1536]{1,0:T(8,128)(2,1)}) custom-call(f32[1]{0:T(128)S(6)} %exp.3.scale_ref.refs_0_, f32[1]{0:T(128)S(6)} %copy.11.bias_ref.refs_1_, bf16[6,128,1024]{2,1,0:T(8,128)(2,1)S(1)} %get-tuple-element.81.even.refs_13_, bf16[6,128,1024]{2,1,0:T(8,128)(2,1)S(1)} %collective-permute-done.15.odd.refs_14_, ...), custom_call_target="tpu_custom_call" | custom-call | flops 2415919104 | bytes 9437184 | tf_op jit(solution)/shard_map/pairs_near/pallas_call | solution.py:116
  101.0 7.2 %pairs_far.1 = (bf16[1536,256]{1,0:T(8,128)(2,1)S(1)}, bf16[512,768]{1,0:T(8,128)(2,1)S(1)}, bf16[768,512]{1,0:T(8,128)(2,1)}, bf16[512,256]{1,0:T(8,128)(2,1)S(...) custom-call(f32[1]{0:T(128)S(6)} %exp.3.scale_ref.refs_0_, f32[1]{0:T(128)S(6)} %copy.11.bias_ref.refs_1_, ...), custom_call_target="tpu_custom_call" | custom-call | flops 2952790016 | bytes 9437184 | tf_op jit(solution)/shard_map/pairs_far/pallas_call | solution.py:116
  108.2 4.3 %pairs_odd.1 = bf16[8,128,1024]{2,1,0:T(8,128)(2,1)S(1)} custom-call(f32[1]{0:T(128)S(6)} %exp.3.scale_ref.refs_0_, f32[1]{0:T(128)S(6)} %copy.11.bias_ref.refs_1_, bf16[1536,768]{1,0:T(8,128)(2,1)} %get-tuple-element.82.refs_2_.near_near, bf16[1536,256]{1,0:T(8,128)(2,1)S(1)} %get-tuple-element.87.refs_3_.near_far, ...), custom_call_target="tpu_custom_call" | custom-call | flops 2147483648 | bytes 8388608 | tf_op jit(solution)/shard_map/pairs_odd/pallas_call | solution.py:116
  114.0 10.1 %pairs_rest.1 = (bf16[2,128,1024]{2,1,0:T(8,128)(2,1)S(1)}, bf16[2,128,1024]{2,1,0:T(8,128)(2,1)S(1)}, bf16[2,128,1024]{2,1,0:T(8,128)(2,1)S(1)}, bf16[8,128,1024]{2,1,0:T(8,128)(2,1)}) custom-call(f32[1]{0:T(128)S(6)} %exp.3.scale_ref.refs_0_, f32[1]{0:T(128)S(6)} %copy.11.bias_ref.refs_1_, bf16[1536,768]{1,0:T(8,128)(2,1)} %get-tuple-element.82.refs_2_.near_near, ...), custom_call_target="tpu_custom_call" | custom-call | flops 5368709120 | bytes 17301504 | tf_op jit(solution)/shard_map/pairs_rest/pallas_call | solution.py:116
  128.9 2.1 collective-permute-start.27
  135.3 6.3 %collective-permute-done.25.p8 = bf16[128,1024]{1,0:T(8,128)(2,1)S(1)} collective-permute-done((bf16[128,1024]{1,0:T(8,128)(2,1)S(1)}, bf16[128,1024]{1,0:T(8,128)(2,1)S(1)}, u32[]{:S(2)}, u32[]{:S(2)}) %collective-permute-start.25) | collective-permute-done | bytes 262176 | tf_op jit(solution)/shard_map/ppermute | solution.py:16
  143.0 2.7 %collective-permute-done.28.g67 = bf16[2,128,1024]{2,1,0:T(8,128)(2,1)S(1)} collective-permute-done((bf16[2,128,1024]{2,1,0:T(8,128)(2,1)S(1)}, bf16[2,128,1024]{2,1,0:T(8,128)(2,1)S(1)}, u32[]{:S(2)}, u32[]{:S(2)}) %collective-permute-start.28) | collective-permute-done | bytes 524320 | tf_op jit(solution)/shard_map/ppermute | solution.py:16
  145.7 2.8 %sums_sixth.1 = (bf16[2,128,1024]{2,1,0:T(8,128)(2,1)S(1)}, bf16[2,128,1024]{2,1,0:T(8,128)(2,1)S(1)}, bf16[2,128,1024]{2,1,0:T(8,128)(2,1)S(1)}, bf16[2,128,1024]{2,1,0:T(8,128)(2,1)S(1)}) custom-call(bf16[8,128,1024]{2,1,0:T(8,128)(2,1)} %get-tuple-element.92.even, bf16[8,128,1024]{2,1,0:T(8,128)(2,1)} %copy-done.14, ...), custom_call_target="tpu_custom_call" | custom-call | bytes 8388608 | tf_op jit(solution)/shard_map/sums_sixth/pallas_call | solution.py:29
  151.1 10.0 %collective-permute-done.29.p46 = bf16[2,128,1024]{2,1,0:T(8,128)(2,1)S(1)} collective-permute-done((bf16[2,128,1024]{2,1,0:T(8,128)(2,1)S(1)}, bf16[2,128,1024]{2,1,0:T(8,128)(2,1)S(1)}, u32[]{:S(2)}, u32[]{:S(2)}) %collective-permute-start.29) | collective-permute-done | bytes 524320 | tf_op jit(solution)/shard_map/ppermute | solution.py:16
  167.7 4.4 %collective-permute-done.34.p2 = bf16[128,1024]{1,0:T(8,128)(2,1)S(1)} collective-permute-done((bf16[128,1024]{1,0:T(8,128)(2,1)S(1)}, bf16[128,1024]{1,0:T(8,128)(2,1)S(1)}, u32[]{:S(2)}, u32[]{:S(2)}) %collective-permute-start.34) | collective-permute-done | bytes 262176 | tf_op jit(solution)/shard_map/ppermute | solution.py:16
  172.5 7.9 %collective-permute-done.35.d1 = bf16[128,1024]{1,0:T(8,128)(2,1)S(1)} collective-permute-done((bf16[128,1024]{1,0:T(8,128)(2,1)S(1)}, bf16[128,1024]{1,0:T(8,128)(2,1)S(1)}, u32[]{:S(2)}, u32[]{:S(2)}) %collective-permute-start.35) | collective-permute-done | bytes 262176 | tf_op jit(solution)/shard_map/ppermute | solution.py:16
  185.9 4.7 %collective-permute-done.36.e4 = bf16[128,1024]{1,0:T(8,128)(2,1)S(1)} collective-permute-done((bf16[128,1024]{1,0:T(8,128)(2,1)}, bf16[128,1024]{1,0:T(8,128)(2,1)S(1)}, u32[]{:S(2)}, u32[]{:S(2)}) %collective-permute-start.36) | collective-permute-done | bytes 262176 | tf_op jit(solution)/shard_map/ppermute | solution.py:16
  192.6 4.1 %weight_image.1 = (bf16[8,64,768]{2,1,0:T(8,128)(2,1)S(1)}, bf16[8,64,768]{2,1,0:T(8,128)(2,1)S(1)}) custom-call(s32[1]{0:T(128)} %bitcast.column_ref, s32[1]{0:T(128)} %bitcast.3.place_ref, bf16[2,128,1024]{2,1,0:T(8,128)(2,1)S(1)} %get-tuple-element.107.e01, bf16[2,128,1024]{2,1,0:T(8,128)(2,1)S(1)} %collective-permute-done.32.e23, ...), custom_call_target="tpu_custom_call" | custom-call | flops 1610612736 | bytes 5242888 | tf_op jit(solution)/shard_map/weight_image/pallas_call | solution.py:29
  200.9 5.0 %all-to-all-start = ((bf16[8,64,768]{2,1,0:T(8,128)(2,1)}), bf16[8,64,768]{2,1,0:T(8,128)(2,1)}, u32[]{:S(2)}, u32[]{:S(2)}) async-start(bf16[8,64,768]{2,1,0:T(8,128)(2,1)} %weight_chip.2), calls=%async_computation | async-start | bytes 1572864 | tf_op jit(solution)/shard_map/all_to_all | solution.py:324
  209.7 2.4 %weight_text.1 = (bf16[8,64,512]{2,1,0:T(8,128)(2,1)S(1)}, bf16[8,64,512]{2,1,0:T(8,128)(2,1)S(1)}) custom-call(s32[1]{0:T(128)} %bitcast.column_ref, s32[1]{0:T(128)} %bitcast.3.place_ref, bf16[2,128,1024]{2,1,0:T(8,128)(2,1)S(1)} %get-tuple-element.113.e01, bf16[2,128,1024]{2,1,0:T(8,128)(2,1)S(1)} %collective-permute-done.38.e23, ...), custom_call_target="tpu_custom_call" | custom-call | flops 1073741824 | bytes 4194312 | tf_op jit(solution)/shard_map/weight_text/pallas_call | solution.py:29
  215.0 2.9 %all-to-all-done = bf16[8,64,768]{2,1,0:T(8,128)(2,1)} async-done(((bf16[8,64,768]{2,1,0:T(8,128)(2,1)}), bf16[8,64,768]{2,1,0:T(8,128)(2,1)}, u32[]{:S(2)}, u32[]{:S(2)}) %all-to-all-start) | async-done | bytes 786464 | tf_op jit(solution)/shard_map/all_to_all | solution.py:324
  217.9 5.2 %all-to-all-start.1 = ((bf16[8,64,512]{2,1,0:T(8,128)(2,1)}), bf16[8,64,512]{2,1,0:T(8,128)(2,1)}, u32[]{:S(2)}, u32[]{:S(2)}) async-start(bf16[8,64,512]{2,1,0:T(8,128)(2,1)} %weight_chip.3), calls=%async_computation.1 | async-start | bytes 1048576 | tf_op jit(solution)/shard_map/all_to_all | solution.py:324
  225.5 4.1 %feature_image.1 = bf16[1024,768]{1,0:T(8,128)(2,1)} custom-call(s32[1]{0:T(128)} %bitcast.column_ref, bf16[2,128,1024]{2,1,0:T(8,128)(2,1)S(1)} %copy-done.13, bf16[2,128,1024]{2,1,0:T(8,128)(2,1)S(1)} %collective-permute-done.32.e23, bf16[2,128,1024]{2,1,0:T(8,128)(2,1)S(1)} %collective-permute-done.33.e67, ...), custom_call_target="tpu_custom_call" | custom-call | flops 1610612736 | bytes 5242884 | tf_op jit(solution)/shard_map/feature_image/pallas_call | solution.py:29
  229.6 2.3 feature_text.1
  (116 shorter events, 70.5 us)
Async XLA Ops:
  5.5 9.3 %collective-permute-start = (bf16[128,1024]{1,0:T(8,128)(2,1)S(1)}, bf16[128,1024]{1,0:T(8,128)(2,1)S(1)}, u32[]{:S(2)}, u32[]{:S(2)}) collective-permute-start(bf16[128,1024]{1,0:T(8,128)(2,1)S(1)} %get-tuple-element.64), channel_id=1, source_target_pairs={{0,6},{1,7},{2,4},{3,5},{4,2},{5,3},{6,0},{7,1},{8,14},{9,15},{10,... | collective-permute-start | bytes 786440 | tf_op jit(solution)/shard_map/ppermute | solution.py:16
  16.2 19.5 %collective-permute-start.2 = (bf16[2,128,1024]{2,1,0:T(8,128)(2,1)S(1)}, bf16[2,128,1024]{2,1,0:T(8,128)(2,1)S(1)}, u32[]{:S(2)}, u32[]{:S(2)}) collective-permute-start(bf16[2,128,1024]{2,1,0:T(8,128)(2,1)S(1)} %get-tuple-element.66), channel_id=1, source_target_pairs={{0,2},{1,3},{2,0},{3,1},{4,6},{5,7},{6,4},{7,5},{8,10},{9,11},{10,... | collective-permute-start | bytes 1572872 | tf_op jit(solution)/shard_map/ppermute | solution.py:16
  16.6 19.1 %collective-permute-start.3 = (bf16[2,128,1024]{2,1,0:T(8,128)(2,1)S(1)}, bf16[2,128,1024]{2,1,0:T(8,128)(2,1)S(1)}, u32[]{:S(2)}, u32[]{:S(2)}) collective-permute-start(bf16[2,128,1024]{2,1,0:T(8,128)(2,1)S(1)} %get-tuple-element.67), channel_id=1, source_target_pairs={{0,6},{1,7},{2,4},{3,5},{4,2},{5,3},{6,0},{7,1},{8,14},{9,15},{10,... | collective-permute-start | bytes 1572872 | tf_op jit(solution)/shard_map/ppermute | solution.py:16
  20.9 14.8 %collective-permute-start.4 = (bf16[128,1024]{1,0:T(8,128)(2,1)S(1)}, bf16[128,1024]{1,0:T(8,128)(2,1)S(1)}, u32[]{:S(2)}, u32[]{:S(2)}) collective-permute-start(bf16[128,1024]{1,0:T(8,128)(2,1)S(1)} %get-tuple-element.70), channel_id=1, source_target_pairs={{0,6},{1,7},{2,4},{3,5},{4,2},{5,3},{6,0},{7,1},{8,14},{9,15},{10,... | collective-permute-start | bytes 786440 | tf_op jit(solution)/shard_map/ppermute | solution.py:16
  22.9 12.8 %collective-permute-start.5 = (bf16[128,1024]{1,0:T(8,128)(2,1)S(1)}, bf16[128,1024]{1,0:T(8,128)(2,1)S(1)}, u32[]{:S(2)}, u32[]{:S(2)}) collective-permute-start(bf16[128,1024]{1,0:T(8,128)(2,1)S(1)} %get-tuple-element.71), channel_id=1, source_target_pairs={{0,2},{1,3},{2,0},{3,1},{4,6},{5,7},{6,4},{7,5},{8,10},{9,11},{10,... | collective-permute-start | bytes 786440 | tf_op jit(solution)/shard_map/ppermute | solution.py:16
  36.0 11.4 %collective-permute-start.7 = (bf16[2,128,1024]{2,1,0:T(8,128)(2,1)S(1)}, bf16[2,128,1024]{2,1,0:T(8,128)(2,1)S(1)}, u32[]{:S(2)}, u32[]{:S(2)}) collective-permute-start(bf16[2,128,1024]{2,1,0:T(8,128)(2,1)S(1)} %get-tuple-element.75), channel_id=1, source_target_pairs={{0,2},{1,3},{2,0},{3,1},{4,6},{5,7},{6,4},{7,5},{8,10},{9,11},{10,... | collective-permute-start | bytes 1572872 | tf_op jit(solution)/shard_map/ppermute | solution.py:16
  36.5 12.2 %collective-permute-start.8 = (bf16[2,128,1024]{2,1,0:T(8,128)(2,1)S(1)}, bf16[2,128,1024]{2,1,0:T(8,128)(2,1)S(1)}, u32[]{:S(2)}, u32[]{:S(2)}) collective-permute-start(bf16[2,128,1024]{2,1,0:T(8,128)(2,1)S(1)} %get-tuple-element.76), channel_id=1, source_target_pairs={{0,6},{1,7},{2,4},{3,5},{4,2},{5,3},{6,0},{7,1},{8,14},{9,15},{10,... | collective-permute-start | bytes 1572872 | tf_op jit(solution)/shard_map/ppermute | solution.py:16
  49.2 17.4 %collective-permute-start.10 = (bf16[2,128,1024]{2,1,0:T(8,128)(2,1)S(1)}, bf16[2,128,1024]{2,1,0:T(8,128)(2,1)S(1)}, u32[]{:S(2)}, u32[]{:S(2)}) collective-permute-start(bf16[2,128,1024]{2,1,0:T(8,128)(2,1)S(1)} %get-tuple-element.78.i01), channel_id=1, source_target_pairs={{0,1},{1,0},{2,3},{3,2},{4,5},{5,4},{6,7},{7,6},{8,9},{9,8},{10,11... | collective-permute-start | bytes 1572872 | tf_op jit(solution)/shard_map/ppermute | solution.py:16
  51.6 15.0 %collective-permute-start.9 = (bf16[128,1024]{1,0:T(8,128)(2,1)S(1)}, bf16[128,1024]{1,0:T(8,128)(2,1)S(1)}, u32[]{:S(2)}, u32[]{:S(2)}) collective-permute-start(bf16[128,1024]{1,0:T(8,128)(2,1)S(1)} %get-tuple-element.77.a0), channel_id=1, source_target_pairs={{0,16},{8,24},{16,0},{24,8},{32,48},{40,56},{48,32},{56,40},{64,80... | collective-permute-start | bytes 786440 | tf_op jit(solution)/shard_map/ppermute | solution.py:16
  66.9 11.5 %collective-permute-start.12 = (bf16[2,128,1024]{2,1,0:T(8,128)(2,1)S(1)}, bf16[2,128,1024]{2,1,0:T(8,128)(2,1)S(1)}, u32[]{:S(2)}, u32[]{:S(2)}) collective-permute-start(bf16[2,128,1024]{2,1,0:T(8,128)(2,1)S(1)} %get-tuple-element.79.a02), channel_id=1, source_target_pairs={{0,96},{8,104},{16,112},{24,120},{32,64},{40,72},{48,80},{56,88},{... | collective-permute-start | bytes 1572872 | tf_op jit(solution)/shard_map/ppermute | solution.py:16
  71.0 10.5 %collective-permute-start.14 = (bf16[2,128,1024]{2,1,0:T(8,128)(2,1)S(1)}, bf16[2,128,1024]{2,1,0:T(8,128)(2,1)S(1)}, u32[]{:S(2)}, u32[]{:S(2)}) collective-permute-start(bf16[2,128,1024]{2,1,0:T(8,128)(2,1)S(1)} %get-tuple-element.80.u01.refs_6_), channel_id=1, source_target_pairs={{0,6},{1,7},{2,4},{3,5},{4,2},{5,3},{6,0},{7,1},{8,14},{9,15},{10,... | collective-permute-start | bytes 1572872 | tf_op jit(solution)/shard_map/ppermute | solution.py:16
  83.2 11.9 %collective-permute-start.15 = (bf16[6,128,1024]{2,1,0:T(8,128)(2,1)S(1)}, bf16[6,128,1024]{2,1,0:T(8,128)(2,1)S(1)}, u32[]{:S(2)}, u32[]{:S(2)}) collective-permute-start(bf16[6,128,1024]{2,1,0:T(8,128)(2,1)S(1)} %get-tuple-element.81.even.refs_13_), channel_id=1, source_target_pairs={{0,8},{8,0},{16,24},{24,16},{32,40},{40,32},{48,56},{56,48},{64,72... | collective-permute-start | bytes 4718600 | tf_op jit(solution)/shard_map/ppermute | solution.py:16
  83.3 9.9 %collective-permute-start.16 = (bf16[128,1024]{1,0:T(8,128)(2,1)S(1)}, bf16[128,1024]{1,0:T(8,128)(2,1)S(1)}, u32[]{:S(2)}, u32[]{:S(2)}) collective-permute-start(bf16[128,1024]{1,0:T(8,128)(2,1)S(1)} %get-tuple-element.83), channel_id=1, source_target_pairs={{0,96},{8,104},{16,112},{24,120},{32,64},{40,72},{48,80},{56,88},{... | collective-permute-start | bytes 786440 | tf_op jit(solution)/shard_map/ppermute | solution.py:16
  83.9 9.3 %collective-permute-start.17 = (bf16[128,1024]{1,0:T(8,128)(2,1)S(1)}, bf16[128,1024]{1,0:T(8,128)(2,1)S(1)}, u32[]{:S(2)}, u32[]{:S(2)}) collective-permute-start(bf16[128,1024]{1,0:T(8,128)(2,1)S(1)} %get-tuple-element.84), channel_id=1, source_target_pairs={{0,32},{8,40},{16,48},{24,56},{32,0},{40,8},{48,16},{56,24},{64,96... | collective-permute-start | bytes 786440 | tf_op jit(solution)/shard_map/ppermute | solution.py:16
  85.5 15.5 %collective-permute-start.20 = (bf16[128,1024]{1,0:T(8,128)(2,1)S(1)}, bf16[128,1024]{1,0:T(8,128)(2,1)S(1)}, u32[]{:S(2)}, u32[]{:S(2)}) collective-permute-start(bf16[128,1024]{1,0:T(8,128)(2,1)S(1)} %get-tuple-element.85), channel_id=1, source_target_pairs={{0,6},{1,7},{2,4},{3,5},{4,2},{5,3},{6,0},{7,1},{8,14},{9,15},{10,... | collective-permute-start | bytes 786440 | tf_op jit(solution)/shard_map/ppermute | solution.py:16
  86.7 14.3 %collective-permute-start.21 = (bf16[128,1024]{1,0:T(8,128)(2,1)S(1)}, bf16[128,1024]{1,0:T(8,128)(2,1)S(1)}, u32[]{:S(2)}, u32[]{:S(2)}) collective-permute-start(bf16[128,1024]{1,0:T(8,128)(2,1)S(1)} %get-tuple-element.86), channel_id=1, source_target_pairs={{0,2},{1,3},{2,0},{3,1},{4,6},{5,7},{6,4},{7,5},{8,10},{9,11},{10,... | collective-permute-start | bytes 786440 | tf_op jit(solution)/shard_map/ppermute | solution.py:16
  112.5 11.7 %collective-permute-start.22 = (bf16[8,128,1024]{2,1,0:T(8,128)(2,1)S(1)}, bf16[8,128,1024]{2,1,0:T(8,128)(2,1)S(1)}, u32[]{:S(2)}, u32[]{:S(2)}) collective-permute-start(bf16[8,128,1024]{2,1,0:T(8,128)(2,1)S(1)} %pairs_odd.1), channel_id=1, source_target_pairs={{0,8},{8,0},{16,24},{24,16},{32,40},{40,32},{48,56},{56,48},{64,72... | collective-permute-start | bytes 6291464 | tf_op jit(solution)/shard_map/ppermute | solution.py:16
  112.5 11.6 %collective-permute-start.23 = (bf16[128,1024]{1,0:T(8,128)(2,1)S(1)}, bf16[128,1024]{1,0:T(8,128)(2,1)S(1)}, u32[]{:S(2)}, u32[]{:S(2)}) collective-permute-start(bf16[128,1024]{1,0:T(8,128)(2,1)S(1)} %get-tuple-element.95), channel_id=1, source_target_pairs={{0,6},{1,7},{2,4},{3,5},{4,2},{5,3},{6,0},{7,1},{8,14},{9,15},{10,... | collective-permute-start | bytes 786440 | tf_op jit(solution)/shard_map/ppermute | solution.py:16
  114.0 10.1 %collective-permute-start.24 = (bf16[128,1024]{1,0:T(8,128)(2,1)S(1)}, bf16[128,1024]{1,0:T(8,128)(2,1)S(1)}, u32[]{:S(2)}, u32[]{:S(2)}) collective-permute-start(bf16[128,1024]{1,0:T(8,128)(2,1)S(1)} %get-tuple-element.96), channel_id=1, source_target_pairs={{0,2},{1,3},{2,0},{3,1},{4,6},{5,7},{6,4},{7,5},{8,10},{9,11},{10,... | collective-permute-start | bytes 786440 | tf_op jit(solution)/shard_map/ppermute | solution.py:16
  128.9 14.1 %collective-permute-start.27 = (bf16[2,128,1024]{2,1,0:T(8,128)(2,1)S(1)}, bf16[2,128,1024]{2,1,0:T(8,128)(2,1)S(1)}, u32[]{:S(2)}, u32[]{:S(2)}) collective-permute-start(bf16[2,128,1024]{2,1,0:T(8,128)(2,1)S(1)} %get-tuple-element.100), channel_id=1, source_target_pairs={{0,2},{1,3},{2,0},{3,1},{4,6},{5,7},{6,4},{7,5},{8,10},{9,11},{10,... | collective-permute-start | bytes 1572872 | tf_op jit(solution)/shard_map/ppermute | solution.py:16
  131.0 14.6 %collective-permute-start.28 = (bf16[2,128,1024]{2,1,0:T(8,128)(2,1)S(1)}, bf16[2,128,1024]{2,1,0:T(8,128)(2,1)S(1)}, u32[]{:S(2)}, u32[]{:S(2)}) collective-permute-start(bf16[2,128,1024]{2,1,0:T(8,128)(2,1)S(1)} %get-tuple-element.101), channel_id=1, source_target_pairs={{0,6},{1,7},{2,4},{3,5},{4,2},{5,3},{6,0},{7,1},{8,14},{9,15},{10,... | collective-permute-start | bytes 1572872 | tf_op jit(solution)/shard_map/ppermute | solution.py:16
  148.5 12.6 %collective-permute-start.29 = (bf16[2,128,1024]{2,1,0:T(8,128)(2,1)S(1)}, bf16[2,128,1024]{2,1,0:T(8,128)(2,1)S(1)}, u32[]{:S(2)}, u32[]{:S(2)}) collective-permute-start(bf16[2,128,1024]{2,1,0:T(8,128)(2,1)S(1)} %get-tuple-element.103), channel_id=1, source_target_pairs={{0,32},{8,40},{16,48},{24,56},{32,0},{40,8},{48,16},{56,24},{64,96... | collective-permute-start | bytes 1572872 | tf_op jit(solution)/shard_map/ppermute | solution.py:16
  149.2 13.4 %collective-permute-start.30 = (bf16[2,128,1024]{2,1,0:T(8,128)(2,1)S(1)}, bf16[2,128,1024]{2,1,0:T(8,128)(2,1)S(1)}, u32[]{:S(2)}, u32[]{:S(2)}) collective-permute-start(bf16[2,128,1024]{2,1,0:T(8,128)(2,1)S(1)} %get-tuple-element.104), channel_id=1, source_target_pairs={{0,96},{8,104},{16,112},{24,120},{32,64},{40,72},{48,80},{56,88},{... | collective-permute-start | bytes 1572872 | tf_op jit(solution)/shard_map/ppermute | solution.py:16
  151.1 13.1 %collective-permute-start.31 = (bf16[2,128,1024]{2,1,0:T(8,128)(2,1)S(1)}, bf16[2,128,1024]{2,1,0:T(8,128)(2,1)S(1)}, u32[]{:S(2)}, u32[]{:S(2)}) collective-permute-start(bf16[2,128,1024]{2,1,0:T(8,128)(2,1)S(1)} %get-tuple-element.105.g01), channel_id=1, source_target_pairs={{0,1},{1,0},{2,3},{3,2},{4,5},{5,4},{6,7},{7,6},{8,9},{9,8},{10,11... | collective-permute-start | bytes 1572872 | tf_op jit(solution)/shard_map/ppermute | solution.py:16
  165.7 14.7 %collective-permute-start.33 = (bf16[2,128,1024]{2,1,0:T(8,128)(2,1)S(1)}, bf16[2,128,1024]{2,1,0:T(8,128)(2,1)S(1)}, u32[]{:S(2)}, u32[]{:S(2)}) collective-permute-start(bf16[2,128,1024]{2,1,0:T(8,128)(2,1)S(1)} %get-tuple-element.107.e01), channel_id=1, source_target_pairs={{0,6},{1,7},{2,4},{3,5},{4,2},{5,3},{6,0},{7,1},{8,14},{9,15},{10,... | collective-permute-start | bytes 1572872 | tf_op jit(solution)/shard_map/ppermute | solution.py:16
  167.7 12.7 %collective-permute-start.32 = (bf16[2,128,1024]{2,1,0:T(8,128)(2,1)S(1)}, bf16[2,128,1024]{2,1,0:T(8,128)(2,1)S(1)}, u32[]{:S(2)}, u32[]{:S(2)}) collective-permute-start(bf16[2,128,1024]{2,1,0:T(8,128)(2,1)S(1)} %get-tuple-element.107.e01), channel_id=1, source_target_pairs={{0,2},{1,3},{2,0},{3,1},{4,6},{5,7},{6,4},{7,5},{8,10},{9,11},{10,... | collective-permute-start | bytes 1572872 | tf_op jit(solution)/shard_map/ppermute | solution.py:16
  181.3 9.3 %collective-permute-start.36 = (bf16[128,1024]{1,0:T(8,128)(2,1)}, bf16[128,1024]{1,0:T(8,128)(2,1)S(1)}, u32[]{:S(2)}, u32[]{:S(2)}) collective-permute-start(bf16[128,1024]{1,0:T(8,128)(2,1)} %get-tuple-element.111), channel_id=1, source_target_pairs={{0,6},{1,7},{2,4},{3,5},{4,2},{5,3},{6,0},{7,1},{8,14},{9,15},{10,... | collective-permute-start | bytes 786440 | tf_op jit(solution)/shard_map/ppermute | solution.py:16
  183.3 13.6 %collective-permute-start.39 = (bf16[2,128,1024]{2,1,0:T(8,128)(2,1)S(1)}, bf16[2,128,1024]{2,1,0:T(8,128)(2,1)S(1)}, u32[]{:S(2)}, u32[]{:S(2)}) collective-permute-start(bf16[2,128,1024]{2,1,0:T(8,128)(2,1)S(1)} %get-tuple-element.113.e01), channel_id=1, source_target_pairs={{0,6},{1,7},{2,4},{3,5},{4,2},{5,3},{6,0},{7,1},{8,14},{9,15},{10,... | collective-permute-start | bytes 1572872 | tf_op jit(solution)/shard_map/ppermute | solution.py:16
  184.5 13.4 %collective-permute-start.38 = (bf16[2,128,1024]{2,1,0:T(8,128)(2,1)S(1)}, bf16[2,128,1024]{2,1,0:T(8,128)(2,1)S(1)}, u32[]{:S(2)}, u32[]{:S(2)}) collective-permute-start(bf16[2,128,1024]{2,1,0:T(8,128)(2,1)S(1)} %get-tuple-element.113.e01), channel_id=1, source_target_pairs={{0,2},{1,3},{2,0},{3,1},{4,6},{5,7},{6,4},{7,5},{8,10},{9,11},{10,... | collective-permute-start | bytes 1572872 | tf_op jit(solution)/shard_map/ppermute | solution.py:16
  198.6 9.8 %collective-permute-start.40 = (bf16[128,1024]{1,0:T(8,128)(2,1)}, bf16[128,1024]{1,0:T(8,128)(2,1)S(1)}, u32[]{:S(2)}, u32[]{:S(2)}) collective-permute-start(bf16[128,1024]{1,0:T(8,128)(2,1)} %slice_bitcast_fusion.1), channel_id=1, source_target_pairs={{0,6},{1,7},{2,4},{3,5},{4,2},{5,3},{6,0},{7,1},{8,14},{9,15},{10,... | collective-permute-start | bytes 786440 | tf_op jit(solution)/shard_map/ppermute | solution.py:16
  200.9 16.9 %all-to-all-start = ((bf16[8,64,768]{2,1,0:T(8,128)(2,1)}), bf16[8,64,768]{2,1,0:T(8,128)(2,1)}, u32[]{:S(2)}, u32[]{:S(2)}) async-start(bf16[8,64,768]{2,1,0:T(8,128)(2,1)} %weight_chip.2), calls=%async_computation | async-start | bytes 1572864 | tf_op jit(solution)/shard_map/all_to_all | solution.py:324
  217.9 16.0 %all-to-all-start.1 = ((bf16[8,64,512]{2,1,0:T(8,128)(2,1)}), bf16[8,64,512]{2,1,0:T(8,128)(2,1)}, u32[]{:S(2)}, u32[]{:S(2)}) async-start(bf16[8,64,512]{2,1,0:T(8,128)(2,1)} %weight_chip.3), calls=%async_computation.1 | async-start | bytes 1048576 | tf_op jit(solution)/shard_map/all_to_all | solution.py:324
  (29 other events, 198.5 us)

commit v2 on v0

v2 whole, which is shorter than its diff:
```python
import jax
import jax.numpy as jnp
from jax import lax
from jax.experimental import pallas as pl
from jax.experimental.pallas import tpu as pltpu
from jax.sharding import PartitionSpec as P

EPS = 1e-06
BF16 = jnp.bfloat16
F32 = jnp.float32
MIB = 1024 * 1024
ORDER_COST = 12 * 10**9
NEAR_FAR = (0, 1, 2, 3, 6, 7, 4, 5)


def swap(value, axis, offset):
    count = lax.axis_size(axis)
    return lax.ppermute(value, axis, [(i, i ^ offset) for i in range(count)])


def shape(*dims, dtype=BF16):
    return jax.ShapeDtypeStruct(dims, dtype)


def call(name, body, outs, ins, flops=0, limit=10, after=None, in_specs=None, scratch=()):
    ins, specs = list(ins), in_specs or [pl.BlockSpec(memory_space=pltpu.VMEM)] * len(ins)
    run = body
    if after is not None:
        after = list(after) if isinstance(after, tuple) else [after]
        ins, specs = after + ins, [pl.BlockSpec(memory_space=pltpu.VMEM)] * len(after) + list(specs)

        def run(*refs):
            body(*refs[len(after) :])

    moved = sum(a.size * a.dtype.itemsize for a in ins + list(outs))
    return pl.pallas_call(
        run,
        out_shape=outs,
        in_specs=specs,
        scratch_shapes=list(scratch),
        compiler_params=pltpu.CompilerParams(vmem_limit_bytes=limit * MIB),
        cost_estimate=pl.CostEstimate(flops=flops, bytes_accessed=moved, transcendentals=0),
        name=name,
    )(*ins)


def tiles(count, size, body):
    def step(index, carry):
        body(pl.ds(pl.multiple_of(index * size, size), size))
        return carry

    lax.fori_loop(0, count, step, 0)


def wide(ref, block=None):
    return (ref[...] if block is None else ref[block]).astype(F32)


def embed(name, feat, weight, column, blocks, tile=256):
    rows, width = feat.shape
    columns = weight.shape[1]
    own = rows // blocks

    def body(column_ref, feat_ref, weight_ref, p01, p23, p67, p4, p5, result):
        def part(k):
            return result[pl.ds(pl.multiple_of((column_ref[0] ^ k) * own, own), own)]

        def columns_at(here):
            result[...] = product(feat_ref[...], weight_ref[:, here]).astype(BF16)
            for k in range(2):
                p01[k, :, here] = part(k)
                p23[k, :, here] = part(2 + k)
                p67[k, :, here] = part(6 + k)
            p4[:, here] = part(4)
            p5[:, here] = part(5)

        tiles(columns // tile, tile, columns_at)

    outs = [shape(2, own, columns)] * 3 + [shape(own, columns)] * 2
    specs = [pl.BlockSpec(memory_space=pltpu.SMEM)] + [pl.BlockSpec(memory_space=pltpu.VMEM)] * 2
    scratch = [pltpu.VMEM((rows, tile), BF16)]
    return call(name, body, outs, (column, feat, weight), 2 * rows * width * columns, 16, None, specs, scratch)


def relay_add(p23, p67, r4, r5, out23, out67):
    out23[0] = (wide(p23, 0) + wide(r4)).astype(BF16)
    out23[1] = p23[1]
    out67[0] = p67[0]
    out67[1] = (wide(p67, 1) + wide(r5)).astype(BF16)


def relay_split(p23, p67, r4, r5, a23, a67, b23, b67):
    half = r4.shape[0] // 2
    for h, (out23, out67) in enumerate(((a23, a67), (b23, b67))):
        rows = slice(h * half, (h + 1) * half)
        out23[0] = (p23[0, rows].astype(F32) + wide(r4, rows)).astype(BF16)
        out23[1] = p23[1, rows]
        out67[0] = p67[0, rows]
        out67[1] = (p67[1, rows].astype(F32) + wide(r5, rows)).astype(BF16)


def add_half(h):
    def body(p01, r23, r67, out):
        half = out.shape[1]
        for k in range(2):
            own = p01[k, h * half : (h + 1) * half].astype(F32)
            out[k] = (own + wide(r23, k) + wide(r67, k)).astype(BF16)

    return body


def norm_half(p01, got01, emb_out, unit_out):
    for k in range(2):
        embedded = wide(p01, k) + wide(got01, 1 - k)
        emb_out[k] = embedded
        unit_out[k] = unit_of(embedded)[0].astype(BF16)


def back_half(g01, got01, emb, out):
    for k in range(2):
        out[k] = norm_back(wide(g01, k) + wide(got01, 1 - k), emb[k]).astype(BF16)


def cut(near, other, first_out, last_out):
    first_out[...] = near[0]
    last_out[...] = other[1]


def stack(first, second, out):
    out[0] = first[...]
    out[1] = second[...]


def grouped(refs, halves):
    return [refs[i * halves : (i + 1) * halves] for i in range(5)]


def block(group, k=None):
    parts = [ref[...] if k is None else ref[k] for ref in group]
    return parts[0] if len(parts) == 1 else jnp.concatenate(parts, axis=0)


def near_far_order(groups):
    g01, g23, g67, g4, g5 = groups
    pairs = [block(g, k) for g in (g01, g23, g67) for k in range(2)]
    return pairs + [block(g4), block(g5)]


def unit_of(embedded):
    inverse = lax.rsqrt(jnp.sum(embedded * embedded, axis=1, keepdims=True) + EPS)
    return embedded * inverse, inverse


def norm_back(unit_grad, embedded):
    unit, inverse = unit_of(embedded)
    return inverse * (unit_grad - unit * jnp.sum(unit * unit_grad, axis=1, keepdims=True))


def flat(ref):
    return ref[...].reshape(-1, ref.shape[-1])


def factors(scale, bias, txt, img):
    affinity = lax.dot_general(txt, img, (((1,), (1,)), ((), ())), preferred_element_type=F32)
    logits = scale * affinity + bias
    return logits, (scale / (1.0 + jnp.exp(-logits))).astype(BF16)


def product(first, second):
    return jnp.dot(first, second, preferred_element_type=F32)


def pair_call(name, body, outs, scale, bias, arrays, flops, limit, scratch=()):
    smem = pl.BlockSpec(memory_space=pltpu.SMEM)
    vmem = pl.BlockSpec(memory_space=pltpu.VMEM)
    moved = sum(a.size * a.dtype.itemsize for a in list(arrays) + outs)
    return pl.pallas_call(
        body,
        in_specs=[smem, smem] + [vmem] * len(arrays),
        out_shape=outs,
        scratch_shapes=list(scratch),
        compiler_params=pltpu.CompilerParams(vmem_limit_bytes=limit * MIB),
        cost_estimate=pl.CostEstimate(flops=flops, bytes_accessed=moved, transcendentals=0),
        name=name,
    )(scale, bias, *arrays)


def image_rows(image_refs, image_all):
    own = image_all.shape[0] // 8
    for k, part in enumerate(near_far_order(grouped(image_refs, 2))):
        image_all[k * own : (k + 1) * own] = part


def factor_rows(scale, bias, texts, image_all, factor_all, flipped):
    def images_at(here):
        factor = factors(scale, bias, flat(texts), image_all[here])[1]
        factor_all[:, here] = factor
        flipped[here] = factor.T

    tiles(image_all.shape[0] // 256, 256, images_at)


def match(scale, bias, texts, image_all, factor_all, flipped):
    own = texts.shape[1]
    logits = factors(scale, bias, texts[0], image_all[:own])[0]
    row = lax.broadcasted_iota(jnp.int32, logits.shape, 0)
    column = lax.broadcasted_iota(jnp.int32, logits.shape, 1)
    pull = (-scale / (1.0 + jnp.exp(logits))).astype(BF16)
    factor = jnp.where(row == column, pull, factor_all[:own, :own])
    factor_all[:own, :own] = factor
    flipped[:own, :own] = factor.T


def text_grads(factor_all, image_all, out):
    def columns_at(here):
        grads = product(factor_all[...], image_all[:, here]).astype(BF16)
        out[:, :, here] = grads.reshape(*out.shape[:2], 256)

    tiles(out.shape[-1] // 256, 256, columns_at)


def pairs_even(scale, bias, texts, images):
    count, own, width = texts.shape
    rows = count * own

    def body(scale_ref, bias_ref, texts, *refs):
        image_refs, (factor_all, flipped, image_all) = refs[:10], refs[10:]
        image_rows(image_refs, image_all)
        scale, bias = scale_ref[0], bias_ref[0]
        factor_rows(scale, bias, texts, image_all, factor_all, flipped)
        match(scale, bias, texts, image_all, factor_all, flipped)

    outs = [shape(rows, rows), shape(rows, rows), shape(rows, width)]
    return pair_call("pairs_even", body, outs, scale, bias, (texts, *images), 2 * rows * rows * width, 24)


def pairs_odd(scale, bias, texts, image_all, after):
    count, own, width = texts.shape
    rows = count * own

    def body(scale_ref, bias_ref, texts, image_all, _, flipped, out, factor_all):
        factor_rows(scale_ref[0], bias_ref[0], texts, image_all, factor_all, flipped)
        text_grads(factor_all, image_all, out)

    outs = [shape(rows, rows), shape(count, own, width)]
    scratch = [pltpu.VMEM((rows, rows), BF16)]
    arrays = (texts, image_all, after)
    return pair_call("pairs_odd", body, outs, scale, bias, arrays, 4 * rows * rows * width, 24, scratch)


def pairs_image(name, flips, texts, start, stop, outs, after=None):
    own, width = texts[0].shape[-2:]

    def body(flip_even, flip_odd, even, odd, *out_refs):
        def columns_at(here):
            factor = jnp.concatenate([flip_even[start:stop], flip_odd[start:stop]], axis=1)
            rows = jnp.concatenate([ref[:, :, here].reshape(-1, 256) for ref in (even, odd)], axis=0)
            total = product(factor, rows).astype(BF16)
            place = 0
            for ref in out_refs:
                size = ref.size // width
                ref[..., here] = total[place : place + size].reshape(*ref.shape[:-1], 256)
                place += size

        tiles(width // 256, 256, columns_at)

    flops = 2 * (stop - start) * 16 * own * width
    return call(name, body, outs, (*flips, *texts), flops, 24, after)


def weight_part(name, column, place, pieces, feat, after):
    halves, width = len(pieces) // 5, pieces[-1].shape[-1]
    rows, features = feat.shape
    own = rows // 8
    strip = width // 16
    tile = 256

    def body(column_ref, place_ref, *refs):
        feat_ref, same, other, flipped, moved, result = refs[5 * halves :]
        for n, part in enumerate(near_far_order(grouped(refs, halves))):
            k = NEAR_FAR[n]
            flipped[:, k * own : (k + 1) * own] = part.T
        def features_at(here):
            for k in range(rows // own):
                start = pl.multiple_of((column_ref[0] ^ k) * own, own)
                moved[k * own : (k + 1) * own] = feat_ref[pl.ds(start, own), here]
            result[...] = product(flipped[...], moved[...]).astype(BF16)
            for j, k in enumerate((0, 2, 4, 6, 12, 14, 8, 10)):
                mine = pl.multiple_of((place_ref[0] ^ k) * strip, strip)
                theirs = pl.multiple_of((place_ref[0] ^ (k + 1)) * strip, strip)
                same[j, :, here] = result[pl.ds(mine, strip)]
                other[j, :, here] = result[pl.ds(theirs, strip)]

        tiles(features // tile, tile, features_at)

    smem, vmem = pl.BlockSpec(memory_space=pltpu.SMEM), pl.BlockSpec(memory_space=pltpu.VMEM)
    specs = [smem, smem] + [vmem] * (len(pieces) + 1)
    scratch = [
        pltpu.VMEM((width, rows), BF16),
        pltpu.VMEM((rows, tile), BF16),
        pltpu.VMEM((width, tile), BF16),
    ]
    outs = [shape(8, strip, features)] * 2
    flops = 2 * rows * width * features
    return call(name, body, outs, (column, place, *pieces, feat), flops, 16, after, specs, scratch)


def feature_grad(name, column, pieces, weight):
    halves, width = len(pieces) // 5, pieces[-1].shape[-1]
    features = weight.shape[0]
    own = pieces[-1].shape[0] * halves
    rows = 8 * own
    tile = 256

    def body(column_ref, *refs):
        weight_ref, out = refs[5 * halves :]
        def features_at(here):
            egrad = jnp.concatenate(near_far_order(grouped(refs, halves)), axis=0)
            result = lax.dot_general(
                egrad, weight_ref[here], (((1,), (1,)), ((), ())), preferred_element_type=F32
            ).astype(BF16)
            for n, k in enumerate(NEAR_FAR):
                start = pl.multiple_of((column_ref[0] ^ k) * own, own)
                out[pl.ds(start, own), here] = result[n * own : (n + 1) * own]

        tiles(features // tile, tile, features_at)

    smem, vmem = pl.BlockSpec(memory_space=pltpu.SMEM), pl.BlockSpec(memory_space=pltpu.VMEM)
    outs, ins = [shape(rows, features)], (column, *pieces, weight)
    return call(name, body, outs, ins, 2 * rows * width * features, 16, None, [smem] + [vmem] * (len(pieces) + 1))[0]


def chip_weight(name, same, other, after=None):
    strip, features = same.shape[1:]

    def body(same, got, *outs):
        for j, out in enumerate(outs):
            out[...] = (wide(same, slice(2 * j, 2 * j + 2)) + wide(got, slice(2 * j, 2 * j + 2))).astype(BF16)

    outs = [shape(2, strip, features)] * 4
    return call(name, body, outs, (same, swap(other, "blk", 1)), after=after)


def sum_weight(p02, p46, p1214, p810):
    strip, features = p02.shape[1:]

    def along_z(p02, p46, p1214, p810, p0_out, p2_out):
        total = wide(p02) + wide(p46) + wide(p1214) + wide(p810)
        p0_out[...] = total[0]
        p2_out[...] = total[1].astype(BF16)

    def along_y(p0, p2, out):
        out[...] = p0[...] + wide(p2)

    p46, p1214, p810 = swap(p46, "blk", 4), swap(p1214, "blk", 12), swap(p810, "blk", 8)
    outs = [shape(strip, features, dtype=F32), shape(strip, features)]
    p0, p2 = call("weight_z", along_z, outs, (p02, p46, p1214, p810))
    p2 = swap(p2, "blk", 2)
    return call("weight_y", along_y, outs[:1], (p0, p2))[0].T, (p46, p1214)


def local(img_feat, txt_feat, img_weight, txt_weight, natural_exponent_multiplier, bias):
    scale = jnp.exp(natural_exponent_multiplier)
    blocks = lax.axis_size("mp")
    column = lax.axis_index("mp").astype(jnp.int32)[None]
    place = lax.axis_index("blk").astype(jnp.int32)[None]
    own = img_feat.shape[0] // blocks
    width = img_weight.shape[1]
    one, two = (own, width), (2, own, width)

    half = (2, own // 2, width)
    own_half = (own // 2, width)

    t01, t23, t67, t4, t5 = embed("embed_text", txt_feat, txt_weight, column, blocks)
    t4, t5 = swap(t4, "mp", 6), swap(t5, "mp", 2)
    i01, i23, i67, i4, i5 = embed("embed_image", img_feat, img_weight, column, blocks)
    t23, t67 = call("relay_text", relay_add, [shape(*two)] * 2, (t23, t67, t4, t5))
    t23, t67 = swap(t23, "mp", 2), swap(t67, "mp", 6)
    i4, i5 = swap(i4, "mp", 6), swap(i5, "mp", 2)

    def second(t01, t23, t67, t0_out, t1_out):
        t0_out[...] = wide(t01, 0) + wide(t23, 0) + wide(t67, 0)
        t1_out[...] = (wide(t01, 1) + wide(t23, 1) + wide(t67, 1)).astype(BF16)

    t0, t1 = call("sums_second", second, [shape(*one, dtype=F32), shape(*one)], (t01, t23, t67))
    t1_got = swap(t1, "mp", 1)
    sent = call("relay_image", relay_split, [shape(*half)] * 4, (i23, i67, i4, i5), after=t1)
    got = [(swap(sent[2 * h], "mp", 2), swap(sent[2 * h + 1], "mp", 6)) for h in range(2)]

    def third(t0, t1, text_out, unit_out):
        embedded = t0[...] + wide(t1)
        text_out[...] = embedded
        unit_out[...] = unit_of(embedded)[0].astype(BF16)

    txt_emb, a0 = call("sums_third", third, [shape(*one, dtype=F32), shape(*one)], (t0, t1_got), after=sent[0])
    a2 = swap(a0, "blk", 2)
    (x_a,) = call("image_x_a", add_half(0), [shape(*half)], (i01, *got[0]), after=a0)
    y_a = swap(x_a, "mp", 1)
    (a02,) = call("stack_text", stack, [shape(*two)], (a0, a2), after=x_a)
    a46, a1214 = swap(a02, "blk", 4), swap(a02, "blk", 12)
    (x_b,) = call("image_x_b", add_half(1), [shape(*half)], (i01, *got[1]), after=a02)
    y_b = swap(x_b, "mp", 1)
    outs = [shape(*half, dtype=F32), shape(*half)]
    emb_a, u01_a = call("image_unit_a", norm_half, outs, (x_a, y_a), after=x_b)
    u23_a, u67_a = swap(u01_a, "mp", 2), swap(u01_a, "mp", 6)
    emb_b, u01_b = call("image_unit_b", norm_half, outs, (x_b, y_b), after=u01_a)
    u23_b, u67_b = swap(u01_b, "mp", 2), swap(u01_b, "mp", 6)
    outs = [shape(*own_half)] * 2
    u2_a, u7_a = call("cut_image_a", cut, outs, (u23_a, u67_a), after=u01_b)
    u4_a, u5_a = swap(u2_a, "mp", 6), swap(u7_a, "mp", 2)
    a4, a14 = call("cut_text", cut, [shape(*one)] * 2, (a46, a1214), after=u2_a)
    a8, a10 = swap(a4, "blk", 12), swap(a14, "blk", 4)
    u2_b, u7_b = call("cut_image_b", cut, outs, (u23_b, u67_b), after=a4)
    u4_b, u5_b = swap(u2_b, "mp", 6), swap(u7_b, "mp", 2)

    def collect(a02, a46, a1214, a8, a10, out):
        for k, ref in enumerate((a02, a46, a1214)):
            out[2 * k : 2 * k + 2] = ref[...]
        out[6] = a8[...]
        out[7] = a10[...]

    (even,) = call("collect", collect, [shape(8, *one)], (a02, a46, a1214, a8, a10), after=(u4_a, u5_a, u4_b, u5_b))
    odd = swap(even, "blk", 1)
    images = (u01_a, u01_b, u23_a, u23_b, u67_a, u67_b, u4_a, u4_b, u5_a, u5_b)
    factor_even, flip_even, image_all = pairs_even(scale, bias, even, images)
    flip_odd, odd_sum = pairs_odd(scale, bias, odd, image_all, flip_even)
    odd_got = swap(odd_sum, "blk", 1)
    flips, texts = (flip_even, flip_odd), (even, odd)
    g4, g5 = pairs_image("pairs_far_images", flips, texts, 6 * own, 8 * own, [shape(*one)] * 2, odd_sum)
    g4_got, g5_got = swap(g4, "mp", 6), swap(g5, "mp", 2)
    flops = 128 * own * own * width
    (even_sum,) = call("text_grads_even", text_grads, [shape(8, *one)], (factor_even, image_all), flops, 20, g4)

    def fifth(even, got, p8, p10):
        p8[...] = (wide(even, 6) + wide(got, 6)).astype(BF16)
        p10[...] = (wide(even, 7) + wide(got, 7)).astype(BF16)

    p8, p10 = call("sums_fifth", fifth, [shape(*one)] * 2, (even_sum, odd_got))
    g01, g23, g67 = pairs_image("pairs_near_images", flips, texts, 0, 6 * own, [shape(*two)] * 3, p8)
    p8_got, p10_got = swap(p8, "blk", 12), swap(p10, "blk", 4)
    sent = call("relay_image_grads", relay_split, [shape(*half)] * 4, (g23, g67, g4_got, g5_got))
    got = [(swap(sent[2 * h], "mp", 2), swap(sent[2 * h + 1], "mp", 6)) for h in range(2)]

    def sixth(even, got, p8, p10, p02, p46, p1214):
        for k in range(2):
            p02[k] = (wide(even, k) + wide(got, k)).astype(BF16)
        p46[0] = (wide(even, 2) + wide(got, 2) + wide(p8)).astype(BF16)
        p46[1] = (wide(even, 3) + wide(got, 3)).astype(BF16)
        p1214[0] = (wide(even, 4) + wide(got, 4)).astype(BF16)
        p1214[1] = (wide(even, 5) + wide(got, 5) + wide(p10)).astype(BF16)

    outs = [shape(*two)] * 3
    p02, p46, p1214 = call("sums_sixth", sixth, outs, (even_sum, odd_got, p8_got, p10_got), after=sent[0])
    p46, p1214 = swap(p46, "blk", 4), swap(p1214, "blk", 12)
    (x_a,) = call("image_grads_x_a", add_half(0), [shape(*half)], (g01, *got[0]), after=p02)
    y_a = swap(x_a, "mp", 1)
    (x_b,) = call("image_grads_x_b", add_half(1), [shape(*half)], (g01, *got[1]), after=x_a)
    y_b = swap(x_b, "mp", 1)
    (e01_a,) = call("image_back_a", back_half, [shape(*half)], (x_a, y_a, emb_a), after=x_b)
    e23_a, e67_a = swap(e01_a, "mp", 2), swap(e01_a, "mp", 6)

    def seventh(p02, p46, p1214, p0_out, p2_out):
        p0_out[...] = wide(p02, 0) + wide(p46, 0) + wide(p1214, 0)
        p2_out[...] = (wide(p02, 1) + wide(p46, 1) + wide(p1214, 1)).astype(BF16)

    outs = [shape(*one, dtype=F32), shape(*one)]
    p0, p2 = call("sums_seventh", seventh, outs, (p02, p46, p1214), after=e01_a)
    p2_got = swap(p2, "blk", 2)
    (e01_b,) = call("image_back_b", back_half, [shape(*half)], (x_b, y_b, emb_b), after=p2)
    e23_b, e67_b = swap(e01_b, "mp", 2), swap(e01_b, "mp", 6)
    outs = [shape(*own_half)] * 2
    e2_a, e7_a = call("cut_image_grads_a", cut, outs, (e23_a, e67_a), after=e01_b)
    e4_a, e5_a = swap(e2_a, "mp", 6), swap(e7_a, "mp", 2)

    def text_back(p0, p2, txt_emb, out):
        out[...] = norm_back(p0[...] + wide(p2), txt_emb[...]).astype(BF16)

    (d0,) = call("text_back", text_back, [shape(*one)], (p0, p2_got, txt_emb), after=e2_a)
    d1 = swap(d0, "mp", 1)
    e2_b, e7_b = call("cut_image_grads_b", cut, outs, (e23_b, e67_b), after=d0)
    e4_b, e5_b = swap(e2_b, "mp", 6), swap(e7_b, "mp", 2)
    (d01,) = call("stack_text_grads", stack, [shape(*two)], (d0, d1), after=(e4_a, e5_a, e4_b, e5_b))
    d23, d67 = swap(d01, "mp", 2), swap(d01, "mp", 6)

    e_all = (e01_a, e01_b, e23_a, e23_b, e67_a, e67_b, e4_a, e4_b, e5_a, e5_b)
    same, other = weight_part("weight_image", column, place, e_all, img_feat, d01)
    d2, d7 = call("cut_text_grads", cut, [shape(*one)] * 2, (d23, d67), ORDER_COST, after=same)
    d4, d5 = swap(d2, "mp", 6), swap(d7, "mp", 2)
    image_chip = chip_weight("weight_image_chip", same, other, None)
    img_weight_grad, image_got = sum_weight(*image_chip)
    d_all = (d01, d23, d67, d4, d5)
    same, other = weight_part("weight_text", column, place, d_all, txt_feat, image_got)
    txt_weight_grad, _ = sum_weight(*chip_weight("weight_text_chip", same, other))
    return (
        feature_grad("feature_image", column, e_all, img_weight),
        feature_grad("feature_text", column, d_all, txt_weight),
        img_weight_grad,
        txt_weight_grad,
    )


def solution(mesh):
    return jax.shard_map(
        local,
        mesh=mesh,
        in_specs=(P("blk", "mp"), P("blk", "mp"), P("mp", None), P("mp", None), P(), P()),
        out_specs=(P("blk", "mp"), P("blk", "mp"), P("mp", "blk"), P("mp", "blk")),
        check_vma=False,
    )
```

time: 812 us -> 199 us (0.25)
  waiting for transfers between devices: 536 us -> 74.9 us
  matrix products: 157 us -> 0 us
  Pallas kernels: 0 us -> 40.6 us
  other arithmetic: 12.7 us -> 0 us
  between operations: 15 us -> 2.31 us
  local copies, waits for them, and re-layouts: 16.5 us -> 5.39 us
    reduce_scatter x3 -> x0, waiting for transfers between devices: 226 us -> none  [the longest x1 116 us: local(): lax.psum_scatter(jnp.concatenate([jnp.dot(img_feat, img_weight, preferred...]
    all_gather x3 -> x0, waiting for transfers between devices: 165 us -> none  [the longest x1 55.8 us: local(): lax.all_gather(txt_egrad, 'mp', axis=0, tiled=True)]
    dot_general x54 -> x0, matrix products: 157 us -> none  [the longest x16 75.6 us: cross_contributions(): lax.dot_general(derivative_multiplier, caption_submatrix, (((0,), (0,)),...]
    unnamed x8 -> x0, waiting for transfers between devices: 84.8 us -> none
    pallas_call x0 -> x43, Pallas kernels: none -> 40.6 us  [the longest x41 29.7 us: call(): pl.pallas_call(run, out_shape=outs, in_specs=specs, scratch_shapes=list(s...]
    ppermute x32 -> x64, waiting for transfers between devices: 59.8 us -> 74.9 us  [swap(): return lax.ppermute(value, axis, [(i, i ^ offset) for i in range(count)])]
    ppermute x32 -> x64, starting transfers between devices: 67.9 us -> 74.3 us  [swap(): return lax.ppermute(value, axis, [(i, i ^ offset) for i in range(count)])]
  transfers between devices with their start and end apart: 39 -> 64, of which waited for: 21 -> 40; matrix products, arithmetic and copies ran while one was open for 12% -> 0% of each run, Pallas kernels for 0% -> 15%
where the time goes in v2:
time: 199 us; the launch traced here: 197 us
  waiting for transfers between devices  74.9 us (38%)
  starting transfers between devices  74.3 us (37%)
  Pallas kernels  40.6 us (20%)
  local copies, waits for them, and re-layouts  5.39 us (3%)
  between operations  2.31 us (1%)
    ppermute x64, waiting for transfers between devices, swap(): return lax.ppermute(value, axis, [(i, i ^ offset) for i in range(count)])  74.9 us
    ppermute x64, starting transfers between devices, swap(): return lax.ppermute(value, axis, [(i, i ^ offset) for i in range(count)])  74.3 us
    pallas_call x41, Pallas kernels, call(): pl.pallas_call(run, out_shape=outs, in_specs=specs, scratch_shapes=list(s...  29.7 us
    pallas_call x2, Pallas kernels, pair_call(): pl.pallas_call(body, in_specs=[smem, smem] + [vmem] * len(arrays), out_sh...  10.9 us
    unnamed x22, local copies, waits for them, and re-layouts  5.39 us
  transfers between devices with their start and end apart: 64, of which 40 were waited for; matrix products, arithmetic and copies ran while one was open for 0% of the time, Pallas kernels for 15%

profile of v2, /device:TPU:8, one launch (start us, length us, event | category | flops | bytes accessed | tf_op | source)
XLA Modules:
  0.0 197.4 jit_solution(12350267913495484320)
XLA Ops:
  3.1 2.1 %embed_text.1 = (bf16[2,128,1024]{2,1,0:T(8,128)(2,1)S(1)}, bf16[2,128,1024]{2,1,0:T(8,128)(2,1)S(1)}, bf16[2,128,1024]{2,1,0:T(8,128)(2,1)S(1)}, bf16[128,1024]{1,0:T(8,128)(2,1)S(1)}, bf16[128,1024]{1,0:T(8,128)(2,1)S(1)}) custom-call(s32[1]{0:T(128)} %bitcast.column_ref.refs_1_.refs_2_, bf16[1024,512]{1,0:T(8,128)(2,1)S(1)} %copy-done.9, ...), custom_call_target="tpu_custom_call" | custom-call | flops 1073741824 | bytes 4194308 | tf_op jit(solution)/shard_map/embed_text/pallas_call | solution.py:36
  5.2 2.8 %collective-permute-start = (bf16[128,1024]{1,0:T(8,128)(2,1)S(1)}, bf16[128,1024]{1,0:T(8,128)(2,1)S(1)}, u32[]{:S(2)}, u32[]{:S(2)}) collective-permute-start(bf16[128,1024]{1,0:T(8,128)(2,1)S(1)} %get-tuple-element.80), channel_id=1, source_target_pairs={{0,6},{1,7},{2,4},{3,5},{4,2},{5,3},{6,0},{7,1},{8,14},{9,15},{10,... | collective-permute-start | bytes 786440 | tf_op jit(solution)/shard_map/ppermute | solution.py:18
  8.2 6.3 %collective-permute-done.r4 = bf16[128,1024]{1,0:T(8,128)(2,1)S(1)} collective-permute-done((bf16[128,1024]{1,0:T(8,128)(2,1)S(1)}, bf16[128,1024]{1,0:T(8,128)(2,1)S(1)}, u32[]{:S(2)}, u32[]{:S(2)}) %collective-permute-start) | collective-permute-done | bytes 262176 | tf_op jit(solution)/shard_map/ppermute | solution.py:18
  17.6 2.6 %embed_image.1 = (bf16[2,128,1024]{2,1,0:T(8,128)(2,1)S(1)}, bf16[2,128,1024]{2,1,0:T(8,128)(2,1)S(1)}, bf16[2,128,1024]{2,1,0:T(8,128)(2,1)S(1)}, bf16[128,1024]{1,0:T(8,128)(2,1)S(1)}, bf16[128,1024]{1,0:T(8,128)(2,1)S(1)}) custom-call(s32[1]{0:T(128)} %bitcast.column_ref.refs_1_.refs_2_, bf16[1024,768]{1,0:T(8,128)(2,1)S(1)} %copy-done.5, ...), custom_call_target="tpu_custom_call" | custom-call | flops 1610612736 | bytes 5242884 | tf_op jit(solution)/shard_map/embed_image/pallas_call | solution.py:36
  22.8 8.1 %collective-permute-done.2.t23 = bf16[2,128,1024]{2,1,0:T(8,128)(2,1)S(1)} collective-permute-done((bf16[2,128,1024]{2,1,0:T(8,128)(2,1)S(1)}, bf16[2,128,1024]{2,1,0:T(8,128)(2,1)S(1)}, u32[]{:S(2)}, u32[]{:S(2)}) %collective-permute-start.2) | collective-permute-done | bytes 524320 | tf_op jit(solution)/shard_map/ppermute | solution.py:18
  32.5 2.4 %collective-permute-start.6 = (bf16[128,1024]{1,0:T(8,128)(2,1)S(1)}, bf16[128,1024]{1,0:T(8,128)(2,1)S(1)}, u32[]{:S(2)}, u32[]{:S(2)}) collective-permute-start(bf16[128,1024]{1,0:T(8,128)(2,1)S(1)} %get-tuple-element.84.refs_0_), channel_id=1, source_target_pairs={{0,1},{1,0},{2,3},{3,2},{4,5},{5,4},{6,7},{7,6},{8,9},{9,8},{10,11... | collective-permute-start | bytes 786440 | tf_op jit(solution)/shard_map/ppermute | solution.py:18
  37.4 4.5 %collective-permute-done.6.refs_2_ = bf16[128,1024]{1,0:T(8,128)(2,1)S(1)} collective-permute-done((bf16[128,1024]{1,0:T(8,128)(2,1)S(1)}, bf16[128,1024]{1,0:T(8,128)(2,1)S(1)}, u32[]{:S(2)}, u32[]{:S(2)}) %collective-permute-start.6) | collective-permute-done | bytes 262176 | tf_op jit(solution)/shard_map/ppermute | solution.py:18
  46.3 2.4 %collective-permute-start.12 = (bf16[2,64,1024]{2,1,0:T(8,128)(2,1)S(1)}, bf16[2,64,1024]{2,1,0:T(8,128)(2,1)S(1)}, u32[]{:S(2)}, u32[]{:S(2)}) collective-permute-start(bf16[2,64,1024]{2,1,0:T(8,128)(2,1)S(1)} %image_x_a.1.refs_0_.refs_1_), channel_id=1, source_target_pairs={{0,1},{1,0},{2,3},{3,2},{4,5},{5,4},{6,7},{7,6},{8,9},{9,8},{10,11... | collective-permute-start | bytes 786440 | tf_op jit(solution)/shard_map/ppermute | solution.py:18
  50.8 4.5 %collective-permute-start.19 = (bf16[2,128,1024]{2,1,0:T(8,128)(2,1)S(1)}, bf16[2,128,1024]{2,1,0:T(8,128)(2,1)S(1)}, u32[]{:S(2)}, u32[]{:S(2)}) collective-permute-start(bf16[2,128,1024]{2,1,0:T(8,128)(2,1)S(1)} %stack_text.1.refs_0_.refs_4_), channel_id=1, source_target_pairs={{0,96},{8,104},{16,112},{24,120},{32,64},{40,72},{48,80},{56,88},{... | collective-permute-start | bytes 1572872 | tf_op jit(solution)/shard_map/ppermute | solution.py:18
  55.4 3.0 %collective-permute-start.13 = (bf16[2,64,1024]{2,1,0:T(8,128)(2,1)S(1)}, bf16[2,64,1024]{2,1,0:T(8,128)(2,1)S(1)}, u32[]{:S(2)}, u32[]{:S(2)}) collective-permute-start(bf16[2,64,1024]{2,1,0:T(8,128)(2,1)S(1)} %image_x_b.1.refs_0_.refs_1_), channel_id=1, source_target_pairs={{0,1},{1,0},{2,3},{3,2},{4,5},{5,4},{6,7},{7,6},{8,9},{9,8},{10,11... | collective-permute-start | bytes 786440 | tf_op jit(solution)/shard_map/ppermute | solution.py:18
  59.9 3.5 %collective-permute-done.13.refs_2_ = bf16[2,64,1024]{2,1,0:T(8,128)(2,1)S(1)} collective-permute-done((bf16[2,64,1024]{2,1,0:T(8,128)(2,1)S(1)}, bf16[2,64,1024]{2,1,0:T(8,128)(2,1)S(1)}, u32[]{:S(2)}, u32[]{:S(2)}) %collective-permute-start.13) | collective-permute-done | bytes 262176 | tf_op jit(solution)/shard_map/ppermute | solution.py:18
  64.5 2.3 %collective-permute-done.15.refs_2_.refs_4_ = bf16[2,64,1024]{2,1,0:T(8,128)(2,1)S(1)} collective-permute-done((bf16[2,64,1024]{2,1,0:T(8,128)(2,1)S(1)}, bf16[2,64,1024]{2,1,0:T(8,128)(2,1)S(1)}, u32[]{:S(2)}, u32[]{:S(2)}) %collective-permute-start.15) | collective-permute-done | bytes 262176 | tf_op jit(solution)/shard_map/ppermute | solution.py:18
  74.7 2.5 %collective-permute-start.22 = (bf16[64,1024]{1,0:T(8,128)(2,1)S(1)}, bf16[64,1024]{1,0:T(8,128)(2,1)S(1)}, u32[]{:S(2)}, u32[]{:S(2)}) collective-permute-start(bf16[64,1024]{1,0:T(8,128)(2,1)S(1)} %get-tuple-element.101), channel_id=1, source_target_pairs={{0,6},{1,7},{2,4},{3,5},{4,2},{5,3},{6,0},{7,1},{8,14},{9,15},{10,... | collective-permute-start | bytes 393224 | tf_op jit(solution)/shard_map/ppermute | solution.py:18
  77.1 2.8 %collective-permute-done.16.refs_0_.refs_6_ = bf16[64,1024]{1,0:T(8,128)(2,1)S(1)} collective-permute-done((bf16[64,1024]{1,0:T(8,128)(2,1)S(1)}, bf16[64,1024]{1,0:T(8,128)(2,1)S(1)}, u32[]{:S(2)}, u32[]{:S(2)}) %collective-permute-start.16) | collective-permute-done | bytes 131104 | tf_op jit(solution)/shard_map/ppermute | solution.py:18
  83.9 4.2 %pairs_even.1 = (bf16[1024,1024]{1,0:T(8,128)(2,1)S(1)}, bf16[1024,1024]{1,0:T(8,128)(2,1)S(1)}, bf16[1024,1024]{1,0:T(8,128)(2,1)S(1)}) custom-call(f32[1]{0:T(128)S(6)} %exp.3.scale_ref, f32[1]{0:T(128)S(6)} %copy.11.bias_ref, bf16[8,128,1024]{2,1,0:T(8,128)(2,1)S(1)} %collect.1.texts.refs_3_, bf16[2,64,1024]{2,1,0:T(8,128)(2,1)S(1)} %get-tuple-element.96.refs_0_, ...), custom_call_target="tpu_custom_call" | custom-call | flops 2147483648 | bytes 10485760 | tf_op jit(solution)/shard_map/pairs_even/pallas_call | solution.py:177
  88.1 6.7 %pairs_odd.1 = (bf16[1024,1024]{1,0:T(8,128)(2,1)S(1)}, bf16[8,128,1024]{2,1,0:T(8,128)(2,1)S(1)}) custom-call(f32[1]{0:T(128)S(6)} %exp.3.scale_ref, f32[1]{0:T(128)S(6)} %copy.11.bias_ref, bf16[8,128,1024]{2,1,0:T(8,128)(2,1)S(1)} %collective-permute-done.26.texts.refs_4_, bf16[1024,1024]{1,0:T(8,128)(2,1)S(1)} %get-tuple-element.104.image_all.refs_2_, ...), custom_call_target="tpu_custom_call" | custom-call | flops 4294967296 | bytes 10485760 | tf_op jit(solution)/shard_map/pairs_odd/pallas_call | solution.py:177
  98.6 2.9 %text_grads_even.1.even.refs_1_ = bf16[8,128,1024]{2,1,0:T(8,128)(2,1)S(1)} custom-call(bf16[128,1024]{1,0:T(8,128)(2,1)S(1)} %get-tuple-element.108.refs_0_, bf16[1024,1024]{1,0:T(8,128)(2,1)S(1)} %get-tuple-element.109.refs_1_, bf16[1024,1024]{1,0:T(8,128)(2,1)S(1)} %get-tuple-element.104.image_all.refs_2_), custom_call_target="tpu_custom_call" | custom-call | flops 2147483648 | bytes 6553600 | tf_op jit(solution)/shard_map/text_grads_even/pallas_call | solution.py:36
  101.7 2.1 %collective-permute-start.31 = (bf16[128,1024]{1,0:T(8,128)(2,1)S(1)}, bf16[128,1024]{1,0:T(8,128)(2,1)S(1)}, u32[]{:S(2)}, u32[]{:S(2)}) collective-permute-start(bf16[128,1024]{1,0:T(8,128)(2,1)S(1)} %get-tuple-element.115), channel_id=1, source_target_pairs={{0,32},{8,40},{16,48},{24,56},{32,0},{40,8},{48,16},{56,24},{64,96... | collective-permute-start | bytes 786440 | tf_op jit(solution)/shard_map/ppermute | solution.py:18
  104.2 4.1 %pairs_near_images.1 = (bf16[2,128,1024]{2,1,0:T(8,128)(2,1)S(1)}, bf16[2,128,1024]{2,1,0:T(8,128)(2,1)S(1)}, bf16[2,128,1024]{2,1,0:T(8,128)(2,1)S(1)}) custom-call(bf16[128,1024]{1,0:T(8,128)(2,1)S(1)} %get-tuple-element.110.refs_0_, bf16[1024,1024]{1,0:T(8,128)(2,1)S(1)} %get-tuple-element.105._.refs_1_, ...), custom_call_target="tpu_custom_call" | custom-call | flops 3221225472 | bytes 10223616 | tf_op jit(solution)/shard_map/pairs_near_images/pallas_call | solution.py:36
  119.5 2.8 %collective-permute-start.36 = (bf16[2,64,1024]{2,1,0:T(8,128)(2,1)S(1)}, bf16[2,64,1024]{2,1,0:T(8,128)(2,1)S(1)}, u32[]{:S(2)}, u32[]{:S(2)}) collective-permute-start(bf16[2,64,1024]{2,1,0:T(8,128)(2,1)S(1)} %image_grads_x_a.1.refs_0_.refs_1_), channel_id=1, source_target_pairs={{0,1},{1,0},{2,3},{3,2},{4,5},{5,4},{6,7},{7,6},{8,9},{9,8},{10,11... | collective-permute-start | bytes 786440 | tf_op jit(solution)/shard_map/ppermute | solution.py:18
  124.9 2.3 %collective-permute-start.39 = (bf16[2,64,1024]{2,1,0:T(8,128)(2,1)S(1)}, bf16[2,64,1024]{2,1,0:T(8,128)(2,1)S(1)}, u32[]{:S(2)}, u32[]{:S(2)}) collective-permute-start(bf16[2,64,1024]{2,1,0:T(8,128)(2,1)S(1)} %image_grads_x_b.1.refs_0_.refs_1_), channel_id=1, source_target_pairs={{0,1},{1,0},{2,3},{3,2},{4,5},{5,4},{6,7},{7,6},{8,9},{9,8},{10,11... | collective-permute-start | bytes 786440 | tf_op jit(solution)/shard_map/ppermute | solution.py:18
  131.3 4.5 %collective-permute-done.39.refs_2_ = bf16[2,64,1024]{2,1,0:T(8,128)(2,1)S(1)} collective-permute-done((bf16[2,64,1024]{2,1,0:T(8,128)(2,1)S(1)}, bf16[2,64,1024]{2,1,0:T(8,128)(2,1)S(1)}, u32[]{:S(2)}, u32[]{:S(2)}) %collective-permute-start.39) | collective-permute-done | bytes 262176 | tf_op jit(solution)/shard_map/ppermute | solution.py:18
  138.6 2.8 %collective-permute-start.49 = (bf16[128,1024]{1,0:T(8,128)(2,1)S(1)}, bf16[128,1024]{1,0:T(8,128)(2,1)S(1)}, u32[]{:S(2)}, u32[]{:S(2)}) collective-permute-start(bf16[128,1024]{1,0:T(8,128)(2,1)S(1)} %text_back.1.refs_0_.refs_4_), channel_id=1, source_target_pairs={{0,1},{1,0},{2,3},{3,2},{4,5},{5,4},{6,7},{7,6},{8,9},{9,8},{10,11... | collective-permute-start | bytes 786440 | tf_op jit(solution)/shard_map/ppermute | solution.py:18
  141.4 3.2 %collective-permute-start.44 = (bf16[64,1024]{1,0:T(8,128)(2,1)S(1)}, bf16[64,1024]{1,0:T(8,128)(2,1)S(1)}, u32[]{:S(2)}, u32[]{:S(2)}) collective-permute-start(bf16[64,1024]{1,0:T(8,128)(2,1)S(1)} %get-tuple-element.126.refs_0_), channel_id=1, source_target_pairs={{0,6},{1,7},{2,4},{3,5},{4,2},{5,3},{6,0},{7,1},{8,14},{9,15},{10,... | collective-permute-start | bytes 393224 | tf_op jit(solution)/shard_map/ppermute | solution.py:18
  149.7 4.3 %collective-permute-done.46.refs_7_.refs_2_.refs_10_ = bf16[64,1024]{1,0:T(8,128)(2,1)S(1)} collective-permute-done((bf16[64,1024]{1,0:T(8,128)(2,1)S(1)}, bf16[64,1024]{1,0:T(8,128)(2,1)S(1)}, u32[]{:S(2)}, u32[]{:S(2)}) %collective-permute-start.46) | collective-permute-done | bytes 131104 | tf_op jit(solution)/shard_map/ppermute | solution.py:18
  158.9 2.9 %weight_image.1 = (bf16[8,64,768]{2,1,0:T(8,128)(2,1)S(1)}, bf16[8,64,768]{2,1,0:T(8,128)(2,1)S(1)}) custom-call(bf16[2,128,1024]{2,1,0:T(8,128)(2,1)S(1)} %stack_text_grads.1.refs_0_.refs_4_, s32[1]{0:T(128)} %bitcast.column_ref.refs_1_.refs_2_, s32[1]{0:T(128)} %bitcast.1.refs_2_.refs_3_, bf16[2,64,1024]{2,1,0:T(8,128)(2,1)S(1)} %image_back_a.1.refs_0_.refs_3_, ...), custom_call_target="tpu_custom_call" | custom-call | flops 1610612736 | bytes 5767176 | tf_op jit(solution)/shard_map/weight_image/pallas_call | solution.py:36
  161.9 3.3 %collective-permute-done.51.refs_2_.refs_6_ = bf16[2,128,1024]{2,1,0:T(8,128)(2,1)S(1)} collective-permute-done((bf16[2,128,1024]{2,1,0:T(8,128)(2,1)S(1)}, bf16[2,128,1024]{2,1,0:T(8,128)(2,1)S(1)}, u32[]{:S(2)}, u32[]{:S(2)}) %collective-permute-start.51) | collective-permute-done | bytes 524320 | tf_op jit(solution)/shard_map/ppermute | solution.py:18
  170.0 3.5 %collective-permute-done.52.refs_3_.refs_7_ = bf16[128,1024]{1,0:T(8,128)(2,1)S(1)} collective-permute-done((bf16[128,1024]{1,0:T(8,128)(2,1)S(1)}, bf16[128,1024]{1,0:T(8,128)(2,1)S(1)}, u32[]{:S(2)}, u32[]{:S(2)}) %collective-permute-start.52) | collective-permute-done | bytes 262176 | tf_op jit(solution)/shard_map/ppermute | solution.py:18
  175.6 2.2 %weight_text.1 = (bf16[8,64,512]{2,1,0:T(8,128)(2,1)S(1)}, bf16[8,64,512]{2,1,0:T(8,128)(2,1)S(1)}) custom-call(bf16[2,64,768]{2,1,0:T(8,128)(2,1)S(1)} %collective-permute-done.55.p46.refs_0_, bf16[2,64,768]{2,1,0:T(8,128)(2,1)S(1)} %collective-permute-done.56.p1214.refs_1_, s32[1]{0:T(128)} %bitcast.column_ref.refs_1_.refs_2_, s32[1]{0:T(128)} %bitcast.1.refs_2_.refs_3_, ...), custom_call_target="tpu_custom_call" | custom-call | flops 1073741824 | bytes 4587528 | tf_op jit(solution)/shard_map/weight_text/pallas_call | solution.py:36
  184.1 3.4 %feature_image.1 = bf16[1024,768]{1,0:T(8,128)(2,1)} custom-call(s32[1]{0:T(128)} %bitcast.column_ref.refs_1_.refs_2_, bf16[2,64,1024]{2,1,0:T(8,128)(2,1)S(1)} %image_back_a.1.refs_0_.refs_3_, bf16[2,64,1024]{2,1,0:T(8,128)(2,1)S(1)} %image_back_b.1.refs_0_.refs_1_.refs_4_, bf16[2,64,1024]{2,1,0:T(8,128)(2,1)S(1)} %collective-permute-done.40.refs_1_.refs_2_.refs_5_, ...), custom_call_target="tpu_custom_call" | custom-call | flops 1610612736 | bytes 5242884 | tf_op jit(solution)/shard_map/feature_image/pallas_call | solution.py:36
  189.9 2.4 %collective-permute-done.62.p810 = bf16[2,64,512]{2,1,0:T(8,128)(2,1)S(1)} collective-permute-done((bf16[2,64,512]{2,1,0:T(8,128)(2,1)S(1)}, bf16[2,64,512]{2,1,0:T(8,128)(2,1)S(1)}, u32[]{:S(2)}, u32[]{:S(2)}) %collective-permute-start.62) | collective-permute-done | bytes 131104 | tf_op jit(solution)/shard_map/ppermute | solution.py:18
  193.0 2.5 %feature_text.1 = bf16[1024,512]{1,0:T(8,128)(2,1)} custom-call(s32[1]{0:T(128)} %bitcast.column_ref.refs_1_.refs_2_, bf16[2,128,1024]{2,1,0:T(8,128)(2,1)S(1)} %stack_text_grads.1.refs_0_.refs_4_, bf16[2,128,1024]{2,1,0:T(8,128)(2,1)S(1)} %collective-permute-done.50.refs_1_.refs_5_, bf16[2,128,1024]{2,1,0:T(8,128)(2,1)S(1)} %collective-permute-done.51.refs_2_.refs_6_, ...), custom_call_target="tpu_custom_call" | custom-call | flops 1073741824 | bytes 4194308 | tf_op jit(solution)/shard_map/feature_text/pallas_call | solution.py:36
  (161 shorter events, 85.4 us)
Async XLA Ops:
  5.2 9.3 %collective-permute-start = (bf16[128,1024]{1,0:T(8,128)(2,1)S(1)}, bf16[128,1024]{1,0:T(8,128)(2,1)S(1)}, u32[]{:S(2)}, u32[]{:S(2)}) collective-permute-start(bf16[128,1024]{1,0:T(8,128)(2,1)S(1)} %get-tuple-element.80), channel_id=1, source_target_pairs={{0,6},{1,7},{2,4},{3,5},{4,2},{5,3},{6,0},{7,1},{8,14},{9,15},{10,... | collective-permute-start | bytes 786440 | tf_op jit(solution)/shard_map/ppermute | solution.py:18
  15.9 14.9 %collective-permute-start.2 = (bf16[2,128,1024]{2,1,0:T(8,128)(2,1)S(1)}, bf16[2,128,1024]{2,1,0:T(8,128)(2,1)S(1)}, u32[]{:S(2)}, u32[]{:S(2)}) collective-permute-start(bf16[2,128,1024]{2,1,0:T(8,128)(2,1)S(1)} %get-tuple-element.82), channel_id=1, source_target_pairs={{0,2},{1,3},{2,0},{3,1},{4,6},{5,7},{6,4},{7,5},{8,10},{9,11},{10,... | collective-permute-start | bytes 1572872 | tf_op jit(solution)/shard_map/ppermute | solution.py:18
  16.3 16.1 %collective-permute-start.3 = (bf16[2,128,1024]{2,1,0:T(8,128)(2,1)S(1)}, bf16[2,128,1024]{2,1,0:T(8,128)(2,1)S(1)}, u32[]{:S(2)}, u32[]{:S(2)}) collective-permute-start(bf16[2,128,1024]{2,1,0:T(8,128)(2,1)S(1)} %get-tuple-element.83), channel_id=1, source_target_pairs={{0,6},{1,7},{2,4},{3,5},{4,2},{5,3},{6,0},{7,1},{8,14},{9,15},{10,... | collective-permute-start | bytes 1572872 | tf_op jit(solution)/shard_map/ppermute | solution.py:18
  20.2 15.1 %collective-permute-start.4 = (bf16[128,1024]{1,0:T(8,128)(2,1)S(1)}, bf16[128,1024]{1,0:T(8,128)(2,1)S(1)}, u32[]{:S(2)}, u32[]{:S(2)}) collective-permute-start(bf16[128,1024]{1,0:T(8,128)(2,1)S(1)} %get-tuple-element.87), channel_id=1, source_target_pairs={{0,6},{1,7},{2,4},{3,5},{4,2},{5,3},{6,0},{7,1},{8,14},{9,15},{10,... | collective-permute-start | bytes 786440 | tf_op jit(solution)/shard_map/ppermute | solution.py:18
  22.2 13.2 %collective-permute-start.5 = (bf16[128,1024]{1,0:T(8,128)(2,1)S(1)}, bf16[128,1024]{1,0:T(8,128)(2,1)S(1)}, u32[]{:S(2)}, u32[]{:S(2)}) collective-permute-start(bf16[128,1024]{1,0:T(8,128)(2,1)S(1)} %get-tuple-element.88), channel_id=1, source_target_pairs={{0,2},{1,3},{2,0},{3,1},{4,6},{5,7},{6,4},{7,5},{8,10},{9,11},{10,... | collective-permute-start | bytes 786440 | tf_op jit(solution)/shard_map/ppermute | solution.py:18
  32.5 9.3 %collective-permute-start.6 = (bf16[128,1024]{1,0:T(8,128)(2,1)S(1)}, bf16[128,1024]{1,0:T(8,128)(2,1)S(1)}, u32[]{:S(2)}, u32[]{:S(2)}) collective-permute-start(bf16[128,1024]{1,0:T(8,128)(2,1)S(1)} %get-tuple-element.84.refs_0_), channel_id=1, source_target_pairs={{0,1},{1,0},{2,3},{3,2},{4,5},{5,4},{6,7},{7,6},{8,9},{9,8},{10,11... | collective-permute-start | bytes 786440 | tf_op jit(solution)/shard_map/ppermute | solution.py:18
  35.5 10.1 %collective-permute-start.8 = (bf16[2,64,1024]{2,1,0:T(8,128)(2,1)S(1)}, bf16[2,64,1024]{2,1,0:T(8,128)(2,1)S(1)}, u32[]{:S(2)}, u32[]{:S(2)}) collective-permute-start(bf16[2,64,1024]{2,1,0:T(8,128)(2,1)S(1)} %get-tuple-element.93), channel_id=1, source_target_pairs={{0,6},{1,7},{2,4},{3,5},{4,2},{5,3},{6,0},{7,1},{8,14},{9,15},{10,... | collective-permute-start | bytes 786440 | tf_op jit(solution)/shard_map/ppermute | solution.py:18
  43.0 12.3 %collective-permute-start.10 = (bf16[2,64,1024]{2,1,0:T(8,128)(2,1)S(1)}, bf16[2,64,1024]{2,1,0:T(8,128)(2,1)S(1)}, u32[]{:S(2)}, u32[]{:S(2)}) collective-permute-start(bf16[2,64,1024]{2,1,0:T(8,128)(2,1)S(1)} %get-tuple-element.94), channel_id=1, source_target_pairs={{0,2},{1,3},{2,0},{3,1},{4,6},{5,7},{6,4},{7,5},{8,10},{9,11},{10,... | collective-permute-start | bytes 786440 | tf_op jit(solution)/shard_map/ppermute | solution.py:18
  43.0 12.3 %collective-permute-start.11 = (bf16[2,64,1024]{2,1,0:T(8,128)(2,1)S(1)}, bf16[2,64,1024]{2,1,0:T(8,128)(2,1)S(1)}, u32[]{:S(2)}, u32[]{:S(2)}) collective-permute-start(bf16[2,64,1024]{2,1,0:T(8,128)(2,1)S(1)} %get-tuple-element.95), channel_id=1, source_target_pairs={{0,6},{1,7},{2,4},{3,5},{4,2},{5,3},{6,0},{7,1},{8,14},{9,15},{10,... | collective-permute-start | bytes 786440 | tf_op jit(solution)/shard_map/ppermute | solution.py:18
  46.3 12.1 %collective-permute-start.12 = (bf16[2,64,1024]{2,1,0:T(8,128)(2,1)S(1)}, bf16[2,64,1024]{2,1,0:T(8,128)(2,1)S(1)}, u32[]{:S(2)}, u32[]{:S(2)}) collective-permute-start(bf16[2,64,1024]{2,1,0:T(8,128)(2,1)S(1)} %image_x_a.1.refs_0_.refs_1_), channel_id=1, source_target_pairs={{0,1},{1,0},{2,3},{3,2},{4,5},{5,4},{6,7},{7,6},{8,9},{9,8},{10,11... | collective-permute-start | bytes 786440 | tf_op jit(solution)/shard_map/ppermute | solution.py:18
  50.8 18.2 %collective-permute-start.19 = (bf16[2,128,1024]{2,1,0:T(8,128)(2,1)S(1)}, bf16[2,128,1024]{2,1,0:T(8,128)(2,1)S(1)}, u32[]{:S(2)}, u32[]{:S(2)}) collective-permute-start(bf16[2,128,1024]{2,1,0:T(8,128)(2,1)S(1)} %stack_text.1.refs_0_.refs_4_), channel_id=1, source_target_pairs={{0,96},{8,104},{16,112},{24,120},{32,64},{40,72},{48,80},{56,88},{... | collective-permute-start | bytes 1572872 | tf_op jit(solution)/shard_map/ppermute | solution.py:18
  55.3 13.7 %collective-permute-start.18 = (bf16[2,128,1024]{2,1,0:T(8,128)(2,1)S(1)}, bf16[2,128,1024]{2,1,0:T(8,128)(2,1)S(1)}, u32[]{:S(2)}, u32[]{:S(2)}) collective-permute-start(bf16[2,128,1024]{2,1,0:T(8,128)(2,1)S(1)} %stack_text.1.refs_0_.refs_4_), channel_id=1, source_target_pairs={{0,32},{8,40},{16,48},{24,56},{32,0},{40,8},{48,16},{56,24},{64,96... | collective-permute-start | bytes 1572872 | tf_op jit(solution)/shard_map/ppermute | solution.py:18
  59.3 8.9 %collective-permute-start.14 = (bf16[2,64,1024]{2,1,0:T(8,128)(2,1)S(1)}, bf16[2,64,1024]{2,1,0:T(8,128)(2,1)S(1)}, u32[]{:S(2)}, u32[]{:S(2)}) collective-permute-start(bf16[2,64,1024]{2,1,0:T(8,128)(2,1)S(1)} %get-tuple-element.96.refs_0_), channel_id=1, source_target_pairs={{0,2},{1,3},{2,0},{3,1},{4,6},{5,7},{6,4},{7,5},{8,10},{9,11},{10,... | collective-permute-start | bytes 786440 | tf_op jit(solution)/shard_map/ppermute | solution.py:18
  63.5 10.3 %collective-permute-start.21 = (bf16[2,64,1024]{2,1,0:T(8,128)(2,1)S(1)}, bf16[2,64,1024]{2,1,0:T(8,128)(2,1)S(1)}, u32[]{:S(2)}, u32[]{:S(2)}) collective-permute-start(bf16[2,64,1024]{2,1,0:T(8,128)(2,1)S(1)} %get-tuple-element.97.refs_0_.refs_1_), channel_id=1, source_target_pairs={{0,6},{1,7},{2,4},{3,5},{4,2},{5,3},{6,0},{7,1},{8,14},{9,15},{10,... | collective-permute-start | bytes 786440 | tf_op jit(solution)/shard_map/ppermute | solution.py:18
  69.0 13.1 %collective-permute-start.25 = (bf16[128,1024]{1,0:T(8,128)(2,1)S(1)}, bf16[128,1024]{1,0:T(8,128)(2,1)S(1)}, u32[]{:S(2)}, u32[]{:S(2)}) collective-permute-start(bf16[128,1024]{1,0:T(8,128)(2,1)S(1)} %get-tuple-element.103), channel_id=1, source_target_pairs={{0,32},{8,40},{16,48},{24,56},{32,0},{40,8},{48,16},{56,24},{64,96... | collective-permute-start | bytes 786440 | tf_op jit(solution)/shard_map/ppermute | solution.py:18
  71.0 11.1 %collective-permute-start.24 = (bf16[128,1024]{1,0:T(8,128)(2,1)S(1)}, bf16[128,1024]{1,0:T(8,128)(2,1)S(1)}, u32[]{:S(2)}, u32[]{:S(2)}) collective-permute-start(bf16[128,1024]{1,0:T(8,128)(2,1)S(1)} %get-tuple-element.100.refs_0_), channel_id=1, source_target_pairs={{0,96},{8,104},{16,112},{24,120},{32,64},{40,72},{48,80},{56,88},{... | collective-permute-start | bytes 786440 | tf_op jit(solution)/shard_map/ppermute | solution.py:18
  97.2 11.1 %collective-permute-start.29 = (bf16[128,1024]{1,0:T(8,128)(2,1)S(1)}, bf16[128,1024]{1,0:T(8,128)(2,1)S(1)}, u32[]{:S(2)}, u32[]{:S(2)}) collective-permute-start(bf16[128,1024]{1,0:T(8,128)(2,1)S(1)} %get-tuple-element.113), channel_id=1, source_target_pairs={{0,2},{1,3},{2,0},{3,1},{4,6},{5,7},{6,4},{7,5},{8,10},{9,11},{10,... | collective-permute-start | bytes 786440 | tf_op jit(solution)/shard_map/ppermute | solution.py:18
  97.3 11.0 %collective-permute-start.28 = (bf16[128,1024]{1,0:T(8,128)(2,1)S(1)}, bf16[128,1024]{1,0:T(8,128)(2,1)S(1)}, u32[]{:S(2)}, u32[]{:S(2)}) collective-permute-start(bf16[128,1024]{1,0:T(8,128)(2,1)S(1)} %get-tuple-element.108.refs_0_), channel_id=1, source_target_pairs={{0,6},{1,7},{2,4},{3,5},{4,2},{5,3},{6,0},{7,1},{8,14},{9,15},{10,... | collective-permute-start | bytes 786440 | tf_op jit(solution)/shard_map/ppermute | solution.py:18
  101.7 9.2 %collective-permute-start.31 = (bf16[128,1024]{1,0:T(8,128)(2,1)S(1)}, bf16[128,1024]{1,0:T(8,128)(2,1)S(1)}, u32[]{:S(2)}, u32[]{:S(2)}) collective-permute-start(bf16[128,1024]{1,0:T(8,128)(2,1)S(1)} %get-tuple-element.115), channel_id=1, source_target_pairs={{0,32},{8,40},{16,48},{24,56},{32,0},{40,8},{48,16},{56,24},{64,96... | collective-permute-start | bytes 786440 | tf_op jit(solution)/shard_map/ppermute | solution.py:18
  103.8 8.9 %collective-permute-start.30 = (bf16[128,1024]{1,0:T(8,128)(2,1)S(1)}, bf16[128,1024]{1,0:T(8,128)(2,1)S(1)}, u32[]{:S(2)}, u32[]{:S(2)}) collective-permute-start(bf16[128,1024]{1,0:T(8,128)(2,1)S(1)} %get-tuple-element.110.refs_0_), channel_id=1, source_target_pairs={{0,96},{8,104},{16,112},{24,120},{32,64},{40,72},{48,80},{56,88},{... | collective-permute-start | bytes 786440 | tf_op jit(solution)/shard_map/ppermute | solution.py:18
  110.1 9.2 %collective-permute-start.32 = (bf16[2,64,1024]{2,1,0:T(8,128)(2,1)S(1)}, bf16[2,64,1024]{2,1,0:T(8,128)(2,1)S(1)}, u32[]{:S(2)}, u32[]{:S(2)}) collective-permute-start(bf16[2,64,1024]{2,1,0:T(8,128)(2,1)S(1)} %get-tuple-element.114.refs_0_), channel_id=1, source_target_pairs={{0,2},{1,3},{2,0},{3,1},{4,6},{5,7},{6,4},{7,5},{8,10},{9,11},{10,... | collective-permute-start | bytes 786440 | tf_op jit(solution)/shard_map/ppermute | solution.py:18
  113.1 16.8 %collective-permute-start.37 = (bf16[2,128,1024]{2,1,0:T(8,128)(2,1)S(1)}, bf16[2,128,1024]{2,1,0:T(8,128)(2,1)S(1)}, u32[]{:S(2)}, u32[]{:S(2)}) collective-permute-start(bf16[2,128,1024]{2,1,0:T(8,128)(2,1)S(1)} %get-tuple-element.122), channel_id=1, source_target_pairs={{0,32},{8,40},{16,48},{24,56},{32,0},{40,8},{48,16},{56,24},{64,96... | collective-permute-start | bytes 1572872 | tf_op jit(solution)/shard_map/ppermute | solution.py:18
  113.2 16.8 %collective-permute-start.38 = (bf16[2,128,1024]{2,1,0:T(8,128)(2,1)S(1)}, bf16[2,128,1024]{2,1,0:T(8,128)(2,1)S(1)}, u32[]{:S(2)}, u32[]{:S(2)}) collective-permute-start(bf16[2,128,1024]{2,1,0:T(8,128)(2,1)S(1)} %get-tuple-element.123), channel_id=1, source_target_pairs={{0,96},{8,104},{16,112},{24,120},{32,64},{40,72},{48,80},{56,88},{... | collective-permute-start | bytes 1572872 | tf_op jit(solution)/shard_map/ppermute | solution.py:18
  124.9 10.8 %collective-permute-start.39 = (bf16[2,64,1024]{2,1,0:T(8,128)(2,1)S(1)}, bf16[2,64,1024]{2,1,0:T(8,128)(2,1)S(1)}, u32[]{:S(2)}, u32[]{:S(2)}) collective-permute-start(bf16[2,64,1024]{2,1,0:T(8,128)(2,1)S(1)} %image_grads_x_b.1.refs_0_.refs_1_), channel_id=1, source_target_pairs={{0,1},{1,0},{2,3},{3,2},{4,5},{5,4},{6,7},{7,6},{8,9},{9,8},{10,11... | collective-permute-start | bytes 786440 | tf_op jit(solution)/shard_map/ppermute | solution.py:18
  128.6 9.3 %collective-permute-start.42 = (bf16[2,64,1024]{2,1,0:T(8,128)(2,1)S(1)}, bf16[2,64,1024]{2,1,0:T(8,128)(2,1)S(1)}, u32[]{:S(2)}, u32[]{:S(2)}) collective-permute-start(bf16[2,64,1024]{2,1,0:T(8,128)(2,1)S(1)} %image_back_a.1.refs_0_.refs_3_), channel_id=1, source_target_pairs={{0,6},{1,7},{2,4},{3,5},{4,2},{5,3},{6,0},{7,1},{8,14},{9,15},{10,... | collective-permute-start | bytes 786440 | tf_op jit(solution)/shard_map/ppermute | solution.py:18
  136.0 9.4 %collective-permute-start.43 = (bf16[2,64,1024]{2,1,0:T(8,128)(2,1)S(1)}, bf16[2,64,1024]{2,1,0:T(8,128)(2,1)S(1)}, u32[]{:S(2)}, u32[]{:S(2)}) collective-permute-start(bf16[2,64,1024]{2,1,0:T(8,128)(2,1)S(1)} %image_back_b.1.refs_0_.refs_1_.refs_4_), channel_id=1, source_target_pairs={{0,6},{1,7},{2,4},{3,5},{4,2},{5,3},{6,0},{7,1},{8,14},{9,15},{10,... | collective-permute-start | bytes 786440 | tf_op jit(solution)/shard_map/ppermute | solution.py:18
  138.6 15.5 %collective-permute-start.49 = (bf16[128,1024]{1,0:T(8,128)(2,1)S(1)}, bf16[128,1024]{1,0:T(8,128)(2,1)S(1)}, u32[]{:S(2)}, u32[]{:S(2)}) collective-permute-start(bf16[128,1024]{1,0:T(8,128)(2,1)S(1)} %text_back.1.refs_0_.refs_4_), channel_id=1, source_target_pairs={{0,1},{1,0},{2,3},{3,2},{4,5},{5,4},{6,7},{7,6},{8,9},{9,8},{10,11... | collective-permute-start | bytes 786440 | tf_op jit(solution)/shard_map/ppermute | solution.py:18
  154.8 10.4 %collective-permute-start.51 = (bf16[2,128,1024]{2,1,0:T(8,128)(2,1)S(1)}, bf16[2,128,1024]{2,1,0:T(8,128)(2,1)S(1)}, u32[]{:S(2)}, u32[]{:S(2)}) collective-permute-start(bf16[2,128,1024]{2,1,0:T(8,128)(2,1)S(1)} %stack_text_grads.1.refs_0_.refs_4_), channel_id=1, source_target_pairs={{0,6},{1,7},{2,4},{3,5},{4,2},{5,3},{6,0},{7,1},{8,14},{9,15},{10,... | collective-permute-start | bytes 1572872 | tf_op jit(solution)/shard_map/ppermute | solution.py:18
  156.6 9.2 %collective-permute-start.50 = (bf16[2,128,1024]{2,1,0:T(8,128)(2,1)S(1)}, bf16[2,128,1024]{2,1,0:T(8,128)(2,1)S(1)}, u32[]{:S(2)}, u32[]{:S(2)}) collective-permute-start(bf16[2,128,1024]{2,1,0:T(8,128)(2,1)S(1)} %stack_text_grads.1.refs_0_.refs_4_), channel_id=1, source_target_pairs={{0,2},{1,3},{2,0},{3,1},{4,6},{5,7},{6,4},{7,5},{8,10},{9,11},{10,... | collective-permute-start | bytes 1572872 | tf_op jit(solution)/shard_map/ppermute | solution.py:18
  177.9 9.6 %collective-permute-start.57 = (bf16[2,64,768]{2,1,0:T(8,128)(2,1)S(1)}, bf16[2,64,768]{2,1,0:T(8,128)(2,1)S(1)}, u32[]{:S(2)}, u32[]{:S(2)}) collective-permute-start(bf16[2,64,768]{2,1,0:T(8,128)(2,1)S(1)} %get-tuple-element.139), channel_id=1, source_target_pairs={{0,64},{8,72},{16,80},{24,88},{32,96},{40,104},{48,112},{56,120},{... | collective-permute-start | bytes 589832 | tf_op jit(solution)/shard_map/ppermute | solution.py:18
  180.3 9.6 %collective-permute-start.61 = (bf16[2,64,512]{2,1,0:T(8,128)(2,1)S(1)}, bf16[2,64,512]{2,1,0:T(8,128)(2,1)S(1)}, u32[]{:S(2)}, u32[]{:S(2)}) collective-permute-start(bf16[2,64,512]{2,1,0:T(8,128)(2,1)S(1)} %get-tuple-element.146), channel_id=1, source_target_pairs={{0,96},{8,104},{16,112},{24,120},{32,64},{40,72},{48,80},{56,88},{... | collective-permute-start | bytes 393224 | tf_op jit(solution)/shard_map/ppermute | solution.py:18
  182.2 10.1 %collective-permute-start.62 = (bf16[2,64,512]{2,1,0:T(8,128)(2,1)S(1)}, bf16[2,64,512]{2,1,0:T(8,128)(2,1)S(1)}, u32[]{:S(2)}, u32[]{:S(2)}) collective-permute-start(bf16[2,64,512]{2,1,0:T(8,128)(2,1)S(1)} %get-tuple-element.147), channel_id=1, source_target_pairs={{0,64},{8,72},{16,80},{24,88},{32,96},{40,104},{48,112},{56,120},{... | collective-permute-start | bytes 393224 | tf_op jit(solution)/shard_map/ppermute | solution.py:18
  (43 other events, 315.5 us)

commit v3 on v2

--- a/solution.py
+++ b/solution.py
@@ -9,7 +9,7 @@
 BF16 = jnp.bfloat16
 F32 = jnp.float32
 MIB = 1024 * 1024
-ORDER_COST = 12 * 10**9
+ORDER_COST = 30 * 10**9
 NEAR_FAR = (0, 1, 2, 3, 6, 7, 4, 5)
 
 
@@ -44,7 +44,12 @@
     )(*ins)
 
 
-def tiles(count, size, body):
+def tiles(count, size, body, unroll=False):
+    if unroll:
+        for index in range(count):
+            body(slice(index * size, (index + 1) * size))
+        return
+
     def step(index, carry):
         body(pl.ds(pl.multiple_of(index * size, size), size))
         return carry
@@ -191,13 +196,13 @@
         image_all[k * own : (k + 1) * own] = part
 
 
-def factor_rows(scale, bias, texts, image_all, factor_all, flipped):
+def factor_rows(scale, bias, texts, image_all, factor_all, flipped, tile, unroll):
     def images_at(here):
         factor = factors(scale, bias, flat(texts), image_all[here])[1]
         factor_all[:, here] = factor
         flipped[here] = factor.T
 
-    tiles(image_all.shape[0] // 256, 256, images_at)
+    tiles(image_all.shape[0] // tile, tile, images_at, unroll)
 
 
 def match(scale, bias, texts, image_all, factor_all, flipped):
@@ -211,12 +216,12 @@
     flipped[:own, :own] = factor.T
 
 
-def text_grads(factor_all, image_all, out):
+def text_grads(factor_all, image_all, out, tile=512, unroll=False):
     def columns_at(here):
         grads = product(factor_all[...], image_all[:, here]).astype(BF16)
-        out[:, :, here] = grads.reshape(*out.shape[:2], 256)
-
-    tiles(out.shape[-1] // 256, 256, columns_at)
+        out[:, :, here] = grads.reshape(*out.shape[:2], tile)
+
+    tiles(out.shape[-1] // tile, tile, columns_at, unroll)
 
 
 def pairs_even(scale, bias, texts, images):
@@ -227,7 +232,7 @@
         image_refs, (factor_all, flipped, image_all) = refs[:10], refs[10:]
         image_rows(image_refs, image_all)
         scale, bias = scale_ref[0], bias_ref[0]
-        factor_rows(scale, bias, texts, image_all, factor_all, flipped)
+        factor_rows(scale, bias, texts, image_all, factor_all, flipped, 512, False)
         match(scale, bias, texts, image_all, factor_all, flipped)
 
     outs = [shape(rows, rows), shape(rows, rows), shape(rows, width)]
@@ -239,8 +244,8 @@
     rows = count * own
 
     def body(scale_ref, bias_ref, texts, image_all, _, flipped, out, factor_all):
-        factor_rows(scale_ref[0], bias_ref[0], texts, image_all, factor_all, flipped)
-        text_grads(factor_all, image_all, out)
+        factor_rows(scale_ref[0], bias_ref[0], texts, image_all, factor_all, flipped, 256, True)
+        text_grads(factor_all, image_all, out, 256, True)
 
     outs = [shape(rows, rows), shape(count, own, width)]
     scratch = [pltpu.VMEM((rows, rows), BF16)]
@@ -248,21 +253,21 @@
     return pair_call("pairs_odd", body, outs, scale, bias, arrays, 4 * rows * rows * width, 24, scratch)
 
 
-def pairs_image(name, flips, texts, start, stop, outs, after=None):
+def pairs_image(name, flips, texts, start, stop, outs, after, tile, unroll):
     own, width = texts[0].shape[-2:]
 
     def body(flip_even, flip_odd, even, odd, *out_refs):
         def columns_at(here):
             factor = jnp.concatenate([flip_even[start:stop], flip_odd[start:stop]], axis=1)
-            rows = jnp.concatenate([ref[:, :, here].reshape(-1, 256) for ref in (even, odd)], axis=0)
+            rows = jnp.concatenate([ref[:, :, here].reshape(-1, tile) for ref in (even, odd)], axis=0)
             total = product(factor, rows).astype(BF16)
             place = 0
             for ref in out_refs:
                 size = ref.size // width
-                ref[..., here] = total[place : place + size].reshape(*ref.shape[:-1], 256)
+                ref[..., here] = total[place : place + size].reshape(*ref.shape[:-1], tile)
                 place += size
 
-        tiles(width // 256, 256, columns_at)
+        tiles(width // tile, tile, columns_at, unroll)
 
     flops = 2 * (stop - start) * 16 * own * width
     return call(name, body, outs, (*flips, *texts), flops, 24, after)
@@ -291,7 +296,7 @@
                 same[j, :, here] = result[pl.ds(mine, strip)]
                 other[j, :, here] = result[pl.ds(theirs, strip)]
 
-        tiles(features // tile, tile, features_at)
+        tiles(features // tile, tile, features_at, True)
 
     smem, vmem = pl.BlockSpec(memory_space=pltpu.SMEM), pl.BlockSpec(memory_space=pltpu.VMEM)
     specs = [smem, smem] + [vmem] * (len(pieces) + 1)
@@ -356,7 +361,7 @@
     outs = [shape(strip, features, dtype=F32), shape(strip, features)]
     p0, p2 = call("weight_z", along_z, outs, (p02, p46, p1214, p810))
     p2 = swap(p2, "blk", 2)
-    return call("weight_y", along_y, outs[:1], (p0, p2))[0].T, (p46, p1214)
+    return call("weight_y", along_y, outs[:1], (p0, p2))[0].T
 
 
 def local(img_feat, txt_feat, img_weight, txt_weight, natural_exponent_multiplier, bias):
@@ -426,7 +431,7 @@
     flip_odd, odd_sum = pairs_odd(scale, bias, odd, image_all, flip_even)
     odd_got = swap(odd_sum, "blk", 1)
     flips, texts = (flip_even, flip_odd), (even, odd)
-    g4, g5 = pairs_image("pairs_far_images", flips, texts, 6 * own, 8 * own, [shape(*one)] * 2, odd_sum)
+    g4, g5 = pairs_image("pairs_far_images", flips, texts, 6 * own, 8 * own, [shape(*one)] * 2, odd_sum, 256, True)
     g4_got, g5_got = swap(g4, "mp", 6), swap(g5, "mp", 2)
     flops = 128 * own * own * width
     (even_sum,) = call("text_grads_even", text_grads, [shape(8, *one)], (factor_even, image_all), flops, 20, g4)
@@ -436,7 +441,7 @@
         p10[...] = (wide(even, 7) + wide(got, 7)).astype(BF16)
 
     p8, p10 = call("sums_fifth", fifth, [shape(*one)] * 2, (even_sum, odd_got))
-    g01, g23, g67 = pairs_image("pairs_near_images", flips, texts, 0, 6 * own, [shape(*two)] * 3, p8)
+    g01, g23, g67 = pairs_image("pairs_near_images", flips, texts, 0, 6 * own, [shape(*two)] * 3, p8, 512, False)
     p8_got, p10_got = swap(p8, "blk", 12), swap(p10, "blk", 4)
     sent = call("relay_image_grads", relay_split, [shape(*half)] * 4, (g23, g67, g4_got, g5_got))
     got = [(swap(sent[2 * h], "mp", 2), swap(sent[2 * h + 1], "mp", 6)) for h in range(2)]
@@ -479,18 +484,24 @@
     d1 = swap(d0, "mp", 1)
     e2_b, e7_b = call("cut_image_grads_b", cut, outs, (e23_b, e67_b), after=d0)
     e4_b, e5_b = swap(e2_b, "mp", 6), swap(e7_b, "mp", 2)
-    (d01,) = call("stack_text_grads", stack, [shape(*two)], (d0, d1), after=(e4_a, e5_a, e4_b, e5_b))
+    (d01,) = call("stack_text_grads", stack, [shape(*two)], (d0, d1), after=(e4_a, e5_a, e2_b))
     d23, d67 = swap(d01, "mp", 2), swap(d01, "mp", 6)
 
     e_all = (e01_a, e01_b, e23_a, e23_b, e67_a, e67_b, e4_a, e4_b, e5_a, e5_b)
-    same, other = weight_part("weight_image", column, place, e_all, img_feat, d01)
-    d2, d7 = call("cut_text_grads", cut, [shape(*one)] * 2, (d23, d67), ORDER_COST, after=same)
+    d2, d7 = call("cut_text_grads", cut, [shape(*one)] * 2, (d23, d67))
     d4, d5 = swap(d2, "mp", 6), swap(d7, "mp", 2)
+    same, other = weight_part("weight_image", column, place, e_all, img_feat, d7)
     image_chip = chip_weight("weight_image_chip", same, other, None)
-    img_weight_grad, image_got = sum_weight(*image_chip)
+    img_weight_grad = sum_weight(*image_chip)
+
+    def keep(first, second, first_out, second_out):
+        first_out[...] = first[...]
+        second_out[...] = second[...]
+
+    d4, d5 = call("keep_text_far", keep, [shape(*one)] * 2, (d4, d5), ORDER_COST)
     d_all = (d01, d23, d67, d4, d5)
-    same, other = weight_part("weight_text", column, place, d_all, txt_feat, image_got)
-    txt_weight_grad, _ = sum_weight(*chip_weight("weight_text_chip", same, other))
+    same, other = weight_part("weight_text", column, place, d_all, txt_feat, image_chip[0])
+    txt_weight_grad = sum_weight(*chip_weight("weight_text_chip", same, other))
     return (
         feature_grad("feature_image", column, e_all, img_weight),
         feature_grad("feature_text", column, d_all, txt_weight),

time: 199 us -> 199 us (level)
    unnamed x22 -> x16, local copies, waits for them, and re-layouts: 5.39 us -> 3.87 us
    pallas_call x41 -> x42, Pallas kernels: 29.7 us -> 31.2 us  [call(): pl.pallas_call(run, out_shape=outs, in_specs=specs, scratch_shapes=list(s...]
  transfers between devices with their start and end apart: 64 -> 64, of which waited for: 40 -> 35; matrix products, arithmetic and copies ran while one was open for 0% -> 0% of each run, Pallas kernels for 15% -> 15%
where the time goes in v3:
time: 199 us; the launch traced here: 198 us
  waiting for transfers between devices  76.8 us (39%)
  starting transfers between devices  75 us (38%)
  Pallas kernels  40.3 us (20%)
  local copies, waits for them, and re-layouts  3.87 us (2%)
  between operations  2.36 us (1%)
    ppermute x64, waiting for transfers between devices, swap(): return lax.ppermute(value, axis, [(i, i ^ offset) for i in range(count)])  76.8 us
    ppermute x64, starting transfers between devices, swap(): return lax.ppermute(value, axis, [(i, i ^ offset) for i in range(count)])  75 us
    pallas_call x42, Pallas kernels, call(): pl.pallas_call(run, out_shape=outs, in_specs=specs, scratch_shapes=list(s...  31.2 us
    pallas_call x2, Pallas kernels, pair_call(): pl.pallas_call(body, in_specs=[smem, smem] + [vmem] * len(arrays), out_sh...  9.11 us
  transfers between devices with their start and end apart: 64, of which 35 were waited for; matrix products, arithmetic and copies ran while one was open for 0% of the time, Pallas kernels for 15%

profile of v3, /device:TPU:8, one launch (start us, length us, event | category | flops | bytes accessed | tf_op | source)
XLA Modules:
  0.0 198.3 jit_solution(12479870037505024832)
XLA Ops:
  5.2 2.8 %collective-permute-start = (bf16[128,1024]{1,0:T(8,128)(2,1)S(1)}, bf16[128,1024]{1,0:T(8,128)(2,1)S(1)}, u32[]{:S(2)}, u32[]{:S(2)}) collective-permute-start(bf16[128,1024]{1,0:T(8,128)(2,1)S(1)} %get-tuple-element.82), channel_id=1, source_target_pairs={{0,6},{1,7},{2,4},{3,5},{4,2},{5,3},{6,0},{7,1},{8,14},{9,15},{10,... | collective-permute-start | bytes 786440 | tf_op jit(solution)/shard_map/ppermute | solution.py:18
  8.2 6.3 %collective-permute-done.r4 = bf16[128,1024]{1,0:T(8,128)(2,1)S(1)} collective-permute-done((bf16[128,1024]{1,0:T(8,128)(2,1)S(1)}, bf16[128,1024]{1,0:T(8,128)(2,1)S(1)}, u32[]{:S(2)}, u32[]{:S(2)}) %collective-permute-start) | collective-permute-done | bytes 262176 | tf_op jit(solution)/shard_map/ppermute | solution.py:18
  17.6 2.6 %embed_image.1 = (bf16[2,128,1024]{2,1,0:T(8,128)(2,1)S(1)}, bf16[2,128,1024]{2,1,0:T(8,128)(2,1)S(1)}, bf16[2,128,1024]{2,1,0:T(8,128)(2,1)S(1)}, bf16[128,1024]{1,0:T(8,128)(2,1)S(1)}, bf16[128,1024]{1,0:T(8,128)(2,1)S(1)}) custom-call(s32[1]{0:T(128)} %bitcast.column_ref.refs_1_, bf16[1024,768]{1,0:T(8,128)(2,1)S(1)} %copy-done.2, ...), custom_call_target="tpu_custom_call" | custom-call | flops 1610612736 | bytes 5242884 | tf_op jit(solution)/shard_map/embed_image/pallas_call | solution.py:36
  22.8 8.1 %collective-permute-done.2.t23 = bf16[2,128,1024]{2,1,0:T(8,128)(2,1)S(1)} collective-permute-done((bf16[2,128,1024]{2,1,0:T(8,128)(2,1)S(1)}, bf16[2,128,1024]{2,1,0:T(8,128)(2,1)S(1)}, u32[]{:S(2)}, u32[]{:S(2)}) %collective-permute-start.2) | collective-permute-done | bytes 524320 | tf_op jit(solution)/shard_map/ppermute | solution.py:18
  32.5 2.4 %collective-permute-start.6 = (bf16[128,1024]{1,0:T(8,128)(2,1)S(1)}, bf16[128,1024]{1,0:T(8,128)(2,1)S(1)}, u32[]{:S(2)}, u32[]{:S(2)}) collective-permute-start(bf16[128,1024]{1,0:T(8,128)(2,1)S(1)} %get-tuple-element.86.refs_0_), channel_id=1, source_target_pairs={{0,1},{1,0},{2,3},{3,2},{4,5},{5,4},{6,7},{7,6},{8,9},{9,8},{10,11... | collective-permute-start | bytes 786440 | tf_op jit(solution)/shard_map/ppermute | solution.py:18
  37.4 4.5 %collective-permute-done.6.refs_2_ = bf16[128,1024]{1,0:T(8,128)(2,1)S(1)} collective-permute-done((bf16[128,1024]{1,0:T(8,128)(2,1)S(1)}, bf16[128,1024]{1,0:T(8,128)(2,1)S(1)}, u32[]{:S(2)}, u32[]{:S(2)}) %collective-permute-start.6) | collective-permute-done | bytes 262176 | tf_op jit(solution)/shard_map/ppermute | solution.py:18
  46.3 2.4 %collective-permute-start.12 = (bf16[2,64,1024]{2,1,0:T(8,128)(2,1)S(1)}, bf16[2,64,1024]{2,1,0:T(8,128)(2,1)S(1)}, u32[]{:S(2)}, u32[]{:S(2)}) collective-permute-start(bf16[2,64,1024]{2,1,0:T(8,128)(2,1)S(1)} %image_x_a.1.refs_0_.refs_1_), channel_id=1, source_target_pairs={{0,1},{1,0},{2,3},{3,2},{4,5},{5,4},{6,7},{7,6},{8,9},{9,8},{10,11... | collective-permute-start | bytes 786440 | tf_op jit(solution)/shard_map/ppermute | solution.py:18
  50.8 4.5 %collective-permute-start.19 = (bf16[2,128,1024]{2,1,0:T(8,128)(2,1)S(1)}, bf16[2,128,1024]{2,1,0:T(8,128)(2,1)S(1)}, u32[]{:S(2)}, u32[]{:S(2)}) collective-permute-start(bf16[2,128,1024]{2,1,0:T(8,128)(2,1)S(1)} %stack_text.1.refs_0_.refs_4_), channel_id=1, source_target_pairs={{0,96},{8,104},{16,112},{24,120},{32,64},{40,72},{48,80},{56,88},{... | collective-permute-start | bytes 1572872 | tf_op jit(solution)/shard_map/ppermute | solution.py:18
  55.4 3.0 %collective-permute-start.13 = (bf16[2,64,1024]{2,1,0:T(8,128)(2,1)S(1)}, bf16[2,64,1024]{2,1,0:T(8,128)(2,1)S(1)}, u32[]{:S(2)}, u32[]{:S(2)}) collective-permute-start(bf16[2,64,1024]{2,1,0:T(8,128)(2,1)S(1)} %image_x_b.1.refs_0_.refs_1_), channel_id=1, source_target_pairs={{0,1},{1,0},{2,3},{3,2},{4,5},{5,4},{6,7},{7,6},{8,9},{9,8},{10,11... | collective-permute-start | bytes 786440 | tf_op jit(solution)/shard_map/ppermute | solution.py:18
  59.9 3.5 %collective-permute-done.13.refs_2_ = bf16[2,64,1024]{2,1,0:T(8,128)(2,1)S(1)} collective-permute-done((bf16[2,64,1024]{2,1,0:T(8,128)(2,1)S(1)}, bf16[2,64,1024]{2,1,0:T(8,128)(2,1)S(1)}, u32[]{:S(2)}, u32[]{:S(2)}) %collective-permute-start.13) | collective-permute-done | bytes 262176 | tf_op jit(solution)/shard_map/ppermute | solution.py:18
  64.5 2.3 %collective-permute-done.15.refs_2_.refs_4_ = bf16[2,64,1024]{2,1,0:T(8,128)(2,1)S(1)} collective-permute-done((bf16[2,64,1024]{2,1,0:T(8,128)(2,1)S(1)}, bf16[2,64,1024]{2,1,0:T(8,128)(2,1)S(1)}, u32[]{:S(2)}, u32[]{:S(2)}) %collective-permute-start.15) | collective-permute-done | bytes 262176 | tf_op jit(solution)/shard_map/ppermute | solution.py:18
  74.7 2.5 %collective-permute-start.22 = (bf16[64,1024]{1,0:T(8,128)(2,1)S(1)}, bf16[64,1024]{1,0:T(8,128)(2,1)S(1)}, u32[]{:S(2)}, u32[]{:S(2)}) collective-permute-start(bf16[64,1024]{1,0:T(8,128)(2,1)S(1)} %get-tuple-element.103), channel_id=1, source_target_pairs={{0,6},{1,7},{2,4},{3,5},{4,2},{5,3},{6,0},{7,1},{8,14},{9,15},{10,... | collective-permute-start | bytes 393224 | tf_op jit(solution)/shard_map/ppermute | solution.py:18
  77.1 2.8 %collective-permute-done.16.refs_0_.refs_6_ = bf16[64,1024]{1,0:T(8,128)(2,1)S(1)} collective-permute-done((bf16[64,1024]{1,0:T(8,128)(2,1)S(1)}, bf16[64,1024]{1,0:T(8,128)(2,1)S(1)}, u32[]{:S(2)}, u32[]{:S(2)}) %collective-permute-start.16) | collective-permute-done | bytes 131104 | tf_op jit(solution)/shard_map/ppermute | solution.py:18
  83.9 4.0 %pairs_even.1 = (bf16[1024,1024]{1,0:T(8,128)(2,1)S(1)}, bf16[1024,1024]{1,0:T(8,128)(2,1)S(1)}, bf16[1024,1024]{1,0:T(8,128)(2,1)S(1)}) custom-call(f32[1]{0:T(128)S(6)} %exp.3.scale_ref, f32[1]{0:T(128)S(6)} %copy.11.bias_ref, bf16[8,128,1024]{2,1,0:T(8,128)(2,1)S(1)} %collect.1.texts.refs_3_, bf16[2,64,1024]{2,1,0:T(8,128)(2,1)S(1)} %get-tuple-element.98.refs_0_, ...), custom_call_target="tpu_custom_call" | custom-call | flops 2147483648 | bytes 10485760 | tf_op jit(solution)/shard_map/pairs_even/pallas_call | solution.py:182
  87.8 5.2 %pairs_odd.1 = (bf16[1024,1024]{1,0:T(8,128)(2,1)S(1)}, bf16[8,128,1024]{2,1,0:T(8,128)(2,1)S(1)}) custom-call(f32[1]{0:T(128)S(6)} %exp.3.scale_ref, f32[1]{0:T(128)S(6)} %copy.11.bias_ref, bf16[8,128,1024]{2,1,0:T(8,128)(2,1)S(1)} %collective-permute-done.26.texts.refs_4_, bf16[1024,1024]{1,0:T(8,128)(2,1)S(1)} %get-tuple-element.106.image_all.refs_2_, ...), custom_call_target="tpu_custom_call" | custom-call | flops 4294967296 | bytes 10485760 | tf_op jit(solution)/shard_map/pairs_odd/pallas_call | solution.py:182
  96.2 2.5 %text_grads_even.1.even.refs_1_ = bf16[8,128,1024]{2,1,0:T(8,128)(2,1)S(1)} custom-call(bf16[128,1024]{1,0:T(8,128)(2,1)S(1)} %get-tuple-element.110.refs_0_, bf16[1024,1024]{1,0:T(8,128)(2,1)S(1)} %get-tuple-element.111.refs_1_, bf16[1024,1024]{1,0:T(8,128)(2,1)S(1)} %get-tuple-element.106.image_all.refs_2_), custom_call_target="tpu_custom_call" | custom-call | flops 2147483648 | bytes 6553600 | tf_op jit(solution)/shard_map/text_grads_even/pallas_call | solution.py:36
  101.4 3.6 %pairs_near_images.1 = (bf16[2,128,1024]{2,1,0:T(8,128)(2,1)S(1)}, bf16[2,128,1024]{2,1,0:T(8,128)(2,1)S(1)}, bf16[2,128,1024]{2,1,0:T(8,128)(2,1)S(1)}) custom-call(bf16[128,1024]{1,0:T(8,128)(2,1)S(1)} %get-tuple-element.112.refs_0_, bf16[1024,1024]{1,0:T(8,128)(2,1)S(1)} %get-tuple-element.107._.refs_1_, ...), custom_call_target="tpu_custom_call" | custom-call | flops 3221225472 | bytes 10223616 | tf_op jit(solution)/shard_map/pairs_near_images/pallas_call | solution.py:36
  107.6 2.3 %collective-permute-done.30.refs_3_ = bf16[128,1024]{1,0:T(8,128)(2,1)S(1)} collective-permute-done((bf16[128,1024]{1,0:T(8,128)(2,1)S(1)}, bf16[128,1024]{1,0:T(8,128)(2,1)S(1)}, u32[]{:S(2)}, u32[]{:S(2)}) %collective-permute-start.30) | collective-permute-done | bytes 262176 | tf_op jit(solution)/shard_map/ppermute | solution.py:18
  116.2 3.0 %collective-permute-start.36 = (bf16[2,64,1024]{2,1,0:T(8,128)(2,1)S(1)}, bf16[2,64,1024]{2,1,0:T(8,128)(2,1)S(1)}, u32[]{:S(2)}, u32[]{:S(2)}) collective-permute-start(bf16[2,64,1024]{2,1,0:T(8,128)(2,1)S(1)} %image_grads_x_a.1.refs_0_.refs_1_), channel_id=1, source_target_pairs={{0,1},{1,0},{2,3},{3,2},{4,5},{5,4},{6,7},{7,6},{8,9},{9,8},{10,11... | collective-permute-start | bytes 786440 | tf_op jit(solution)/shard_map/ppermute | solution.py:18
  121.7 2.3 %collective-permute-start.39 = (bf16[2,64,1024]{2,1,0:T(8,128)(2,1)S(1)}, bf16[2,64,1024]{2,1,0:T(8,128)(2,1)S(1)}, u32[]{:S(2)}, u32[]{:S(2)}) collective-permute-start(bf16[2,64,1024]{2,1,0:T(8,128)(2,1)S(1)} %image_grads_x_b.1.refs_0_.refs_1_), channel_id=1, source_target_pairs={{0,1},{1,0},{2,3},{3,2},{4,5},{5,4},{6,7},{7,6},{8,9},{9,8},{10,11... | collective-permute-start | bytes 786440 | tf_op jit(solution)/shard_map/ppermute | solution.py:18
  128.5 4.0 %collective-permute-done.39.refs_2_ = bf16[2,64,1024]{2,1,0:T(8,128)(2,1)S(1)} collective-permute-done((bf16[2,64,1024]{2,1,0:T(8,128)(2,1)S(1)}, bf16[2,64,1024]{2,1,0:T(8,128)(2,1)S(1)}, u32[]{:S(2)}, u32[]{:S(2)}) %collective-permute-start.39) | collective-permute-done | bytes 262176 | tf_op jit(solution)/shard_map/ppermute | solution.py:18
  135.6 3.2 %collective-permute-start.49 = (bf16[128,1024]{1,0:T(8,128)(2,1)S(1)}, bf16[128,1024]{1,0:T(8,128)(2,1)S(1)}, u32[]{:S(2)}, u32[]{:S(2)}) collective-permute-start(bf16[128,1024]{1,0:T(8,128)(2,1)S(1)} %text_back.1.refs_0_.refs_3_), channel_id=1, source_target_pairs={{0,1},{1,0},{2,3},{3,2},{4,5},{5,4},{6,7},{7,6},{8,9},{9,8},{10,11... | collective-permute-start | bytes 786440 | tf_op jit(solution)/shard_map/ppermute | solution.py:18
  140.5 3.1 %collective-permute-start.44 = (bf16[64,1024]{1,0:T(8,128)(2,1)S(1)}, bf16[64,1024]{1,0:T(8,128)(2,1)S(1)}, u32[]{:S(2)}, u32[]{:S(2)}) collective-permute-start(bf16[64,1024]{1,0:T(8,128)(2,1)S(1)} %get-tuple-element.128.refs_0_), channel_id=1, source_target_pairs={{0,6},{1,7},{2,4},{3,5},{4,2},{5,3},{6,0},{7,1},{8,14},{9,15},{10,... | collective-permute-start | bytes 393224 | tf_op jit(solution)/shard_map/ppermute | solution.py:18
  144.3 3.9 %collective-permute-done.44.refs_6_.refs_0_.refs_9_ = bf16[64,1024]{1,0:T(8,128)(2,1)S(1)} collective-permute-done((bf16[64,1024]{1,0:T(8,128)(2,1)S(1)}, bf16[64,1024]{1,0:T(8,128)(2,1)S(1)}, u32[]{:S(2)}, u32[]{:S(2)}) %collective-permute-start.44) | collective-permute-done | bytes 131104 | tf_op jit(solution)/shard_map/ppermute | solution.py:18
  148.2 3.2 %collective-permute-start.51 = (bf16[2,128,1024]{2,1,0:T(8,128)(2,1)S(1)}, bf16[2,128,1024]{2,1,0:T(8,128)(2,1)S(1)}, u32[]{:S(2)}, u32[]{:S(2)}) collective-permute-start(bf16[2,128,1024]{2,1,0:T(8,128)(2,1)S(1)} %stack_text_grads.1.refs_0_.refs_3_), channel_id=1, source_target_pairs={{0,6},{1,7},{2,4},{3,5},{4,2},{5,3},{6,0},{7,1},{8,14},{9,15},{10,... | collective-permute-start | bytes 1572872 | tf_op jit(solution)/shard_map/ppermute | solution.py:18
  153.5 7.9 %collective-permute-done.51.other.refs_2_.refs_5_ = bf16[2,128,1024]{2,1,0:T(8,128)(2,1)S(1)} collective-permute-done((bf16[2,128,1024]{2,1,0:T(8,128)(2,1)S(1)}, bf16[2,128,1024]{2,1,0:T(8,128)(2,1)S(1)}, u32[]{:S(2)}, u32[]{:S(2)}) %collective-permute-start.51) | collective-permute-done | bytes 524320 | tf_op jit(solution)/shard_map/ppermute | solution.py:18
  166.8 3.2 %weight_image.1 = (bf16[8,64,768]{2,1,0:T(8,128)(2,1)S(1)}, bf16[8,64,768]{2,1,0:T(8,128)(2,1)S(1)}) custom-call(bf16[128,1024]{1,0:T(8,128)(2,1)} %get-tuple-element.135.refs_0_, s32[1]{0:T(128)} %bitcast.column_ref.refs_1_, s32[1]{0:T(128)} %bitcast.1.refs_2_, bf16[2,64,1024]{2,1,0:T(8,128)(2,1)S(1)} %image_back_a.1.refs_0_.refs_3_, ...), custom_call_target="tpu_custom_call" | custom-call | flops 1610612736 | bytes 5505032 | tf_op jit(solution)/shard_map/weight_image/pallas_call | solution.py:36
  175.3 3.8 %collective-permute-start.57 = (bf16[2,64,768]{2,1,0:T(8,128)(2,1)S(1)}, bf16[2,64,768]{2,1,0:T(8,128)(2,1)S(1)}, u32[]{:S(2)}, u32[]{:S(2)}) collective-permute-start(bf16[2,64,768]{2,1,0:T(8,128)(2,1)S(1)} %get-tuple-element.143), channel_id=1, source_target_pairs={{0,64},{8,72},{16,80},{24,88},{32,96},{40,104},{48,112},{56,120},{... | collective-permute-start | bytes 589832 | tf_op jit(solution)/shard_map/ppermute | solution.py:18
  180.0 2.7 %collective-permute-done.55.p46 = bf16[2,64,768]{2,1,0:T(8,128)(2,1)S(1)} collective-permute-done((bf16[2,64,768]{2,1,0:T(8,128)(2,1)S(1)}, bf16[2,64,768]{2,1,0:T(8,128)(2,1)S(1)}, u32[]{:S(2)}, u32[]{:S(2)}) %collective-permute-start.55) | collective-permute-done | bytes 196640 | tf_op jit(solution)/shard_map/ppermute | solution.py:18
  183.4 4.4 %feature_image.1 = bf16[1024,768]{1,0:T(8,128)(2,1)} custom-call(s32[1]{0:T(128)} %bitcast.column_ref.refs_1_, bf16[2,64,1024]{2,1,0:T(8,128)(2,1)S(1)} %image_back_a.1.refs_0_.refs_3_, bf16[2,64,1024]{2,1,0:T(8,128)(2,1)S(1)} %image_back_b.1.refs_0_.refs_1_.refs_4_, bf16[2,64,1024]{2,1,0:T(8,128)(2,1)S(1)} %collective-permute-done.40.refs_1_.refs_2_.refs_5_, ...), custom_call_target="tpu_custom_call" | custom-call | flops 1610612736 | bytes 5242884 | tf_op jit(solution)/shard_map/feature_image/pallas_call | solution.py:36
  189.8 3.5 %collective-permute-done.61.p1214 = bf16[2,64,512]{2,1,0:T(8,128)(2,1)S(1)} collective-permute-done((bf16[2,64,512]{2,1,0:T(8,128)(2,1)S(1)}, bf16[2,64,512]{2,1,0:T(8,128)(2,1)S(1)}, u32[]{:S(2)}, u32[]{:S(2)}) %collective-permute-start.61) | collective-permute-done | bytes 131104 | tf_op jit(solution)/shard_map/ppermute | solution.py:18
  194.1 2.5 %feature_text.1 = bf16[1024,512]{1,0:T(8,128)(2,1)} custom-call(s32[1]{0:T(128)} %bitcast.column_ref.refs_1_, bf16[2,128,1024]{2,1,0:T(8,128)(2,1)S(1)} %stack_text_grads.1.refs_0_.refs_3_, bf16[2,128,1024]{2,1,0:T(8,128)(2,1)S(1)} %collective-permute-done.50.near.refs_1_.refs_4_, bf16[2,128,1024]{2,1,0:T(8,128)(2,1)S(1)} %collective-permute-done.51.other.refs_2_.refs_5_, ...), custom_call_target="tpu_custom_call" | custom-call | flops 1073741824 | bytes 4194308 | tf_op jit(solution)/shard_map/feature_text/pallas_call | solution.py:36
  (156 shorter events, 80.2 us)
Async XLA Ops:
  5.2 9.3 %collective-permute-start = (bf16[128,1024]{1,0:T(8,128)(2,1)S(1)}, bf16[128,1024]{1,0:T(8,128)(2,1)S(1)}, u32[]{:S(2)}, u32[]{:S(2)}) collective-permute-start(bf16[128,1024]{1,0:T(8,128)(2,1)S(1)} %get-tuple-element.82), channel_id=1, source_target_pairs={{0,6},{1,7},{2,4},{3,5},{4,2},{5,3},{6,0},{7,1},{8,14},{9,15},{10,... | collective-permute-start | bytes 786440 | tf_op jit(solution)/shard_map/ppermute | solution.py:18
  15.9 14.9 %collective-permute-start.2 = (bf16[2,128,1024]{2,1,0:T(8,128)(2,1)S(1)}, bf16[2,128,1024]{2,1,0:T(8,128)(2,1)S(1)}, u32[]{:S(2)}, u32[]{:S(2)}) collective-permute-start(bf16[2,128,1024]{2,1,0:T(8,128)(2,1)S(1)} %get-tuple-element.84), channel_id=1, source_target_pairs={{0,2},{1,3},{2,0},{3,1},{4,6},{5,7},{6,4},{7,5},{8,10},{9,11},{10,... | collective-permute-start | bytes 1572872 | tf_op jit(solution)/shard_map/ppermute | solution.py:18
  16.3 16.1 %collective-permute-start.3 = (bf16[2,128,1024]{2,1,0:T(8,128)(2,1)S(1)}, bf16[2,128,1024]{2,1,0:T(8,128)(2,1)S(1)}, u32[]{:S(2)}, u32[]{:S(2)}) collective-permute-start(bf16[2,128,1024]{2,1,0:T(8,128)(2,1)S(1)} %get-tuple-element.85), channel_id=1, source_target_pairs={{0,6},{1,7},{2,4},{3,5},{4,2},{5,3},{6,0},{7,1},{8,14},{9,15},{10,... | collective-permute-start | bytes 1572872 | tf_op jit(solution)/shard_map/ppermute | solution.py:18
  20.2 15.1 %collective-permute-start.4 = (bf16[128,1024]{1,0:T(8,128)(2,1)S(1)}, bf16[128,1024]{1,0:T(8,128)(2,1)S(1)}, u32[]{:S(2)}, u32[]{:S(2)}) collective-permute-start(bf16[128,1024]{1,0:T(8,128)(2,1)S(1)} %get-tuple-element.89), channel_id=1, source_target_pairs={{0,6},{1,7},{2,4},{3,5},{4,2},{5,3},{6,0},{7,1},{8,14},{9,15},{10,... | collective-permute-start | bytes 786440 | tf_op jit(solution)/shard_map/ppermute | solution.py:18
  22.2 13.2 %collective-permute-start.5 = (bf16[128,1024]{1,0:T(8,128)(2,1)S(1)}, bf16[128,1024]{1,0:T(8,128)(2,1)S(1)}, u32[]{:S(2)}, u32[]{:S(2)}) collective-permute-start(bf16[128,1024]{1,0:T(8,128)(2,1)S(1)} %get-tuple-element.90), channel_id=1, source_target_pairs={{0,2},{1,3},{2,0},{3,1},{4,6},{5,7},{6,4},{7,5},{8,10},{9,11},{10,... | collective-permute-start | bytes 786440 | tf_op jit(solution)/shard_map/ppermute | solution.py:18
  32.5 9.3 %collective-permute-start.6 = (bf16[128,1024]{1,0:T(8,128)(2,1)S(1)}, bf16[128,1024]{1,0:T(8,128)(2,1)S(1)}, u32[]{:S(2)}, u32[]{:S(2)}) collective-permute-start(bf16[128,1024]{1,0:T(8,128)(2,1)S(1)} %get-tuple-element.86.refs_0_), channel_id=1, source_target_pairs={{0,1},{1,0},{2,3},{3,2},{4,5},{5,4},{6,7},{7,6},{8,9},{9,8},{10,11... | collective-permute-start | bytes 786440 | tf_op jit(solution)/shard_map/ppermute | solution.py:18
  35.5 10.1 %collective-permute-start.8 = (bf16[2,64,1024]{2,1,0:T(8,128)(2,1)S(1)}, bf16[2,64,1024]{2,1,0:T(8,128)(2,1)S(1)}, u32[]{:S(2)}, u32[]{:S(2)}) collective-permute-start(bf16[2,64,1024]{2,1,0:T(8,128)(2,1)S(1)} %get-tuple-element.95), channel_id=1, source_target_pairs={{0,6},{1,7},{2,4},{3,5},{4,2},{5,3},{6,0},{7,1},{8,14},{9,15},{10,... | collective-permute-start | bytes 786440 | tf_op jit(solution)/shard_map/ppermute | solution.py:18
  43.0 12.3 %collective-permute-start.10 = (bf16[2,64,1024]{2,1,0:T(8,128)(2,1)S(1)}, bf16[2,64,1024]{2,1,0:T(8,128)(2,1)S(1)}, u32[]{:S(2)}, u32[]{:S(2)}) collective-permute-start(bf16[2,64,1024]{2,1,0:T(8,128)(2,1)S(1)} %get-tuple-element.96), channel_id=1, source_target_pairs={{0,2},{1,3},{2,0},{3,1},{4,6},{5,7},{6,4},{7,5},{8,10},{9,11},{10,... | collective-permute-start | bytes 786440 | tf_op jit(solution)/shard_map/ppermute | solution.py:18
  43.0 12.3 %collective-permute-start.11 = (bf16[2,64,1024]{2,1,0:T(8,128)(2,1)S(1)}, bf16[2,64,1024]{2,1,0:T(8,128)(2,1)S(1)}, u32[]{:S(2)}, u32[]{:S(2)}) collective-permute-start(bf16[2,64,1024]{2,1,0:T(8,128)(2,1)S(1)} %get-tuple-element.97), channel_id=1, source_target_pairs={{0,6},{1,7},{2,4},{3,5},{4,2},{5,3},{6,0},{7,1},{8,14},{9,15},{10,... | collective-permute-start | bytes 786440 | tf_op jit(solution)/shard_map/ppermute | solution.py:18
  46.3 12.1 %collective-permute-start.12 = (bf16[2,64,1024]{2,1,0:T(8,128)(2,1)S(1)}, bf16[2,64,1024]{2,1,0:T(8,128)(2,1)S(1)}, u32[]{:S(2)}, u32[]{:S(2)}) collective-permute-start(bf16[2,64,1024]{2,1,0:T(8,128)(2,1)S(1)} %image_x_a.1.refs_0_.refs_1_), channel_id=1, source_target_pairs={{0,1},{1,0},{2,3},{3,2},{4,5},{5,4},{6,7},{7,6},{8,9},{9,8},{10,11... | collective-permute-start | bytes 786440 | tf_op jit(solution)/shard_map/ppermute | solution.py:18
  50.8 18.2 %collective-permute-start.19 = (bf16[2,128,1024]{2,1,0:T(8,128)(2,1)S(1)}, bf16[2,128,1024]{2,1,0:T(8,128)(2,1)S(1)}, u32[]{:S(2)}, u32[]{:S(2)}) collective-permute-start(bf16[2,128,1024]{2,1,0:T(8,128)(2,1)S(1)} %stack_text.1.refs_0_.refs_4_), channel_id=1, source_target_pairs={{0,96},{8,104},{16,112},{24,120},{32,64},{40,72},{48,80},{56,88},{... | collective-permute-start | bytes 1572872 | tf_op jit(solution)/shard_map/ppermute | solution.py:18
  55.3 13.7 %collective-permute-start.18 = (bf16[2,128,1024]{2,1,0:T(8,128)(2,1)S(1)}, bf16[2,128,1024]{2,1,0:T(8,128)(2,1)S(1)}, u32[]{:S(2)}, u32[]{:S(2)}) collective-permute-start(bf16[2,128,1024]{2,1,0:T(8,128)(2,1)S(1)} %stack_text.1.refs_0_.refs_4_), channel_id=1, source_target_pairs={{0,32},{8,40},{16,48},{24,56},{32,0},{40,8},{48,16},{56,24},{64,96... | collective-permute-start | bytes 1572872 | tf_op jit(solution)/shard_map/ppermute | solution.py:18
  63.5 10.3 %collective-permute-start.21 = (bf16[2,64,1024]{2,1,0:T(8,128)(2,1)S(1)}, bf16[2,64,1024]{2,1,0:T(8,128)(2,1)S(1)}, u32[]{:S(2)}, u32[]{:S(2)}) collective-permute-start(bf16[2,64,1024]{2,1,0:T(8,128)(2,1)S(1)} %get-tuple-element.99.refs_0_.refs_1_), channel_id=1, source_target_pairs={{0,6},{1,7},{2,4},{3,5},{4,2},{5,3},{6,0},{7,1},{8,14},{9,15},{10,... | collective-permute-start | bytes 786440 | tf_op jit(solution)/shard_map/ppermute | solution.py:18
  69.0 13.1 %collective-permute-start.25 = (bf16[128,1024]{1,0:T(8,128)(2,1)S(1)}, bf16[128,1024]{1,0:T(8,128)(2,1)S(1)}, u32[]{:S(2)}, u32[]{:S(2)}) collective-permute-start(bf16[128,1024]{1,0:T(8,128)(2,1)S(1)} %get-tuple-element.105), channel_id=1, source_target_pairs={{0,32},{8,40},{16,48},{24,56},{32,0},{40,8},{48,16},{56,24},{64,96... | collective-permute-start | bytes 786440 | tf_op jit(solution)/shard_map/ppermute | solution.py:18
  71.0 11.1 %collective-permute-start.24 = (bf16[128,1024]{1,0:T(8,128)(2,1)S(1)}, bf16[128,1024]{1,0:T(8,128)(2,1)S(1)}, u32[]{:S(2)}, u32[]{:S(2)}) collective-permute-start(bf16[128,1024]{1,0:T(8,128)(2,1)S(1)} %get-tuple-element.102.refs_0_), channel_id=1, source_target_pairs={{0,96},{8,104},{16,112},{24,120},{32,64},{40,72},{48,80},{56,88},{... | collective-permute-start | bytes 786440 | tf_op jit(solution)/shard_map/ppermute | solution.py:18
  94.8 10.2 %collective-permute-start.29 = (bf16[128,1024]{1,0:T(8,128)(2,1)S(1)}, bf16[128,1024]{1,0:T(8,128)(2,1)S(1)}, u32[]{:S(2)}, u32[]{:S(2)}) collective-permute-start(bf16[128,1024]{1,0:T(8,128)(2,1)S(1)} %get-tuple-element.115), channel_id=1, source_target_pairs={{0,2},{1,3},{2,0},{3,1},{4,6},{5,7},{6,4},{7,5},{8,10},{9,11},{10,... | collective-permute-start | bytes 786440 | tf_op jit(solution)/shard_map/ppermute | solution.py:18
  94.9 10.1 %collective-permute-start.28 = (bf16[128,1024]{1,0:T(8,128)(2,1)S(1)}, bf16[128,1024]{1,0:T(8,128)(2,1)S(1)}, u32[]{:S(2)}, u32[]{:S(2)}) collective-permute-start(bf16[128,1024]{1,0:T(8,128)(2,1)S(1)} %get-tuple-element.110.refs_0_), channel_id=1, source_target_pairs={{0,6},{1,7},{2,4},{3,5},{4,2},{5,3},{6,0},{7,1},{8,14},{9,15},{10,... | collective-permute-start | bytes 786440 | tf_op jit(solution)/shard_map/ppermute | solution.py:18
  110.3 16.6 %collective-permute-start.37 = (bf16[2,128,1024]{2,1,0:T(8,128)(2,1)S(1)}, bf16[2,128,1024]{2,1,0:T(8,128)(2,1)S(1)}, u32[]{:S(2)}, u32[]{:S(2)}) collective-permute-start(bf16[2,128,1024]{2,1,0:T(8,128)(2,1)S(1)} %get-tuple-element.124), channel_id=1, source_target_pairs={{0,32},{8,40},{16,48},{24,56},{32,0},{40,8},{48,16},{56,24},{64,96... | collective-permute-start | bytes 1572872 | tf_op jit(solution)/shard_map/ppermute | solution.py:18
  110.4 16.5 %collective-permute-start.38 = (bf16[2,128,1024]{2,1,0:T(8,128)(2,1)S(1)}, bf16[2,128,1024]{2,1,0:T(8,128)(2,1)S(1)}, u32[]{:S(2)}, u32[]{:S(2)}) collective-permute-start(bf16[2,128,1024]{2,1,0:T(8,128)(2,1)S(1)} %get-tuple-element.125), channel_id=1, source_target_pairs={{0,96},{8,104},{16,112},{24,120},{32,64},{40,72},{48,80},{56,88},{... | collective-permute-start | bytes 1572872 | tf_op jit(solution)/shard_map/ppermute | solution.py:18
  116.2 9.3 %collective-permute-start.36 = (bf16[2,64,1024]{2,1,0:T(8,128)(2,1)S(1)}, bf16[2,64,1024]{2,1,0:T(8,128)(2,1)S(1)}, u32[]{:S(2)}, u32[]{:S(2)}) collective-permute-start(bf16[2,64,1024]{2,1,0:T(8,128)(2,1)S(1)} %image_grads_x_a.1.refs_0_.refs_1_), channel_id=1, source_target_pairs={{0,1},{1,0},{2,3},{3,2},{4,5},{5,4},{6,7},{7,6},{8,9},{9,8},{10,11... | collective-permute-start | bytes 786440 | tf_op jit(solution)/shard_map/ppermute | solution.py:18
  121.7 10.8 %collective-permute-start.39 = (bf16[2,64,1024]{2,1,0:T(8,128)(2,1)S(1)}, bf16[2,64,1024]{2,1,0:T(8,128)(2,1)S(1)}, u32[]{:S(2)}, u32[]{:S(2)}) collective-permute-start(bf16[2,64,1024]{2,1,0:T(8,128)(2,1)S(1)} %image_grads_x_b.1.refs_0_.refs_1_), channel_id=1, source_target_pairs={{0,1},{1,0},{2,3},{3,2},{4,5},{5,4},{6,7},{7,6},{8,9},{9,8},{10,11... | collective-permute-start | bytes 786440 | tf_op jit(solution)/shard_map/ppermute | solution.py:18
  132.7 10.8 %collective-permute-start.43 = (bf16[2,64,1024]{2,1,0:T(8,128)(2,1)S(1)}, bf16[2,64,1024]{2,1,0:T(8,128)(2,1)S(1)}, u32[]{:S(2)}, u32[]{:S(2)}) collective-permute-start(bf16[2,64,1024]{2,1,0:T(8,128)(2,1)S(1)} %image_back_b.1.refs_0_.refs_1_.refs_4_), channel_id=1, source_target_pairs={{0,6},{1,7},{2,4},{3,5},{4,2},{5,3},{6,0},{7,1},{8,14},{9,15},{10,... | collective-permute-start | bytes 786440 | tf_op jit(solution)/shard_map/ppermute | solution.py:18
  135.6 12.5 %collective-permute-start.49 = (bf16[128,1024]{1,0:T(8,128)(2,1)S(1)}, bf16[128,1024]{1,0:T(8,128)(2,1)S(1)}, u32[]{:S(2)}, u32[]{:S(2)}) collective-permute-start(bf16[128,1024]{1,0:T(8,128)(2,1)S(1)} %text_back.1.refs_0_.refs_3_), channel_id=1, source_target_pairs={{0,1},{1,0},{2,3},{3,2},{4,5},{5,4},{6,7},{7,6},{8,9},{9,8},{10,11... | collective-permute-start | bytes 786440 | tf_op jit(solution)/shard_map/ppermute | solution.py:18
  148.2 13.3 %collective-permute-start.51 = (bf16[2,128,1024]{2,1,0:T(8,128)(2,1)S(1)}, bf16[2,128,1024]{2,1,0:T(8,128)(2,1)S(1)}, u32[]{:S(2)}, u32[]{:S(2)}) collective-permute-start(bf16[2,128,1024]{2,1,0:T(8,128)(2,1)S(1)} %stack_text_grads.1.refs_0_.refs_3_), channel_id=1, source_target_pairs={{0,6},{1,7},{2,4},{3,5},{4,2},{5,3},{6,0},{7,1},{8,14},{9,15},{10,... | collective-permute-start | bytes 1572872 | tf_op jit(solution)/shard_map/ppermute | solution.py:18
  151.4 12.0 %collective-permute-start.50 = (bf16[2,128,1024]{2,1,0:T(8,128)(2,1)S(1)}, bf16[2,128,1024]{2,1,0:T(8,128)(2,1)S(1)}, u32[]{:S(2)}, u32[]{:S(2)}) collective-permute-start(bf16[2,128,1024]{2,1,0:T(8,128)(2,1)S(1)} %stack_text_grads.1.refs_0_.refs_3_), channel_id=1, source_target_pairs={{0,2},{1,3},{2,0},{3,1},{4,6},{5,7},{6,4},{7,5},{8,10},{9,11},{10,... | collective-permute-start | bytes 1572872 | tf_op jit(solution)/shard_map/ppermute | solution.py:18
  151.4 14.0 %collective-permute-start.48 = (bf16[64,1024]{1,0:T(8,128)(2,1)}, bf16[64,1024]{1,0:T(8,128)(2,1)}, u32[]{:S(2)}, u32[]{:S(2)}) collective-permute-start(bf16[64,1024]{1,0:T(8,128)(2,1)} %get-tuple-element.133), channel_id=1, source_target_pairs={{0,2},{1,3},{2,0},{3,1},{4,6},{5,7},{6,4},{7,5},{8,10},{9,11},{10,... | collective-permute-start | bytes 393224 | tf_op jit(solution)/shard_map/ppermute | solution.py:18
  153.4 12.0 %collective-permute-start.46 = (bf16[64,1024]{1,0:T(8,128)(2,1)S(1)}, bf16[64,1024]{1,0:T(8,128)(2,1)}, u32[]{:S(2)}, u32[]{:S(2)}) collective-permute-start(bf16[64,1024]{1,0:T(8,128)(2,1)S(1)} %get-tuple-element.131.refs_2_), channel_id=1, source_target_pairs={{0,6},{1,7},{2,4},{3,5},{4,2},{5,3},{6,0},{7,1},{8,14},{9,15},{10,... | collective-permute-start | bytes 393224 | tf_op jit(solution)/shard_map/ppermute | solution.py:18
  175.0 13.2 %collective-permute-start.56 = (bf16[2,64,768]{2,1,0:T(8,128)(2,1)S(1)}, bf16[2,64,768]{2,1,0:T(8,128)(2,1)S(1)}, u32[]{:S(2)}, u32[]{:S(2)}) collective-permute-start(bf16[2,64,768]{2,1,0:T(8,128)(2,1)S(1)} %get-tuple-element.142), channel_id=1, source_target_pairs={{0,96},{8,104},{16,112},{24,120},{32,64},{40,72},{48,80},{56,88},{... | collective-permute-start | bytes 589832 | tf_op jit(solution)/shard_map/ppermute | solution.py:18
  175.3 13.0 %collective-permute-start.57 = (bf16[2,64,768]{2,1,0:T(8,128)(2,1)S(1)}, bf16[2,64,768]{2,1,0:T(8,128)(2,1)S(1)}, u32[]{:S(2)}, u32[]{:S(2)}) collective-permute-start(bf16[2,64,768]{2,1,0:T(8,128)(2,1)S(1)} %get-tuple-element.143), channel_id=1, source_target_pairs={{0,64},{8,72},{16,80},{24,88},{32,96},{40,104},{48,112},{56,120},{... | collective-permute-start | bytes 589832 | tf_op jit(solution)/shard_map/ppermute | solution.py:18
  179.2 10.6 %collective-permute-start.60 = (bf16[2,64,512]{2,1,0:T(8,128)(2,1)S(1)}, bf16[2,64,512]{2,1,0:T(8,128)(2,1)S(1)}, u32[]{:S(2)}, u32[]{:S(2)}) collective-permute-start(bf16[2,64,512]{2,1,0:T(8,128)(2,1)S(1)} %get-tuple-element.149), channel_id=1, source_target_pairs={{0,32},{8,40},{16,48},{24,56},{32,0},{40,8},{48,16},{56,24},{64,96... | collective-permute-start | bytes 393224 | tf_op jit(solution)/shard_map/ppermute | solution.py:18
  179.4 13.9 %collective-permute-start.61 = (bf16[2,64,512]{2,1,0:T(8,128)(2,1)S(1)}, bf16[2,64,512]{2,1,0:T(8,128)(2,1)S(1)}, u32[]{:S(2)}, u32[]{:S(2)}) collective-permute-start(bf16[2,64,512]{2,1,0:T(8,128)(2,1)S(1)} %get-tuple-element.150), channel_id=1, source_target_pairs={{0,96},{8,104},{16,112},{24,120},{32,64},{40,72},{48,80},{56,88},{... | collective-permute-start | bytes 393224 | tf_op jit(solution)/shard_map/ppermute | solution.py:18
  182.7 10.6 %collective-permute-start.62 = (bf16[2,64,512]{2,1,0:T(8,128)(2,1)S(1)}, bf16[2,64,512]{2,1,0:T(8,128)(2,1)S(1)}, u32[]{:S(2)}, u32[]{:S(2)}) collective-permute-start(bf16[2,64,512]{2,1,0:T(8,128)(2,1)S(1)} %get-tuple-element.151), channel_id=1, source_target_pairs={{0,64},{8,72},{16,80},{24,88},{32,96},{40,104},{48,112},{56,120},{... | collective-permute-start | bytes 393224 | tf_op jit(solution)/shard_map/ppermute | solution.py:18
  (40 other events, 296.5 us)

commit v4 on v3

--- a/solution.py
+++ b/solution.py
@@ -9,7 +9,7 @@
 BF16 = jnp.bfloat16
 F32 = jnp.float32
 MIB = 1024 * 1024
-ORDER_COST = 30 * 10**9
+ORDER_COST = 12 * 10**9
 NEAR_FAR = (0, 1, 2, 3, 6, 7, 4, 5)
 
 
@@ -137,7 +137,7 @@
 
 
 def grouped(refs, halves):
-    return [refs[i * halves : (i + 1) * halves] for i in range(5)]
+    return [refs[i : i + halves] for i in range(0, len(refs), halves)]
 
 
 def block(group, k=None):
@@ -146,9 +146,10 @@
 
 
 def near_far_order(groups):
-    g01, g23, g67, g4, g5 = groups
-    pairs = [block(g, k) for g in (g01, g23, g67) for k in range(2)]
-    return pairs + [block(g4), block(g5)]
+    pairs = [block(g, k) for g in groups[:3] for k in range(2)]
+    if len(groups) == 4:
+        return pairs + [block(groups[3], k) for k in range(2)]
+    return pairs + [block(g) for g in groups[3:]]
 
 
 def unit_of(embedded):
@@ -273,16 +274,16 @@
     return call(name, body, outs, (*flips, *texts), flops, 24, after)
 
 
-def weight_part(name, column, place, pieces, feat, after):
-    halves, width = len(pieces) // 5, pieces[-1].shape[-1]
+def weight_part(name, column, place, pieces, halves, feat, after):
+    count, width = len(pieces), pieces[-1].shape[-1]
     rows, features = feat.shape
     own = rows // 8
     strip = width // 16
     tile = 256
 
     def body(column_ref, place_ref, *refs):
-        feat_ref, same, other, flipped, moved, result = refs[5 * halves :]
-        for n, part in enumerate(near_far_order(grouped(refs, halves))):
+        feat_ref, same, other, flipped, moved, result = refs[count:]
+        for n, part in enumerate(near_far_order(grouped(refs[:count], halves))):
             k = NEAR_FAR[n]
             flipped[:, k * own : (k + 1) * own] = part.T
         def features_at(here):
@@ -310,17 +311,17 @@
     return call(name, body, outs, (column, place, *pieces, feat), flops, 16, after, specs, scratch)
 
 
-def feature_grad(name, column, pieces, weight):
-    halves, width = len(pieces) // 5, pieces[-1].shape[-1]
+def feature_grad(name, column, pieces, halves, weight):
+    count, width = len(pieces), pieces[-1].shape[-1]
     features = weight.shape[0]
-    own = pieces[-1].shape[0] * halves
+    own = pieces[0].shape[1] * halves
     rows = 8 * own
     tile = 256
 
     def body(column_ref, *refs):
-        weight_ref, out = refs[5 * halves :]
+        weight_ref, out = refs[count:]
         def features_at(here):
-            egrad = jnp.concatenate(near_far_order(grouped(refs, halves)), axis=0)
+            egrad = jnp.concatenate(near_far_order(grouped(refs[:count], halves)), axis=0)
             result = lax.dot_general(
                 egrad, weight_ref[here], (((1,), (1,)), ((), ())), preferred_element_type=F32
             ).astype(BF16)
@@ -362,6 +363,36 @@
     p0, p2 = call("weight_z", along_z, outs, (p02, p46, p1214, p810))
     p2 = swap(p2, "blk", 2)
     return call("weight_y", along_y, outs[:1], (p0, p2))[0].T
+
+
+def chip_weight_y(name, same, other, after=None):
+    strip, features = same.shape[1:]
+
+    def body(same, got, mine, theirs):
+        for j in range(4):
+            for k, out in enumerate((mine, theirs)):
+                out[j] = (wide(same, 2 * j + k) + wide(got, 2 * j + k)).astype(BF16)
+
+    outs = [shape(4, strip, features)] * 2
+    return call(name, body, outs, (same, swap(other, "blk", 1)), after=after)
+
+
+def sum_weight_y(mine, theirs):
+    strip, features = mine.shape[1:]
+    one = (strip, features)
+
+    def along_y(mine, got, p0, p4, p12, p8):
+        p0[...] = wide(mine, 0) + wide(got, 0)
+        for j, out in ((1, p4), (2, p12), (3, p8)):
+            out[...] = (wide(mine, j) + wide(got, j)).astype(BF16)
+
+    def along_z(p0, p4, p12, p8, out):
+        out[...] = p0[...] + wide(p4) + wide(p12) + wide(p8)
+
+    outs = [shape(*one, dtype=F32)] + [shape(*one)] * 3
+    p0, p4, p12, p8 = call("weight_image_y", along_y, outs, (mine, swap(theirs, "blk", 2)))
+    p4, p12, p8 = swap(p4, "blk", 4), swap(p12, "blk", 12), swap(p8, "blk", 8)
+    return call("weight_image_z", along_z, outs[:1], (p0, p4, p12, p8))[0].T
 
 
 def local(img_feat, txt_feat, img_weight, txt_weight, natural_exponent_multiplier, bias):
@@ -462,7 +493,7 @@
     (x_b,) = call("image_grads_x_b", add_half(1), [shape(*half)], (g01, *got[1]), after=x_a)
     y_b = swap(x_b, "mp", 1)
     (e01_a,) = call("image_back_a", back_half, [shape(*half)], (x_a, y_a, emb_a), after=x_b)
-    e23_a, e67_a = swap(e01_a, "mp", 2), swap(e01_a, "mp", 6)
+    e23_a, e67_a, e45_a = swap(e01_a, "mp", 2), swap(e01_a, "mp", 6), swap(e01_a, "mp", 4)
 
     def seventh(p02, p46, p1214, p0_out, p2_out):
         p0_out[...] = wide(p02, 0) + wide(p46, 0) + wide(p1214, 0)
@@ -472,39 +503,28 @@
     p0, p2 = call("sums_seventh", seventh, outs, (p02, p46, p1214), after=e01_a)
     p2_got = swap(p2, "blk", 2)
     (e01_b,) = call("image_back_b", back_half, [shape(*half)], (x_b, y_b, emb_b), after=p2)
-    e23_b, e67_b = swap(e01_b, "mp", 2), swap(e01_b, "mp", 6)
-    outs = [shape(*own_half)] * 2
-    e2_a, e7_a = call("cut_image_grads_a", cut, outs, (e23_a, e67_a), after=e01_b)
-    e4_a, e5_a = swap(e2_a, "mp", 6), swap(e7_a, "mp", 2)
+    e23_b, e67_b, e45_b = swap(e01_b, "mp", 2), swap(e01_b, "mp", 6), swap(e01_b, "mp", 4)
 
     def text_back(p0, p2, txt_emb, out):
         out[...] = norm_back(p0[...] + wide(p2), txt_emb[...]).astype(BF16)
 
-    (d0,) = call("text_back", text_back, [shape(*one)], (p0, p2_got, txt_emb), after=e2_a)
+    (d0,) = call("text_back", text_back, [shape(*one)], (p0, p2_got, txt_emb), after=(e01_b, e23_a, e67_a, e45_a))
     d1 = swap(d0, "mp", 1)
-    e2_b, e7_b = call("cut_image_grads_b", cut, outs, (e23_b, e67_b), after=d0)
-    e4_b, e5_b = swap(e2_b, "mp", 6), swap(e7_b, "mp", 2)
-    (d01,) = call("stack_text_grads", stack, [shape(*two)], (d0, d1), after=(e4_a, e5_a, e2_b))
+    (d01,) = call("stack_text_grads", stack, [shape(*two)], (d0, d1), after=(e23_b, e67_b, e45_b))
     d23, d67 = swap(d01, "mp", 2), swap(d01, "mp", 6)
 
-    e_all = (e01_a, e01_b, e23_a, e23_b, e67_a, e67_b, e4_a, e4_b, e5_a, e5_b)
-    d2, d7 = call("cut_text_grads", cut, [shape(*one)] * 2, (d23, d67))
+    e_all = (e01_a, e01_b, e23_a, e23_b, e67_a, e67_b, e45_a, e45_b)
+    same, other = weight_part("weight_image", column, place, e_all, 2, img_feat, d01)
+    d2, d7 = call("cut_text_grads", cut, [shape(*one)] * 2, (d23, d67), ORDER_COST, after=same)
     d4, d5 = swap(d2, "mp", 6), swap(d7, "mp", 2)
-    same, other = weight_part("weight_image", column, place, e_all, img_feat, d7)
-    image_chip = chip_weight("weight_image_chip", same, other, None)
-    img_weight_grad = sum_weight(*image_chip)
-
-    def keep(first, second, first_out, second_out):
-        first_out[...] = first[...]
-        second_out[...] = second[...]
-
-    d4, d5 = call("keep_text_far", keep, [shape(*one)] * 2, (d4, d5), ORDER_COST)
+    image_chip = chip_weight_y("weight_image_chip", same, other)
+    img_weight_grad = sum_weight_y(*image_chip)
     d_all = (d01, d23, d67, d4, d5)
-    same, other = weight_part("weight_text", column, place, d_all, txt_feat, image_chip[0])
+    same, other = weight_part("weight_text", column, place, d_all, 1, txt_feat, image_chip[0])
     txt_weight_grad = sum_weight(*chip_weight("weight_text_chip", same, other))
     return (
-        feature_grad("feature_image", column, e_all, img_weight),
-        feature_grad("feature_text", column, d_all, txt_weight),
+        feature_grad("feature_image", column, e_all, 2, img_weight),
+        feature_grad("feature_text", column, d_all, 1, txt_weight),
         img_weight_grad,
         txt_weight_grad,
     )

time: 199 us -> 197 us (0.990)
  starting transfers between devices: 75 us -> 80 us
  Pallas kernels: 40.3 us -> 35.8 us
  waiting for transfers between devices: 76.8 us -> 74 us
    ppermute x64 -> x62, starting transfers between devices: 75 us -> 80 us  [swap(): return lax.ppermute(value, axis, [(i, i ^ offset) for i in range(count)])]
    pallas_call x42 -> x39, Pallas kernels: 31.2 us -> 26.6 us  [call(): pl.pallas_call(run, out_shape=outs, in_specs=specs, scratch_shapes=list(s...]
    ppermute x64 -> x62, waiting for transfers between devices: 76.8 us -> 74 us  [swap(): return lax.ppermute(value, axis, [(i, i ^ offset) for i in range(count)])]
    unnamed x16 -> x22, local copies, waits for them, and re-layouts: 3.87 us -> 4.83 us
  transfers between devices with their start and end apart: 64 -> 62, of which waited for: 35 -> 34; matrix products, arithmetic and copies ran while one was open for 0% -> 0% of each run, Pallas kernels for 15% -> 13%
where the time goes in v4:
time: 197 us
  starting transfers between devices  80 us (41%)
  waiting for transfers between devices  74 us (38%)
  Pallas kernels  35.8 us (18%)
  local copies, waits for them, and re-layouts  4.83 us (2%)
  between operations  2.34 us (1%)
    ppermute x62, starting transfers between devices, swap(): return lax.ppermute(value, axis, [(i, i ^ offset) for i in range(count)])  80 us
    ppermute x62, waiting for transfers between devices, swap(): return lax.ppermute(value, axis, [(i, i ^ offset) for i in range(count)])  74 us
    pallas_call x39, Pallas kernels, call(): pl.pallas_call(run, out_shape=outs, in_specs=specs, scratch_shapes=list(s...  26.6 us
    pallas_call x2, Pallas kernels, pair_call(): pl.pallas_call(body, in_specs=[smem, smem] + [vmem] * len(arrays), out_sh...  9.11 us
    unnamed x22, local copies, waits for them, and re-layouts  4.83 us
  transfers between devices with their start and end apart: 62, of which 34 were waited for; matrix products, arithmetic and copies ran while one was open for 0% of the time, Pallas kernels for 13%

profile of v4, /device:TPU:8, one launch (start us, length us, event | category | flops | bytes accessed | tf_op | source)
XLA Modules:
  0.0 196.9 jit_solution(5760387481324472428)
XLA Ops:
  5.2 2.8 %collective-permute-start = (bf16[128,1024]{1,0:T(8,128)(2,1)S(1)}, bf16[128,1024]{1,0:T(8,128)(2,1)S(1)}, u32[]{:S(2)}, u32[]{:S(2)}) collective-permute-start(bf16[128,1024]{1,0:T(8,128)(2,1)S(1)} %get-tuple-element.76), channel_id=1, source_target_pairs={{0,6},{1,7},{2,4},{3,5},{4,2},{5,3},{6,0},{7,1},{8,14},{9,15},{10,... | collective-permute-start | bytes 786440 | tf_op jit(solution)/shard_map/ppermute | solution.py:18
  8.2 6.3 %collective-permute-done.r4 = bf16[128,1024]{1,0:T(8,128)(2,1)S(1)} collective-permute-done((bf16[128,1024]{1,0:T(8,128)(2,1)S(1)}, bf16[128,1024]{1,0:T(8,128)(2,1)S(1)}, u32[]{:S(2)}, u32[]{:S(2)}) %collective-permute-start) | collective-permute-done | bytes 262176 | tf_op jit(solution)/shard_map/ppermute | solution.py:18
  17.6 2.6 %embed_image.1 = (bf16[2,128,1024]{2,1,0:T(8,128)(2,1)S(1)}, bf16[2,128,1024]{2,1,0:T(8,128)(2,1)S(1)}, bf16[2,128,1024]{2,1,0:T(8,128)(2,1)S(1)}, bf16[128,1024]{1,0:T(8,128)(2,1)S(1)}, bf16[128,1024]{1,0:T(8,128)(2,1)S(1)}) custom-call(s32[1]{0:T(128)} %bitcast.column_ref.refs_1_, bf16[1024,768]{1,0:T(8,128)(2,1)S(1)} %copy-done.5, ...), custom_call_target="tpu_custom_call" | custom-call | flops 1610612736 | bytes 5242884 | tf_op jit(solution)/shard_map/embed_image/pallas_call | solution.py:36
  22.8 8.1 %collective-permute-done.2.t23 = bf16[2,128,1024]{2,1,0:T(8,128)(2,1)S(1)} collective-permute-done((bf16[2,128,1024]{2,1,0:T(8,128)(2,1)S(1)}, bf16[2,128,1024]{2,1,0:T(8,128)(2,1)S(1)}, u32[]{:S(2)}, u32[]{:S(2)}) %collective-permute-start.2) | collective-permute-done | bytes 524320 | tf_op jit(solution)/shard_map/ppermute | solution.py:18
  32.5 2.4 %collective-permute-start.6 = (bf16[128,1024]{1,0:T(8,128)(2,1)S(1)}, bf16[128,1024]{1,0:T(8,128)(2,1)S(1)}, u32[]{:S(2)}, u32[]{:S(2)}) collective-permute-start(bf16[128,1024]{1,0:T(8,128)(2,1)S(1)} %get-tuple-element.80.refs_0_), channel_id=1, source_target_pairs={{0,1},{1,0},{2,3},{3,2},{4,5},{5,4},{6,7},{7,6},{8,9},{9,8},{10,11... | collective-permute-start | bytes 786440 | tf_op jit(solution)/shard_map/ppermute | solution.py:18
  37.4 4.5 %collective-permute-done.6.refs_2_ = bf16[128,1024]{1,0:T(8,128)(2,1)S(1)} collective-permute-done((bf16[128,1024]{1,0:T(8,128)(2,1)S(1)}, bf16[128,1024]{1,0:T(8,128)(2,1)S(1)}, u32[]{:S(2)}, u32[]{:S(2)}) %collective-permute-start.6) | collective-permute-done | bytes 262176 | tf_op jit(solution)/shard_map/ppermute | solution.py:18
  46.3 2.4 %collective-permute-start.12 = (bf16[2,64,1024]{2,1,0:T(8,128)(2,1)S(1)}, bf16[2,64,1024]{2,1,0:T(8,128)(2,1)S(1)}, u32[]{:S(2)}, u32[]{:S(2)}) collective-permute-start(bf16[2,64,1024]{2,1,0:T(8,128)(2,1)S(1)} %image_x_a.1.refs_0_.refs_1_), channel_id=1, source_target_pairs={{0,1},{1,0},{2,3},{3,2},{4,5},{5,4},{6,7},{7,6},{8,9},{9,8},{10,11... | collective-permute-start | bytes 786440 | tf_op jit(solution)/shard_map/ppermute | solution.py:18
  50.8 4.5 %collective-permute-start.19 = (bf16[2,128,1024]{2,1,0:T(8,128)(2,1)S(1)}, bf16[2,128,1024]{2,1,0:T(8,128)(2,1)S(1)}, u32[]{:S(2)}, u32[]{:S(2)}) collective-permute-start(bf16[2,128,1024]{2,1,0:T(8,128)(2,1)S(1)} %stack_text.1.refs_0_.refs_4_), channel_id=1, source_target_pairs={{0,96},{8,104},{16,112},{24,120},{32,64},{40,72},{48,80},{56,88},{... | collective-permute-start | bytes 1572872 | tf_op jit(solution)/shard_map/ppermute | solution.py:18
  55.4 3.0 %collective-permute-start.13 = (bf16[2,64,1024]{2,1,0:T(8,128)(2,1)S(1)}, bf16[2,64,1024]{2,1,0:T(8,128)(2,1)S(1)}, u32[]{:S(2)}, u32[]{:S(2)}) collective-permute-start(bf16[2,64,1024]{2,1,0:T(8,128)(2,1)S(1)} %image_x_b.1.refs_0_.refs_1_), channel_id=1, source_target_pairs={{0,1},{1,0},{2,3},{3,2},{4,5},{5,4},{6,7},{7,6},{8,9},{9,8},{10,11... | collective-permute-start | bytes 786440 | tf_op jit(solution)/shard_map/ppermute | solution.py:18
  59.9 3.5 %collective-permute-done.13.refs_2_ = bf16[2,64,1024]{2,1,0:T(8,128)(2,1)S(1)} collective-permute-done((bf16[2,64,1024]{2,1,0:T(8,128)(2,1)S(1)}, bf16[2,64,1024]{2,1,0:T(8,128)(2,1)S(1)}, u32[]{:S(2)}, u32[]{:S(2)}) %collective-permute-start.13) | collective-permute-done | bytes 262176 | tf_op jit(solution)/shard_map/ppermute | solution.py:18
  64.5 2.3 %collective-permute-done.15.refs_2_.refs_4_ = bf16[2,64,1024]{2,1,0:T(8,128)(2,1)S(1)} collective-permute-done((bf16[2,64,1024]{2,1,0:T(8,128)(2,1)S(1)}, bf16[2,64,1024]{2,1,0:T(8,128)(2,1)S(1)}, u32[]{:S(2)}, u32[]{:S(2)}) %collective-permute-start.15) | collective-permute-done | bytes 262176 | tf_op jit(solution)/shard_map/ppermute | solution.py:18
  74.7 2.5 %collective-permute-start.22 = (bf16[64,1024]{1,0:T(8,128)(2,1)S(1)}, bf16[64,1024]{1,0:T(8,128)(2,1)S(1)}, u32[]{:S(2)}, u32[]{:S(2)}) collective-permute-start(bf16[64,1024]{1,0:T(8,128)(2,1)S(1)} %get-tuple-element.97), channel_id=1, source_target_pairs={{0,6},{1,7},{2,4},{3,5},{4,2},{5,3},{6,0},{7,1},{8,14},{9,15},{10,... | collective-permute-start | bytes 393224 | tf_op jit(solution)/shard_map/ppermute | solution.py:18
  77.1 2.8 %collective-permute-done.16.refs_0_.refs_6_ = bf16[64,1024]{1,0:T(8,128)(2,1)S(1)} collective-permute-done((bf16[64,1024]{1,0:T(8,128)(2,1)S(1)}, bf16[64,1024]{1,0:T(8,128)(2,1)S(1)}, u32[]{:S(2)}, u32[]{:S(2)}) %collective-permute-start.16) | collective-permute-done | bytes 131104 | tf_op jit(solution)/shard_map/ppermute | solution.py:18
  83.9 4.0 %pairs_even.1 = (bf16[1024,1024]{1,0:T(8,128)(2,1)S(1)}, bf16[1024,1024]{1,0:T(8,128)(2,1)S(1)}, bf16[1024,1024]{1,0:T(8,128)(2,1)S(1)}) custom-call(f32[1]{0:T(128)S(6)} %exp.3.scale_ref, f32[1]{0:T(128)S(6)} %copy.11.bias_ref, bf16[8,128,1024]{2,1,0:T(8,128)(2,1)S(1)} %collect.1.texts.refs_3_, bf16[2,64,1024]{2,1,0:T(8,128)(2,1)S(1)} %get-tuple-element.92.refs_0_, ...), custom_call_target="tpu_custom_call" | custom-call | flops 2147483648 | bytes 10485760 | tf_op jit(solution)/shard_map/pairs_even/pallas_call | solution.py:183
  87.8 5.2 %pairs_odd.1 = (bf16[1024,1024]{1,0:T(8,128)(2,1)S(1)}, bf16[8,128,1024]{2,1,0:T(8,128)(2,1)S(1)}) custom-call(f32[1]{0:T(128)S(6)} %exp.3.scale_ref, f32[1]{0:T(128)S(6)} %copy.11.bias_ref, bf16[8,128,1024]{2,1,0:T(8,128)(2,1)S(1)} %collective-permute-done.26.texts.refs_4_, bf16[1024,1024]{1,0:T(8,128)(2,1)S(1)} %get-tuple-element.100.image_all.refs_2_, ...), custom_call_target="tpu_custom_call" | custom-call | flops 4294967296 | bytes 10485760 | tf_op jit(solution)/shard_map/pairs_odd/pallas_call | solution.py:183
  96.2 2.5 %text_grads_even.1.even.refs_1_ = bf16[8,128,1024]{2,1,0:T(8,128)(2,1)S(1)} custom-call(bf16[128,1024]{1,0:T(8,128)(2,1)S(1)} %get-tuple-element.104.refs_0_, bf16[1024,1024]{1,0:T(8,128)(2,1)S(1)} %get-tuple-element.105.refs_1_, bf16[1024,1024]{1,0:T(8,128)(2,1)S(1)} %get-tuple-element.100.image_all.refs_2_), custom_call_target="tpu_custom_call" | custom-call | flops 2147483648 | bytes 6553600 | tf_op jit(solution)/shard_map/text_grads_even/pallas_call | solution.py:36
  101.4 3.6 %pairs_near_images.1 = (bf16[2,128,1024]{2,1,0:T(8,128)(2,1)S(1)}, bf16[2,128,1024]{2,1,0:T(8,128)(2,1)S(1)}, bf16[2,128,1024]{2,1,0:T(8,128)(2,1)S(1)}) custom-call(bf16[128,1024]{1,0:T(8,128)(2,1)S(1)} %get-tuple-element.106.refs_0_, bf16[1024,1024]{1,0:T(8,128)(2,1)S(1)} %get-tuple-element.101._.refs_1_, ...), custom_call_target="tpu_custom_call" | custom-call | flops 3221225472 | bytes 10223616 | tf_op jit(solution)/shard_map/pairs_near_images/pallas_call | solution.py:36
  107.6 2.3 %collective-permute-done.30.refs_3_ = bf16[128,1024]{1,0:T(8,128)(2,1)S(1)} collective-permute-done((bf16[128,1024]{1,0:T(8,128)(2,1)S(1)}, bf16[128,1024]{1,0:T(8,128)(2,1)S(1)}, u32[]{:S(2)}, u32[]{:S(2)}) %collective-permute-start.30) | collective-permute-done | bytes 262176 | tf_op jit(solution)/shard_map/ppermute | solution.py:18
  116.2 3.0 %collective-permute-start.36 = (bf16[2,64,1024]{2,1,0:T(8,128)(2,1)S(1)}, bf16[2,64,1024]{2,1,0:T(8,128)(2,1)S(1)}, u32[]{:S(2)}, u32[]{:S(2)}) collective-permute-start(bf16[2,64,1024]{2,1,0:T(8,128)(2,1)S(1)} %image_grads_x_a.1.refs_0_.refs_1_), channel_id=1, source_target_pairs={{0,1},{1,0},{2,3},{3,2},{4,5},{5,4},{6,7},{7,6},{8,9},{9,8},{10,11... | collective-permute-start | bytes 786440 | tf_op jit(solution)/shard_map/ppermute | solution.py:18
  121.7 2.3 %collective-permute-start.39 = (bf16[2,64,1024]{2,1,0:T(8,128)(2,1)S(1)}, bf16[2,64,1024]{2,1,0:T(8,128)(2,1)S(1)}, u32[]{:S(2)}, u32[]{:S(2)}) collective-permute-start(bf16[2,64,1024]{2,1,0:T(8,128)(2,1)S(1)} %image_grads_x_b.1.refs_0_.refs_1_), channel_id=1, source_target_pairs={{0,1},{1,0},{2,3},{3,2},{4,5},{5,4},{6,7},{7,6},{8,9},{9,8},{10,11... | collective-permute-start | bytes 786440 | tf_op jit(solution)/shard_map/ppermute | solution.py:18
  126.0 3.5 %collective-permute-start.42 = (bf16[2,64,1024]{2,1,0:T(8,128)(2,1)S(1)}, bf16[2,64,1024]{2,1,0:T(8,128)(2,1)S(1)}, u32[]{:S(2)}, u32[]{:S(2)}) collective-permute-start(bf16[2,64,1024]{2,1,0:T(8,128)(2,1)S(1)} %image_back_a.1.refs_0_.refs_3_), channel_id=1, source_target_pairs={{0,6},{1,7},{2,4},{3,5},{4,2},{5,3},{6,0},{7,1},{8,14},{9,15},{10,... | collective-permute-start | bytes 786440 | tf_op jit(solution)/shard_map/ppermute | solution.py:18
  133.5 3.2 %collective-permute-done.44.refs_6_.refs_3_.refs_9_ = bf16[2,64,1024]{2,1,0:T(8,128)(2,1)S(1)} collective-permute-done((bf16[2,64,1024]{2,1,0:T(8,128)(2,1)S(1)}, bf16[2,64,1024]{2,1,0:T(8,128)(2,1)S(1)}, u32[]{:S(2)}, u32[]{:S(2)}) %collective-permute-start.44) | collective-permute-done | bytes 262176 | tf_op jit(solution)/shard_map/ppermute | solution.py:18
  137.2 5.1 %collective-permute-done.42.refs_4_.refs_2_.refs_7_ = bf16[2,64,1024]{2,1,0:T(8,128)(2,1)S(1)} collective-permute-done((bf16[2,64,1024]{2,1,0:T(8,128)(2,1)S(1)}, bf16[2,64,1024]{2,1,0:T(8,128)(2,1)S(1)}, u32[]{:S(2)}, u32[]{:S(2)}) %collective-permute-start.42) | collective-permute-done | bytes 262176 | tf_op jit(solution)/shard_map/ppermute | solution.py:18
  142.6 4.1 %collective-permute-start.47 = (bf16[128,1024]{1,0:T(8,128)(2,1)S(1)}, bf16[128,1024]{1,0:T(8,128)(2,1)S(1)}, u32[]{:S(2)}, u32[]{:S(2)}) collective-permute-start(bf16[128,1024]{1,0:T(8,128)(2,1)S(1)} %text_back.1.refs_3_), channel_id=1, source_target_pairs={{0,1},{1,0},{2,3},{3,2},{4,5},{5,4},{6,7},{7,6},{8,9},{9,8},{10,11... | collective-permute-start | bytes 786440 | tf_op jit(solution)/shard_map/ppermute | solution.py:18
  148.7 2.4 %collective-permute-done.47.refs_4_ = bf16[128,1024]{1,0:T(8,128)(2,1)S(1)} collective-permute-done((bf16[128,1024]{1,0:T(8,128)(2,1)S(1)}, bf16[128,1024]{1,0:T(8,128)(2,1)S(1)}, u32[]{:S(2)}, u32[]{:S(2)}) %collective-permute-start.47) | collective-permute-done | bytes 262176 | tf_op jit(solution)/shard_map/ppermute | solution.py:18
  159.2 2.4 %collective-permute-done.49.refs_2_.refs_5_ = bf16[2,128,1024]{2,1,0:T(8,128)(2,1)S(1)} collective-permute-done((bf16[2,128,1024]{2,1,0:T(8,128)(2,1)S(1)}, bf16[2,128,1024]{2,1,0:T(8,128)(2,1)S(1)}, u32[]{:S(2)}, u32[]{:S(2)}) %collective-permute-start.49) | collective-permute-done | bytes 524320 | tf_op jit(solution)/shard_map/ppermute | solution.py:18
  164.7 5.4 %collective-permute-done.50.refs_3_.refs_6_ = bf16[128,1024]{1,0:T(8,128)(2,1)S(1)} collective-permute-done((bf16[128,1024]{1,0:T(8,128)(2,1)S(1)}, bf16[128,1024]{1,0:T(8,128)(2,1)S(1)}, u32[]{:S(2)}, u32[]{:S(2)}) %collective-permute-start.50) | collective-permute-done | bytes 262176 | tf_op jit(solution)/shard_map/ppermute | solution.py:18
  171.7 3.5 %collective-permute-start.53 = (bf16[4,64,768]{2,1,0:T(8,128)(2,1)S(1)}, bf16[4,64,768]{2,1,0:T(8,128)(2,1)S(1)}, u32[]{:S(2)}, u32[]{:S(2)}) collective-permute-start(bf16[4,64,768]{2,1,0:T(8,128)(2,1)S(1)} %get-tuple-element.129), channel_id=1, source_target_pairs={{0,16},{8,24},{16,0},{24,8},{32,48},{40,56},{48,32},{56,40},{64,80... | collective-permute-start | bytes 1179656 | tf_op jit(solution)/shard_map/ppermute | solution.py:18
  175.9 3.9 %collective-permute-start.59 = (bf16[2,64,512]{2,1,0:T(8,128)(2,1)S(1)}, bf16[2,64,512]{2,1,0:T(8,128)(2,1)S(1)}, u32[]{:S(2)}, u32[]{:S(2)}) collective-permute-start(bf16[2,64,512]{2,1,0:T(8,128)(2,1)S(1)} %get-tuple-element.138), channel_id=1, source_target_pairs={{0,96},{8,104},{16,112},{24,120},{32,64},{40,72},{48,80},{56,88},{... | collective-permute-start | bytes 393224 | tf_op jit(solution)/shard_map/ppermute | solution.py:18
  181.2 3.4 %feature_image.1 = bf16[1024,768]{1,0:T(8,128)(2,1)} custom-call(s32[1]{0:T(128)} %bitcast.column_ref.refs_1_, bf16[2,64,1024]{2,1,0:T(8,128)(2,1)S(1)} %image_back_a.1.refs_0_.refs_3_, bf16[2,64,1024]{2,1,0:T(8,128)(2,1)S(1)} %image_back_b.1.refs_1_.refs_0_.refs_4_, bf16[2,64,1024]{2,1,0:T(8,128)(2,1)S(1)} %collective-permute-done.40.refs_2_.refs_1_.refs_5_, ...), custom_call_target="tpu_custom_call" | custom-call | flops 1610612736 | bytes 5242884 | tf_op jit(solution)/shard_map/feature_image/pallas_call | solution.py:36
  185.5 3.9 %collective-permute-start.55 = (bf16[64,768]{1,0:T(8,128)(2,1)S(1)}, bf16[64,768]{1,0:T(8,128)(2,1)S(1)}, u32[]{:S(2)}, u32[]{:S(2)}) collective-permute-start(bf16[64,768]{1,0:T(8,128)(2,1)S(1)} %get-tuple-element.132), channel_id=1, source_target_pairs={{0,96},{8,104},{16,112},{24,120},{32,64},{40,72},{48,80},{56,88},{... | collective-permute-start | bytes 294920 | tf_op jit(solution)/shard_map/ppermute | solution.py:18
  191.2 2.5 %feature_text.1 = bf16[1024,512]{1,0:T(8,128)(2,1)} custom-call(s32[1]{0:T(128)} %bitcast.column_ref.refs_1_, bf16[2,128,1024]{2,1,0:T(8,128)(2,1)S(1)} %stack_text_grads.1.refs_0_.refs_3_, bf16[2,128,1024]{2,1,0:T(8,128)(2,1)S(1)} %collective-permute-done.48.refs_1_.refs_4_, bf16[2,128,1024]{2,1,0:T(8,128)(2,1)S(1)} %collective-permute-done.49.refs_2_.refs_5_, ...), custom_call_target="tpu_custom_call" | custom-call | flops 1073741824 | bytes 4194308 | tf_op jit(solution)/shard_map/feature_text/pallas_call | solution.py:36
  (155 shorter events, 80.9 us)
Async XLA Ops:
  5.2 9.3 %collective-permute-start = (bf16[128,1024]{1,0:T(8,128)(2,1)S(1)}, bf16[128,1024]{1,0:T(8,128)(2,1)S(1)}, u32[]{:S(2)}, u32[]{:S(2)}) collective-permute-start(bf16[128,1024]{1,0:T(8,128)(2,1)S(1)} %get-tuple-element.76), channel_id=1, source_target_pairs={{0,6},{1,7},{2,4},{3,5},{4,2},{5,3},{6,0},{7,1},{8,14},{9,15},{10,... | collective-permute-start | bytes 786440 | tf_op jit(solution)/shard_map/ppermute | solution.py:18
  15.9 14.9 %collective-permute-start.2 = (bf16[2,128,1024]{2,1,0:T(8,128)(2,1)S(1)}, bf16[2,128,1024]{2,1,0:T(8,128)(2,1)S(1)}, u32[]{:S(2)}, u32[]{:S(2)}) collective-permute-start(bf16[2,128,1024]{2,1,0:T(8,128)(2,1)S(1)} %get-tuple-element.78), channel_id=1, source_target_pairs={{0,2},{1,3},{2,0},{3,1},{4,6},{5,7},{6,4},{7,5},{8,10},{9,11},{10,... | collective-permute-start | bytes 1572872 | tf_op jit(solution)/shard_map/ppermute | solution.py:18
  16.3 16.1 %collective-permute-start.3 = (bf16[2,128,1024]{2,1,0:T(8,128)(2,1)S(1)}, bf16[2,128,1024]{2,1,0:T(8,128)(2,1)S(1)}, u32[]{:S(2)}, u32[]{:S(2)}) collective-permute-start(bf16[2,128,1024]{2,1,0:T(8,128)(2,1)S(1)} %get-tuple-element.79), channel_id=1, source_target_pairs={{0,6},{1,7},{2,4},{3,5},{4,2},{5,3},{6,0},{7,1},{8,14},{9,15},{10,... | collective-permute-start | bytes 1572872 | tf_op jit(solution)/shard_map/ppermute | solution.py:18
  20.2 15.1 %collective-permute-start.4 = (bf16[128,1024]{1,0:T(8,128)(2,1)S(1)}, bf16[128,1024]{1,0:T(8,128)(2,1)S(1)}, u32[]{:S(2)}, u32[]{:S(2)}) collective-permute-start(bf16[128,1024]{1,0:T(8,128)(2,1)S(1)} %get-tuple-element.83), channel_id=1, source_target_pairs={{0,6},{1,7},{2,4},{3,5},{4,2},{5,3},{6,0},{7,1},{8,14},{9,15},{10,... | collective-permute-start | bytes 786440 | tf_op jit(solution)/shard_map/ppermute | solution.py:18
  22.2 13.2 %collective-permute-start.5 = (bf16[128,1024]{1,0:T(8,128)(2,1)S(1)}, bf16[128,1024]{1,0:T(8,128)(2,1)S(1)}, u32[]{:S(2)}, u32[]{:S(2)}) collective-permute-start(bf16[128,1024]{1,0:T(8,128)(2,1)S(1)} %get-tuple-element.84), channel_id=1, source_target_pairs={{0,2},{1,3},{2,0},{3,1},{4,6},{5,7},{6,4},{7,5},{8,10},{9,11},{10,... | collective-permute-start | bytes 786440 | tf_op jit(solution)/shard_map/ppermute | solution.py:18
  32.5 9.3 %collective-permute-start.6 = (bf16[128,1024]{1,0:T(8,128)(2,1)S(1)}, bf16[128,1024]{1,0:T(8,128)(2,1)S(1)}, u32[]{:S(2)}, u32[]{:S(2)}) collective-permute-start(bf16[128,1024]{1,0:T(8,128)(2,1)S(1)} %get-tuple-element.80.refs_0_), channel_id=1, source_target_pairs={{0,1},{1,0},{2,3},{3,2},{4,5},{5,4},{6,7},{7,6},{8,9},{9,8},{10,11... | collective-permute-start | bytes 786440 | tf_op jit(solution)/shard_map/ppermute | solution.py:18
  35.5 10.1 %collective-permute-start.8 = (bf16[2,64,1024]{2,1,0:T(8,128)(2,1)S(1)}, bf16[2,64,1024]{2,1,0:T(8,128)(2,1)S(1)}, u32[]{:S(2)}, u32[]{:S(2)}) collective-permute-start(bf16[2,64,1024]{2,1,0:T(8,128)(2,1)S(1)} %get-tuple-element.89), channel_id=1, source_target_pairs={{0,6},{1,7},{2,4},{3,5},{4,2},{5,3},{6,0},{7,1},{8,14},{9,15},{10,... | collective-permute-start | bytes 786440 | tf_op jit(solution)/shard_map/ppermute | solution.py:18
  43.0 12.3 %collective-permute-start.10 = (bf16[2,64,1024]{2,1,0:T(8,128)(2,1)S(1)}, bf16[2,64,1024]{2,1,0:T(8,128)(2,1)S(1)}, u32[]{:S(2)}, u32[]{:S(2)}) collective-permute-start(bf16[2,64,1024]{2,1,0:T(8,128)(2,1)S(1)} %get-tuple-element.90), channel_id=1, source_target_pairs={{0,2},{1,3},{2,0},{3,1},{4,6},{5,7},{6,4},{7,5},{8,10},{9,11},{10,... | collective-permute-start | bytes 786440 | tf_op jit(solution)/shard_map/ppermute | solution.py:18
  43.0 12.3 %collective-permute-start.11 = (bf16[2,64,1024]{2,1,0:T(8,128)(2,1)S(1)}, bf16[2,64,1024]{2,1,0:T(8,128)(2,1)S(1)}, u32[]{:S(2)}, u32[]{:S(2)}) collective-permute-start(bf16[2,64,1024]{2,1,0:T(8,128)(2,1)S(1)} %get-tuple-element.91), channel_id=1, source_target_pairs={{0,6},{1,7},{2,4},{3,5},{4,2},{5,3},{6,0},{7,1},{8,14},{9,15},{10,... | collective-permute-start | bytes 786440 | tf_op jit(solution)/shard_map/ppermute | solution.py:18
  46.3 12.1 %collective-permute-start.12 = (bf16[2,64,1024]{2,1,0:T(8,128)(2,1)S(1)}, bf16[2,64,1024]{2,1,0:T(8,128)(2,1)S(1)}, u32[]{:S(2)}, u32[]{:S(2)}) collective-permute-start(bf16[2,64,1024]{2,1,0:T(8,128)(2,1)S(1)} %image_x_a.1.refs_0_.refs_1_), channel_id=1, source_target_pairs={{0,1},{1,0},{2,3},{3,2},{4,5},{5,4},{6,7},{7,6},{8,9},{9,8},{10,11... | collective-permute-start | bytes 786440 | tf_op jit(solution)/shard_map/ppermute | solution.py:18
  50.8 18.2 %collective-permute-start.19 = (bf16[2,128,1024]{2,1,0:T(8,128)(2,1)S(1)}, bf16[2,128,1024]{2,1,0:T(8,128)(2,1)S(1)}, u32[]{:S(2)}, u32[]{:S(2)}) collective-permute-start(bf16[2,128,1024]{2,1,0:T(8,128)(2,1)S(1)} %stack_text.1.refs_0_.refs_4_), channel_id=1, source_target_pairs={{0,96},{8,104},{16,112},{24,120},{32,64},{40,72},{48,80},{56,88},{... | collective-permute-start | bytes 1572872 | tf_op jit(solution)/shard_map/ppermute | solution.py:18
  55.3 13.7 %collective-permute-start.18 = (bf16[2,128,1024]{2,1,0:T(8,128)(2,1)S(1)}, bf16[2,128,1024]{2,1,0:T(8,128)(2,1)S(1)}, u32[]{:S(2)}, u32[]{:S(2)}) collective-permute-start(bf16[2,128,1024]{2,1,0:T(8,128)(2,1)S(1)} %stack_text.1.refs_0_.refs_4_), channel_id=1, source_target_pairs={{0,32},{8,40},{16,48},{24,56},{32,0},{40,8},{48,16},{56,24},{64,96... | collective-permute-start | bytes 1572872 | tf_op jit(solution)/shard_map/ppermute | solution.py:18
  63.5 10.3 %collective-permute-start.21 = (bf16[2,64,1024]{2,1,0:T(8,128)(2,1)S(1)}, bf16[2,64,1024]{2,1,0:T(8,128)(2,1)S(1)}, u32[]{:S(2)}, u32[]{:S(2)}) collective-permute-start(bf16[2,64,1024]{2,1,0:T(8,128)(2,1)S(1)} %get-tuple-element.93.refs_0_.refs_1_), channel_id=1, source_target_pairs={{0,6},{1,7},{2,4},{3,5},{4,2},{5,3},{6,0},{7,1},{8,14},{9,15},{10,... | collective-permute-start | bytes 786440 | tf_op jit(solution)/shard_map/ppermute | solution.py:18
  69.0 13.1 %collective-permute-start.25 = (bf16[128,1024]{1,0:T(8,128)(2,1)S(1)}, bf16[128,1024]{1,0:T(8,128)(2,1)S(1)}, u32[]{:S(2)}, u32[]{:S(2)}) collective-permute-start(bf16[128,1024]{1,0:T(8,128)(2,1)S(1)} %get-tuple-element.99), channel_id=1, source_target_pairs={{0,32},{8,40},{16,48},{24,56},{32,0},{40,8},{48,16},{56,24},{64,96... | collective-permute-start | bytes 786440 | tf_op jit(solution)/shard_map/ppermute | solution.py:18
  71.0 11.1 %collective-permute-start.24 = (bf16[128,1024]{1,0:T(8,128)(2,1)S(1)}, bf16[128,1024]{1,0:T(8,128)(2,1)S(1)}, u32[]{:S(2)}, u32[]{:S(2)}) collective-permute-start(bf16[128,1024]{1,0:T(8,128)(2,1)S(1)} %get-tuple-element.96.refs_0_), channel_id=1, source_target_pairs={{0,96},{8,104},{16,112},{24,120},{32,64},{40,72},{48,80},{56,88},{... | collective-permute-start | bytes 786440 | tf_op jit(solution)/shard_map/ppermute | solution.py:18
  94.8 10.2 %collective-permute-start.29 = (bf16[128,1024]{1,0:T(8,128)(2,1)S(1)}, bf16[128,1024]{1,0:T(8,128)(2,1)S(1)}, u32[]{:S(2)}, u32[]{:S(2)}) collective-permute-start(bf16[128,1024]{1,0:T(8,128)(2,1)S(1)} %get-tuple-element.109), channel_id=1, source_target_pairs={{0,2},{1,3},{2,0},{3,1},{4,6},{5,7},{6,4},{7,5},{8,10},{9,11},{10,... | collective-permute-start | bytes 786440 | tf_op jit(solution)/shard_map/ppermute | solution.py:18
  94.9 10.1 %collective-permute-start.28 = (bf16[128,1024]{1,0:T(8,128)(2,1)S(1)}, bf16[128,1024]{1,0:T(8,128)(2,1)S(1)}, u32[]{:S(2)}, u32[]{:S(2)}) collective-permute-start(bf16[128,1024]{1,0:T(8,128)(2,1)S(1)} %get-tuple-element.104.refs_0_), channel_id=1, source_target_pairs={{0,6},{1,7},{2,4},{3,5},{4,2},{5,3},{6,0},{7,1},{8,14},{9,15},{10,... | collective-permute-start | bytes 786440 | tf_op jit(solution)/shard_map/ppermute | solution.py:18
  110.3 19.2 %collective-permute-start.37 = (bf16[2,128,1024]{2,1,0:T(8,128)(2,1)S(1)}, bf16[2,128,1024]{2,1,0:T(8,128)(2,1)S(1)}, u32[]{:S(2)}, u32[]{:S(2)}) collective-permute-start(bf16[2,128,1024]{2,1,0:T(8,128)(2,1)S(1)} %get-tuple-element.118), channel_id=1, source_target_pairs={{0,32},{8,40},{16,48},{24,56},{32,0},{40,8},{48,16},{56,24},{64,96... | collective-permute-start | bytes 1572872 | tf_op jit(solution)/shard_map/ppermute | solution.py:18
  110.4 19.1 %collective-permute-start.38 = (bf16[2,128,1024]{2,1,0:T(8,128)(2,1)S(1)}, bf16[2,128,1024]{2,1,0:T(8,128)(2,1)S(1)}, u32[]{:S(2)}, u32[]{:S(2)}) collective-permute-start(bf16[2,128,1024]{2,1,0:T(8,128)(2,1)S(1)} %get-tuple-element.119), channel_id=1, source_target_pairs={{0,96},{8,104},{16,112},{24,120},{32,64},{40,72},{48,80},{56,88},{... | collective-permute-start | bytes 1572872 | tf_op jit(solution)/shard_map/ppermute | solution.py:18
  116.2 9.3 %collective-permute-start.36 = (bf16[2,64,1024]{2,1,0:T(8,128)(2,1)S(1)}, bf16[2,64,1024]{2,1,0:T(8,128)(2,1)S(1)}, u32[]{:S(2)}, u32[]{:S(2)}) collective-permute-start(bf16[2,64,1024]{2,1,0:T(8,128)(2,1)S(1)} %image_grads_x_a.1.refs_0_.refs_1_), channel_id=1, source_target_pairs={{0,1},{1,0},{2,3},{3,2},{4,5},{5,4},{6,7},{7,6},{8,9},{9,8},{10,11... | collective-permute-start | bytes 786440 | tf_op jit(solution)/shard_map/ppermute | solution.py:18
  121.7 10.8 %collective-permute-start.39 = (bf16[2,64,1024]{2,1,0:T(8,128)(2,1)S(1)}, bf16[2,64,1024]{2,1,0:T(8,128)(2,1)S(1)}, u32[]{:S(2)}, u32[]{:S(2)}) collective-permute-start(bf16[2,64,1024]{2,1,0:T(8,128)(2,1)S(1)} %image_grads_x_b.1.refs_0_.refs_1_), channel_id=1, source_target_pairs={{0,1},{1,0},{2,3},{3,2},{4,5},{5,4},{6,7},{7,6},{8,9},{9,8},{10,11... | collective-permute-start | bytes 786440 | tf_op jit(solution)/shard_map/ppermute | solution.py:18
  125.8 10.9 %collective-permute-start.44 = (bf16[2,64,1024]{2,1,0:T(8,128)(2,1)S(1)}, bf16[2,64,1024]{2,1,0:T(8,128)(2,1)S(1)}, u32[]{:S(2)}, u32[]{:S(2)}) collective-permute-start(bf16[2,64,1024]{2,1,0:T(8,128)(2,1)S(1)} %image_back_a.1.refs_0_.refs_3_), channel_id=1, source_target_pairs={{0,4},{1,5},{2,6},{3,7},{4,0},{5,1},{6,2},{7,3},{8,12},{9,13},{10,... | collective-permute-start | bytes 786440 | tf_op jit(solution)/shard_map/ppermute | solution.py:18
  126.0 16.3 %collective-permute-start.42 = (bf16[2,64,1024]{2,1,0:T(8,128)(2,1)S(1)}, bf16[2,64,1024]{2,1,0:T(8,128)(2,1)S(1)}, u32[]{:S(2)}, u32[]{:S(2)}) collective-permute-start(bf16[2,64,1024]{2,1,0:T(8,128)(2,1)S(1)} %image_back_a.1.refs_0_.refs_3_), channel_id=1, source_target_pairs={{0,6},{1,7},{2,4},{3,5},{4,2},{5,3},{6,0},{7,1},{8,14},{9,15},{10,... | collective-permute-start | bytes 786440 | tf_op jit(solution)/shard_map/ppermute | solution.py:18
  129.5 12.8 %collective-permute-start.40 = (bf16[2,64,1024]{2,1,0:T(8,128)(2,1)S(1)}, bf16[2,64,1024]{2,1,0:T(8,128)(2,1)S(1)}, u32[]{:S(2)}, u32[]{:S(2)}) collective-permute-start(bf16[2,64,1024]{2,1,0:T(8,128)(2,1)S(1)} %image_back_a.1.refs_0_.refs_3_), channel_id=1, source_target_pairs={{0,2},{1,3},{2,0},{3,1},{4,6},{5,7},{6,4},{7,5},{8,10},{9,11},{10,... | collective-permute-start | bytes 786440 | tf_op jit(solution)/shard_map/ppermute | solution.py:18
  129.7 12.6 %collective-permute-start.46 = (bf16[128,1024]{1,0:T(8,128)(2,1)S(1)}, bf16[128,1024]{1,0:T(8,128)(2,1)S(1)}, u32[]{:S(2)}, u32[]{:S(2)}) collective-permute-start(bf16[128,1024]{1,0:T(8,128)(2,1)S(1)} %get-tuple-element.120.refs_0_), channel_id=1, source_target_pairs={{0,16},{8,24},{16,0},{24,8},{32,48},{40,56},{48,32},{56,40},{64,80... | collective-permute-start | bytes 786440 | tf_op jit(solution)/shard_map/ppermute | solution.py:18
  132.7 13.9 %collective-permute-start.45 = (bf16[2,64,1024]{2,1,0:T(8,128)(2,1)S(1)}, bf16[2,64,1024]{2,1,0:T(8,128)(2,1)S(1)}, u32[]{:S(2)}, u32[]{:S(2)}) collective-permute-start(bf16[2,64,1024]{2,1,0:T(8,128)(2,1)S(1)} %image_back_b.1.refs_1_.refs_0_.refs_4_), channel_id=1, source_target_pairs={{0,4},{1,5},{2,6},{3,7},{4,0},{5,1},{6,2},{7,3},{8,12},{9,13},{10,... | collective-permute-start | bytes 786440 | tf_op jit(solution)/shard_map/ppermute | solution.py:18
  136.7 11.6 %collective-permute-start.43 = (bf16[2,64,1024]{2,1,0:T(8,128)(2,1)S(1)}, bf16[2,64,1024]{2,1,0:T(8,128)(2,1)S(1)}, u32[]{:S(2)}, u32[]{:S(2)}) collective-permute-start(bf16[2,64,1024]{2,1,0:T(8,128)(2,1)S(1)} %image_back_b.1.refs_1_.refs_0_.refs_4_), channel_id=1, source_target_pairs={{0,6},{1,7},{2,4},{3,5},{4,2},{5,3},{6,0},{7,1},{8,14},{9,15},{10,... | collective-permute-start | bytes 786440 | tf_op jit(solution)/shard_map/ppermute | solution.py:18
  151.1 10.5 %collective-permute-start.49 = (bf16[2,128,1024]{2,1,0:T(8,128)(2,1)S(1)}, bf16[2,128,1024]{2,1,0:T(8,128)(2,1)S(1)}, u32[]{:S(2)}, u32[]{:S(2)}) collective-permute-start(bf16[2,128,1024]{2,1,0:T(8,128)(2,1)S(1)} %stack_text_grads.1.refs_0_.refs_3_), channel_id=1, source_target_pairs={{0,6},{1,7},{2,4},{3,5},{4,2},{5,3},{6,0},{7,1},{8,14},{9,15},{10,... | collective-permute-start | bytes 1572872 | tf_op jit(solution)/shard_map/ppermute | solution.py:18
  171.7 13.2 %collective-permute-start.53 = (bf16[4,64,768]{2,1,0:T(8,128)(2,1)S(1)}, bf16[4,64,768]{2,1,0:T(8,128)(2,1)S(1)}, u32[]{:S(2)}, u32[]{:S(2)}) collective-permute-start(bf16[4,64,768]{2,1,0:T(8,128)(2,1)S(1)} %get-tuple-element.129), channel_id=1, source_target_pairs={{0,16},{8,24},{16,0},{24,8},{32,48},{40,56},{48,32},{56,40},{64,80... | collective-permute-start | bytes 1179656 | tf_op jit(solution)/shard_map/ppermute | solution.py:18
  175.3 14.1 %collective-permute-start.58 = (bf16[2,64,512]{2,1,0:T(8,128)(2,1)S(1)}, bf16[2,64,512]{2,1,0:T(8,128)(2,1)S(1)}, u32[]{:S(2)}, u32[]{:S(2)}) collective-permute-start(bf16[2,64,512]{2,1,0:T(8,128)(2,1)S(1)} %get-tuple-element.137), channel_id=1, source_target_pairs={{0,32},{8,40},{16,48},{24,56},{32,0},{40,8},{48,16},{56,24},{64,96... | collective-permute-start | bytes 393224 | tf_op jit(solution)/shard_map/ppermute | solution.py:18
  175.9 14.9 %collective-permute-start.59 = (bf16[2,64,512]{2,1,0:T(8,128)(2,1)S(1)}, bf16[2,64,512]{2,1,0:T(8,128)(2,1)S(1)}, u32[]{:S(2)}, u32[]{:S(2)}) collective-permute-start(bf16[2,64,512]{2,1,0:T(8,128)(2,1)S(1)} %get-tuple-element.138), channel_id=1, source_target_pairs={{0,96},{8,104},{16,112},{24,120},{32,64},{40,72},{48,80},{56,88},{... | collective-permute-start | bytes 393224 | tf_op jit(solution)/shard_map/ppermute | solution.py:18
  179.8 11.0 %collective-permute-start.60 = (bf16[2,64,512]{2,1,0:T(8,128)(2,1)S(1)}, bf16[2,64,512]{2,1,0:T(8,128)(2,1)S(1)}, u32[]{:S(2)}, u32[]{:S(2)}) collective-permute-start(bf16[2,64,512]{2,1,0:T(8,128)(2,1)S(1)} %get-tuple-element.139), channel_id=1, source_target_pairs={{0,64},{8,72},{16,80},{24,88},{32,96},{40,104},{48,112},{56,120},{... | collective-permute-start | bytes 393224 | tf_op jit(solution)/shard_map/ppermute | solution.py:18
  (41 other events, 300.7 us)

commit v5 on v4

--- a/solution.py
+++ b/solution.py
@@ -9,7 +9,7 @@
 BF16 = jnp.bfloat16
 F32 = jnp.float32
 MIB = 1024 * 1024
-ORDER_COST = 12 * 10**9
+ORDER_COST = 10 * 10**9
 NEAR_FAR = (0, 1, 2, 3, 6, 7, 4, 5)
 
 
@@ -319,7 +319,8 @@
     tile = 256
 
     def body(column_ref, *refs):
-        weight_ref, out = refs[count:]
+        weight_ref, out, mark = refs[count:]
+        mark[...] = jnp.zeros_like(mark)
         def features_at(here):
             egrad = jnp.concatenate(near_far_order(grouped(refs[:count], halves)), axis=0)
             result = lax.dot_general(
@@ -332,8 +333,8 @@
         tiles(features // tile, tile, features_at)
 
     smem, vmem = pl.BlockSpec(memory_space=pltpu.SMEM), pl.BlockSpec(memory_space=pltpu.VMEM)
-    outs, ins = [shape(rows, features)], (column, *pieces, weight)
-    return call(name, body, outs, ins, 2 * rows * width * features, 16, None, [smem] + [vmem] * (len(pieces) + 1))[0]
+    outs, ins = [shape(rows, features), shape(16, 128)], (column, *pieces, weight)
+    return call(name, body, outs, ins, 2 * rows * width * features, 16, None, [smem] + [vmem] * (len(pieces) + 1))
 
 
 def chip_weight(name, same, other, after=None):
@@ -392,7 +393,7 @@
     outs = [shape(*one, dtype=F32)] + [shape(*one)] * 3
     p0, p4, p12, p8 = call("weight_image_y", along_y, outs, (mine, swap(theirs, "blk", 2)))
     p4, p12, p8 = swap(p4, "blk", 4), swap(p12, "blk", 12), swap(p8, "blk", 8)
-    return call("weight_image_z", along_z, outs[:1], (p0, p4, p12, p8))[0].T
+    return call("weight_image_z", along_z, outs[:1], (p0, p4, p12, p8))[0].T, p0
 
 
 def local(img_feat, txt_feat, img_weight, txt_weight, natural_exponent_multiplier, bias):
@@ -488,46 +489,43 @@
     outs = [shape(*two)] * 3
     p02, p46, p1214 = call("sums_sixth", sixth, outs, (even_sum, odd_got, p8_got, p10_got), after=sent[0])
     p46, p1214 = swap(p46, "blk", 4), swap(p1214, "blk", 12)
-    (x_a,) = call("image_grads_x_a", add_half(0), [shape(*half)], (g01, *got[0]), after=p02)
+    (x_a,) = call("image_grads_x_a", add_half(0), [shape(*half)], (g01, *got[0]), ORDER_COST // 2, after=p02)
     y_a = swap(x_a, "mp", 1)
     (x_b,) = call("image_grads_x_b", add_half(1), [shape(*half)], (g01, *got[1]), after=x_a)
     y_b = swap(x_b, "mp", 1)
-    (e01_a,) = call("image_back_a", back_half, [shape(*half)], (x_a, y_a, emb_a), after=x_b)
-    e23_a, e67_a, e45_a = swap(e01_a, "mp", 2), swap(e01_a, "mp", 6), swap(e01_a, "mp", 4)
-
     def seventh(p02, p46, p1214, p0_out, p2_out):
         p0_out[...] = wide(p02, 0) + wide(p46, 0) + wide(p1214, 0)
         p2_out[...] = (wide(p02, 1) + wide(p46, 1) + wide(p1214, 1)).astype(BF16)
 
     outs = [shape(*one, dtype=F32), shape(*one)]
-    p0, p2 = call("sums_seventh", seventh, outs, (p02, p46, p1214), after=e01_a)
+    p0, p2 = call("sums_seventh", seventh, outs, (p02, p46, p1214), after=x_b)
     p2_got = swap(p2, "blk", 2)
-    (e01_b,) = call("image_back_b", back_half, [shape(*half)], (x_b, y_b, emb_b), after=p2)
-    e23_b, e67_b, e45_b = swap(e01_b, "mp", 2), swap(e01_b, "mp", 6), swap(e01_b, "mp", 4)
+    (e01_a,) = call("image_back_a", back_half, [shape(*half)], (x_a, y_a, emb_a), after=p2)
+    e23_a, e67_a, e45_a = swap(e01_a, "mp", 2), swap(e01_a, "mp", 6), swap(e01_a, "mp", 4)
 
     def text_back(p0, p2, txt_emb, out):
         out[...] = norm_back(p0[...] + wide(p2), txt_emb[...]).astype(BF16)
 
-    (d0,) = call("text_back", text_back, [shape(*one)], (p0, p2_got, txt_emb), after=(e01_b, e23_a, e67_a, e45_a))
+    (d0,) = call("text_back", text_back, [shape(*one)], (p0, p2_got, txt_emb), after=e01_a)
     d1 = swap(d0, "mp", 1)
-    (d01,) = call("stack_text_grads", stack, [shape(*two)], (d0, d1), after=(e23_b, e67_b, e45_b))
+    (e01_b,) = call("image_back_b", back_half, [shape(*half)], (x_b, y_b, emb_b), after=d0)
+    e23_b, e67_b, e45_b = swap(e01_b, "mp", 2), swap(e01_b, "mp", 6), swap(e01_b, "mp", 4)
+
+    (d01,) = call("stack_text_grads", stack, [shape(*two)], (d0, d1), after=(e01_b, e23_a, e67_a, e45_a))
     d23, d67 = swap(d01, "mp", 2), swap(d01, "mp", 6)
 
     e_all = (e01_a, e01_b, e23_a, e23_b, e67_a, e67_b, e45_a, e45_b)
     same, other = weight_part("weight_image", column, place, e_all, 2, img_feat, d01)
-    d2, d7 = call("cut_text_grads", cut, [shape(*one)] * 2, (d23, d67), ORDER_COST, after=same)
+    img_feat_grad, image_done = feature_grad("feature_image", column, e_all, 2, img_weight)
+    d2, d7 = call("cut_text_grads", cut, [shape(*one)] * 2, (d23, d67), ORDER_COST, after=(same, image_done))
     d4, d5 = swap(d2, "mp", 6), swap(d7, "mp", 2)
     image_chip = chip_weight_y("weight_image_chip", same, other)
-    img_weight_grad = sum_weight_y(*image_chip)
+    img_weight_grad, image_y = sum_weight_y(*image_chip)
     d_all = (d01, d23, d67, d4, d5)
     same, other = weight_part("weight_text", column, place, d_all, 1, txt_feat, image_chip[0])
     txt_weight_grad = sum_weight(*chip_weight("weight_text_chip", same, other))
-    return (
-        feature_grad("feature_image", column, e_all, 2, img_weight),
-        feature_grad("feature_text", column, d_all, 1, txt_weight),
-        img_weight_grad,
-        txt_weight_grad,
-    )
+    txt_feat_grad, _ = feature_grad("feature_text", column, d_all, 1, txt_weight)
+    return (img_feat_grad, txt_feat_grad, img_weight_grad, txt_weight_grad)
 
 
 def solution(mesh):

time: 197 us -> 200 us (1.015)
  Pallas kernels: 35.8 us -> 41.7 us
  starting transfers between devices: 80 us -> 74.7 us
  waiting for transfers between devices: 74 us -> 78.4 us
  local copies, waits for them, and re-layouts: 4.83 us -> 2.47 us
    pallas_call x39, Pallas kernels: 26.6 us -> 32.6 us  [call(): pl.pallas_call(run, out_shape=outs, in_specs=specs, scratch_shapes=list(s...]
    ppermute x62, starting transfers between devices: 80 us -> 74.7 us  [swap(): return lax.ppermute(value, axis, [(i, i ^ offset) for i in range(count)])]
    ppermute x62, waiting for transfers between devices: 74 us -> 78.4 us  [swap(): return lax.ppermute(value, axis, [(i, i ^ offset) for i in range(count)])]
    unnamed x22 -> x14, local copies, waits for them, and re-layouts: 4.83 us -> 2.47 us
  transfers between devices with their start and end apart: 62 -> 62, of which waited for: 34 -> 32; matrix products, arithmetic and copies ran while one was open for 0% -> 0% of each run, Pallas kernels for 13% -> 15%
where the time goes in v5:
time: 200 us
  waiting for transfers between devices  78.4 us (39%)
  starting transfers between devices  74.7 us (37%)
  Pallas kernels  41.7 us (21%)
  local copies, waits for them, and re-layouts  2.47 us (1%)
  between operations  2.34 us (1%)
    ppermute x62, waiting for transfers between devices, swap(): return lax.ppermute(value, axis, [(i, i ^ offset) for i in range(count)])  78.4 us
    ppermute x62, starting transfers between devices, swap(): return lax.ppermute(value, axis, [(i, i ^ offset) for i in range(count)])  74.7 us
    pallas_call x39, Pallas kernels, call(): pl.pallas_call(run, out_shape=outs, in_specs=specs, scratch_shapes=list(s...  32.6 us
    pallas_call x2, Pallas kernels, pair_call(): pl.pallas_call(body, in_specs=[smem, smem] + [vmem] * len(arrays), out_sh...  9.11 us
  transfers between devices with their start and end apart: 62, of which 32 were waited for; matrix products, arithmetic and copies ran while one was open for 0% of the time, Pallas kernels for 15%

profile of v5, /device:TPU:8, one launch (start us, length us, event | category | flops | bytes accessed | tf_op | source)
XLA Modules:
  0.0 199.6 jit_solution(7736824343501819525)
XLA Ops:
  5.2 2.8 %collective-permute-start = (bf16[128,1024]{1,0:T(8,128)(2,1)S(1)}, bf16[128,1024]{1,0:T(8,128)(2,1)S(1)}, u32[]{:S(2)}, u32[]{:S(2)}) collective-permute-start(bf16[128,1024]{1,0:T(8,128)(2,1)S(1)} %get-tuple-element.79), channel_id=1, source_target_pairs={{0,6},{1,7},{2,4},{3,5},{4,2},{5,3},{6,0},{7,1},{8,14},{9,15},{10,... | collective-permute-start | bytes 786440 | tf_op jit(solution)/shard_map/ppermute | solution.py:18
  8.2 6.3 %collective-permute-done.r4 = bf16[128,1024]{1,0:T(8,128)(2,1)S(1)} collective-permute-done((bf16[128,1024]{1,0:T(8,128)(2,1)S(1)}, bf16[128,1024]{1,0:T(8,128)(2,1)S(1)}, u32[]{:S(2)}, u32[]{:S(2)}) %collective-permute-start) | collective-permute-done | bytes 262176 | tf_op jit(solution)/shard_map/ppermute | solution.py:18
  17.6 2.6 %embed_image.1 = (bf16[2,128,1024]{2,1,0:T(8,128)(2,1)S(1)}, bf16[2,128,1024]{2,1,0:T(8,128)(2,1)S(1)}, bf16[2,128,1024]{2,1,0:T(8,128)(2,1)S(1)}, bf16[128,1024]{1,0:T(8,128)(2,1)S(1)}, bf16[128,1024]{1,0:T(8,128)(2,1)S(1)}) custom-call(s32[1]{0:T(128)} %bitcast.column_ref.refs_1_, bf16[1024,768]{1,0:T(8,128)(2,1)S(1)} %copy-done, ...), custom_call_target="tpu_custom_call" | custom-call | flops 1610612736 | bytes 5242884 | tf_op jit(solution)/shard_map/embed_image/pallas_call | solution.py:36
  22.8 8.1 %collective-permute-done.2.t23 = bf16[2,128,1024]{2,1,0:T(8,128)(2,1)S(1)} collective-permute-done((bf16[2,128,1024]{2,1,0:T(8,128)(2,1)S(1)}, bf16[2,128,1024]{2,1,0:T(8,128)(2,1)S(1)}, u32[]{:S(2)}, u32[]{:S(2)}) %collective-permute-start.2) | collective-permute-done | bytes 524320 | tf_op jit(solution)/shard_map/ppermute | solution.py:18
  32.5 2.4 %collective-permute-start.6 = (bf16[128,1024]{1,0:T(8,128)(2,1)S(1)}, bf16[128,1024]{1,0:T(8,128)(2,1)S(1)}, u32[]{:S(2)}, u32[]{:S(2)}) collective-permute-start(bf16[128,1024]{1,0:T(8,128)(2,1)S(1)} %get-tuple-element.83.refs_0_), channel_id=1, source_target_pairs={{0,1},{1,0},{2,3},{3,2},{4,5},{5,4},{6,7},{7,6},{8,9},{9,8},{10,11... | collective-permute-start | bytes 786440 | tf_op jit(solution)/shard_map/ppermute | solution.py:18
  37.4 4.5 %collective-permute-done.6.refs_2_ = bf16[128,1024]{1,0:T(8,128)(2,1)S(1)} collective-permute-done((bf16[128,1024]{1,0:T(8,128)(2,1)S(1)}, bf16[128,1024]{1,0:T(8,128)(2,1)S(1)}, u32[]{:S(2)}, u32[]{:S(2)}) %collective-permute-start.6) | collective-permute-done | bytes 262176 | tf_op jit(solution)/shard_map/ppermute | solution.py:18
  46.3 2.4 %collective-permute-start.12 = (bf16[2,64,1024]{2,1,0:T(8,128)(2,1)S(1)}, bf16[2,64,1024]{2,1,0:T(8,128)(2,1)S(1)}, u32[]{:S(2)}, u32[]{:S(2)}) collective-permute-start(bf16[2,64,1024]{2,1,0:T(8,128)(2,1)S(1)} %image_x_a.1.refs_0_.refs_1_), channel_id=1, source_target_pairs={{0,1},{1,0},{2,3},{3,2},{4,5},{5,4},{6,7},{7,6},{8,9},{9,8},{10,11... | collective-permute-start | bytes 786440 | tf_op jit(solution)/shard_map/ppermute | solution.py:18
  50.8 4.5 %collective-permute-start.19 = (bf16[2,128,1024]{2,1,0:T(8,128)(2,1)S(1)}, bf16[2,128,1024]{2,1,0:T(8,128)(2,1)S(1)}, u32[]{:S(2)}, u32[]{:S(2)}) collective-permute-start(bf16[2,128,1024]{2,1,0:T(8,128)(2,1)S(1)} %stack_text.1.refs_0_.refs_4_), channel_id=1, source_target_pairs={{0,96},{8,104},{16,112},{24,120},{32,64},{40,72},{48,80},{56,88},{... | collective-permute-start | bytes 1572872 | tf_op jit(solution)/shard_map/ppermute | solution.py:18
  55.4 3.0 %collective-permute-start.13 = (bf16[2,64,1024]{2,1,0:T(8,128)(2,1)S(1)}, bf16[2,64,1024]{2,1,0:T(8,128)(2,1)S(1)}, u32[]{:S(2)}, u32[]{:S(2)}) collective-permute-start(bf16[2,64,1024]{2,1,0:T(8,128)(2,1)S(1)} %image_x_b.1.refs_0_.refs_1_), channel_id=1, source_target_pairs={{0,1},{1,0},{2,3},{3,2},{4,5},{5,4},{6,7},{7,6},{8,9},{9,8},{10,11... | collective-permute-start | bytes 786440 | tf_op jit(solution)/shard_map/ppermute | solution.py:18
  59.9 3.5 %collective-permute-done.13.refs_2_ = bf16[2,64,1024]{2,1,0:T(8,128)(2,1)S(1)} collective-permute-done((bf16[2,64,1024]{2,1,0:T(8,128)(2,1)S(1)}, bf16[2,64,1024]{2,1,0:T(8,128)(2,1)S(1)}, u32[]{:S(2)}, u32[]{:S(2)}) %collective-permute-start.13) | collective-permute-done | bytes 262176 | tf_op jit(solution)/shard_map/ppermute | solution.py:18
  64.5 2.3 %collective-permute-done.15.refs_2_.refs_4_ = bf16[2,64,1024]{2,1,0:T(8,128)(2,1)S(1)} collective-permute-done((bf16[2,64,1024]{2,1,0:T(8,128)(2,1)S(1)}, bf16[2,64,1024]{2,1,0:T(8,128)(2,1)S(1)}, u32[]{:S(2)}, u32[]{:S(2)}) %collective-permute-start.15) | collective-permute-done | bytes 262176 | tf_op jit(solution)/shard_map/ppermute | solution.py:18
  74.7 2.5 %collective-permute-start.22 = (bf16[64,1024]{1,0:T(8,128)(2,1)S(1)}, bf16[64,1024]{1,0:T(8,128)(2,1)S(1)}, u32[]{:S(2)}, u32[]{:S(2)}) collective-permute-start(bf16[64,1024]{1,0:T(8,128)(2,1)S(1)} %get-tuple-element.100), channel_id=1, source_target_pairs={{0,6},{1,7},{2,4},{3,5},{4,2},{5,3},{6,0},{7,1},{8,14},{9,15},{10,... | collective-permute-start | bytes 393224 | tf_op jit(solution)/shard_map/ppermute | solution.py:18
  77.1 2.8 %collective-permute-done.16.refs_0_.refs_6_ = bf16[64,1024]{1,0:T(8,128)(2,1)S(1)} collective-permute-done((bf16[64,1024]{1,0:T(8,128)(2,1)S(1)}, bf16[64,1024]{1,0:T(8,128)(2,1)S(1)}, u32[]{:S(2)}, u32[]{:S(2)}) %collective-permute-start.16) | collective-permute-done | bytes 131104 | tf_op jit(solution)/shard_map/ppermute | solution.py:18
  83.9 4.0 %pairs_even.1 = (bf16[1024,1024]{1,0:T(8,128)(2,1)S(1)}, bf16[1024,1024]{1,0:T(8,128)(2,1)S(1)}, bf16[1024,1024]{1,0:T(8,128)(2,1)S(1)}) custom-call(f32[1]{0:T(128)S(6)} %exp.3.scale_ref, f32[1]{0:T(128)S(6)} %copy.11.bias_ref, bf16[8,128,1024]{2,1,0:T(8,128)(2,1)S(1)} %collect.1.texts.refs_3_, bf16[2,64,1024]{2,1,0:T(8,128)(2,1)S(1)} %get-tuple-element.95.refs_0_, ...), custom_call_target="tpu_custom_call" | custom-call | flops 2147483648 | bytes 10485760 | tf_op jit(solution)/shard_map/pairs_even/pallas_call | solution.py:183
  87.8 5.2 %pairs_odd.1 = (bf16[1024,1024]{1,0:T(8,128)(2,1)S(1)}, bf16[8,128,1024]{2,1,0:T(8,128)(2,1)S(1)}) custom-call(f32[1]{0:T(128)S(6)} %exp.3.scale_ref, f32[1]{0:T(128)S(6)} %copy.11.bias_ref, bf16[8,128,1024]{2,1,0:T(8,128)(2,1)S(1)} %collective-permute-done.26.texts.refs_4_, bf16[1024,1024]{1,0:T(8,128)(2,1)S(1)} %get-tuple-element.103.image_all.refs_2_, ...), custom_call_target="tpu_custom_call" | custom-call | flops 4294967296 | bytes 10485760 | tf_op jit(solution)/shard_map/pairs_odd/pallas_call | solution.py:183
  96.2 2.5 %text_grads_even.1.even.refs_1_ = bf16[8,128,1024]{2,1,0:T(8,128)(2,1)S(1)} custom-call(bf16[128,1024]{1,0:T(8,128)(2,1)S(1)} %get-tuple-element.107.refs_0_, bf16[1024,1024]{1,0:T(8,128)(2,1)S(1)} %get-tuple-element.108.refs_1_, bf16[1024,1024]{1,0:T(8,128)(2,1)S(1)} %get-tuple-element.103.image_all.refs_2_), custom_call_target="tpu_custom_call" | custom-call | flops 2147483648 | bytes 6553600 | tf_op jit(solution)/shard_map/text_grads_even/pallas_call | solution.py:36
  101.4 3.6 %pairs_near_images.1 = (bf16[2,128,1024]{2,1,0:T(8,128)(2,1)S(1)}, bf16[2,128,1024]{2,1,0:T(8,128)(2,1)S(1)}, bf16[2,128,1024]{2,1,0:T(8,128)(2,1)S(1)}) custom-call(bf16[128,1024]{1,0:T(8,128)(2,1)S(1)} %get-tuple-element.109.refs_0_, bf16[1024,1024]{1,0:T(8,128)(2,1)S(1)} %get-tuple-element.104._.refs_1_, ...), custom_call_target="tpu_custom_call" | custom-call | flops 3221225472 | bytes 10223616 | tf_op jit(solution)/shard_map/pairs_near_images/pallas_call | solution.py:36
  107.6 2.3 %collective-permute-done.30.refs_3_ = bf16[128,1024]{1,0:T(8,128)(2,1)S(1)} collective-permute-done((bf16[128,1024]{1,0:T(8,128)(2,1)S(1)}, bf16[128,1024]{1,0:T(8,128)(2,1)S(1)}, u32[]{:S(2)}, u32[]{:S(2)}) %collective-permute-start.30) | collective-permute-done | bytes 262176 | tf_op jit(solution)/shard_map/ppermute | solution.py:18
  116.2 3.0 %collective-permute-start.38 = (bf16[2,64,1024]{2,1,0:T(8,128)(2,1)S(1)}, bf16[2,64,1024]{2,1,0:T(8,128)(2,1)S(1)}, u32[]{:S(2)}, u32[]{:S(2)}) collective-permute-start(bf16[2,64,1024]{2,1,0:T(8,128)(2,1)S(1)} %image_grads_x_a.1.refs_0_.refs_1_), channel_id=1, source_target_pairs={{0,1},{1,0},{2,3},{3,2},{4,5},{5,4},{6,7},{7,6},{8,9},{9,8},{10,11... | collective-permute-start | bytes 786440 | tf_op jit(solution)/shard_map/ppermute | solution.py:18
  126.4 2.3 %collective-permute-start.45 = (bf16[2,64,1024]{2,1,0:T(8,128)(2,1)S(1)}, bf16[2,64,1024]{2,1,0:T(8,128)(2,1)S(1)}, u32[]{:S(2)}, u32[]{:S(2)}) collective-permute-start(bf16[2,64,1024]{2,1,0:T(8,128)(2,1)S(1)} %image_back_a.1.refs_0_.refs_3_), channel_id=1, source_target_pairs={{0,4},{1,5},{2,6},{3,7},{4,0},{5,1},{6,2},{7,3},{8,12},{9,13},{10,... | collective-permute-start | bytes 786440 | tf_op jit(solution)/shard_map/ppermute | solution.py:18
  129.9 3.6 %collective-permute-done.39.refs_2_ = bf16[128,1024]{1,0:T(8,128)(2,1)S(1)} collective-permute-done((bf16[128,1024]{1,0:T(8,128)(2,1)S(1)}, bf16[128,1024]{1,0:T(8,128)(2,1)S(1)}, u32[]{:S(2)}, u32[]{:S(2)}) %collective-permute-start.39) | collective-permute-done | bytes 262176 | tf_op jit(solution)/shard_map/ppermute | solution.py:18
  135.4 3.0 %collective-permute-done.40.refs_2_ = bf16[2,64,1024]{2,1,0:T(8,128)(2,1)S(1)} collective-permute-done((bf16[2,64,1024]{2,1,0:T(8,128)(2,1)S(1)}, bf16[2,64,1024]{2,1,0:T(8,128)(2,1)S(1)}, u32[]{:S(2)}, u32[]{:S(2)}) %collective-permute-start.40) | collective-permute-done | bytes 262176 | tf_op jit(solution)/shard_map/ppermute | solution.py:18
  147.0 2.6 %collective-permute-done.46.refs_7_.refs_10_ = bf16[2,64,1024]{2,1,0:T(8,128)(2,1)} collective-permute-done((bf16[2,64,1024]{2,1,0:T(8,128)(2,1)S(1)}, bf16[2,64,1024]{2,1,0:T(8,128)(2,1)}, u32[]{:S(2)}, u32[]{:S(2)}) %collective-permute-start.46) | collective-permute-done | bytes 262176 | tf_op jit(solution)/shard_map/ppermute | solution.py:18
  149.6 3.6 %collective-permute-done.44.refs_5_.refs_8_ = bf16[2,64,1024]{2,1,0:T(8,128)(2,1)} collective-permute-done((bf16[2,64,1024]{2,1,0:T(8,128)(2,1)S(1)}, bf16[2,64,1024]{2,1,0:T(8,128)(2,1)}, u32[]{:S(2)}, u32[]{:S(2)}) %collective-permute-start.44) | collective-permute-done | bytes 262176 | tf_op jit(solution)/shard_map/ppermute | solution.py:18
  154.5 3.3 %weight_image.1 = (bf16[8,64,768]{2,1,0:T(8,128)(2,1)S(1)}, bf16[8,64,768]{2,1,0:T(8,128)(2,1)S(1)}) custom-call(bf16[2,128,1024]{2,1,0:T(8,128)(2,1)S(1)} %stack_text_grads.1.refs_0_.refs_3_, s32[1]{0:T(128)} %bitcast.column_ref.refs_1_, s32[1]{0:T(128)} %bitcast.1.refs_2_, bf16[2,64,1024]{2,1,0:T(8,128)(2,1)S(1)} %image_back_a.1.refs_0_.refs_3_, ...), custom_call_target="tpu_custom_call" | custom-call | flops 1610612736 | bytes 5767176 | tf_op jit(solution)/shard_map/weight_image/pallas_call | solution.py:36
  157.9 4.5 %feature_image.1 = (bf16[1024,768]{1,0:T(8,128)(2,1)}, bf16[16,128]{1,0:T(8,128)(2,1)S(1)}) custom-call(s32[1]{0:T(128)} %bitcast.column_ref.refs_1_, bf16[2,64,1024]{2,1,0:T(8,128)(2,1)S(1)} %image_back_a.1.refs_0_.refs_3_, bf16[2,64,1024]{2,1,0:T(8,128)(2,1)S(1)} %image_back_b.1.refs_1_.refs_0_.refs_4_, ...), custom_call_target="tpu_custom_call" | custom-call | flops 1610612736 | bytes 5246980 | tf_op jit(solution)/shard_map/feature_image/pallas_call | solution.py:36
  165.8 8.0 %collective-permute-done.50.refs_3_.refs_6_ = bf16[128,1024]{1,0:T(8,128)(2,1)S(1)} collective-permute-done((bf16[128,1024]{1,0:T(8,128)(2,1)S(1)}, bf16[128,1024]{1,0:T(8,128)(2,1)S(1)}, u32[]{:S(2)}, u32[]{:S(2)}) %collective-permute-start.50) | collective-permute-done | bytes 262176 | tf_op jit(solution)/shard_map/ppermute | solution.py:18
  173.8 2.6 %weight_text.1 = (bf16[8,64,512]{2,1,0:T(8,128)(2,1)S(1)}, bf16[8,64,512]{2,1,0:T(8,128)(2,1)S(1)}) custom-call(bf16[4,64,768]{2,1,0:T(8,128)(2,1)S(1)} %get-tuple-element.134.mine.refs_0_, s32[1]{0:T(128)} %bitcast.column_ref.refs_1_, s32[1]{0:T(128)} %bitcast.1.refs_2_, bf16[2,128,1024]{2,1,0:T(8,128)(2,1)S(1)} %stack_text_grads.1.refs_0_.refs_3_, ...), custom_call_target="tpu_custom_call" | custom-call | flops 1073741824 | bytes 4587528 | tf_op jit(solution)/shard_map/weight_text/pallas_call | solution.py:36
  176.5 2.2 %collective-permute-start.53 = (bf16[4,64,768]{2,1,0:T(8,128)(2,1)S(1)}, bf16[4,64,768]{2,1,0:T(8,128)(2,1)S(1)}, u32[]{:S(2)}, u32[]{:S(2)}) collective-permute-start(bf16[4,64,768]{2,1,0:T(8,128)(2,1)S(1)} %get-tuple-element.135), channel_id=1, source_target_pairs={{0,16},{8,24},{16,0},{24,8},{32,48},{40,56},{48,32},{56,40},{64,80... | collective-permute-start | bytes 1179656 | tf_op jit(solution)/shard_map/ppermute | solution.py:18
  183.0 5.4 %collective-permute-done.53.got = bf16[4,64,768]{2,1,0:T(8,128)(2,1)S(1)} collective-permute-done((bf16[4,64,768]{2,1,0:T(8,128)(2,1)S(1)}, bf16[4,64,768]{2,1,0:T(8,128)(2,1)S(1)}, u32[]{:S(2)}, u32[]{:S(2)}) %collective-permute-start.53) | collective-permute-done | bytes 393248 | tf_op jit(solution)/shard_map/ppermute | solution.py:18
  190.5 2.2 %collective-permute-start.56 = (bf16[64,768]{1,0:T(8,128)(2,1)S(1)}, bf16[64,768]{1,0:T(8,128)(2,1)S(1)}, u32[]{:S(2)}, u32[]{:S(2)}) collective-permute-start(bf16[64,768]{1,0:T(8,128)(2,1)S(1)} %get-tuple-element.139), channel_id=1, source_target_pairs={{0,64},{8,72},{16,80},{24,88},{32,96},{40,104},{48,112},{56,120},{... | collective-permute-start | bytes 294920 | tf_op jit(solution)/shard_map/ppermute | solution.py:18
  194.6 3.7 %feature_text.1 = (bf16[1024,512]{1,0:T(8,128)(2,1)}, bf16[16,128]{1,0:T(8,128)(2,1)}) custom-call(s32[1]{0:T(128)} %bitcast.column_ref.refs_1_, bf16[2,128,1024]{2,1,0:T(8,128)(2,1)S(1)} %stack_text_grads.1.refs_0_.refs_3_, bf16[2,128,1024]{2,1,0:T(8,128)(2,1)} %collective-permute-done.48.refs_2_.refs_1_.refs_4_, ...), custom_call_target="tpu_custom_call" | custom-call | flops 1073741824 | bytes 4198404 | tf_op jit(solution)/shard_map/feature_text/pallas_call | solution.py:36
  (147 shorter events, 82.0 us)
Async XLA Ops:
  15.9 14.9 %collective-permute-start.2 = (bf16[2,128,1024]{2,1,0:T(8,128)(2,1)S(1)}, bf16[2,128,1024]{2,1,0:T(8,128)(2,1)S(1)}, u32[]{:S(2)}, u32[]{:S(2)}) collective-permute-start(bf16[2,128,1024]{2,1,0:T(8,128)(2,1)S(1)} %get-tuple-element.81), channel_id=1, source_target_pairs={{0,2},{1,3},{2,0},{3,1},{4,6},{5,7},{6,4},{7,5},{8,10},{9,11},{10,... | collective-permute-start | bytes 1572872 | tf_op jit(solution)/shard_map/ppermute | solution.py:18
  16.3 16.1 %collective-permute-start.3 = (bf16[2,128,1024]{2,1,0:T(8,128)(2,1)S(1)}, bf16[2,128,1024]{2,1,0:T(8,128)(2,1)S(1)}, u32[]{:S(2)}, u32[]{:S(2)}) collective-permute-start(bf16[2,128,1024]{2,1,0:T(8,128)(2,1)S(1)} %get-tuple-element.82), channel_id=1, source_target_pairs={{0,6},{1,7},{2,4},{3,5},{4,2},{5,3},{6,0},{7,1},{8,14},{9,15},{10,... | collective-permute-start | bytes 1572872 | tf_op jit(solution)/shard_map/ppermute | solution.py:18
  20.2 15.1 %collective-permute-start.4 = (bf16[128,1024]{1,0:T(8,128)(2,1)S(1)}, bf16[128,1024]{1,0:T(8,128)(2,1)S(1)}, u32[]{:S(2)}, u32[]{:S(2)}) collective-permute-start(bf16[128,1024]{1,0:T(8,128)(2,1)S(1)} %get-tuple-element.86), channel_id=1, source_target_pairs={{0,6},{1,7},{2,4},{3,5},{4,2},{5,3},{6,0},{7,1},{8,14},{9,15},{10,... | collective-permute-start | bytes 786440 | tf_op jit(solution)/shard_map/ppermute | solution.py:18
  22.3 13.1 %collective-permute-start.5 = (bf16[128,1024]{1,0:T(8,128)(2,1)S(1)}, bf16[128,1024]{1,0:T(8,128)(2,1)S(1)}, u32[]{:S(2)}, u32[]{:S(2)}) collective-permute-start(bf16[128,1024]{1,0:T(8,128)(2,1)S(1)} %get-tuple-element.87), channel_id=1, source_target_pairs={{0,2},{1,3},{2,0},{3,1},{4,6},{5,7},{6,4},{7,5},{8,10},{9,11},{10,... | collective-permute-start | bytes 786440 | tf_op jit(solution)/shard_map/ppermute | solution.py:18
  35.5 10.1 %collective-permute-start.8 = (bf16[2,64,1024]{2,1,0:T(8,128)(2,1)S(1)}, bf16[2,64,1024]{2,1,0:T(8,128)(2,1)S(1)}, u32[]{:S(2)}, u32[]{:S(2)}) collective-permute-start(bf16[2,64,1024]{2,1,0:T(8,128)(2,1)S(1)} %get-tuple-element.92), channel_id=1, source_target_pairs={{0,6},{1,7},{2,4},{3,5},{4,2},{5,3},{6,0},{7,1},{8,14},{9,15},{10,... | collective-permute-start | bytes 786440 | tf_op jit(solution)/shard_map/ppermute | solution.py:18
  43.0 12.3 %collective-permute-start.10 = (bf16[2,64,1024]{2,1,0:T(8,128)(2,1)S(1)}, bf16[2,64,1024]{2,1,0:T(8,128)(2,1)S(1)}, u32[]{:S(2)}, u32[]{:S(2)}) collective-permute-start(bf16[2,64,1024]{2,1,0:T(8,128)(2,1)S(1)} %get-tuple-element.93), channel_id=1, source_target_pairs={{0,2},{1,3},{2,0},{3,1},{4,6},{5,7},{6,4},{7,5},{8,10},{9,11},{10,... | collective-permute-start | bytes 786440 | tf_op jit(solution)/shard_map/ppermute | solution.py:18
  43.0 12.3 %collective-permute-start.11 = (bf16[2,64,1024]{2,1,0:T(8,128)(2,1)S(1)}, bf16[2,64,1024]{2,1,0:T(8,128)(2,1)S(1)}, u32[]{:S(2)}, u32[]{:S(2)}) collective-permute-start(bf16[2,64,1024]{2,1,0:T(8,128)(2,1)S(1)} %get-tuple-element.94), channel_id=1, source_target_pairs={{0,6},{1,7},{2,4},{3,5},{4,2},{5,3},{6,0},{7,1},{8,14},{9,15},{10,... | collective-permute-start | bytes 786440 | tf_op jit(solution)/shard_map/ppermute | solution.py:18
  46.3 12.1 %collective-permute-start.12 = (bf16[2,64,1024]{2,1,0:T(8,128)(2,1)S(1)}, bf16[2,64,1024]{2,1,0:T(8,128)(2,1)S(1)}, u32[]{:S(2)}, u32[]{:S(2)}) collective-permute-start(bf16[2,64,1024]{2,1,0:T(8,128)(2,1)S(1)} %image_x_a.1.refs_0_.refs_1_), channel_id=1, source_target_pairs={{0,1},{1,0},{2,3},{3,2},{4,5},{5,4},{6,7},{7,6},{8,9},{9,8},{10,11... | collective-permute-start | bytes 786440 | tf_op jit(solution)/shard_map/ppermute | solution.py:18
  50.8 18.2 %collective-permute-start.19 = (bf16[2,128,1024]{2,1,0:T(8,128)(2,1)S(1)}, bf16[2,128,1024]{2,1,0:T(8,128)(2,1)S(1)}, u32[]{:S(2)}, u32[]{:S(2)}) collective-permute-start(bf16[2,128,1024]{2,1,0:T(8,128)(2,1)S(1)} %stack_text.1.refs_0_.refs_4_), channel_id=1, source_target_pairs={{0,96},{8,104},{16,112},{24,120},{32,64},{40,72},{48,80},{56,88},{... | collective-permute-start | bytes 1572872 | tf_op jit(solution)/shard_map/ppermute | solution.py:18
  55.3 13.7 %collective-permute-start.18 = (bf16[2,128,1024]{2,1,0:T(8,128)(2,1)S(1)}, bf16[2,128,1024]{2,1,0:T(8,128)(2,1)S(1)}, u32[]{:S(2)}, u32[]{:S(2)}) collective-permute-start(bf16[2,128,1024]{2,1,0:T(8,128)(2,1)S(1)} %stack_text.1.refs_0_.refs_4_), channel_id=1, source_target_pairs={{0,32},{8,40},{16,48},{24,56},{32,0},{40,8},{48,16},{56,24},{64,96... | collective-permute-start | bytes 1572872 | tf_op jit(solution)/shard_map/ppermute | solution.py:18
  63.5 10.3 %collective-permute-start.21 = (bf16[2,64,1024]{2,1,0:T(8,128)(2,1)S(1)}, bf16[2,64,1024]{2,1,0:T(8,128)(2,1)S(1)}, u32[]{:S(2)}, u32[]{:S(2)}) collective-permute-start(bf16[2,64,1024]{2,1,0:T(8,128)(2,1)S(1)} %get-tuple-element.96.refs_0_.refs_1_), channel_id=1, source_target_pairs={{0,6},{1,7},{2,4},{3,5},{4,2},{5,3},{6,0},{7,1},{8,14},{9,15},{10,... | collective-permute-start | bytes 786440 | tf_op jit(solution)/shard_map/ppermute | solution.py:18
  69.0 13.1 %collective-permute-start.25 = (bf16[128,1024]{1,0:T(8,128)(2,1)S(1)}, bf16[128,1024]{1,0:T(8,128)(2,1)S(1)}, u32[]{:S(2)}, u32[]{:S(2)}) collective-permute-start(bf16[128,1024]{1,0:T(8,128)(2,1)S(1)} %get-tuple-element.102), channel_id=1, source_target_pairs={{0,32},{8,40},{16,48},{24,56},{32,0},{40,8},{48,16},{56,24},{64,96... | collective-permute-start | bytes 786440 | tf_op jit(solution)/shard_map/ppermute | solution.py:18
  71.0 11.1 %collective-permute-start.24 = (bf16[128,1024]{1,0:T(8,128)(2,1)S(1)}, bf16[128,1024]{1,0:T(8,128)(2,1)S(1)}, u32[]{:S(2)}, u32[]{:S(2)}) collective-permute-start(bf16[128,1024]{1,0:T(8,128)(2,1)S(1)} %get-tuple-element.99.refs_0_), channel_id=1, source_target_pairs={{0,96},{8,104},{16,112},{24,120},{32,64},{40,72},{48,80},{56,88},{... | collective-permute-start | bytes 786440 | tf_op jit(solution)/shard_map/ppermute | solution.py:18
  94.8 10.2 %collective-permute-start.29 = (bf16[128,1024]{1,0:T(8,128)(2,1)S(1)}, bf16[128,1024]{1,0:T(8,128)(2,1)S(1)}, u32[]{:S(2)}, u32[]{:S(2)}) collective-permute-start(bf16[128,1024]{1,0:T(8,128)(2,1)S(1)} %get-tuple-element.112), channel_id=1, source_target_pairs={{0,2},{1,3},{2,0},{3,1},{4,6},{5,7},{6,4},{7,5},{8,10},{9,11},{10,... | collective-permute-start | bytes 786440 | tf_op jit(solution)/shard_map/ppermute | solution.py:18
  94.9 10.1 %collective-permute-start.28 = (bf16[128,1024]{1,0:T(8,128)(2,1)S(1)}, bf16[128,1024]{1,0:T(8,128)(2,1)S(1)}, u32[]{:S(2)}, u32[]{:S(2)}) collective-permute-start(bf16[128,1024]{1,0:T(8,128)(2,1)S(1)} %get-tuple-element.107.refs_0_), channel_id=1, source_target_pairs={{0,6},{1,7},{2,4},{3,5},{4,2},{5,3},{6,0},{7,1},{8,14},{9,15},{10,... | collective-permute-start | bytes 786440 | tf_op jit(solution)/shard_map/ppermute | solution.py:18
  110.3 12.4 %collective-permute-start.36 = (bf16[2,128,1024]{2,1,0:T(8,128)(2,1)S(1)}, bf16[2,128,1024]{2,1,0:T(8,128)(2,1)S(1)}, u32[]{:S(2)}, u32[]{:S(2)}) collective-permute-start(bf16[2,128,1024]{2,1,0:T(8,128)(2,1)S(1)} %get-tuple-element.120), channel_id=1, source_target_pairs={{0,32},{8,40},{16,48},{24,56},{32,0},{40,8},{48,16},{56,24},{64,96... | collective-permute-start | bytes 1572872 | tf_op jit(solution)/shard_map/ppermute | solution.py:18
  110.4 13.7 %collective-permute-start.37 = (bf16[2,128,1024]{2,1,0:T(8,128)(2,1)S(1)}, bf16[2,128,1024]{2,1,0:T(8,128)(2,1)S(1)}, u32[]{:S(2)}, u32[]{:S(2)}) collective-permute-start(bf16[2,128,1024]{2,1,0:T(8,128)(2,1)S(1)} %get-tuple-element.121), channel_id=1, source_target_pairs={{0,96},{8,104},{16,112},{24,120},{32,64},{40,72},{48,80},{56,88},{... | collective-permute-start | bytes 1572872 | tf_op jit(solution)/shard_map/ppermute | solution.py:18
  124.7 13.8 %collective-permute-start.40 = (bf16[2,64,1024]{2,1,0:T(8,128)(2,1)S(1)}, bf16[2,64,1024]{2,1,0:T(8,128)(2,1)S(1)}, u32[]{:S(2)}, u32[]{:S(2)}) collective-permute-start(bf16[2,64,1024]{2,1,0:T(8,128)(2,1)S(1)} %image_grads_x_b.1.refs_0_.refs_1_), channel_id=1, source_target_pairs={{0,1},{1,0},{2,3},{3,2},{4,5},{5,4},{6,7},{7,6},{8,9},{9,8},{10,11... | collective-permute-start | bytes 786440 | tf_op jit(solution)/shard_map/ppermute | solution.py:18
  126.4 14.3 %collective-permute-start.45 = (bf16[2,64,1024]{2,1,0:T(8,128)(2,1)S(1)}, bf16[2,64,1024]{2,1,0:T(8,128)(2,1)S(1)}, u32[]{:S(2)}, u32[]{:S(2)}) collective-permute-start(bf16[2,64,1024]{2,1,0:T(8,128)(2,1)S(1)} %image_back_a.1.refs_0_.refs_3_), channel_id=1, source_target_pairs={{0,4},{1,5},{2,6},{3,7},{4,0},{5,1},{6,2},{7,3},{8,12},{9,13},{10,... | collective-permute-start | bytes 786440 | tf_op jit(solution)/shard_map/ppermute | solution.py:18
  128.7 14.7 %collective-permute-start.43 = (bf16[2,64,1024]{2,1,0:T(8,128)(2,1)S(1)}, bf16[2,64,1024]{2,1,0:T(8,128)(2,1)S(1)}, u32[]{:S(2)}, u32[]{:S(2)}) collective-permute-start(bf16[2,64,1024]{2,1,0:T(8,128)(2,1)S(1)} %image_back_a.1.refs_0_.refs_3_), channel_id=1, source_target_pairs={{0,6},{1,7},{2,4},{3,5},{4,2},{5,3},{6,0},{7,1},{8,14},{9,15},{10,... | collective-permute-start | bytes 786440 | tf_op jit(solution)/shard_map/ppermute | solution.py:18
  129.9 14.0 %collective-permute-start.41 = (bf16[2,64,1024]{2,1,0:T(8,128)(2,1)S(1)}, bf16[2,64,1024]{2,1,0:T(8,128)(2,1)S(1)}, u32[]{:S(2)}, u32[]{:S(2)}) collective-permute-start(bf16[2,64,1024]{2,1,0:T(8,128)(2,1)S(1)} %image_back_a.1.refs_0_.refs_3_), channel_id=1, source_target_pairs={{0,2},{1,3},{2,0},{3,1},{4,6},{5,7},{6,4},{7,5},{8,10},{9,11},{10,... | collective-permute-start | bytes 786440 | tf_op jit(solution)/shard_map/ppermute | solution.py:18
  133.8 10.1 %collective-permute-start.47 = (bf16[128,1024]{1,0:T(8,128)(2,1)S(1)}, bf16[128,1024]{1,0:T(8,128)(2,1)S(1)}, u32[]{:S(2)}, u32[]{:S(2)}) collective-permute-start(bf16[128,1024]{1,0:T(8,128)(2,1)S(1)} %text_back.1.refs_0_.refs_4_), channel_id=1, source_target_pairs={{0,1},{1,0},{2,3},{3,2},{4,5},{5,4},{6,7},{7,6},{8,9},{9,8},{10,11... | collective-permute-start | bytes 786440 | tf_op jit(solution)/shard_map/ppermute | solution.py:18
  138.7 10.9 %collective-permute-start.46 = (bf16[2,64,1024]{2,1,0:T(8,128)(2,1)S(1)}, bf16[2,64,1024]{2,1,0:T(8,128)(2,1)}, u32[]{:S(2)}, u32[]{:S(2)}) collective-permute-start(bf16[2,64,1024]{2,1,0:T(8,128)(2,1)S(1)} %image_back_b.1.refs_1_.refs_0_.refs_4_), channel_id=1, source_target_pairs={{0,4},{1,5},{2,6},{3,7},{4,0},{5,1},{6,2},{7,3},{8,12},{9,13},{10,... | collective-permute-start | bytes 786440 | tf_op jit(solution)/shard_map/ppermute | solution.py:18
  140.7 12.6 %collective-permute-start.44 = (bf16[2,64,1024]{2,1,0:T(8,128)(2,1)S(1)}, bf16[2,64,1024]{2,1,0:T(8,128)(2,1)}, u32[]{:S(2)}, u32[]{:S(2)}) collective-permute-start(bf16[2,64,1024]{2,1,0:T(8,128)(2,1)S(1)} %image_back_b.1.refs_1_.refs_0_.refs_4_), channel_id=1, source_target_pairs={{0,6},{1,7},{2,4},{3,5},{4,2},{5,3},{6,0},{7,1},{8,14},{9,15},{10,... | collective-permute-start | bytes 786440 | tf_op jit(solution)/shard_map/ppermute | solution.py:18
  143.4 11.1 %collective-permute-start.42 = (bf16[2,64,1024]{2,1,0:T(8,128)(2,1)S(1)}, bf16[2,64,1024]{2,1,0:T(8,128)(2,1)}, u32[]{:S(2)}, u32[]{:S(2)}) collective-permute-start(bf16[2,64,1024]{2,1,0:T(8,128)(2,1)S(1)} %image_back_b.1.refs_1_.refs_0_.refs_4_), channel_id=1, source_target_pairs={{0,2},{1,3},{2,0},{3,1},{4,6},{5,7},{6,4},{7,5},{8,10},{9,11},{10,... | collective-permute-start | bytes 786440 | tf_op jit(solution)/shard_map/ppermute | solution.py:18
  144.0 18.5 %collective-permute-start.49 = (bf16[2,128,1024]{2,1,0:T(8,128)(2,1)S(1)}, bf16[2,128,1024]{2,1,0:T(8,128)(2,1)}, u32[]{:S(2)}, u32[]{:S(2)}) collective-permute-start(bf16[2,128,1024]{2,1,0:T(8,128)(2,1)S(1)} %stack_text_grads.1.refs_0_.refs_3_), channel_id=1, source_target_pairs={{0,6},{1,7},{2,4},{3,5},{4,2},{5,3},{6,0},{7,1},{8,14},{9,15},{10,... | collective-permute-start | bytes 1572872 | tf_op jit(solution)/shard_map/ppermute | solution.py:18
  145.6 16.9 %collective-permute-start.48 = (bf16[2,128,1024]{2,1,0:T(8,128)(2,1)S(1)}, bf16[2,128,1024]{2,1,0:T(8,128)(2,1)}, u32[]{:S(2)}, u32[]{:S(2)}) collective-permute-start(bf16[2,128,1024]{2,1,0:T(8,128)(2,1)S(1)} %stack_text_grads.1.refs_0_.refs_3_), channel_id=1, source_target_pairs={{0,2},{1,3},{2,0},{3,1},{4,6},{5,7},{6,4},{7,5},{8,10},{9,11},{10,... | collective-permute-start | bytes 1572872 | tf_op jit(solution)/shard_map/ppermute | solution.py:18
  163.8 10.0 %collective-permute-start.50 = (bf16[128,1024]{1,0:T(8,128)(2,1)S(1)}, bf16[128,1024]{1,0:T(8,128)(2,1)S(1)}, u32[]{:S(2)}, u32[]{:S(2)}) collective-permute-start(bf16[128,1024]{1,0:T(8,128)(2,1)S(1)} %get-tuple-element.130), channel_id=1, source_target_pairs={{0,6},{1,7},{2,4},{3,5},{4,2},{5,3},{6,0},{7,1},{8,14},{9,15},{10,... | collective-permute-start | bytes 786440 | tf_op jit(solution)/shard_map/ppermute | solution.py:18
  176.5 11.8 %collective-permute-start.53 = (bf16[4,64,768]{2,1,0:T(8,128)(2,1)S(1)}, bf16[4,64,768]{2,1,0:T(8,128)(2,1)S(1)}, u32[]{:S(2)}, u32[]{:S(2)}) collective-permute-start(bf16[4,64,768]{2,1,0:T(8,128)(2,1)S(1)} %get-tuple-element.135), channel_id=1, source_target_pairs={{0,16},{8,24},{16,0},{24,8},{32,48},{40,56},{48,32},{56,40},{64,80... | collective-permute-start | bytes 1179656 | tf_op jit(solution)/shard_map/ppermute | solution.py:18
  178.8 11.7 %collective-permute-start.58 = (bf16[2,64,512]{2,1,0:T(8,128)(2,1)S(1)}, bf16[2,64,512]{2,1,0:T(8,128)(2,1)S(1)}, u32[]{:S(2)}, u32[]{:S(2)}) collective-permute-start(bf16[2,64,512]{2,1,0:T(8,128)(2,1)S(1)} %get-tuple-element.143), channel_id=1, source_target_pairs={{0,32},{8,40},{16,48},{24,56},{32,0},{40,8},{48,16},{56,24},{64,96... | collective-permute-start | bytes 393224 | tf_op jit(solution)/shard_map/ppermute | solution.py:18
  179.3 13.3 %collective-permute-start.59 = (bf16[2,64,512]{2,1,0:T(8,128)(2,1)S(1)}, bf16[2,64,512]{2,1,0:T(8,128)(2,1)S(1)}, u32[]{:S(2)}, u32[]{:S(2)}) collective-permute-start(bf16[2,64,512]{2,1,0:T(8,128)(2,1)S(1)} %get-tuple-element.144), channel_id=1, source_target_pairs={{0,96},{8,104},{16,112},{24,120},{32,64},{40,72},{48,80},{56,88},{... | collective-permute-start | bytes 393224 | tf_op jit(solution)/shard_map/ppermute | solution.py:18
  180.9 11.8 %collective-permute-start.60 = (bf16[2,64,512]{2,1,0:T(8,128)(2,1)S(1)}, bf16[2,64,512]{2,1,0:T(8,128)(2,1)S(1)}, u32[]{:S(2)}, u32[]{:S(2)}) collective-permute-start(bf16[2,64,512]{2,1,0:T(8,128)(2,1)S(1)} %get-tuple-element.145), channel_id=1, source_target_pairs={{0,64},{8,72},{16,80},{24,88},{32,96},{40,104},{48,112},{56,120},{... | collective-permute-start | bytes 393224 | tf_op jit(solution)/shard_map/ppermute | solution.py:18
  (37 other events, 301.8 us)

commit v6 on v5

--- a/solution.py
+++ b/solution.py
@@ -274,7 +274,7 @@
     return call(name, body, outs, (*flips, *texts), flops, 24, after)
 
 
-def weight_part(name, column, place, pieces, halves, feat, after):
+def weight_part(name, column, place, pieces, halves, feat, after, more=0):
     count, width = len(pieces), pieces[-1].shape[-1]
     rows, features = feat.shape
     own = rows // 8
@@ -307,7 +307,7 @@
         pltpu.VMEM((width, tile), BF16),
     ]
     outs = [shape(8, strip, features)] * 2
-    flops = 2 * rows * width * features
+    flops = 2 * rows * width * features + more
     return call(name, body, outs, (column, place, *pieces, feat), flops, 16, after, specs, scratch)
 
 
@@ -319,8 +319,7 @@
     tile = 256
 
     def body(column_ref, *refs):
-        weight_ref, out, mark = refs[count:]
-        mark[...] = jnp.zeros_like(mark)
+        weight_ref, out = refs[count:]
         def features_at(here):
             egrad = jnp.concatenate(near_far_order(grouped(refs[:count], halves)), axis=0)
             result = lax.dot_general(
@@ -333,8 +332,8 @@
         tiles(features // tile, tile, features_at)
 
     smem, vmem = pl.BlockSpec(memory_space=pltpu.SMEM), pl.BlockSpec(memory_space=pltpu.VMEM)
-    outs, ins = [shape(rows, features), shape(16, 128)], (column, *pieces, weight)
-    return call(name, body, outs, ins, 2 * rows * width * features, 16, None, [smem] + [vmem] * (len(pieces) + 1))
+    outs, ins = [shape(rows, features)], (column, *pieces, weight)
+    return call(name, body, outs, ins, 2 * rows * width * features, 16, None, [smem] + [vmem] * (len(pieces) + 1))[0]
 
 
 def chip_weight(name, same, other, after=None):
@@ -515,17 +514,20 @@
     d23, d67 = swap(d01, "mp", 2), swap(d01, "mp", 6)
 
     e_all = (e01_a, e01_b, e23_a, e23_b, e67_a, e67_b, e45_a, e45_b)
-    same, other = weight_part("weight_image", column, place, e_all, 2, img_feat, d01)
-    img_feat_grad, image_done = feature_grad("feature_image", column, e_all, 2, img_weight)
-    d2, d7 = call("cut_text_grads", cut, [shape(*one)] * 2, (d23, d67), ORDER_COST, after=(same, image_done))
+    same, other = weight_part("weight_image", column, place, e_all, 2, img_feat, d01, ORDER_COST // 4)
+    d2, d7 = call("cut_text_grads", cut, [shape(*one)] * 2, (d23, d67), ORDER_COST, after=same)
     d4, d5 = swap(d2, "mp", 6), swap(d7, "mp", 2)
     image_chip = chip_weight_y("weight_image_chip", same, other)
     img_weight_grad, image_y = sum_weight_y(*image_chip)
     d_all = (d01, d23, d67, d4, d5)
     same, other = weight_part("weight_text", column, place, d_all, 1, txt_feat, image_chip[0])
     txt_weight_grad = sum_weight(*chip_weight("weight_text_chip", same, other))
-    txt_feat_grad, _ = feature_grad("feature_text", column, d_all, 1, txt_weight)
-    return (img_feat_grad, txt_feat_grad, img_weight_grad, txt_weight_grad)
+    return (
+        feature_grad("feature_image", column, e_all, 2, img_weight),
+        feature_grad("feature_text", column, d_all, 1, txt_weight),
+        img_weight_grad,
+        txt_weight_grad,
+    )
 
 
 def solution(mesh):

time: 200 us -> 197 us (0.985)
  waiting for transfers between devices: 78.4 us -> 73.6 us
  Pallas kernels: 41.7 us -> 37.6 us
  starting transfers between devices: 74.7 us -> 78.2 us
    ppermute x62, waiting for transfers between devices: 78.4 us -> 73.6 us  [swap(): return lax.ppermute(value, axis, [(i, i ^ offset) for i in range(count)])]
    pallas_call x39, Pallas kernels: 32.6 us -> 28.5 us  [call(): pl.pallas_call(run, out_shape=outs, in_specs=specs, scratch_shapes=list(s...]
    ppermute x62, starting transfers between devices: 74.7 us -> 78.2 us  [swap(): return lax.ppermute(value, axis, [(i, i ^ offset) for i in range(count)])]
  transfers between devices with their start and end apart: 62 -> 62, of which waited for: 32 -> 30; matrix products, arithmetic and copies ran while one was open for 0% -> 0% of each run, Pallas kernels for 15% -> 14%
where the time goes in v6:
time: 197 us; the launch traced here: 196 us
  starting transfers between devices  78.2 us (40%)
  waiting for transfers between devices  73.6 us (37%)
  Pallas kernels  37.6 us (19%)
  local copies, waits for them, and re-layouts  3.87 us (2%)
  between operations  2.33 us (1%)
    ppermute x62, starting transfers between devices, swap(): return lax.ppermute(value, axis, [(i, i ^ offset) for i in range(count)])  78.2 us
    ppermute x62, waiting for transfers between devices, swap(): return lax.ppermute(value, axis, [(i, i ^ offset) for i in range(count)])  73.6 us
    pallas_call x39, Pallas kernels, call(): pl.pallas_call(run, out_shape=outs, in_specs=specs, scratch_shapes=list(s...  28.5 us
    pallas_call x2, Pallas kernels, pair_call(): pl.pallas_call(body, in_specs=[smem, smem] + [vmem] * len(arrays), out_sh...  9.11 us
  transfers between devices with their start and end apart: 62, of which 30 were waited for; matrix products, arithmetic and copies ran while one was open for 0% of the time, Pallas kernels for 14%

profile of v6, /device:TPU:8, one launch (start us, length us, event | category | flops | bytes accessed | tf_op | source)
XLA Modules:
  0.0 195.6 jit_solution(10354757083023083745)
XLA Ops:
  5.2 2.8 %collective-permute-start = (bf16[128,1024]{1,0:T(8,128)(2,1)S(1)}, bf16[128,1024]{1,0:T(8,128)(2,1)S(1)}, u32[]{:S(2)}, u32[]{:S(2)}) collective-permute-start(bf16[128,1024]{1,0:T(8,128)(2,1)S(1)} %get-tuple-element.76), channel_id=1, source_target_pairs={{0,6},{1,7},{2,4},{3,5},{4,2},{5,3},{6,0},{7,1},{8,14},{9,15},{10,... | collective-permute-start | bytes 786440 | tf_op jit(solution)/shard_map/ppermute | solution.py:18
  8.2 6.3 %collective-permute-done.r4 = bf16[128,1024]{1,0:T(8,128)(2,1)S(1)} collective-permute-done((bf16[128,1024]{1,0:T(8,128)(2,1)S(1)}, bf16[128,1024]{1,0:T(8,128)(2,1)S(1)}, u32[]{:S(2)}, u32[]{:S(2)}) %collective-permute-start) | collective-permute-done | bytes 262176 | tf_op jit(solution)/shard_map/ppermute | solution.py:18
  17.6 2.6 %embed_image.1 = (bf16[2,128,1024]{2,1,0:T(8,128)(2,1)S(1)}, bf16[2,128,1024]{2,1,0:T(8,128)(2,1)S(1)}, bf16[2,128,1024]{2,1,0:T(8,128)(2,1)S(1)}, bf16[128,1024]{1,0:T(8,128)(2,1)S(1)}, bf16[128,1024]{1,0:T(8,128)(2,1)S(1)}) custom-call(s32[1]{0:T(128)} %bitcast.column_ref.refs_1_, bf16[1024,768]{1,0:T(8,128)(2,1)S(1)} %copy-done.2, ...), custom_call_target="tpu_custom_call" | custom-call | flops 1610612736 | bytes 5242884 | tf_op jit(solution)/shard_map/embed_image/pallas_call | solution.py:36
  22.8 8.1 %collective-permute-done.2.t23 = bf16[2,128,1024]{2,1,0:T(8,128)(2,1)S(1)} collective-permute-done((bf16[2,128,1024]{2,1,0:T(8,128)(2,1)S(1)}, bf16[2,128,1024]{2,1,0:T(8,128)(2,1)S(1)}, u32[]{:S(2)}, u32[]{:S(2)}) %collective-permute-start.2) | collective-permute-done | bytes 524320 | tf_op jit(solution)/shard_map/ppermute | solution.py:18
  32.5 2.4 %collective-permute-start.6 = (bf16[128,1024]{1,0:T(8,128)(2,1)S(1)}, bf16[128,1024]{1,0:T(8,128)(2,1)S(1)}, u32[]{:S(2)}, u32[]{:S(2)}) collective-permute-start(bf16[128,1024]{1,0:T(8,128)(2,1)S(1)} %get-tuple-element.80.refs_0_), channel_id=1, source_target_pairs={{0,1},{1,0},{2,3},{3,2},{4,5},{5,4},{6,7},{7,6},{8,9},{9,8},{10,11... | collective-permute-start | bytes 786440 | tf_op jit(solution)/shard_map/ppermute | solution.py:18
  37.4 4.5 %collective-permute-done.6.refs_2_ = bf16[128,1024]{1,0:T(8,128)(2,1)S(1)} collective-permute-done((bf16[128,1024]{1,0:T(8,128)(2,1)S(1)}, bf16[128,1024]{1,0:T(8,128)(2,1)S(1)}, u32[]{:S(2)}, u32[]{:S(2)}) %collective-permute-start.6) | collective-permute-done | bytes 262176 | tf_op jit(solution)/shard_map/ppermute | solution.py:18
  46.3 2.4 %collective-permute-start.12 = (bf16[2,64,1024]{2,1,0:T(8,128)(2,1)S(1)}, bf16[2,64,1024]{2,1,0:T(8,128)(2,1)S(1)}, u32[]{:S(2)}, u32[]{:S(2)}) collective-permute-start(bf16[2,64,1024]{2,1,0:T(8,128)(2,1)S(1)} %image_x_a.1.refs_0_.refs_1_), channel_id=1, source_target_pairs={{0,1},{1,0},{2,3},{3,2},{4,5},{5,4},{6,7},{7,6},{8,9},{9,8},{10,11... | collective-permute-start | bytes 786440 | tf_op jit(solution)/shard_map/ppermute | solution.py:18
  50.8 4.5 %collective-permute-start.19 = (bf16[2,128,1024]{2,1,0:T(8,128)(2,1)S(1)}, bf16[2,128,1024]{2,1,0:T(8,128)(2,1)S(1)}, u32[]{:S(2)}, u32[]{:S(2)}) collective-permute-start(bf16[2,128,1024]{2,1,0:T(8,128)(2,1)S(1)} %stack_text.1.refs_0_.refs_4_), channel_id=1, source_target_pairs={{0,96},{8,104},{16,112},{24,120},{32,64},{40,72},{48,80},{56,88},{... | collective-permute-start | bytes 1572872 | tf_op jit(solution)/shard_map/ppermute | solution.py:18
  55.4 3.0 %collective-permute-start.13 = (bf16[2,64,1024]{2,1,0:T(8,128)(2,1)S(1)}, bf16[2,64,1024]{2,1,0:T(8,128)(2,1)S(1)}, u32[]{:S(2)}, u32[]{:S(2)}) collective-permute-start(bf16[2,64,1024]{2,1,0:T(8,128)(2,1)S(1)} %image_x_b.1.refs_0_.refs_1_), channel_id=1, source_target_pairs={{0,1},{1,0},{2,3},{3,2},{4,5},{5,4},{6,7},{7,6},{8,9},{9,8},{10,11... | collective-permute-start | bytes 786440 | tf_op jit(solution)/shard_map/ppermute | solution.py:18
  59.9 3.5 %collective-permute-done.13.refs_2_ = bf16[2,64,1024]{2,1,0:T(8,128)(2,1)S(1)} collective-permute-done((bf16[2,64,1024]{2,1,0:T(8,128)(2,1)S(1)}, bf16[2,64,1024]{2,1,0:T(8,128)(2,1)S(1)}, u32[]{:S(2)}, u32[]{:S(2)}) %collective-permute-start.13) | collective-permute-done | bytes 262176 | tf_op jit(solution)/shard_map/ppermute | solution.py:18
  64.5 2.3 %collective-permute-done.15.refs_2_.refs_4_ = bf16[2,64,1024]{2,1,0:T(8,128)(2,1)S(1)} collective-permute-done((bf16[2,64,1024]{2,1,0:T(8,128)(2,1)S(1)}, bf16[2,64,1024]{2,1,0:T(8,128)(2,1)S(1)}, u32[]{:S(2)}, u32[]{:S(2)}) %collective-permute-start.15) | collective-permute-done | bytes 262176 | tf_op jit(solution)/shard_map/ppermute | solution.py:18
  74.7 2.5 %collective-permute-start.22 = (bf16[64,1024]{1,0:T(8,128)(2,1)S(1)}, bf16[64,1024]{1,0:T(8,128)(2,1)S(1)}, u32[]{:S(2)}, u32[]{:S(2)}) collective-permute-start(bf16[64,1024]{1,0:T(8,128)(2,1)S(1)} %get-tuple-element.97), channel_id=1, source_target_pairs={{0,6},{1,7},{2,4},{3,5},{4,2},{5,3},{6,0},{7,1},{8,14},{9,15},{10,... | collective-permute-start | bytes 393224 | tf_op jit(solution)/shard_map/ppermute | solution.py:18
  77.1 2.8 %collective-permute-done.16.refs_0_.refs_6_ = bf16[64,1024]{1,0:T(8,128)(2,1)S(1)} collective-permute-done((bf16[64,1024]{1,0:T(8,128)(2,1)S(1)}, bf16[64,1024]{1,0:T(8,128)(2,1)S(1)}, u32[]{:S(2)}, u32[]{:S(2)}) %collective-permute-start.16) | collective-permute-done | bytes 131104 | tf_op jit(solution)/shard_map/ppermute | solution.py:18
  83.9 4.0 %pairs_even.1 = (bf16[1024,1024]{1,0:T(8,128)(2,1)S(1)}, bf16[1024,1024]{1,0:T(8,128)(2,1)S(1)}, bf16[1024,1024]{1,0:T(8,128)(2,1)S(1)}) custom-call(f32[1]{0:T(128)S(6)} %exp.3.scale_ref, f32[1]{0:T(128)S(6)} %copy.11.bias_ref, bf16[8,128,1024]{2,1,0:T(8,128)(2,1)S(1)} %collect.1.texts.refs_3_, bf16[2,64,1024]{2,1,0:T(8,128)(2,1)S(1)} %get-tuple-element.92.refs_0_, ...), custom_call_target="tpu_custom_call" | custom-call | flops 2147483648 | bytes 10485760 | tf_op jit(solution)/shard_map/pairs_even/pallas_call | solution.py:183
  87.8 5.2 %pairs_odd.1 = (bf16[1024,1024]{1,0:T(8,128)(2,1)S(1)}, bf16[8,128,1024]{2,1,0:T(8,128)(2,1)S(1)}) custom-call(f32[1]{0:T(128)S(6)} %exp.3.scale_ref, f32[1]{0:T(128)S(6)} %copy.11.bias_ref, bf16[8,128,1024]{2,1,0:T(8,128)(2,1)S(1)} %collective-permute-done.26.texts.refs_4_, bf16[1024,1024]{1,0:T(8,128)(2,1)S(1)} %get-tuple-element.100.image_all.refs_2_, ...), custom_call_target="tpu_custom_call" | custom-call | flops 4294967296 | bytes 10485760 | tf_op jit(solution)/shard_map/pairs_odd/pallas_call | solution.py:183
  96.2 2.5 %text_grads_even.1.even.refs_1_ = bf16[8,128,1024]{2,1,0:T(8,128)(2,1)S(1)} custom-call(bf16[128,1024]{1,0:T(8,128)(2,1)S(1)} %get-tuple-element.104.refs_0_, bf16[1024,1024]{1,0:T(8,128)(2,1)S(1)} %get-tuple-element.105.refs_1_, bf16[1024,1024]{1,0:T(8,128)(2,1)S(1)} %get-tuple-element.100.image_all.refs_2_), custom_call_target="tpu_custom_call" | custom-call | flops 2147483648 | bytes 6553600 | tf_op jit(solution)/shard_map/text_grads_even/pallas_call | solution.py:36
  101.4 3.6 %pairs_near_images.1 = (bf16[2,128,1024]{2,1,0:T(8,128)(2,1)S(1)}, bf16[2,128,1024]{2,1,0:T(8,128)(2,1)S(1)}, bf16[2,128,1024]{2,1,0:T(8,128)(2,1)S(1)}) custom-call(bf16[128,1024]{1,0:T(8,128)(2,1)S(1)} %get-tuple-element.106.refs_0_, bf16[1024,1024]{1,0:T(8,128)(2,1)S(1)} %get-tuple-element.101._.refs_1_, ...), custom_call_target="tpu_custom_call" | custom-call | flops 3221225472 | bytes 10223616 | tf_op jit(solution)/shard_map/pairs_near_images/pallas_call | solution.py:36
  112.5 3.2 %collective-permute-done.33.refs_3_ = bf16[2,64,1024]{2,1,0:T(8,128)(2,1)S(1)} collective-permute-done((bf16[2,64,1024]{2,1,0:T(8,128)(2,1)S(1)}, bf16[2,64,1024]{2,1,0:T(8,128)(2,1)S(1)}, u32[]{:S(2)}, u32[]{:S(2)}) %collective-permute-start.33) | collective-permute-done | bytes 262176 | tf_op jit(solution)/shard_map/ppermute | solution.py:18
  115.7 2.8 %collective-permute-start.37 = (bf16[2,128,1024]{2,1,0:T(8,128)(2,1)S(1)}, bf16[2,128,1024]{2,1,0:T(8,128)(2,1)S(1)}, u32[]{:S(2)}, u32[]{:S(2)}) collective-permute-start(bf16[2,128,1024]{2,1,0:T(8,128)(2,1)S(1)} %get-tuple-element.118), channel_id=1, source_target_pairs={{0,96},{8,104},{16,112},{24,120},{32,64},{40,72},{48,80},{56,88},{... | collective-permute-start | bytes 1572872 | tf_op jit(solution)/shard_map/ppermute | solution.py:18
  120.5 2.4 %collective-permute-done.36.refs_2_ = bf16[2,128,1024]{2,1,0:T(8,128)(2,1)S(1)} collective-permute-done((bf16[2,128,1024]{2,1,0:T(8,128)(2,1)S(1)}, bf16[2,128,1024]{2,1,0:T(8,128)(2,1)S(1)}, u32[]{:S(2)}, u32[]{:S(2)}) %collective-permute-start.36) | collective-permute-done | bytes 524320 | tf_op jit(solution)/shard_map/ppermute | solution.py:18
  123.0 4.2 %collective-permute-done.37.refs_3_ = bf16[2,128,1024]{2,1,0:T(8,128)(2,1)S(1)} collective-permute-done((bf16[2,128,1024]{2,1,0:T(8,128)(2,1)S(1)}, bf16[2,128,1024]{2,1,0:T(8,128)(2,1)S(1)}, u32[]{:S(2)}, u32[]{:S(2)}) %collective-permute-start.37) | collective-permute-done | bytes 524320 | tf_op jit(solution)/shard_map/ppermute | solution.py:18
  127.8 2.4 %collective-permute-start.40 = (bf16[2,64,1024]{2,1,0:T(8,128)(2,1)S(1)}, bf16[2,64,1024]{2,1,0:T(8,128)(2,1)S(1)}, u32[]{:S(2)}, u32[]{:S(2)}) collective-permute-start(bf16[2,64,1024]{2,1,0:T(8,128)(2,1)S(1)} %image_grads_x_b.1.refs_0_.refs_1_), channel_id=1, source_target_pairs={{0,1},{1,0},{2,3},{3,2},{4,5},{5,4},{6,7},{7,6},{8,9},{9,8},{10,11... | collective-permute-start | bytes 786440 | tf_op jit(solution)/shard_map/ppermute | solution.py:18
  135.4 3.3 %collective-permute-start.47 = (bf16[128,1024]{1,0:T(8,128)(2,1)S(1)}, bf16[128,1024]{1,0:T(8,128)(2,1)S(1)}, u32[]{:S(2)}, u32[]{:S(2)}) collective-permute-start(bf16[128,1024]{1,0:T(8,128)(2,1)S(1)} %text_back.1.refs_0_.refs_4_), channel_id=1, source_target_pairs={{0,1},{1,0},{2,3},{3,2},{4,5},{5,4},{6,7},{7,6},{8,9},{9,8},{10,11... | collective-permute-start | bytes 786440 | tf_op jit(solution)/shard_map/ppermute | solution.py:18
  144.0 3.2 %collective-permute-done.43.refs_4_.refs_2_.refs_7_ = bf16[2,64,1024]{2,1,0:T(8,128)(2,1)S(1)} collective-permute-done((bf16[2,64,1024]{2,1,0:T(8,128)(2,1)S(1)}, bf16[2,64,1024]{2,1,0:T(8,128)(2,1)S(1)}, u32[]{:S(2)}, u32[]{:S(2)}) %collective-permute-start.43) | collective-permute-done | bytes 262176 | tf_op jit(solution)/shard_map/ppermute | solution.py:18
  151.9 3.5 %collective-permute-done.44.refs_5_.refs_8_ = bf16[2,64,1024]{2,1,0:T(8,128)(2,1)S(1)} collective-permute-done((bf16[2,64,1024]{2,1,0:T(8,128)(2,1)S(1)}, bf16[2,64,1024]{2,1,0:T(8,128)(2,1)S(1)}, u32[]{:S(2)}, u32[]{:S(2)}) %collective-permute-start.44) | collective-permute-done | bytes 262176 | tf_op jit(solution)/shard_map/ppermute | solution.py:18
  158.4 3.1 %weight_image.1 = (bf16[8,64,768]{2,1,0:T(8,128)(2,1)S(1)}, bf16[8,64,768]{2,1,0:T(8,128)(2,1)S(1)}) custom-call(bf16[2,128,1024]{2,1,0:T(8,128)(2,1)S(1)} %stack_text_grads.1.refs_0_.refs_3_, s32[1]{0:T(128)} %bitcast.column_ref.refs_1_, s32[1]{0:T(128)} %bitcast.1.refs_2_, bf16[2,64,1024]{2,1,0:T(8,128)(2,1)S(1)} %image_back_a.1.refs_0_.refs_3_, ...), custom_call_target="tpu_custom_call" | custom-call | flops 4110612736 | bytes 5767176 | tf_op jit(solution)/shard_map/weight_image/pallas_call | solution.py:36
  165.6 6.0 %collective-permute-done.50.refs_3_.refs_6_ = bf16[128,1024]{1,0:T(8,128)(2,1)S(1)} collective-permute-done((bf16[128,1024]{1,0:T(8,128)(2,1)S(1)}, bf16[128,1024]{1,0:T(8,128)(2,1)S(1)}, u32[]{:S(2)}, u32[]{:S(2)}) %collective-permute-start.50) | collective-permute-done | bytes 262176 | tf_op jit(solution)/shard_map/ppermute | solution.py:18
  173.3 2.5 %collective-permute-start.53 = (bf16[4,64,768]{2,1,0:T(8,128)(2,1)S(1)}, bf16[4,64,768]{2,1,0:T(8,128)(2,1)S(1)}, u32[]{:S(2)}, u32[]{:S(2)}) collective-permute-start(bf16[4,64,768]{2,1,0:T(8,128)(2,1)S(1)} %get-tuple-element.129), channel_id=1, source_target_pairs={{0,16},{8,24},{16,0},{24,8},{32,48},{40,56},{48,32},{56,40},{64,80... | collective-permute-start | bytes 1179656 | tf_op jit(solution)/shard_map/ppermute | solution.py:18
  177.9 2.2 %collective-permute-start.60 = (bf16[2,64,512]{2,1,0:T(8,128)(2,1)S(1)}, bf16[2,64,512]{2,1,0:T(8,128)(2,1)S(1)}, u32[]{:S(2)}, u32[]{:S(2)}) collective-permute-start(bf16[2,64,512]{2,1,0:T(8,128)(2,1)S(1)} %get-tuple-element.139), channel_id=1, source_target_pairs={{0,64},{8,72},{16,80},{24,88},{32,96},{40,104},{48,112},{56,120},{... | collective-permute-start | bytes 393224 | tf_op jit(solution)/shard_map/ppermute | solution.py:18
  180.2 4.3 %feature_image.1 = bf16[1024,768]{1,0:T(8,128)(2,1)} custom-call(s32[1]{0:T(128)} %bitcast.column_ref.refs_1_, bf16[2,64,1024]{2,1,0:T(8,128)(2,1)S(1)} %image_back_a.1.refs_0_.refs_3_, bf16[2,64,1024]{2,1,0:T(8,128)(2,1)S(1)} %image_back_b.1.refs_1_.refs_0_.refs_4_, bf16[2,64,1024]{2,1,0:T(8,128)(2,1)S(1)} %collective-permute-done.41.refs_2_.refs_1_.refs_5_, ...), custom_call_target="tpu_custom_call" | custom-call | flops 1610612736 | bytes 5242884 | tf_op jit(solution)/shard_map/feature_image/pallas_call | solution.py:36
  187.6 2.2 %collective-permute-start.56 = (bf16[64,768]{1,0:T(8,128)(2,1)S(1)}, bf16[64,768]{1,0:T(8,128)(2,1)S(1)}, u32[]{:S(2)}, u32[]{:S(2)}) collective-permute-start(bf16[64,768]{1,0:T(8,128)(2,1)S(1)} %get-tuple-element.133), channel_id=1, source_target_pairs={{0,64},{8,72},{16,80},{24,88},{32,96},{40,104},{48,112},{56,120},{... | collective-permute-start | bytes 294920 | tf_op jit(solution)/shard_map/ppermute | solution.py:18
  191.8 2.5 %feature_text.1 = bf16[1024,512]{1,0:T(8,128)(2,1)} custom-call(s32[1]{0:T(128)} %bitcast.column_ref.refs_1_, bf16[2,128,1024]{2,1,0:T(8,128)(2,1)S(1)} %stack_text_grads.1.refs_0_.refs_3_, bf16[2,128,1024]{2,1,0:T(8,128)(2,1)S(1)} %collective-permute-done.48.refs_1_.refs_4_, bf16[2,128,1024]{2,1,0:T(8,128)(2,1)S(1)} %collective-permute-done.49.refs_2_.refs_5_, ...), custom_call_target="tpu_custom_call" | custom-call | flops 1073741824 | bytes 4194308 | tf_op jit(solution)/shard_map/feature_text/pallas_call | solution.py:36
  (149 shorter events, 82.5 us)
Async XLA Ops:
  15.9 14.9 %collective-permute-start.2 = (bf16[2,128,1024]{2,1,0:T(8,128)(2,1)S(1)}, bf16[2,128,1024]{2,1,0:T(8,128)(2,1)S(1)}, u32[]{:S(2)}, u32[]{:S(2)}) collective-permute-start(bf16[2,128,1024]{2,1,0:T(8,128)(2,1)S(1)} %get-tuple-element.78), channel_id=1, source_target_pairs={{0,2},{1,3},{2,0},{3,1},{4,6},{5,7},{6,4},{7,5},{8,10},{9,11},{10,... | collective-permute-start | bytes 1572872 | tf_op jit(solution)/shard_map/ppermute | solution.py:18
  16.3 16.1 %collective-permute-start.3 = (bf16[2,128,1024]{2,1,0:T(8,128)(2,1)S(1)}, bf16[2,128,1024]{2,1,0:T(8,128)(2,1)S(1)}, u32[]{:S(2)}, u32[]{:S(2)}) collective-permute-start(bf16[2,128,1024]{2,1,0:T(8,128)(2,1)S(1)} %get-tuple-element.79), channel_id=1, source_target_pairs={{0,6},{1,7},{2,4},{3,5},{4,2},{5,3},{6,0},{7,1},{8,14},{9,15},{10,... | collective-permute-start | bytes 1572872 | tf_op jit(solution)/shard_map/ppermute | solution.py:18
  20.2 15.1 %collective-permute-start.4 = (bf16[128,1024]{1,0:T(8,128)(2,1)S(1)}, bf16[128,1024]{1,0:T(8,128)(2,1)S(1)}, u32[]{:S(2)}, u32[]{:S(2)}) collective-permute-start(bf16[128,1024]{1,0:T(8,128)(2,1)S(1)} %get-tuple-element.83), channel_id=1, source_target_pairs={{0,6},{1,7},{2,4},{3,5},{4,2},{5,3},{6,0},{7,1},{8,14},{9,15},{10,... | collective-permute-start | bytes 786440 | tf_op jit(solution)/shard_map/ppermute | solution.py:18
  22.2 13.2 %collective-permute-start.5 = (bf16[128,1024]{1,0:T(8,128)(2,1)S(1)}, bf16[128,1024]{1,0:T(8,128)(2,1)S(1)}, u32[]{:S(2)}, u32[]{:S(2)}) collective-permute-start(bf16[128,1024]{1,0:T(8,128)(2,1)S(1)} %get-tuple-element.84), channel_id=1, source_target_pairs={{0,2},{1,3},{2,0},{3,1},{4,6},{5,7},{6,4},{7,5},{8,10},{9,11},{10,... | collective-permute-start | bytes 786440 | tf_op jit(solution)/shard_map/ppermute | solution.py:18
  43.0 12.3 %collective-permute-start.10 = (bf16[2,64,1024]{2,1,0:T(8,128)(2,1)S(1)}, bf16[2,64,1024]{2,1,0:T(8,128)(2,1)S(1)}, u32[]{:S(2)}, u32[]{:S(2)}) collective-permute-start(bf16[2,64,1024]{2,1,0:T(8,128)(2,1)S(1)} %get-tuple-element.90), channel_id=1, source_target_pairs={{0,2},{1,3},{2,0},{3,1},{4,6},{5,7},{6,4},{7,5},{8,10},{9,11},{10,... | collective-permute-start | bytes 786440 | tf_op jit(solution)/shard_map/ppermute | solution.py:18
  43.0 12.3 %collective-permute-start.11 = (bf16[2,64,1024]{2,1,0:T(8,128)(2,1)S(1)}, bf16[2,64,1024]{2,1,0:T(8,128)(2,1)S(1)}, u32[]{:S(2)}, u32[]{:S(2)}) collective-permute-start(bf16[2,64,1024]{2,1,0:T(8,128)(2,1)S(1)} %get-tuple-element.91), channel_id=1, source_target_pairs={{0,6},{1,7},{2,4},{3,5},{4,2},{5,3},{6,0},{7,1},{8,14},{9,15},{10,... | collective-permute-start | bytes 786440 | tf_op jit(solution)/shard_map/ppermute | solution.py:18
  46.3 12.1 %collective-permute-start.12 = (bf16[2,64,1024]{2,1,0:T(8,128)(2,1)S(1)}, bf16[2,64,1024]{2,1,0:T(8,128)(2,1)S(1)}, u32[]{:S(2)}, u32[]{:S(2)}) collective-permute-start(bf16[2,64,1024]{2,1,0:T(8,128)(2,1)S(1)} %image_x_a.1.refs_0_.refs_1_), channel_id=1, source_target_pairs={{0,1},{1,0},{2,3},{3,2},{4,5},{5,4},{6,7},{7,6},{8,9},{9,8},{10,11... | collective-permute-start | bytes 786440 | tf_op jit(solution)/shard_map/ppermute | solution.py:18
  50.8 18.2 %collective-permute-start.19 = (bf16[2,128,1024]{2,1,0:T(8,128)(2,1)S(1)}, bf16[2,128,1024]{2,1,0:T(8,128)(2,1)S(1)}, u32[]{:S(2)}, u32[]{:S(2)}) collective-permute-start(bf16[2,128,1024]{2,1,0:T(8,128)(2,1)S(1)} %stack_text.1.refs_0_.refs_4_), channel_id=1, source_target_pairs={{0,96},{8,104},{16,112},{24,120},{32,64},{40,72},{48,80},{56,88},{... | collective-permute-start | bytes 1572872 | tf_op jit(solution)/shard_map/ppermute | solution.py:18
  55.3 13.7 %collective-permute-start.18 = (bf16[2,128,1024]{2,1,0:T(8,128)(2,1)S(1)}, bf16[2,128,1024]{2,1,0:T(8,128)(2,1)S(1)}, u32[]{:S(2)}, u32[]{:S(2)}) collective-permute-start(bf16[2,128,1024]{2,1,0:T(8,128)(2,1)S(1)} %stack_text.1.refs_0_.refs_4_), channel_id=1, source_target_pairs={{0,32},{8,40},{16,48},{24,56},{32,0},{40,8},{48,16},{56,24},{64,96... | collective-permute-start | bytes 1572872 | tf_op jit(solution)/shard_map/ppermute | solution.py:18
  63.5 10.3 %collective-permute-start.21 = (bf16[2,64,1024]{2,1,0:T(8,128)(2,1)S(1)}, bf16[2,64,1024]{2,1,0:T(8,128)(2,1)S(1)}, u32[]{:S(2)}, u32[]{:S(2)}) collective-permute-start(bf16[2,64,1024]{2,1,0:T(8,128)(2,1)S(1)} %get-tuple-element.93.refs_0_.refs_1_), channel_id=1, source_target_pairs={{0,6},{1,7},{2,4},{3,5},{4,2},{5,3},{6,0},{7,1},{8,14},{9,15},{10,... | collective-permute-start | bytes 786440 | tf_op jit(solution)/shard_map/ppermute | solution.py:18
  69.0 13.1 %collective-permute-start.25 = (bf16[128,1024]{1,0:T(8,128)(2,1)S(1)}, bf16[128,1024]{1,0:T(8,128)(2,1)S(1)}, u32[]{:S(2)}, u32[]{:S(2)}) collective-permute-start(bf16[128,1024]{1,0:T(8,128)(2,1)S(1)} %get-tuple-element.99), channel_id=1, source_target_pairs={{0,32},{8,40},{16,48},{24,56},{32,0},{40,8},{48,16},{56,24},{64,96... | collective-permute-start | bytes 786440 | tf_op jit(solution)/shard_map/ppermute | solution.py:18
  71.0 11.1 %collective-permute-start.24 = (bf16[128,1024]{1,0:T(8,128)(2,1)S(1)}, bf16[128,1024]{1,0:T(8,128)(2,1)S(1)}, u32[]{:S(2)}, u32[]{:S(2)}) collective-permute-start(bf16[128,1024]{1,0:T(8,128)(2,1)S(1)} %get-tuple-element.96.refs_0_), channel_id=1, source_target_pairs={{0,96},{8,104},{16,112},{24,120},{32,64},{40,72},{48,80},{56,88},{... | collective-permute-start | bytes 786440 | tf_op jit(solution)/shard_map/ppermute | solution.py:18
  105.2 10.5 %collective-permute-start.33 = (bf16[2,64,1024]{2,1,0:T(8,128)(2,1)S(1)}, bf16[2,64,1024]{2,1,0:T(8,128)(2,1)S(1)}, u32[]{:S(2)}, u32[]{:S(2)}) collective-permute-start(bf16[2,64,1024]{2,1,0:T(8,128)(2,1)S(1)} %get-tuple-element.114), channel_id=1, source_target_pairs={{0,6},{1,7},{2,4},{3,5},{4,2},{5,3},{6,0},{7,1},{8,14},{9,15},{10,... | collective-permute-start | bytes 786440 | tf_op jit(solution)/shard_map/ppermute | solution.py:18
  106.9 11.7 %collective-permute-start.32 = (bf16[2,64,1024]{2,1,0:T(8,128)(2,1)S(1)}, bf16[2,64,1024]{2,1,0:T(8,128)(2,1)S(1)}, u32[]{:S(2)}, u32[]{:S(2)}) collective-permute-start(bf16[2,64,1024]{2,1,0:T(8,128)(2,1)S(1)} %get-tuple-element.110.refs_0_), channel_id=1, source_target_pairs={{0,2},{1,3},{2,0},{3,1},{4,6},{5,7},{6,4},{7,5},{8,10},{9,11},{10,... | collective-permute-start | bytes 786440 | tf_op jit(solution)/shard_map/ppermute | solution.py:18
  107.6 12.8 %collective-permute-start.34 = (bf16[2,64,1024]{2,1,0:T(8,128)(2,1)S(1)}, bf16[2,64,1024]{2,1,0:T(8,128)(2,1)S(1)}, u32[]{:S(2)}, u32[]{:S(2)}) collective-permute-start(bf16[2,64,1024]{2,1,0:T(8,128)(2,1)S(1)} %get-tuple-element.115), channel_id=1, source_target_pairs={{0,2},{1,3},{2,0},{3,1},{4,6},{5,7},{6,4},{7,5},{8,10},{9,11},{10,... | collective-permute-start | bytes 786440 | tf_op jit(solution)/shard_map/ppermute | solution.py:18
  108.9 11.5 %collective-permute-start.35 = (bf16[2,64,1024]{2,1,0:T(8,128)(2,1)S(1)}, bf16[2,64,1024]{2,1,0:T(8,128)(2,1)S(1)}, u32[]{:S(2)}, u32[]{:S(2)}) collective-permute-start(bf16[2,64,1024]{2,1,0:T(8,128)(2,1)S(1)} %get-tuple-element.116), channel_id=1, source_target_pairs={{0,6},{1,7},{2,4},{3,5},{4,2},{5,3},{6,0},{7,1},{8,14},{9,15},{10,... | collective-permute-start | bytes 786440 | tf_op jit(solution)/shard_map/ppermute | solution.py:18
  111.0 12.0 %collective-permute-start.36 = (bf16[2,128,1024]{2,1,0:T(8,128)(2,1)S(1)}, bf16[2,128,1024]{2,1,0:T(8,128)(2,1)S(1)}, u32[]{:S(2)}, u32[]{:S(2)}) collective-permute-start(bf16[2,128,1024]{2,1,0:T(8,128)(2,1)S(1)} %get-tuple-element.117), channel_id=1, source_target_pairs={{0,32},{8,40},{16,48},{24,56},{32,0},{40,8},{48,16},{56,24},{64,96... | collective-permute-start | bytes 1572872 | tf_op jit(solution)/shard_map/ppermute | solution.py:18
  115.7 11.4 %collective-permute-start.37 = (bf16[2,128,1024]{2,1,0:T(8,128)(2,1)S(1)}, bf16[2,128,1024]{2,1,0:T(8,128)(2,1)S(1)}, u32[]{:S(2)}, u32[]{:S(2)}) collective-permute-start(bf16[2,128,1024]{2,1,0:T(8,128)(2,1)S(1)} %get-tuple-element.118), channel_id=1, source_target_pairs={{0,96},{8,104},{16,112},{24,120},{32,64},{40,72},{48,80},{56,88},{... | collective-permute-start | bytes 1572872 | tf_op jit(solution)/shard_map/ppermute | solution.py:18
  118.6 11.6 %collective-permute-start.38 = (bf16[2,64,1024]{2,1,0:T(8,128)(2,1)S(1)}, bf16[2,64,1024]{2,1,0:T(8,128)(2,1)S(1)}, u32[]{:S(2)}, u32[]{:S(2)}) collective-permute-start(bf16[2,64,1024]{2,1,0:T(8,128)(2,1)S(1)} %image_grads_x_a.1.refs_0_.refs_1_), channel_id=1, source_target_pairs={{0,1},{1,0},{2,3},{3,2},{4,5},{5,4},{6,7},{7,6},{8,9},{9,8},{10,11... | collective-permute-start | bytes 786440 | tf_op jit(solution)/shard_map/ppermute | solution.py:18
  127.8 13.1 %collective-permute-start.40 = (bf16[2,64,1024]{2,1,0:T(8,128)(2,1)S(1)}, bf16[2,64,1024]{2,1,0:T(8,128)(2,1)S(1)}, u32[]{:S(2)}, u32[]{:S(2)}) collective-permute-start(bf16[2,64,1024]{2,1,0:T(8,128)(2,1)S(1)} %image_grads_x_b.1.refs_0_.refs_1_), channel_id=1, source_target_pairs={{0,1},{1,0},{2,3},{3,2},{4,5},{5,4},{6,7},{7,6},{8,9},{9,8},{10,11... | collective-permute-start | bytes 786440 | tf_op jit(solution)/shard_map/ppermute | solution.py:18
  130.5 12.3 %collective-permute-start.45 = (bf16[2,64,1024]{2,1,0:T(8,128)(2,1)S(1)}, bf16[2,64,1024]{2,1,0:T(8,128)(2,1)S(1)}, u32[]{:S(2)}, u32[]{:S(2)}) collective-permute-start(bf16[2,64,1024]{2,1,0:T(8,128)(2,1)S(1)} %image_back_a.1.refs_0_.refs_3_), channel_id=1, source_target_pairs={{0,4},{1,5},{2,6},{3,7},{4,0},{5,1},{6,2},{7,3},{8,12},{9,13},{10,... | collective-permute-start | bytes 786440 | tf_op jit(solution)/shard_map/ppermute | solution.py:18
  131.2 16.0 %collective-permute-start.43 = (bf16[2,64,1024]{2,1,0:T(8,128)(2,1)S(1)}, bf16[2,64,1024]{2,1,0:T(8,128)(2,1)S(1)}, u32[]{:S(2)}, u32[]{:S(2)}) collective-permute-start(bf16[2,64,1024]{2,1,0:T(8,128)(2,1)S(1)} %image_back_a.1.refs_0_.refs_3_), channel_id=1, source_target_pairs={{0,6},{1,7},{2,4},{3,5},{4,2},{5,3},{6,0},{7,1},{8,14},{9,15},{10,... | collective-permute-start | bytes 786440 | tf_op jit(solution)/shard_map/ppermute | solution.py:18
  132.8 14.4 %collective-permute-start.41 = (bf16[2,64,1024]{2,1,0:T(8,128)(2,1)S(1)}, bf16[2,64,1024]{2,1,0:T(8,128)(2,1)S(1)}, u32[]{:S(2)}, u32[]{:S(2)}) collective-permute-start(bf16[2,64,1024]{2,1,0:T(8,128)(2,1)S(1)} %image_back_a.1.refs_0_.refs_3_), channel_id=1, source_target_pairs={{0,2},{1,3},{2,0},{3,1},{4,6},{5,7},{6,4},{7,5},{8,10},{9,11},{10,... | collective-permute-start | bytes 786440 | tf_op jit(solution)/shard_map/ppermute | solution.py:18
  135.4 11.8 %collective-permute-start.47 = (bf16[128,1024]{1,0:T(8,128)(2,1)S(1)}, bf16[128,1024]{1,0:T(8,128)(2,1)S(1)}, u32[]{:S(2)}, u32[]{:S(2)}) collective-permute-start(bf16[128,1024]{1,0:T(8,128)(2,1)S(1)} %text_back.1.refs_0_.refs_4_), channel_id=1, source_target_pairs={{0,1},{1,0},{2,3},{3,2},{4,5},{5,4},{6,7},{7,6},{8,9},{9,8},{10,11... | collective-permute-start | bytes 786440 | tf_op jit(solution)/shard_map/ppermute | solution.py:18
  141.1 10.8 %collective-permute-start.46 = (bf16[2,64,1024]{2,1,0:T(8,128)(2,1)S(1)}, bf16[2,64,1024]{2,1,0:T(8,128)(2,1)S(1)}, u32[]{:S(2)}, u32[]{:S(2)}) collective-permute-start(bf16[2,64,1024]{2,1,0:T(8,128)(2,1)S(1)} %image_back_b.1.refs_1_.refs_0_.refs_4_), channel_id=1, source_target_pairs={{0,4},{1,5},{2,6},{3,7},{4,0},{5,1},{6,2},{7,3},{8,12},{9,13},{10,... | collective-permute-start | bytes 786440 | tf_op jit(solution)/shard_map/ppermute | solution.py:18
  142.8 12.7 %collective-permute-start.44 = (bf16[2,64,1024]{2,1,0:T(8,128)(2,1)S(1)}, bf16[2,64,1024]{2,1,0:T(8,128)(2,1)S(1)}, u32[]{:S(2)}, u32[]{:S(2)}) collective-permute-start(bf16[2,64,1024]{2,1,0:T(8,128)(2,1)S(1)} %image_back_b.1.refs_1_.refs_0_.refs_4_), channel_id=1, source_target_pairs={{0,6},{1,7},{2,4},{3,5},{4,2},{5,3},{6,0},{7,1},{8,14},{9,15},{10,... | collective-permute-start | bytes 786440 | tf_op jit(solution)/shard_map/ppermute | solution.py:18
  147.2 16.5 %collective-permute-start.49 = (bf16[2,128,1024]{2,1,0:T(8,128)(2,1)S(1)}, bf16[2,128,1024]{2,1,0:T(8,128)(2,1)S(1)}, u32[]{:S(2)}, u32[]{:S(2)}) collective-permute-start(bf16[2,128,1024]{2,1,0:T(8,128)(2,1)S(1)} %stack_text_grads.1.refs_0_.refs_3_), channel_id=1, source_target_pairs={{0,6},{1,7},{2,4},{3,5},{4,2},{5,3},{6,0},{7,1},{8,14},{9,15},{10,... | collective-permute-start | bytes 1572872 | tf_op jit(solution)/shard_map/ppermute | solution.py:18
  148.5 15.2 %collective-permute-start.48 = (bf16[2,128,1024]{2,1,0:T(8,128)(2,1)S(1)}, bf16[2,128,1024]{2,1,0:T(8,128)(2,1)S(1)}, u32[]{:S(2)}, u32[]{:S(2)}) collective-permute-start(bf16[2,128,1024]{2,1,0:T(8,128)(2,1)S(1)} %stack_text_grads.1.refs_0_.refs_3_), channel_id=1, source_target_pairs={{0,2},{1,3},{2,0},{3,1},{4,6},{5,7},{6,4},{7,5},{8,10},{9,11},{10,... | collective-permute-start | bytes 1572872 | tf_op jit(solution)/shard_map/ppermute | solution.py:18
  173.3 12.2 %collective-permute-start.53 = (bf16[4,64,768]{2,1,0:T(8,128)(2,1)S(1)}, bf16[4,64,768]{2,1,0:T(8,128)(2,1)S(1)}, u32[]{:S(2)}, u32[]{:S(2)}) collective-permute-start(bf16[4,64,768]{2,1,0:T(8,128)(2,1)S(1)} %get-tuple-element.129), channel_id=1, source_target_pairs={{0,16},{8,24},{16,0},{24,8},{32,48},{40,56},{48,32},{56,40},{64,80... | collective-permute-start | bytes 1179656 | tf_op jit(solution)/shard_map/ppermute | solution.py:18
  176.0 11.6 %collective-permute-start.58 = (bf16[2,64,512]{2,1,0:T(8,128)(2,1)S(1)}, bf16[2,64,512]{2,1,0:T(8,128)(2,1)S(1)}, u32[]{:S(2)}, u32[]{:S(2)}) collective-permute-start(bf16[2,64,512]{2,1,0:T(8,128)(2,1)S(1)} %get-tuple-element.137), channel_id=1, source_target_pairs={{0,32},{8,40},{16,48},{24,56},{32,0},{40,8},{48,16},{56,24},{64,96... | collective-permute-start | bytes 393224 | tf_op jit(solution)/shard_map/ppermute | solution.py:18
  176.1 13.7 %collective-permute-start.59 = (bf16[2,64,512]{2,1,0:T(8,128)(2,1)S(1)}, bf16[2,64,512]{2,1,0:T(8,128)(2,1)S(1)}, u32[]{:S(2)}, u32[]{:S(2)}) collective-permute-start(bf16[2,64,512]{2,1,0:T(8,128)(2,1)S(1)} %get-tuple-element.138), channel_id=1, source_target_pairs={{0,96},{8,104},{16,112},{24,120},{32,64},{40,72},{48,80},{56,88},{... | collective-permute-start | bytes 393224 | tf_op jit(solution)/shard_map/ppermute | solution.py:18
  177.9 11.9 %collective-permute-start.60 = (bf16[2,64,512]{2,1,0:T(8,128)(2,1)S(1)}, bf16[2,64,512]{2,1,0:T(8,128)(2,1)S(1)}, u32[]{:S(2)}, u32[]{:S(2)}) collective-permute-start(bf16[2,64,512]{2,1,0:T(8,128)(2,1)S(1)} %get-tuple-element.139), channel_id=1, source_target_pairs={{0,64},{8,72},{16,80},{24,88},{32,96},{40,104},{48,112},{56,120},{... | collective-permute-start | bytes 393224 | tf_op jit(solution)/shard_map/ppermute | solution.py:18
  (38 other events, 295.2 us)

commit v7 on v5

--- a/solution.py
+++ b/solution.py
@@ -274,7 +274,7 @@
     return call(name, body, outs, (*flips, *texts), flops, 24, after)
 
 
-def weight_part(name, column, place, pieces, halves, feat, after):
+def weight_part(name, column, place, pieces, halves, feat, after, more=0):
     count, width = len(pieces), pieces[-1].shape[-1]
     rows, features = feat.shape
     own = rows // 8
@@ -307,11 +307,11 @@
         pltpu.VMEM((width, tile), BF16),
     ]
     outs = [shape(8, strip, features)] * 2
-    flops = 2 * rows * width * features
+    flops = 2 * rows * width * features + more
     return call(name, body, outs, (column, place, *pieces, feat), flops, 16, after, specs, scratch)
 
 
-def feature_grad(name, column, pieces, halves, weight):
+def feature_grad(name, column, pieces, halves, weight, after=None):
     count, width = len(pieces), pieces[-1].shape[-1]
     features = weight.shape[0]
     own = pieces[0].shape[1] * halves
@@ -334,7 +334,7 @@
 
     smem, vmem = pl.BlockSpec(memory_space=pltpu.SMEM), pl.BlockSpec(memory_space=pltpu.VMEM)
     outs, ins = [shape(rows, features), shape(16, 128)], (column, *pieces, weight)
-    return call(name, body, outs, ins, 2 * rows * width * features, 16, None, [smem] + [vmem] * (len(pieces) + 1))
+    return call(name, body, outs, ins, 2 * rows * width * features, 16, after, [smem] + [vmem] * (len(pieces) + 1))
 
 
 def chip_weight(name, same, other, after=None):
@@ -391,7 +391,7 @@
         out[...] = p0[...] + wide(p4) + wide(p12) + wide(p8)
 
     outs = [shape(*one, dtype=F32)] + [shape(*one)] * 3
-    p0, p4, p12, p8 = call("weight_image_y", along_y, outs, (mine, swap(theirs, "blk", 2)))
+    p0, p4, p12, p8 = call("weight_image_y", along_y, outs, (mine, swap(theirs, "blk", 2)), ORDER_COST * 2 // 5)
     p4, p12, p8 = swap(p4, "blk", 4), swap(p12, "blk", 12), swap(p8, "blk", 8)
     return call("weight_image_z", along_z, outs[:1], (p0, p4, p12, p8))[0].T, p0
 
@@ -515,15 +515,15 @@
     d23, d67 = swap(d01, "mp", 2), swap(d01, "mp", 6)
 
     e_all = (e01_a, e01_b, e23_a, e23_b, e67_a, e67_b, e45_a, e45_b)
-    same, other = weight_part("weight_image", column, place, e_all, 2, img_feat, d01)
-    img_feat_grad, image_done = feature_grad("feature_image", column, e_all, 2, img_weight)
-    d2, d7 = call("cut_text_grads", cut, [shape(*one)] * 2, (d23, d67), ORDER_COST, after=(same, image_done))
+    same, other = weight_part("weight_image", column, place, e_all, 2, img_feat, d01, ORDER_COST // 4)
+    d2, d7 = call("cut_text_grads", cut, [shape(*one)] * 2, (d23, d67), ORDER_COST, after=same)
     d4, d5 = swap(d2, "mp", 6), swap(d7, "mp", 2)
     image_chip = chip_weight_y("weight_image_chip", same, other)
+    img_feat_grad, image_done = feature_grad("feature_image", column, e_all, 2, img_weight, image_chip[0])
     img_weight_grad, image_y = sum_weight_y(*image_chip)
     d_all = (d01, d23, d67, d4, d5)
-    same, other = weight_part("weight_text", column, place, d_all, 1, txt_feat, image_chip[0])
-    txt_weight_grad = sum_weight(*chip_weight("weight_text_chip", same, other))
+    same, other = weight_part("weight_text", column, place, d_all, 1, txt_feat, image_done)
+    txt_weight_grad = sum_weight(*chip_weight("weight_text_chip", same, other, image_y))
     txt_feat_grad, _ = feature_grad("feature_text", column, d_all, 1, txt_weight)
     return (img_feat_grad, txt_feat_grad, img_weight_grad, txt_weight_grad)
 

time: 200 us -> 197 us (0.985)
  waiting for transfers between devices: 78.4 us -> 72.1 us
  starting transfers between devices: 74.7 us -> 77.5 us
    ppermute x62, waiting for transfers between devices: 78.4 us -> 72.1 us  [swap(): return lax.ppermute(value, axis, [(i, i ^ offset) for i in range(count)])]
    ppermute x62, starting transfers between devices: 74.7 us -> 77.5 us  [swap(): return lax.ppermute(value, axis, [(i, i ^ offset) for i in range(count)])]
  transfers between devices with their start and end apart: 62 -> 62, of which waited for: 32 -> 31; matrix products, arithmetic and copies ran while one was open for 0% -> 0% of each run, Pallas kernels for 15% -> 17%
where the time goes in v7:
time: 197 us; the launch traced here: 196 us
  starting transfers between devices  77.5 us (39%)
  waiting for transfers between devices  72.1 us (37%)
  Pallas kernels  41.8 us (21%)
  local copies, waits for them, and re-layouts  2.47 us (1%)
  between operations  2.35 us (1%)
    ppermute x62, starting transfers between devices, swap(): return lax.ppermute(value, axis, [(i, i ^ offset) for i in range(count)])  77.5 us
    ppermute x62, waiting for transfers between devices, swap(): return lax.ppermute(value, axis, [(i, i ^ offset) for i in range(count)])  72.1 us
    pallas_call x39, Pallas kernels, call(): pl.pallas_call(run, out_shape=outs, in_specs=specs, scratch_shapes=list(s...  32.6 us
    pallas_call x2, Pallas kernels, pair_call(): pl.pallas_call(body, in_specs=[smem, smem] + [vmem] * len(arrays), out_sh...  9.11 us
  transfers between devices with their start and end apart: 62, of which 31 were waited for; matrix products, arithmetic and copies ran while one was open for 0% of the time, Pallas kernels for 17%

profile of v7, /device:TPU:8, one launch (start us, length us, event | category | flops | bytes accessed | tf_op | source)
XLA Modules:
  0.0 196.2 jit_solution(2628200261684416968)
XLA Ops:
  5.2 2.8 %collective-permute-start = (bf16[128,1024]{1,0:T(8,128)(2,1)S(1)}, bf16[128,1024]{1,0:T(8,128)(2,1)S(1)}, u32[]{:S(2)}, u32[]{:S(2)}) collective-permute-start(bf16[128,1024]{1,0:T(8,128)(2,1)S(1)} %get-tuple-element.79), channel_id=1, source_target_pairs={{0,6},{1,7},{2,4},{3,5},{4,2},{5,3},{6,0},{7,1},{8,14},{9,15},{10,... | collective-permute-start | bytes 786440 | tf_op jit(solution)/shard_map/ppermute | solution.py:18
  8.2 6.3 %collective-permute-done.r4 = bf16[128,1024]{1,0:T(8,128)(2,1)S(1)} collective-permute-done((bf16[128,1024]{1,0:T(8,128)(2,1)S(1)}, bf16[128,1024]{1,0:T(8,128)(2,1)S(1)}, u32[]{:S(2)}, u32[]{:S(2)}) %collective-permute-start) | collective-permute-done | bytes 262176 | tf_op jit(solution)/shard_map/ppermute | solution.py:18
  17.6 2.6 %embed_image.1 = (bf16[2,128,1024]{2,1,0:T(8,128)(2,1)S(1)}, bf16[2,128,1024]{2,1,0:T(8,128)(2,1)S(1)}, bf16[2,128,1024]{2,1,0:T(8,128)(2,1)S(1)}, bf16[128,1024]{1,0:T(8,128)(2,1)S(1)}, bf16[128,1024]{1,0:T(8,128)(2,1)S(1)}) custom-call(s32[1]{0:T(128)} %bitcast.column_ref.refs_1_, bf16[1024,768]{1,0:T(8,128)(2,1)S(1)} %copy-done, ...), custom_call_target="tpu_custom_call" | custom-call | flops 1610612736 | bytes 5242884 | tf_op jit(solution)/shard_map/embed_image/pallas_call | solution.py:36
  22.8 8.1 %collective-permute-done.2.t23 = bf16[2,128,1024]{2,1,0:T(8,128)(2,1)S(1)} collective-permute-done((bf16[2,128,1024]{2,1,0:T(8,128)(2,1)S(1)}, bf16[2,128,1024]{2,1,0:T(8,128)(2,1)S(1)}, u32[]{:S(2)}, u32[]{:S(2)}) %collective-permute-start.2) | collective-permute-done | bytes 524320 | tf_op jit(solution)/shard_map/ppermute | solution.py:18
  32.5 2.4 %collective-permute-start.6 = (bf16[128,1024]{1,0:T(8,128)(2,1)S(1)}, bf16[128,1024]{1,0:T(8,128)(2,1)S(1)}, u32[]{:S(2)}, u32[]{:S(2)}) collective-permute-start(bf16[128,1024]{1,0:T(8,128)(2,1)S(1)} %get-tuple-element.83.refs_0_), channel_id=1, source_target_pairs={{0,1},{1,0},{2,3},{3,2},{4,5},{5,4},{6,7},{7,6},{8,9},{9,8},{10,11... | collective-permute-start | bytes 786440 | tf_op jit(solution)/shard_map/ppermute | solution.py:18
  37.4 4.5 %collective-permute-done.6.refs_2_ = bf16[128,1024]{1,0:T(8,128)(2,1)S(1)} collective-permute-done((bf16[128,1024]{1,0:T(8,128)(2,1)S(1)}, bf16[128,1024]{1,0:T(8,128)(2,1)S(1)}, u32[]{:S(2)}, u32[]{:S(2)}) %collective-permute-start.6) | collective-permute-done | bytes 262176 | tf_op jit(solution)/shard_map/ppermute | solution.py:18
  46.3 2.4 %collective-permute-start.12 = (bf16[2,64,1024]{2,1,0:T(8,128)(2,1)S(1)}, bf16[2,64,1024]{2,1,0:T(8,128)(2,1)S(1)}, u32[]{:S(2)}, u32[]{:S(2)}) collective-permute-start(bf16[2,64,1024]{2,1,0:T(8,128)(2,1)S(1)} %image_x_a.1.refs_0_.refs_1_), channel_id=1, source_target_pairs={{0,1},{1,0},{2,3},{3,2},{4,5},{5,4},{6,7},{7,6},{8,9},{9,8},{10,11... | collective-permute-start | bytes 786440 | tf_op jit(solution)/shard_map/ppermute | solution.py:18
  50.8 4.5 %collective-permute-start.19 = (bf16[2,128,1024]{2,1,0:T(8,128)(2,1)S(1)}, bf16[2,128,1024]{2,1,0:T(8,128)(2,1)S(1)}, u32[]{:S(2)}, u32[]{:S(2)}) collective-permute-start(bf16[2,128,1024]{2,1,0:T(8,128)(2,1)S(1)} %stack_text.1.refs_0_.refs_4_), channel_id=1, source_target_pairs={{0,96},{8,104},{16,112},{24,120},{32,64},{40,72},{48,80},{56,88},{... | collective-permute-start | bytes 1572872 | tf_op jit(solution)/shard_map/ppermute | solution.py:18
  55.4 3.0 %collective-permute-start.13 = (bf16[2,64,1024]{2,1,0:T(8,128)(2,1)S(1)}, bf16[2,64,1024]{2,1,0:T(8,128)(2,1)S(1)}, u32[]{:S(2)}, u32[]{:S(2)}) collective-permute-start(bf16[2,64,1024]{2,1,0:T(8,128)(2,1)S(1)} %image_x_b.1.refs_0_.refs_1_), channel_id=1, source_target_pairs={{0,1},{1,0},{2,3},{3,2},{4,5},{5,4},{6,7},{7,6},{8,9},{9,8},{10,11... | collective-permute-start | bytes 786440 | tf_op jit(solution)/shard_map/ppermute | solution.py:18
  59.9 3.5 %collective-permute-done.13.refs_2_ = bf16[2,64,1024]{2,1,0:T(8,128)(2,1)S(1)} collective-permute-done((bf16[2,64,1024]{2,1,0:T(8,128)(2,1)S(1)}, bf16[2,64,1024]{2,1,0:T(8,128)(2,1)S(1)}, u32[]{:S(2)}, u32[]{:S(2)}) %collective-permute-start.13) | collective-permute-done | bytes 262176 | tf_op jit(solution)/shard_map/ppermute | solution.py:18
  64.5 2.3 %collective-permute-done.15.refs_2_.refs_4_ = bf16[2,64,1024]{2,1,0:T(8,128)(2,1)S(1)} collective-permute-done((bf16[2,64,1024]{2,1,0:T(8,128)(2,1)S(1)}, bf16[2,64,1024]{2,1,0:T(8,128)(2,1)S(1)}, u32[]{:S(2)}, u32[]{:S(2)}) %collective-permute-start.15) | collective-permute-done | bytes 262176 | tf_op jit(solution)/shard_map/ppermute | solution.py:18
  74.7 2.5 %collective-permute-start.22 = (bf16[64,1024]{1,0:T(8,128)(2,1)S(1)}, bf16[64,1024]{1,0:T(8,128)(2,1)S(1)}, u32[]{:S(2)}, u32[]{:S(2)}) collective-permute-start(bf16[64,1024]{1,0:T(8,128)(2,1)S(1)} %get-tuple-element.100), channel_id=1, source_target_pairs={{0,6},{1,7},{2,4},{3,5},{4,2},{5,3},{6,0},{7,1},{8,14},{9,15},{10,... | collective-permute-start | bytes 393224 | tf_op jit(solution)/shard_map/ppermute | solution.py:18
  77.1 2.8 %collective-permute-done.16.refs_0_.refs_6_ = bf16[64,1024]{1,0:T(8,128)(2,1)S(1)} collective-permute-done((bf16[64,1024]{1,0:T(8,128)(2,1)S(1)}, bf16[64,1024]{1,0:T(8,128)(2,1)S(1)}, u32[]{:S(2)}, u32[]{:S(2)}) %collective-permute-start.16) | collective-permute-done | bytes 131104 | tf_op jit(solution)/shard_map/ppermute | solution.py:18
  83.9 4.0 %pairs_even.1 = (bf16[1024,1024]{1,0:T(8,128)(2,1)S(1)}, bf16[1024,1024]{1,0:T(8,128)(2,1)S(1)}, bf16[1024,1024]{1,0:T(8,128)(2,1)S(1)}) custom-call(f32[1]{0:T(128)S(6)} %exp.3.scale_ref, f32[1]{0:T(128)S(6)} %copy.11.bias_ref, bf16[8,128,1024]{2,1,0:T(8,128)(2,1)S(1)} %collect.1.texts.refs_3_, bf16[2,64,1024]{2,1,0:T(8,128)(2,1)S(1)} %get-tuple-element.95.refs_0_, ...), custom_call_target="tpu_custom_call" | custom-call | flops 2147483648 | bytes 10485760 | tf_op jit(solution)/shard_map/pairs_even/pallas_call | solution.py:183
  87.8 5.2 %pairs_odd.1 = (bf16[1024,1024]{1,0:T(8,128)(2,1)S(1)}, bf16[8,128,1024]{2,1,0:T(8,128)(2,1)S(1)}) custom-call(f32[1]{0:T(128)S(6)} %exp.3.scale_ref, f32[1]{0:T(128)S(6)} %copy.11.bias_ref, bf16[8,128,1024]{2,1,0:T(8,128)(2,1)S(1)} %collective-permute-done.26.texts.refs_4_, bf16[1024,1024]{1,0:T(8,128)(2,1)S(1)} %get-tuple-element.103.image_all.refs_2_, ...), custom_call_target="tpu_custom_call" | custom-call | flops 4294967296 | bytes 10485760 | tf_op jit(solution)/shard_map/pairs_odd/pallas_call | solution.py:183
  96.2 2.5 %text_grads_even.1.even.refs_1_ = bf16[8,128,1024]{2,1,0:T(8,128)(2,1)S(1)} custom-call(bf16[128,1024]{1,0:T(8,128)(2,1)S(1)} %get-tuple-element.107.refs_0_, bf16[1024,1024]{1,0:T(8,128)(2,1)S(1)} %get-tuple-element.108.refs_1_, bf16[1024,1024]{1,0:T(8,128)(2,1)S(1)} %get-tuple-element.103.image_all.refs_2_), custom_call_target="tpu_custom_call" | custom-call | flops 2147483648 | bytes 6553600 | tf_op jit(solution)/shard_map/text_grads_even/pallas_call | solution.py:36
  101.4 3.6 %pairs_near_images.1 = (bf16[2,128,1024]{2,1,0:T(8,128)(2,1)S(1)}, bf16[2,128,1024]{2,1,0:T(8,128)(2,1)S(1)}, bf16[2,128,1024]{2,1,0:T(8,128)(2,1)S(1)}) custom-call(bf16[128,1024]{1,0:T(8,128)(2,1)S(1)} %get-tuple-element.109.refs_0_, bf16[1024,1024]{1,0:T(8,128)(2,1)S(1)} %get-tuple-element.104._.refs_1_, ...), custom_call_target="tpu_custom_call" | custom-call | flops 3221225472 | bytes 10223616 | tf_op jit(solution)/shard_map/pairs_near_images/pallas_call | solution.py:36
  112.5 3.2 %collective-permute-done.33.refs_3_ = bf16[2,64,1024]{2,1,0:T(8,128)(2,1)S(1)} collective-permute-done((bf16[2,64,1024]{2,1,0:T(8,128)(2,1)S(1)}, bf16[2,64,1024]{2,1,0:T(8,128)(2,1)S(1)}, u32[]{:S(2)}, u32[]{:S(2)}) %collective-permute-start.33) | collective-permute-done | bytes 262176 | tf_op jit(solution)/shard_map/ppermute | solution.py:18
  115.7 2.8 %collective-permute-start.37 = (bf16[2,128,1024]{2,1,0:T(8,128)(2,1)S(1)}, bf16[2,128,1024]{2,1,0:T(8,128)(2,1)S(1)}, u32[]{:S(2)}, u32[]{:S(2)}) collective-permute-start(bf16[2,128,1024]{2,1,0:T(8,128)(2,1)S(1)} %get-tuple-element.121), channel_id=1, source_target_pairs={{0,96},{8,104},{16,112},{24,120},{32,64},{40,72},{48,80},{56,88},{... | collective-permute-start | bytes 1572872 | tf_op jit(solution)/shard_map/ppermute | solution.py:18
  120.5 2.4 %collective-permute-done.36.refs_2_ = bf16[2,128,1024]{2,1,0:T(8,128)(2,1)S(1)} collective-permute-done((bf16[2,128,1024]{2,1,0:T(8,128)(2,1)S(1)}, bf16[2,128,1024]{2,1,0:T(8,128)(2,1)S(1)}, u32[]{:S(2)}, u32[]{:S(2)}) %collective-permute-start.36) | collective-permute-done | bytes 524320 | tf_op jit(solution)/shard_map/ppermute | solution.py:18
  123.0 4.2 %collective-permute-done.37.refs_3_ = bf16[2,128,1024]{2,1,0:T(8,128)(2,1)S(1)} collective-permute-done((bf16[2,128,1024]{2,1,0:T(8,128)(2,1)S(1)}, bf16[2,128,1024]{2,1,0:T(8,128)(2,1)S(1)}, u32[]{:S(2)}, u32[]{:S(2)}) %collective-permute-start.37) | collective-permute-done | bytes 524320 | tf_op jit(solution)/shard_map/ppermute | solution.py:18
  127.8 2.4 %collective-permute-start.40 = (bf16[2,64,1024]{2,1,0:T(8,128)(2,1)S(1)}, bf16[2,64,1024]{2,1,0:T(8,128)(2,1)S(1)}, u32[]{:S(2)}, u32[]{:S(2)}) collective-permute-start(bf16[2,64,1024]{2,1,0:T(8,128)(2,1)S(1)} %image_grads_x_b.1.refs_0_.refs_1_), channel_id=1, source_target_pairs={{0,1},{1,0},{2,3},{3,2},{4,5},{5,4},{6,7},{7,6},{8,9},{9,8},{10,11... | collective-permute-start | bytes 786440 | tf_op jit(solution)/shard_map/ppermute | solution.py:18
  135.4 3.3 %collective-permute-start.44 = (bf16[128,1024]{1,0:T(8,128)(2,1)S(1)}, bf16[128,1024]{1,0:T(8,128)(2,1)S(1)}, u32[]{:S(2)}, u32[]{:S(2)}) collective-permute-start(bf16[128,1024]{1,0:T(8,128)(2,1)S(1)} %text_back.1.refs_0_.refs_4_), channel_id=1, source_target_pairs={{0,1},{1,0},{2,3},{3,2},{4,5},{5,4},{6,7},{7,6},{8,9},{9,8},{10,11... | collective-permute-start | bytes 786440 | tf_op jit(solution)/shard_map/ppermute | solution.py:18
  144.0 3.1 %collective-permute-done.42.refs_2_.refs_7_.refs_6_ = bf16[2,64,1024]{2,1,0:T(8,128)(2,1)S(1)} collective-permute-done((bf16[2,64,1024]{2,1,0:T(8,128)(2,1)S(1)}, bf16[2,64,1024]{2,1,0:T(8,128)(2,1)S(1)}, u32[]{:S(2)}, u32[]{:S(2)}) %collective-permute-start.42) | collective-permute-done | bytes 262176 | tf_op jit(solution)/shard_map/ppermute | solution.py:18
  152.1 3.5 %collective-permute-done.46.refs_8_.refs_7_ = bf16[2,64,1024]{2,1,0:T(8,128)(2,1)} collective-permute-done((bf16[2,64,1024]{2,1,0:T(8,128)(2,1)S(1)}, bf16[2,64,1024]{2,1,0:T(8,128)(2,1)}, u32[]{:S(2)}, u32[]{:S(2)}) %collective-permute-start.46) | collective-permute-done | bytes 262176 | tf_op jit(solution)/shard_map/ppermute | solution.py:18
  157.0 3.2 %weight_image.1 = (bf16[8,64,768]{2,1,0:T(8,128)(2,1)S(1)}, bf16[8,64,768]{2,1,0:T(8,128)(2,1)S(1)}) custom-call(bf16[2,128,1024]{2,1,0:T(8,128)(2,1)S(1)} %stack_text_grads.1.refs_0_.refs_3_, s32[1]{0:T(128)} %bitcast.column_ref.refs_1_, s32[1]{0:T(128)} %bitcast.1.refs_2_, bf16[2,64,1024]{2,1,0:T(8,128)(2,1)S(1)} %image_back_a.1.refs_0_.refs_3_.refs_2_, ...), custom_call_target="tpu_custom_call" | custom-call | flops 4110612736 | bytes 5767176 | tf_op jit(solution)/shard_map/weight_image/pallas_call | solution.py:36
  160.3 3.5 %collective-permute-done.50.refs_2_.refs_5_ = bf16[2,128,1024]{2,1,0:T(8,128)(2,1)} collective-permute-done((bf16[2,128,1024]{2,1,0:T(8,128)(2,1)S(1)}, bf16[2,128,1024]{2,1,0:T(8,128)(2,1)}, u32[]{:S(2)}, u32[]{:S(2)}) %collective-permute-start.50) | collective-permute-done | bytes 524320 | tf_op jit(solution)/shard_map/ppermute | solution.py:18
  167.0 2.5 %collective-permute-start.53 = (bf16[4,64,768]{2,1,0:T(8,128)(2,1)S(1)}, bf16[4,64,768]{2,1,0:T(8,128)(2,1)S(1)}, u32[]{:S(2)}, u32[]{:S(2)}) collective-permute-start(bf16[4,64,768]{2,1,0:T(8,128)(2,1)S(1)} %get-tuple-element.134), channel_id=1, source_target_pairs={{0,16},{8,24},{16,0},{24,8},{32,48},{40,56},{48,32},{56,40},{64,80... | collective-permute-start | bytes 1179656 | tf_op jit(solution)/shard_map/ppermute | solution.py:18
  169.6 4.6 %feature_image.1 = (bf16[1024,768]{1,0:T(8,128)(2,1)}, bf16[16,128]{1,0:T(8,128)(2,1)S(1)}) custom-call(bf16[4,64,768]{2,1,0:T(8,128)(2,1)S(1)} %get-tuple-element.129.refs_0_.mine, s32[1]{0:T(128)} %bitcast.column_ref.refs_1_, bf16[2,64,1024]{2,1,0:T(8,128)(2,1)S(1)} %image_back_a.1.refs_0_.refs_3_.refs_2_, ...), custom_call_target="tpu_custom_call" | custom-call | flops 1610612736 | bytes 5640196 | tf_op jit(solution)/shard_map/feature_image/pallas_call | solution.py:36
  174.2 2.7 %weight_text.1 = (bf16[8,64,512]{2,1,0:T(8,128)(2,1)S(1)}, bf16[8,64,512]{2,1,0:T(8,128)(2,1)S(1)}) custom-call(bf16[16,128]{1,0:T(8,128)(2,1)S(1)} %get-tuple-element.139.refs_0_, s32[1]{0:T(128)} %bitcast.column_ref.refs_1_, s32[1]{0:T(128)} %bitcast.1.refs_2_, bf16[2,128,1024]{2,1,0:T(8,128)(2,1)S(1)} %stack_text_grads.1.refs_0_.refs_3_, ...), custom_call_target="tpu_custom_call" | custom-call | flops 1073741824 | bytes 4198408 | tf_op jit(solution)/shard_map/weight_text/pallas_call | solution.py:36
  180.9 2.2 %collective-permute-start.60 = (bf16[2,64,512]{2,1,0:T(8,128)(2,1)S(1)}, bf16[2,64,512]{2,1,0:T(8,128)(2,1)S(1)}, u32[]{:S(2)}, u32[]{:S(2)}) collective-permute-start(bf16[2,64,512]{2,1,0:T(8,128)(2,1)S(1)} %get-tuple-element.145), channel_id=1, source_target_pairs={{0,64},{8,72},{16,80},{24,88},{32,96},{40,104},{48,112},{56,120},{... | collective-permute-start | bytes 393224 | tf_op jit(solution)/shard_map/ppermute | solution.py:18
  191.1 3.7 %feature_text.1 = (bf16[1024,512]{1,0:T(8,128)(2,1)}, bf16[16,128]{1,0:T(8,128)(2,1)}) custom-call(s32[1]{0:T(128)} %bitcast.column_ref.refs_1_, bf16[2,128,1024]{2,1,0:T(8,128)(2,1)S(1)} %stack_text_grads.1.refs_0_.refs_3_, bf16[2,128,1024]{2,1,0:T(8,128)(2,1)} %collective-permute-done.49.refs_1_.refs_4_, ...), custom_call_target="tpu_custom_call" | custom-call | flops 1073741824 | bytes 4198404 | tf_op jit(solution)/shard_map/feature_text/pallas_call | solution.py:36
  (147 shorter events, 83.6 us)
Async XLA Ops:
  15.9 14.9 %collective-permute-start.2 = (bf16[2,128,1024]{2,1,0:T(8,128)(2,1)S(1)}, bf16[2,128,1024]{2,1,0:T(8,128)(2,1)S(1)}, u32[]{:S(2)}, u32[]{:S(2)}) collective-permute-start(bf16[2,128,1024]{2,1,0:T(8,128)(2,1)S(1)} %get-tuple-element.81), channel_id=1, source_target_pairs={{0,2},{1,3},{2,0},{3,1},{4,6},{5,7},{6,4},{7,5},{8,10},{9,11},{10,... | collective-permute-start | bytes 1572872 | tf_op jit(solution)/shard_map/ppermute | solution.py:18
  16.3 16.1 %collective-permute-start.3 = (bf16[2,128,1024]{2,1,0:T(8,128)(2,1)S(1)}, bf16[2,128,1024]{2,1,0:T(8,128)(2,1)S(1)}, u32[]{:S(2)}, u32[]{:S(2)}) collective-permute-start(bf16[2,128,1024]{2,1,0:T(8,128)(2,1)S(1)} %get-tuple-element.82), channel_id=1, source_target_pairs={{0,6},{1,7},{2,4},{3,5},{4,2},{5,3},{6,0},{7,1},{8,14},{9,15},{10,... | collective-permute-start | bytes 1572872 | tf_op jit(solution)/shard_map/ppermute | solution.py:18
  20.2 15.1 %collective-permute-start.4 = (bf16[128,1024]{1,0:T(8,128)(2,1)S(1)}, bf16[128,1024]{1,0:T(8,128)(2,1)S(1)}, u32[]{:S(2)}, u32[]{:S(2)}) collective-permute-start(bf16[128,1024]{1,0:T(8,128)(2,1)S(1)} %get-tuple-element.86), channel_id=1, source_target_pairs={{0,6},{1,7},{2,4},{3,5},{4,2},{5,3},{6,0},{7,1},{8,14},{9,15},{10,... | collective-permute-start | bytes 786440 | tf_op jit(solution)/shard_map/ppermute | solution.py:18
  22.3 13.1 %collective-permute-start.5 = (bf16[128,1024]{1,0:T(8,128)(2,1)S(1)}, bf16[128,1024]{1,0:T(8,128)(2,1)S(1)}, u32[]{:S(2)}, u32[]{:S(2)}) collective-permute-start(bf16[128,1024]{1,0:T(8,128)(2,1)S(1)} %get-tuple-element.87), channel_id=1, source_target_pairs={{0,2},{1,3},{2,0},{3,1},{4,6},{5,7},{6,4},{7,5},{8,10},{9,11},{10,... | collective-permute-start | bytes 786440 | tf_op jit(solution)/shard_map/ppermute | solution.py:18
  43.0 12.3 %collective-permute-start.10 = (bf16[2,64,1024]{2,1,0:T(8,128)(2,1)S(1)}, bf16[2,64,1024]{2,1,0:T(8,128)(2,1)S(1)}, u32[]{:S(2)}, u32[]{:S(2)}) collective-permute-start(bf16[2,64,1024]{2,1,0:T(8,128)(2,1)S(1)} %get-tuple-element.93), channel_id=1, source_target_pairs={{0,2},{1,3},{2,0},{3,1},{4,6},{5,7},{6,4},{7,5},{8,10},{9,11},{10,... | collective-permute-start | bytes 786440 | tf_op jit(solution)/shard_map/ppermute | solution.py:18
  43.0 12.3 %collective-permute-start.11 = (bf16[2,64,1024]{2,1,0:T(8,128)(2,1)S(1)}, bf16[2,64,1024]{2,1,0:T(8,128)(2,1)S(1)}, u32[]{:S(2)}, u32[]{:S(2)}) collective-permute-start(bf16[2,64,1024]{2,1,0:T(8,128)(2,1)S(1)} %get-tuple-element.94), channel_id=1, source_target_pairs={{0,6},{1,7},{2,4},{3,5},{4,2},{5,3},{6,0},{7,1},{8,14},{9,15},{10,... | collective-permute-start | bytes 786440 | tf_op jit(solution)/shard_map/ppermute | solution.py:18
  46.3 12.1 %collective-permute-start.12 = (bf16[2,64,1024]{2,1,0:T(8,128)(2,1)S(1)}, bf16[2,64,1024]{2,1,0:T(8,128)(2,1)S(1)}, u32[]{:S(2)}, u32[]{:S(2)}) collective-permute-start(bf16[2,64,1024]{2,1,0:T(8,128)(2,1)S(1)} %image_x_a.1.refs_0_.refs_1_), channel_id=1, source_target_pairs={{0,1},{1,0},{2,3},{3,2},{4,5},{5,4},{6,7},{7,6},{8,9},{9,8},{10,11... | collective-permute-start | bytes 786440 | tf_op jit(solution)/shard_map/ppermute | solution.py:18
  50.8 18.2 %collective-permute-start.19 = (bf16[2,128,1024]{2,1,0:T(8,128)(2,1)S(1)}, bf16[2,128,1024]{2,1,0:T(8,128)(2,1)S(1)}, u32[]{:S(2)}, u32[]{:S(2)}) collective-permute-start(bf16[2,128,1024]{2,1,0:T(8,128)(2,1)S(1)} %stack_text.1.refs_0_.refs_4_), channel_id=1, source_target_pairs={{0,96},{8,104},{16,112},{24,120},{32,64},{40,72},{48,80},{56,88},{... | collective-permute-start | bytes 1572872 | tf_op jit(solution)/shard_map/ppermute | solution.py:18
  55.3 13.7 %collective-permute-start.18 = (bf16[2,128,1024]{2,1,0:T(8,128)(2,1)S(1)}, bf16[2,128,1024]{2,1,0:T(8,128)(2,1)S(1)}, u32[]{:S(2)}, u32[]{:S(2)}) collective-permute-start(bf16[2,128,1024]{2,1,0:T(8,128)(2,1)S(1)} %stack_text.1.refs_0_.refs_4_), channel_id=1, source_target_pairs={{0,32},{8,40},{16,48},{24,56},{32,0},{40,8},{48,16},{56,24},{64,96... | collective-permute-start | bytes 1572872 | tf_op jit(solution)/shard_map/ppermute | solution.py:18
  63.5 10.3 %collective-permute-start.21 = (bf16[2,64,1024]{2,1,0:T(8,128)(2,1)S(1)}, bf16[2,64,1024]{2,1,0:T(8,128)(2,1)S(1)}, u32[]{:S(2)}, u32[]{:S(2)}) collective-permute-start(bf16[2,64,1024]{2,1,0:T(8,128)(2,1)S(1)} %get-tuple-element.96.refs_0_.refs_1_), channel_id=1, source_target_pairs={{0,6},{1,7},{2,4},{3,5},{4,2},{5,3},{6,0},{7,1},{8,14},{9,15},{10,... | collective-permute-start | bytes 786440 | tf_op jit(solution)/shard_map/ppermute | solution.py:18
  69.0 13.1 %collective-permute-start.25 = (bf16[128,1024]{1,0:T(8,128)(2,1)S(1)}, bf16[128,1024]{1,0:T(8,128)(2,1)S(1)}, u32[]{:S(2)}, u32[]{:S(2)}) collective-permute-start(bf16[128,1024]{1,0:T(8,128)(2,1)S(1)} %get-tuple-element.102), channel_id=1, source_target_pairs={{0,32},{8,40},{16,48},{24,56},{32,0},{40,8},{48,16},{56,24},{64,96... | collective-permute-start | bytes 786440 | tf_op jit(solution)/shard_map/ppermute | solution.py:18
  71.0 11.1 %collective-permute-start.24 = (bf16[128,1024]{1,0:T(8,128)(2,1)S(1)}, bf16[128,1024]{1,0:T(8,128)(2,1)S(1)}, u32[]{:S(2)}, u32[]{:S(2)}) collective-permute-start(bf16[128,1024]{1,0:T(8,128)(2,1)S(1)} %get-tuple-element.99.refs_0_), channel_id=1, source_target_pairs={{0,96},{8,104},{16,112},{24,120},{32,64},{40,72},{48,80},{56,88},{... | collective-permute-start | bytes 786440 | tf_op jit(solution)/shard_map/ppermute | solution.py:18
  94.8 10.2 %collective-permute-start.29 = (bf16[128,1024]{1,0:T(8,128)(2,1)S(1)}, bf16[128,1024]{1,0:T(8,128)(2,1)S(1)}, u32[]{:S(2)}, u32[]{:S(2)}) collective-permute-start(bf16[128,1024]{1,0:T(8,128)(2,1)S(1)} %get-tuple-element.112), channel_id=1, source_target_pairs={{0,2},{1,3},{2,0},{3,1},{4,6},{5,7},{6,4},{7,5},{8,10},{9,11},{10,... | collective-permute-start | bytes 786440 | tf_op jit(solution)/shard_map/ppermute | solution.py:18
  94.9 10.1 %collective-permute-start.28 = (bf16[128,1024]{1,0:T(8,128)(2,1)S(1)}, bf16[128,1024]{1,0:T(8,128)(2,1)S(1)}, u32[]{:S(2)}, u32[]{:S(2)}) collective-permute-start(bf16[128,1024]{1,0:T(8,128)(2,1)S(1)} %get-tuple-element.107.refs_0_), channel_id=1, source_target_pairs={{0,6},{1,7},{2,4},{3,5},{4,2},{5,3},{6,0},{7,1},{8,14},{9,15},{10,... | collective-permute-start | bytes 786440 | tf_op jit(solution)/shard_map/ppermute | solution.py:18
  105.2 10.5 %collective-permute-start.33 = (bf16[2,64,1024]{2,1,0:T(8,128)(2,1)S(1)}, bf16[2,64,1024]{2,1,0:T(8,128)(2,1)S(1)}, u32[]{:S(2)}, u32[]{:S(2)}) collective-permute-start(bf16[2,64,1024]{2,1,0:T(8,128)(2,1)S(1)} %get-tuple-element.117), channel_id=1, source_target_pairs={{0,6},{1,7},{2,4},{3,5},{4,2},{5,3},{6,0},{7,1},{8,14},{9,15},{10,... | collective-permute-start | bytes 786440 | tf_op jit(solution)/shard_map/ppermute | solution.py:18
  106.9 11.7 %collective-permute-start.32 = (bf16[2,64,1024]{2,1,0:T(8,128)(2,1)S(1)}, bf16[2,64,1024]{2,1,0:T(8,128)(2,1)S(1)}, u32[]{:S(2)}, u32[]{:S(2)}) collective-permute-start(bf16[2,64,1024]{2,1,0:T(8,128)(2,1)S(1)} %get-tuple-element.113.refs_0_), channel_id=1, source_target_pairs={{0,2},{1,3},{2,0},{3,1},{4,6},{5,7},{6,4},{7,5},{8,10},{9,11},{10,... | collective-permute-start | bytes 786440 | tf_op jit(solution)/shard_map/ppermute | solution.py:18
  107.6 12.8 %collective-permute-start.34 = (bf16[2,64,1024]{2,1,0:T(8,128)(2,1)S(1)}, bf16[2,64,1024]{2,1,0:T(8,128)(2,1)S(1)}, u32[]{:S(2)}, u32[]{:S(2)}) collective-permute-start(bf16[2,64,1024]{2,1,0:T(8,128)(2,1)S(1)} %get-tuple-element.118), channel_id=1, source_target_pairs={{0,2},{1,3},{2,0},{3,1},{4,6},{5,7},{6,4},{7,5},{8,10},{9,11},{10,... | collective-permute-start | bytes 786440 | tf_op jit(solution)/shard_map/ppermute | solution.py:18
  108.9 11.5 %collective-permute-start.35 = (bf16[2,64,1024]{2,1,0:T(8,128)(2,1)S(1)}, bf16[2,64,1024]{2,1,0:T(8,128)(2,1)S(1)}, u32[]{:S(2)}, u32[]{:S(2)}) collective-permute-start(bf16[2,64,1024]{2,1,0:T(8,128)(2,1)S(1)} %get-tuple-element.119), channel_id=1, source_target_pairs={{0,6},{1,7},{2,4},{3,5},{4,2},{5,3},{6,0},{7,1},{8,14},{9,15},{10,... | collective-permute-start | bytes 786440 | tf_op jit(solution)/shard_map/ppermute | solution.py:18
  111.0 12.0 %collective-permute-start.36 = (bf16[2,128,1024]{2,1,0:T(8,128)(2,1)S(1)}, bf16[2,128,1024]{2,1,0:T(8,128)(2,1)S(1)}, u32[]{:S(2)}, u32[]{:S(2)}) collective-permute-start(bf16[2,128,1024]{2,1,0:T(8,128)(2,1)S(1)} %get-tuple-element.120), channel_id=1, source_target_pairs={{0,32},{8,40},{16,48},{24,56},{32,0},{40,8},{48,16},{56,24},{64,96... | collective-permute-start | bytes 1572872 | tf_op jit(solution)/shard_map/ppermute | solution.py:18
  115.7 11.4 %collective-permute-start.37 = (bf16[2,128,1024]{2,1,0:T(8,128)(2,1)S(1)}, bf16[2,128,1024]{2,1,0:T(8,128)(2,1)S(1)}, u32[]{:S(2)}, u32[]{:S(2)}) collective-permute-start(bf16[2,128,1024]{2,1,0:T(8,128)(2,1)S(1)} %get-tuple-element.121), channel_id=1, source_target_pairs={{0,96},{8,104},{16,112},{24,120},{32,64},{40,72},{48,80},{56,88},{... | collective-permute-start | bytes 1572872 | tf_op jit(solution)/shard_map/ppermute | solution.py:18
  118.6 11.6 %collective-permute-start.38 = (bf16[2,64,1024]{2,1,0:T(8,128)(2,1)S(1)}, bf16[2,64,1024]{2,1,0:T(8,128)(2,1)S(1)}, u32[]{:S(2)}, u32[]{:S(2)}) collective-permute-start(bf16[2,64,1024]{2,1,0:T(8,128)(2,1)S(1)} %image_grads_x_a.1.refs_0_.refs_1_), channel_id=1, source_target_pairs={{0,1},{1,0},{2,3},{3,2},{4,5},{5,4},{6,7},{7,6},{8,9},{9,8},{10,11... | collective-permute-start | bytes 786440 | tf_op jit(solution)/shard_map/ppermute | solution.py:18
  127.8 13.1 %collective-permute-start.40 = (bf16[2,64,1024]{2,1,0:T(8,128)(2,1)S(1)}, bf16[2,64,1024]{2,1,0:T(8,128)(2,1)S(1)}, u32[]{:S(2)}, u32[]{:S(2)}) collective-permute-start(bf16[2,64,1024]{2,1,0:T(8,128)(2,1)S(1)} %image_grads_x_b.1.refs_0_.refs_1_), channel_id=1, source_target_pairs={{0,1},{1,0},{2,3},{3,2},{4,5},{5,4},{6,7},{7,6},{8,9},{9,8},{10,11... | collective-permute-start | bytes 786440 | tf_op jit(solution)/shard_map/ppermute | solution.py:18
  130.5 12.3 %collective-permute-start.43 = (bf16[2,64,1024]{2,1,0:T(8,128)(2,1)S(1)}, bf16[2,64,1024]{2,1,0:T(8,128)(2,1)S(1)}, u32[]{:S(2)}, u32[]{:S(2)}) collective-permute-start(bf16[2,64,1024]{2,1,0:T(8,128)(2,1)S(1)} %image_back_a.1.refs_0_.refs_3_.refs_2_), channel_id=1, source_target_pairs={{0,4},{1,5},{2,6},{3,7},{4,0},{5,1},{6,2},{7,3},{8,12},{9,13},{10,... | collective-permute-start | bytes 786440 | tf_op jit(solution)/shard_map/ppermute | solution.py:18
  131.1 16.0 %collective-permute-start.42 = (bf16[2,64,1024]{2,1,0:T(8,128)(2,1)S(1)}, bf16[2,64,1024]{2,1,0:T(8,128)(2,1)S(1)}, u32[]{:S(2)}, u32[]{:S(2)}) collective-permute-start(bf16[2,64,1024]{2,1,0:T(8,128)(2,1)S(1)} %image_back_a.1.refs_0_.refs_3_.refs_2_), channel_id=1, source_target_pairs={{0,6},{1,7},{2,4},{3,5},{4,2},{5,3},{6,0},{7,1},{8,14},{9,15},{10,... | collective-permute-start | bytes 786440 | tf_op jit(solution)/shard_map/ppermute | solution.py:18
  132.8 14.4 %collective-permute-start.41 = (bf16[2,64,1024]{2,1,0:T(8,128)(2,1)S(1)}, bf16[2,64,1024]{2,1,0:T(8,128)(2,1)S(1)}, u32[]{:S(2)}, u32[]{:S(2)}) collective-permute-start(bf16[2,64,1024]{2,1,0:T(8,128)(2,1)S(1)} %image_back_a.1.refs_0_.refs_3_.refs_2_), channel_id=1, source_target_pairs={{0,2},{1,3},{2,0},{3,1},{4,6},{5,7},{6,4},{7,5},{8,10},{9,11},{10,... | collective-permute-start | bytes 786440 | tf_op jit(solution)/shard_map/ppermute | solution.py:18
  135.4 11.7 %collective-permute-start.44 = (bf16[128,1024]{1,0:T(8,128)(2,1)S(1)}, bf16[128,1024]{1,0:T(8,128)(2,1)S(1)}, u32[]{:S(2)}, u32[]{:S(2)}) collective-permute-start(bf16[128,1024]{1,0:T(8,128)(2,1)S(1)} %text_back.1.refs_0_.refs_4_), channel_id=1, source_target_pairs={{0,1},{1,0},{2,3},{3,2},{4,5},{5,4},{6,7},{7,6},{8,9},{9,8},{10,11... | collective-permute-start | bytes 786440 | tf_op jit(solution)/shard_map/ppermute | solution.py:18
  141.1 10.9 %collective-permute-start.47 = (bf16[2,64,1024]{2,1,0:T(8,128)(2,1)S(1)}, bf16[2,64,1024]{2,1,0:T(8,128)(2,1)}, u32[]{:S(2)}, u32[]{:S(2)}) collective-permute-start(bf16[2,64,1024]{2,1,0:T(8,128)(2,1)S(1)} %image_back_b.1.refs_0_.refs_4_.refs_3_), channel_id=1, source_target_pairs={{0,4},{1,5},{2,6},{3,7},{4,0},{5,1},{6,2},{7,3},{8,12},{9,13},{10,... | collective-permute-start | bytes 786440 | tf_op jit(solution)/shard_map/ppermute | solution.py:18
  142.8 12.8 %collective-permute-start.46 = (bf16[2,64,1024]{2,1,0:T(8,128)(2,1)S(1)}, bf16[2,64,1024]{2,1,0:T(8,128)(2,1)}, u32[]{:S(2)}, u32[]{:S(2)}) collective-permute-start(bf16[2,64,1024]{2,1,0:T(8,128)(2,1)S(1)} %image_back_b.1.refs_0_.refs_4_.refs_3_), channel_id=1, source_target_pairs={{0,6},{1,7},{2,4},{3,5},{4,2},{5,3},{6,0},{7,1},{8,14},{9,15},{10,... | collective-permute-start | bytes 786440 | tf_op jit(solution)/shard_map/ppermute | solution.py:18
  147.2 16.6 %collective-permute-start.50 = (bf16[2,128,1024]{2,1,0:T(8,128)(2,1)S(1)}, bf16[2,128,1024]{2,1,0:T(8,128)(2,1)}, u32[]{:S(2)}, u32[]{:S(2)}) collective-permute-start(bf16[2,128,1024]{2,1,0:T(8,128)(2,1)S(1)} %stack_text_grads.1.refs_0_.refs_3_), channel_id=1, source_target_pairs={{0,6},{1,7},{2,4},{3,5},{4,2},{5,3},{6,0},{7,1},{8,14},{9,15},{10,... | collective-permute-start | bytes 1572872 | tf_op jit(solution)/shard_map/ppermute | solution.py:18
  148.5 15.3 %collective-permute-start.49 = (bf16[2,128,1024]{2,1,0:T(8,128)(2,1)S(1)}, bf16[2,128,1024]{2,1,0:T(8,128)(2,1)}, u32[]{:S(2)}, u32[]{:S(2)}) collective-permute-start(bf16[2,128,1024]{2,1,0:T(8,128)(2,1)S(1)} %stack_text_grads.1.refs_0_.refs_3_), channel_id=1, source_target_pairs={{0,2},{1,3},{2,0},{3,1},{4,6},{5,7},{6,4},{7,5},{8,10},{9,11},{10,... | collective-permute-start | bytes 1572872 | tf_op jit(solution)/shard_map/ppermute | solution.py:18
  183.2 11.6 %collective-permute-start.54 = (bf16[64,768]{1,0:T(8,128)(2,1)S(1)}, bf16[64,768]{1,0:T(8,128)(2,1)S(1)}, u32[]{:S(2)}, u32[]{:S(2)}) collective-permute-start(bf16[64,768]{1,0:T(8,128)(2,1)S(1)} %get-tuple-element.136), channel_id=1, source_target_pairs={{0,32},{8,40},{16,48},{24,56},{32,0},{40,8},{48,16},{56,24},{64,96... | collective-permute-start | bytes 294920 | tf_op jit(solution)/shard_map/ppermute | solution.py:18
  183.2 11.5 %collective-permute-start.55 = (bf16[64,768]{1,0:T(8,128)(2,1)S(1)}, bf16[64,768]{1,0:T(8,128)(2,1)S(1)}, u32[]{:S(2)}, u32[]{:S(2)}) collective-permute-start(bf16[64,768]{1,0:T(8,128)(2,1)S(1)} %get-tuple-element.137), channel_id=1, source_target_pairs={{0,96},{8,104},{16,112},{24,120},{32,64},{40,72},{48,80},{56,88},{... | collective-permute-start | bytes 294920 | tf_op jit(solution)/shard_map/ppermute | solution.py:18
  (37 other events, 292.7 us)

commit v8 on v6

--- a/solution.py
+++ b/solution.py
@@ -390,7 +390,7 @@
         out[...] = p0[...] + wide(p4) + wide(p12) + wide(p8)
 
     outs = [shape(*one, dtype=F32)] + [shape(*one)] * 3
-    p0, p4, p12, p8 = call("weight_image_y", along_y, outs, (mine, swap(theirs, "blk", 2)))
+    p0, p4, p12, p8 = call("weight_image_y", along_y, outs, (mine, swap(theirs, "blk", 2)), ORDER_COST * 2 // 5)
     p4, p12, p8 = swap(p4, "blk", 4), swap(p12, "blk", 12), swap(p8, "blk", 8)
     return call("weight_image_z", along_z, outs[:1], (p0, p4, p12, p8))[0].T, p0
 
@@ -488,7 +488,7 @@
     outs = [shape(*two)] * 3
     p02, p46, p1214 = call("sums_sixth", sixth, outs, (even_sum, odd_got, p8_got, p10_got), after=sent[0])
     p46, p1214 = swap(p46, "blk", 4), swap(p1214, "blk", 12)
-    (x_a,) = call("image_grads_x_a", add_half(0), [shape(*half)], (g01, *got[0]), ORDER_COST // 2, after=p02)
+    (x_a,) = call("image_grads_x_a", add_half(0), [shape(*half)], (g01, *got[0]), ORDER_COST * 3 // 10, after=p02)
     y_a = swap(x_a, "mp", 1)
     (x_b,) = call("image_grads_x_b", add_half(1), [shape(*half)], (g01, *got[1]), after=x_a)
     y_b = swap(x_b, "mp", 1)
@@ -521,7 +521,7 @@
     img_weight_grad, image_y = sum_weight_y(*image_chip)
     d_all = (d01, d23, d67, d4, d5)
     same, other = weight_part("weight_text", column, place, d_all, 1, txt_feat, image_chip[0])
-    txt_weight_grad = sum_weight(*chip_weight("weight_text_chip", same, other))
+    txt_weight_grad = sum_weight(*chip_weight("weight_text_chip", same, other, image_y))
     return (
         feature_grad("feature_image", column, e_all, 2, img_weight),
         feature_grad("feature_text", column, d_all, 1, txt_weight),

time: 197 us -> 193 us (0.980)
  starting transfers between devices: 78.2 us -> 74.9 us
    ppermute x62, starting transfers between devices: 78.2 us -> 74.9 us  [swap(): return lax.ppermute(value, axis, [(i, i ^ offset) for i in range(count)])]
  transfers between devices with their start and end apart: 62 -> 62, of which waited for: 30 -> 35; matrix products, arithmetic and copies ran while one was open for 0% -> 0% of each run, Pallas kernels for 14% -> 15%
where the time goes in v8:
time: 193 us; the launch traced here: 192 us
  starting transfers between devices  74.9 us (39%)
  waiting for transfers between devices  73.3 us (38%)
  Pallas kernels  37.6 us (19%)
  local copies, waits for them, and re-layouts  3.87 us (2%)
  between operations  2.32 us (1%)
    ppermute x62, starting transfers between devices, swap(): return lax.ppermute(value, axis, [(i, i ^ offset) for i in range(count)])  74.9 us
    ppermute x62, waiting for transfers between devices, swap(): return lax.ppermute(value, axis, [(i, i ^ offset) for i in range(count)])  73.3 us
    pallas_call x39, Pallas kernels, call(): pl.pallas_call(run, out_shape=outs, in_specs=specs, scratch_shapes=list(s...  28.5 us
    pallas_call x2, Pallas kernels, pair_call(): pl.pallas_call(body, in_specs=[smem, smem] + [vmem] * len(arrays), out_sh...  9.11 us
    unnamed x16, local copies, waits for them, and re-layouts  3.87 us
  transfers between devices with their start and end apart: 62, of which 35 were waited for; matrix products, arithmetic and copies ran while one was open for 0% of the time, Pallas kernels for 15%

profile of v8, /device:TPU:8, one launch (start us, length us, event | category | flops | bytes accessed | tf_op | source)
XLA Modules:
  0.0 192.0 jit_solution(12660662521203935644)
XLA Ops:
  5.2 2.8 %collective-permute-start = (bf16[128,1024]{1,0:T(8,128)(2,1)S(1)}, bf16[128,1024]{1,0:T(8,128)(2,1)S(1)}, u32[]{:S(2)}, u32[]{:S(2)}) collective-permute-start(bf16[128,1024]{1,0:T(8,128)(2,1)S(1)} %get-tuple-element.76), channel_id=1, source_target_pairs={{0,6},{1,7},{2,4},{3,5},{4,2},{5,3},{6,0},{7,1},{8,14},{9,15},{10,... | collective-permute-start | bytes 786440 | tf_op jit(solution)/shard_map/ppermute | solution.py:18
  8.2 6.3 %collective-permute-done.r4 = bf16[128,1024]{1,0:T(8,128)(2,1)S(1)} collective-permute-done((bf16[128,1024]{1,0:T(8,128)(2,1)S(1)}, bf16[128,1024]{1,0:T(8,128)(2,1)S(1)}, u32[]{:S(2)}, u32[]{:S(2)}) %collective-permute-start) | collective-permute-done | bytes 262176 | tf_op jit(solution)/shard_map/ppermute | solution.py:18
  17.6 2.6 %embed_image.1 = (bf16[2,128,1024]{2,1,0:T(8,128)(2,1)S(1)}, bf16[2,128,1024]{2,1,0:T(8,128)(2,1)S(1)}, bf16[2,128,1024]{2,1,0:T(8,128)(2,1)S(1)}, bf16[128,1024]{1,0:T(8,128)(2,1)S(1)}, bf16[128,1024]{1,0:T(8,128)(2,1)S(1)}) custom-call(s32[1]{0:T(128)} %bitcast.column_ref.refs_1_, bf16[1024,768]{1,0:T(8,128)(2,1)S(1)} %copy-done.2, ...), custom_call_target="tpu_custom_call" | custom-call | flops 1610612736 | bytes 5242884 | tf_op jit(solution)/shard_map/embed_image/pallas_call | solution.py:36
  22.8 8.1 %collective-permute-done.2.t23 = bf16[2,128,1024]{2,1,0:T(8,128)(2,1)S(1)} collective-permute-done((bf16[2,128,1024]{2,1,0:T(8,128)(2,1)S(1)}, bf16[2,128,1024]{2,1,0:T(8,128)(2,1)S(1)}, u32[]{:S(2)}, u32[]{:S(2)}) %collective-permute-start.2) | collective-permute-done | bytes 524320 | tf_op jit(solution)/shard_map/ppermute | solution.py:18
  32.5 2.4 %collective-permute-start.6 = (bf16[128,1024]{1,0:T(8,128)(2,1)S(1)}, bf16[128,1024]{1,0:T(8,128)(2,1)S(1)}, u32[]{:S(2)}, u32[]{:S(2)}) collective-permute-start(bf16[128,1024]{1,0:T(8,128)(2,1)S(1)} %get-tuple-element.80.refs_0_), channel_id=1, source_target_pairs={{0,1},{1,0},{2,3},{3,2},{4,5},{5,4},{6,7},{7,6},{8,9},{9,8},{10,11... | collective-permute-start | bytes 786440 | tf_op jit(solution)/shard_map/ppermute | solution.py:18
  37.4 4.5 %collective-permute-done.6.refs_2_ = bf16[128,1024]{1,0:T(8,128)(2,1)S(1)} collective-permute-done((bf16[128,1024]{1,0:T(8,128)(2,1)S(1)}, bf16[128,1024]{1,0:T(8,128)(2,1)S(1)}, u32[]{:S(2)}, u32[]{:S(2)}) %collective-permute-start.6) | collective-permute-done | bytes 262176 | tf_op jit(solution)/shard_map/ppermute | solution.py:18
  46.3 2.4 %collective-permute-start.12 = (bf16[2,64,1024]{2,1,0:T(8,128)(2,1)S(1)}, bf16[2,64,1024]{2,1,0:T(8,128)(2,1)S(1)}, u32[]{:S(2)}, u32[]{:S(2)}) collective-permute-start(bf16[2,64,1024]{2,1,0:T(8,128)(2,1)S(1)} %image_x_a.1.refs_0_.refs_1_), channel_id=1, source_target_pairs={{0,1},{1,0},{2,3},{3,2},{4,5},{5,4},{6,7},{7,6},{8,9},{9,8},{10,11... | collective-permute-start | bytes 786440 | tf_op jit(solution)/shard_map/ppermute | solution.py:18
  50.8 4.5 %collective-permute-start.19 = (bf16[2,128,1024]{2,1,0:T(8,128)(2,1)S(1)}, bf16[2,128,1024]{2,1,0:T(8,128)(2,1)S(1)}, u32[]{:S(2)}, u32[]{:S(2)}) collective-permute-start(bf16[2,128,1024]{2,1,0:T(8,128)(2,1)S(1)} %stack_text.1.refs_0_.refs_4_), channel_id=1, source_target_pairs={{0,96},{8,104},{16,112},{24,120},{32,64},{40,72},{48,80},{56,88},{... | collective-permute-start | bytes 1572872 | tf_op jit(solution)/shard_map/ppermute | solution.py:18
  55.4 3.0 %collective-permute-start.13 = (bf16[2,64,1024]{2,1,0:T(8,128)(2,1)S(1)}, bf16[2,64,1024]{2,1,0:T(8,128)(2,1)S(1)}, u32[]{:S(2)}, u32[]{:S(2)}) collective-permute-start(bf16[2,64,1024]{2,1,0:T(8,128)(2,1)S(1)} %image_x_b.1.refs_0_.refs_1_), channel_id=1, source_target_pairs={{0,1},{1,0},{2,3},{3,2},{4,5},{5,4},{6,7},{7,6},{8,9},{9,8},{10,11... | collective-permute-start | bytes 786440 | tf_op jit(solution)/shard_map/ppermute | solution.py:18
  59.9 3.5 %collective-permute-done.13.refs_2_ = bf16[2,64,1024]{2,1,0:T(8,128)(2,1)S(1)} collective-permute-done((bf16[2,64,1024]{2,1,0:T(8,128)(2,1)S(1)}, bf16[2,64,1024]{2,1,0:T(8,128)(2,1)S(1)}, u32[]{:S(2)}, u32[]{:S(2)}) %collective-permute-start.13) | collective-permute-done | bytes 262176 | tf_op jit(solution)/shard_map/ppermute | solution.py:18
  64.5 2.3 %collective-permute-done.15.refs_2_.refs_4_ = bf16[2,64,1024]{2,1,0:T(8,128)(2,1)S(1)} collective-permute-done((bf16[2,64,1024]{2,1,0:T(8,128)(2,1)S(1)}, bf16[2,64,1024]{2,1,0:T(8,128)(2,1)S(1)}, u32[]{:S(2)}, u32[]{:S(2)}) %collective-permute-start.15) | collective-permute-done | bytes 262176 | tf_op jit(solution)/shard_map/ppermute | solution.py:18
  74.7 2.5 %collective-permute-start.22 = (bf16[64,1024]{1,0:T(8,128)(2,1)S(1)}, bf16[64,1024]{1,0:T(8,128)(2,1)S(1)}, u32[]{:S(2)}, u32[]{:S(2)}) collective-permute-start(bf16[64,1024]{1,0:T(8,128)(2,1)S(1)} %get-tuple-element.97), channel_id=1, source_target_pairs={{0,6},{1,7},{2,4},{3,5},{4,2},{5,3},{6,0},{7,1},{8,14},{9,15},{10,... | collective-permute-start | bytes 393224 | tf_op jit(solution)/shard_map/ppermute | solution.py:18
  77.1 2.8 %collective-permute-done.16.refs_0_.refs_6_ = bf16[64,1024]{1,0:T(8,128)(2,1)S(1)} collective-permute-done((bf16[64,1024]{1,0:T(8,128)(2,1)S(1)}, bf16[64,1024]{1,0:T(8,128)(2,1)S(1)}, u32[]{:S(2)}, u32[]{:S(2)}) %collective-permute-start.16) | collective-permute-done | bytes 131104 | tf_op jit(solution)/shard_map/ppermute | solution.py:18
  83.9 4.0 %pairs_even.1 = (bf16[1024,1024]{1,0:T(8,128)(2,1)S(1)}, bf16[1024,1024]{1,0:T(8,128)(2,1)S(1)}, bf16[1024,1024]{1,0:T(8,128)(2,1)S(1)}) custom-call(f32[1]{0:T(128)S(6)} %exp.3.scale_ref, f32[1]{0:T(128)S(6)} %copy.11.bias_ref, bf16[8,128,1024]{2,1,0:T(8,128)(2,1)S(1)} %collect.1.texts.refs_3_, bf16[2,64,1024]{2,1,0:T(8,128)(2,1)S(1)} %get-tuple-element.92.refs_0_, ...), custom_call_target="tpu_custom_call" | custom-call | flops 2147483648 | bytes 10485760 | tf_op jit(solution)/shard_map/pairs_even/pallas_call | solution.py:183
  87.8 5.2 %pairs_odd.1 = (bf16[1024,1024]{1,0:T(8,128)(2,1)S(1)}, bf16[8,128,1024]{2,1,0:T(8,128)(2,1)S(1)}) custom-call(f32[1]{0:T(128)S(6)} %exp.3.scale_ref, f32[1]{0:T(128)S(6)} %copy.11.bias_ref, bf16[8,128,1024]{2,1,0:T(8,128)(2,1)S(1)} %collective-permute-done.26.texts.refs_4_, bf16[1024,1024]{1,0:T(8,128)(2,1)S(1)} %get-tuple-element.100.image_all.refs_2_, ...), custom_call_target="tpu_custom_call" | custom-call | flops 4294967296 | bytes 10485760 | tf_op jit(solution)/shard_map/pairs_odd/pallas_call | solution.py:183
  96.2 2.5 %text_grads_even.1.even.refs_1_ = bf16[8,128,1024]{2,1,0:T(8,128)(2,1)S(1)} custom-call(bf16[128,1024]{1,0:T(8,128)(2,1)S(1)} %get-tuple-element.104.refs_0_, bf16[1024,1024]{1,0:T(8,128)(2,1)S(1)} %get-tuple-element.105.refs_1_, bf16[1024,1024]{1,0:T(8,128)(2,1)S(1)} %get-tuple-element.100.image_all.refs_2_), custom_call_target="tpu_custom_call" | custom-call | flops 2147483648 | bytes 6553600 | tf_op jit(solution)/shard_map/text_grads_even/pallas_call | solution.py:36
  98.9 2.1 %collective-permute-start.31 = (bf16[128,1024]{1,0:T(8,128)(2,1)S(1)}, bf16[128,1024]{1,0:T(8,128)(2,1)S(1)}, u32[]{:S(2)}, u32[]{:S(2)}) collective-permute-start(bf16[128,1024]{1,0:T(8,128)(2,1)S(1)} %get-tuple-element.111), channel_id=1, source_target_pairs={{0,32},{8,40},{16,48},{24,56},{32,0},{40,8},{48,16},{56,24},{64,96... | collective-permute-start | bytes 786440 | tf_op jit(solution)/shard_map/ppermute | solution.py:18
  101.4 3.6 %pairs_near_images.1 = (bf16[2,128,1024]{2,1,0:T(8,128)(2,1)S(1)}, bf16[2,128,1024]{2,1,0:T(8,128)(2,1)S(1)}, bf16[2,128,1024]{2,1,0:T(8,128)(2,1)S(1)}) custom-call(bf16[128,1024]{1,0:T(8,128)(2,1)S(1)} %get-tuple-element.106.refs_0_, bf16[1024,1024]{1,0:T(8,128)(2,1)S(1)} %get-tuple-element.101._.refs_1_, ...), custom_call_target="tpu_custom_call" | custom-call | flops 3221225472 | bytes 10223616 | tf_op jit(solution)/shard_map/pairs_near_images/pallas_call | solution.py:36
  107.6 2.3 %collective-permute-done.30.refs_3_ = bf16[128,1024]{1,0:T(8,128)(2,1)S(1)} collective-permute-done((bf16[128,1024]{1,0:T(8,128)(2,1)S(1)}, bf16[128,1024]{1,0:T(8,128)(2,1)S(1)}, u32[]{:S(2)}, u32[]{:S(2)}) %collective-permute-start.30) | collective-permute-done | bytes 262176 | tf_op jit(solution)/shard_map/ppermute | solution.py:18
  116.2 3.0 %collective-permute-start.38 = (bf16[2,64,1024]{2,1,0:T(8,128)(2,1)S(1)}, bf16[2,64,1024]{2,1,0:T(8,128)(2,1)S(1)}, u32[]{:S(2)}, u32[]{:S(2)}) collective-permute-start(bf16[2,64,1024]{2,1,0:T(8,128)(2,1)S(1)} %image_grads_x_a.1.refs_0_.refs_1_), channel_id=1, source_target_pairs={{0,1},{1,0},{2,3},{3,2},{4,5},{5,4},{6,7},{7,6},{8,9},{9,8},{10,11... | collective-permute-start | bytes 786440 | tf_op jit(solution)/shard_map/ppermute | solution.py:18
  126.4 2.3 %collective-permute-start.45 = (bf16[2,64,1024]{2,1,0:T(8,128)(2,1)S(1)}, bf16[2,64,1024]{2,1,0:T(8,128)(2,1)S(1)}, u32[]{:S(2)}, u32[]{:S(2)}) collective-permute-start(bf16[2,64,1024]{2,1,0:T(8,128)(2,1)S(1)} %image_back_a.1.refs_0_.refs_3_), channel_id=1, source_target_pairs={{0,4},{1,5},{2,6},{3,7},{4,0},{5,1},{6,2},{7,3},{8,12},{9,13},{10,... | collective-permute-start | bytes 786440 | tf_op jit(solution)/shard_map/ppermute | solution.py:18
  129.9 3.6 %collective-permute-done.39.refs_2_ = bf16[128,1024]{1,0:T(8,128)(2,1)S(1)} collective-permute-done((bf16[128,1024]{1,0:T(8,128)(2,1)S(1)}, bf16[128,1024]{1,0:T(8,128)(2,1)S(1)}, u32[]{:S(2)}, u32[]{:S(2)}) %collective-permute-start.39) | collective-permute-done | bytes 262176 | tf_op jit(solution)/shard_map/ppermute | solution.py:18
  135.4 3.0 %collective-permute-done.40.refs_2_ = bf16[2,64,1024]{2,1,0:T(8,128)(2,1)S(1)} collective-permute-done((bf16[2,64,1024]{2,1,0:T(8,128)(2,1)S(1)}, bf16[2,64,1024]{2,1,0:T(8,128)(2,1)S(1)}, u32[]{:S(2)}, u32[]{:S(2)}) %collective-permute-start.40) | collective-permute-done | bytes 262176 | tf_op jit(solution)/shard_map/ppermute | solution.py:18
  147.0 2.5 %collective-permute-done.46.refs_7_.refs_10_ = bf16[2,64,1024]{2,1,0:T(8,128)(2,1)S(1)} collective-permute-done((bf16[2,64,1024]{2,1,0:T(8,128)(2,1)S(1)}, bf16[2,64,1024]{2,1,0:T(8,128)(2,1)S(1)}, u32[]{:S(2)}, u32[]{:S(2)}) %collective-permute-start.46) | collective-permute-done | bytes 262176 | tf_op jit(solution)/shard_map/ppermute | solution.py:18
  149.5 3.6 %collective-permute-done.44.refs_5_.refs_8_ = bf16[2,64,1024]{2,1,0:T(8,128)(2,1)S(1)} collective-permute-done((bf16[2,64,1024]{2,1,0:T(8,128)(2,1)S(1)}, bf16[2,64,1024]{2,1,0:T(8,128)(2,1)S(1)}, u32[]{:S(2)}, u32[]{:S(2)}) %collective-permute-start.44) | collective-permute-done | bytes 262176 | tf_op jit(solution)/shard_map/ppermute | solution.py:18
  155.9 3.1 %weight_image.1 = (bf16[8,64,768]{2,1,0:T(8,128)(2,1)S(1)}, bf16[8,64,768]{2,1,0:T(8,128)(2,1)S(1)}) custom-call(bf16[2,128,1024]{2,1,0:T(8,128)(2,1)S(1)} %stack_text_grads.1.refs_0_.refs_3_, s32[1]{0:T(128)} %bitcast.column_ref.refs_1_, s32[1]{0:T(128)} %bitcast.1.refs_2_, bf16[2,64,1024]{2,1,0:T(8,128)(2,1)S(1)} %image_back_a.1.refs_0_.refs_3_, ...), custom_call_target="tpu_custom_call" | custom-call | flops 4110612736 | bytes 5767176 | tf_op jit(solution)/shard_map/weight_image/pallas_call | solution.py:36
  159.1 2.3 %collective-permute-done.49.refs_2_.refs_5_ = bf16[2,128,1024]{2,1,0:T(8,128)(2,1)S(1)} collective-permute-done((bf16[2,128,1024]{2,1,0:T(8,128)(2,1)S(1)}, bf16[2,128,1024]{2,1,0:T(8,128)(2,1)S(1)}, u32[]{:S(2)}, u32[]{:S(2)}) %collective-permute-start.49) | collective-permute-done | bytes 524320 | tf_op jit(solution)/shard_map/ppermute | solution.py:18
  165.7 3.4 %collective-permute-done.50.refs_3_.refs_6_ = bf16[128,1024]{1,0:T(8,128)(2,1)S(1)} collective-permute-done((bf16[128,1024]{1,0:T(8,128)(2,1)S(1)}, bf16[128,1024]{1,0:T(8,128)(2,1)S(1)}, u32[]{:S(2)}, u32[]{:S(2)}) %collective-permute-start.50) | collective-permute-done | bytes 262176 | tf_op jit(solution)/shard_map/ppermute | solution.py:18
  175.3 2.3 %collective-permute-start.60 = (bf16[2,64,512]{2,1,0:T(8,128)(2,1)S(1)}, bf16[2,64,512]{2,1,0:T(8,128)(2,1)S(1)}, u32[]{:S(2)}, u32[]{:S(2)}) collective-permute-start(bf16[2,64,512]{2,1,0:T(8,128)(2,1)S(1)} %get-tuple-element.139), channel_id=1, source_target_pairs={{0,64},{8,72},{16,80},{24,88},{32,96},{40,104},{48,112},{56,120},{... | collective-permute-start | bytes 393224 | tf_op jit(solution)/shard_map/ppermute | solution.py:18
  177.6 4.3 %feature_image.1 = bf16[1024,768]{1,0:T(8,128)(2,1)} custom-call(s32[1]{0:T(128)} %bitcast.column_ref.refs_1_, bf16[2,64,1024]{2,1,0:T(8,128)(2,1)S(1)} %image_back_a.1.refs_0_.refs_3_, bf16[2,64,1024]{2,1,0:T(8,128)(2,1)S(1)} %image_back_b.1.refs_1_.refs_0_.refs_4_, bf16[2,64,1024]{2,1,0:T(8,128)(2,1)S(1)} %collective-permute-done.41.refs_2_.refs_1_.refs_5_, ...), custom_call_target="tpu_custom_call" | custom-call | flops 1610612736 | bytes 5242884 | tf_op jit(solution)/shard_map/feature_image/pallas_call | solution.py:36
  183.7 2.3 %collective-permute-start.56 = (bf16[64,768]{1,0:T(8,128)(2,1)S(1)}, bf16[64,768]{1,0:T(8,128)(2,1)S(1)}, u32[]{:S(2)}, u32[]{:S(2)}) collective-permute-start(bf16[64,768]{1,0:T(8,128)(2,1)S(1)} %get-tuple-element.133), channel_id=1, source_target_pairs={{0,64},{8,72},{16,80},{24,88},{32,96},{40,104},{48,112},{56,120},{... | collective-permute-start | bytes 294920 | tf_op jit(solution)/shard_map/ppermute | solution.py:18
  188.2 2.5 %feature_text.1 = bf16[1024,512]{1,0:T(8,128)(2,1)} custom-call(s32[1]{0:T(128)} %bitcast.column_ref.refs_1_, bf16[2,128,1024]{2,1,0:T(8,128)(2,1)S(1)} %stack_text_grads.1.refs_0_.refs_3_, bf16[2,128,1024]{2,1,0:T(8,128)(2,1)S(1)} %collective-permute-done.48.refs_1_.refs_4_, bf16[2,128,1024]{2,1,0:T(8,128)(2,1)S(1)} %collective-permute-done.49.refs_2_.refs_5_, ...), custom_call_target="tpu_custom_call" | custom-call | flops 1073741824 | bytes 4194308 | tf_op jit(solution)/shard_map/feature_text/pallas_call | solution.py:36
  (149 shorter events, 84.1 us)
Async XLA Ops:
  15.9 14.9 %collective-permute-start.2 = (bf16[2,128,1024]{2,1,0:T(8,128)(2,1)S(1)}, bf16[2,128,1024]{2,1,0:T(8,128)(2,1)S(1)}, u32[]{:S(2)}, u32[]{:S(2)}) collective-permute-start(bf16[2,128,1024]{2,1,0:T(8,128)(2,1)S(1)} %get-tuple-element.78), channel_id=1, source_target_pairs={{0,2},{1,3},{2,0},{3,1},{4,6},{5,7},{6,4},{7,5},{8,10},{9,11},{10,... | collective-permute-start | bytes 1572872 | tf_op jit(solution)/shard_map/ppermute | solution.py:18
  16.3 16.1 %collective-permute-start.3 = (bf16[2,128,1024]{2,1,0:T(8,128)(2,1)S(1)}, bf16[2,128,1024]{2,1,0:T(8,128)(2,1)S(1)}, u32[]{:S(2)}, u32[]{:S(2)}) collective-permute-start(bf16[2,128,1024]{2,1,0:T(8,128)(2,1)S(1)} %get-tuple-element.79), channel_id=1, source_target_pairs={{0,6},{1,7},{2,4},{3,5},{4,2},{5,3},{6,0},{7,1},{8,14},{9,15},{10,... | collective-permute-start | bytes 1572872 | tf_op jit(solution)/shard_map/ppermute | solution.py:18
  20.2 15.1 %collective-permute-start.4 = (bf16[128,1024]{1,0:T(8,128)(2,1)S(1)}, bf16[128,1024]{1,0:T(8,128)(2,1)S(1)}, u32[]{:S(2)}, u32[]{:S(2)}) collective-permute-start(bf16[128,1024]{1,0:T(8,128)(2,1)S(1)} %get-tuple-element.83), channel_id=1, source_target_pairs={{0,6},{1,7},{2,4},{3,5},{4,2},{5,3},{6,0},{7,1},{8,14},{9,15},{10,... | collective-permute-start | bytes 786440 | tf_op jit(solution)/shard_map/ppermute | solution.py:18
  22.2 13.2 %collective-permute-start.5 = (bf16[128,1024]{1,0:T(8,128)(2,1)S(1)}, bf16[128,1024]{1,0:T(8,128)(2,1)S(1)}, u32[]{:S(2)}, u32[]{:S(2)}) collective-permute-start(bf16[128,1024]{1,0:T(8,128)(2,1)S(1)} %get-tuple-element.84), channel_id=1, source_target_pairs={{0,2},{1,3},{2,0},{3,1},{4,6},{5,7},{6,4},{7,5},{8,10},{9,11},{10,... | collective-permute-start | bytes 786440 | tf_op jit(solution)/shard_map/ppermute | solution.py:18
  35.5 10.1 %collective-permute-start.8 = (bf16[2,64,1024]{2,1,0:T(8,128)(2,1)S(1)}, bf16[2,64,1024]{2,1,0:T(8,128)(2,1)S(1)}, u32[]{:S(2)}, u32[]{:S(2)}) collective-permute-start(bf16[2,64,1024]{2,1,0:T(8,128)(2,1)S(1)} %get-tuple-element.89), channel_id=1, source_target_pairs={{0,6},{1,7},{2,4},{3,5},{4,2},{5,3},{6,0},{7,1},{8,14},{9,15},{10,... | collective-permute-start | bytes 786440 | tf_op jit(solution)/shard_map/ppermute | solution.py:18
  43.0 12.3 %collective-permute-start.10 = (bf16[2,64,1024]{2,1,0:T(8,128)(2,1)S(1)}, bf16[2,64,1024]{2,1,0:T(8,128)(2,1)S(1)}, u32[]{:S(2)}, u32[]{:S(2)}) collective-permute-start(bf16[2,64,1024]{2,1,0:T(8,128)(2,1)S(1)} %get-tuple-element.90), channel_id=1, source_target_pairs={{0,2},{1,3},{2,0},{3,1},{4,6},{5,7},{6,4},{7,5},{8,10},{9,11},{10,... | collective-permute-start | bytes 786440 | tf_op jit(solution)/shard_map/ppermute | solution.py:18
  43.0 12.3 %collective-permute-start.11 = (bf16[2,64,1024]{2,1,0:T(8,128)(2,1)S(1)}, bf16[2,64,1024]{2,1,0:T(8,128)(2,1)S(1)}, u32[]{:S(2)}, u32[]{:S(2)}) collective-permute-start(bf16[2,64,1024]{2,1,0:T(8,128)(2,1)S(1)} %get-tuple-element.91), channel_id=1, source_target_pairs={{0,6},{1,7},{2,4},{3,5},{4,2},{5,3},{6,0},{7,1},{8,14},{9,15},{10,... | collective-permute-start | bytes 786440 | tf_op jit(solution)/shard_map/ppermute | solution.py:18
  46.3 12.1 %collective-permute-start.12 = (bf16[2,64,1024]{2,1,0:T(8,128)(2,1)S(1)}, bf16[2,64,1024]{2,1,0:T(8,128)(2,1)S(1)}, u32[]{:S(2)}, u32[]{:S(2)}) collective-permute-start(bf16[2,64,1024]{2,1,0:T(8,128)(2,1)S(1)} %image_x_a.1.refs_0_.refs_1_), channel_id=1, source_target_pairs={{0,1},{1,0},{2,3},{3,2},{4,5},{5,4},{6,7},{7,6},{8,9},{9,8},{10,11... | collective-permute-start | bytes 786440 | tf_op jit(solution)/shard_map/ppermute | solution.py:18
  50.8 18.2 %collective-permute-start.19 = (bf16[2,128,1024]{2,1,0:T(8,128)(2,1)S(1)}, bf16[2,128,1024]{2,1,0:T(8,128)(2,1)S(1)}, u32[]{:S(2)}, u32[]{:S(2)}) collective-permute-start(bf16[2,128,1024]{2,1,0:T(8,128)(2,1)S(1)} %stack_text.1.refs_0_.refs_4_), channel_id=1, source_target_pairs={{0,96},{8,104},{16,112},{24,120},{32,64},{40,72},{48,80},{56,88},{... | collective-permute-start | bytes 1572872 | tf_op jit(solution)/shard_map/ppermute | solution.py:18
  55.3 13.7 %collective-permute-start.18 = (bf16[2,128,1024]{2,1,0:T(8,128)(2,1)S(1)}, bf16[2,128,1024]{2,1,0:T(8,128)(2,1)S(1)}, u32[]{:S(2)}, u32[]{:S(2)}) collective-permute-start(bf16[2,128,1024]{2,1,0:T(8,128)(2,1)S(1)} %stack_text.1.refs_0_.refs_4_), channel_id=1, source_target_pairs={{0,32},{8,40},{16,48},{24,56},{32,0},{40,8},{48,16},{56,24},{64,96... | collective-permute-start | bytes 1572872 | tf_op jit(solution)/shard_map/ppermute | solution.py:18
  63.5 10.3 %collective-permute-start.21 = (bf16[2,64,1024]{2,1,0:T(8,128)(2,1)S(1)}, bf16[2,64,1024]{2,1,0:T(8,128)(2,1)S(1)}, u32[]{:S(2)}, u32[]{:S(2)}) collective-permute-start(bf16[2,64,1024]{2,1,0:T(8,128)(2,1)S(1)} %get-tuple-element.93.refs_0_.refs_1_), channel_id=1, source_target_pairs={{0,6},{1,7},{2,4},{3,5},{4,2},{5,3},{6,0},{7,1},{8,14},{9,15},{10,... | collective-permute-start | bytes 786440 | tf_op jit(solution)/shard_map/ppermute | solution.py:18
  69.0 13.1 %collective-permute-start.25 = (bf16[128,1024]{1,0:T(8,128)(2,1)S(1)}, bf16[128,1024]{1,0:T(8,128)(2,1)S(1)}, u32[]{:S(2)}, u32[]{:S(2)}) collective-permute-start(bf16[128,1024]{1,0:T(8,128)(2,1)S(1)} %get-tuple-element.99), channel_id=1, source_target_pairs={{0,32},{8,40},{16,48},{24,56},{32,0},{40,8},{48,16},{56,24},{64,96... | collective-permute-start | bytes 786440 | tf_op jit(solution)/shard_map/ppermute | solution.py:18
  71.0 11.1 %collective-permute-start.24 = (bf16[128,1024]{1,0:T(8,128)(2,1)S(1)}, bf16[128,1024]{1,0:T(8,128)(2,1)S(1)}, u32[]{:S(2)}, u32[]{:S(2)}) collective-permute-start(bf16[128,1024]{1,0:T(8,128)(2,1)S(1)} %get-tuple-element.96.refs_0_), channel_id=1, source_target_pairs={{0,96},{8,104},{16,112},{24,120},{32,64},{40,72},{48,80},{56,88},{... | collective-permute-start | bytes 786440 | tf_op jit(solution)/shard_map/ppermute | solution.py:18
  94.8 10.2 %collective-permute-start.29 = (bf16[128,1024]{1,0:T(8,128)(2,1)S(1)}, bf16[128,1024]{1,0:T(8,128)(2,1)S(1)}, u32[]{:S(2)}, u32[]{:S(2)}) collective-permute-start(bf16[128,1024]{1,0:T(8,128)(2,1)S(1)} %get-tuple-element.109), channel_id=1, source_target_pairs={{0,2},{1,3},{2,0},{3,1},{4,6},{5,7},{6,4},{7,5},{8,10},{9,11},{10,... | collective-permute-start | bytes 786440 | tf_op jit(solution)/shard_map/ppermute | solution.py:18
  94.9 10.1 %collective-permute-start.28 = (bf16[128,1024]{1,0:T(8,128)(2,1)S(1)}, bf16[128,1024]{1,0:T(8,128)(2,1)S(1)}, u32[]{:S(2)}, u32[]{:S(2)}) collective-permute-start(bf16[128,1024]{1,0:T(8,128)(2,1)S(1)} %get-tuple-element.104.refs_0_), channel_id=1, source_target_pairs={{0,6},{1,7},{2,4},{3,5},{4,2},{5,3},{6,0},{7,1},{8,14},{9,15},{10,... | collective-permute-start | bytes 786440 | tf_op jit(solution)/shard_map/ppermute | solution.py:18
  110.3 12.4 %collective-permute-start.36 = (bf16[2,128,1024]{2,1,0:T(8,128)(2,1)S(1)}, bf16[2,128,1024]{2,1,0:T(8,128)(2,1)S(1)}, u32[]{:S(2)}, u32[]{:S(2)}) collective-permute-start(bf16[2,128,1024]{2,1,0:T(8,128)(2,1)S(1)} %get-tuple-element.117), channel_id=1, source_target_pairs={{0,32},{8,40},{16,48},{24,56},{32,0},{40,8},{48,16},{56,24},{64,96... | collective-permute-start | bytes 1572872 | tf_op jit(solution)/shard_map/ppermute | solution.py:18
  110.4 13.7 %collective-permute-start.37 = (bf16[2,128,1024]{2,1,0:T(8,128)(2,1)S(1)}, bf16[2,128,1024]{2,1,0:T(8,128)(2,1)S(1)}, u32[]{:S(2)}, u32[]{:S(2)}) collective-permute-start(bf16[2,128,1024]{2,1,0:T(8,128)(2,1)S(1)} %get-tuple-element.118), channel_id=1, source_target_pairs={{0,96},{8,104},{16,112},{24,120},{32,64},{40,72},{48,80},{56,88},{... | collective-permute-start | bytes 1572872 | tf_op jit(solution)/shard_map/ppermute | solution.py:18
  116.2 9.9 %collective-permute-start.38 = (bf16[2,64,1024]{2,1,0:T(8,128)(2,1)S(1)}, bf16[2,64,1024]{2,1,0:T(8,128)(2,1)S(1)}, u32[]{:S(2)}, u32[]{:S(2)}) collective-permute-start(bf16[2,64,1024]{2,1,0:T(8,128)(2,1)S(1)} %image_grads_x_a.1.refs_0_.refs_1_), channel_id=1, source_target_pairs={{0,1},{1,0},{2,3},{3,2},{4,5},{5,4},{6,7},{7,6},{8,9},{9,8},{10,11... | collective-permute-start | bytes 786440 | tf_op jit(solution)/shard_map/ppermute | solution.py:18
  124.7 13.8 %collective-permute-start.40 = (bf16[2,64,1024]{2,1,0:T(8,128)(2,1)S(1)}, bf16[2,64,1024]{2,1,0:T(8,128)(2,1)S(1)}, u32[]{:S(2)}, u32[]{:S(2)}) collective-permute-start(bf16[2,64,1024]{2,1,0:T(8,128)(2,1)S(1)} %image_grads_x_b.1.refs_0_.refs_1_), channel_id=1, source_target_pairs={{0,1},{1,0},{2,3},{3,2},{4,5},{5,4},{6,7},{7,6},{8,9},{9,8},{10,11... | collective-permute-start | bytes 786440 | tf_op jit(solution)/shard_map/ppermute | solution.py:18
  126.4 14.3 %collective-permute-start.45 = (bf16[2,64,1024]{2,1,0:T(8,128)(2,1)S(1)}, bf16[2,64,1024]{2,1,0:T(8,128)(2,1)S(1)}, u32[]{:S(2)}, u32[]{:S(2)}) collective-permute-start(bf16[2,64,1024]{2,1,0:T(8,128)(2,1)S(1)} %image_back_a.1.refs_0_.refs_3_), channel_id=1, source_target_pairs={{0,4},{1,5},{2,6},{3,7},{4,0},{5,1},{6,2},{7,3},{8,12},{9,13},{10,... | collective-permute-start | bytes 786440 | tf_op jit(solution)/shard_map/ppermute | solution.py:18
  128.7 14.7 %collective-permute-start.43 = (bf16[2,64,1024]{2,1,0:T(8,128)(2,1)S(1)}, bf16[2,64,1024]{2,1,0:T(8,128)(2,1)S(1)}, u32[]{:S(2)}, u32[]{:S(2)}) collective-permute-start(bf16[2,64,1024]{2,1,0:T(8,128)(2,1)S(1)} %image_back_a.1.refs_0_.refs_3_), channel_id=1, source_target_pairs={{0,6},{1,7},{2,4},{3,5},{4,2},{5,3},{6,0},{7,1},{8,14},{9,15},{10,... | collective-permute-start | bytes 786440 | tf_op jit(solution)/shard_map/ppermute | solution.py:18
  129.9 14.0 %collective-permute-start.41 = (bf16[2,64,1024]{2,1,0:T(8,128)(2,1)S(1)}, bf16[2,64,1024]{2,1,0:T(8,128)(2,1)S(1)}, u32[]{:S(2)}, u32[]{:S(2)}) collective-permute-start(bf16[2,64,1024]{2,1,0:T(8,128)(2,1)S(1)} %image_back_a.1.refs_0_.refs_3_), channel_id=1, source_target_pairs={{0,2},{1,3},{2,0},{3,1},{4,6},{5,7},{6,4},{7,5},{8,10},{9,11},{10,... | collective-permute-start | bytes 786440 | tf_op jit(solution)/shard_map/ppermute | solution.py:18
  133.8 10.1 %collective-permute-start.47 = (bf16[128,1024]{1,0:T(8,128)(2,1)S(1)}, bf16[128,1024]{1,0:T(8,128)(2,1)S(1)}, u32[]{:S(2)}, u32[]{:S(2)}) collective-permute-start(bf16[128,1024]{1,0:T(8,128)(2,1)S(1)} %text_back.1.refs_0_.refs_4_), channel_id=1, source_target_pairs={{0,1},{1,0},{2,3},{3,2},{4,5},{5,4},{6,7},{7,6},{8,9},{9,8},{10,11... | collective-permute-start | bytes 786440 | tf_op jit(solution)/shard_map/ppermute | solution.py:18
  138.7 10.8 %collective-permute-start.46 = (bf16[2,64,1024]{2,1,0:T(8,128)(2,1)S(1)}, bf16[2,64,1024]{2,1,0:T(8,128)(2,1)S(1)}, u32[]{:S(2)}, u32[]{:S(2)}) collective-permute-start(bf16[2,64,1024]{2,1,0:T(8,128)(2,1)S(1)} %image_back_b.1.refs_1_.refs_0_.refs_4_), channel_id=1, source_target_pairs={{0,4},{1,5},{2,6},{3,7},{4,0},{5,1},{6,2},{7,3},{8,12},{9,13},{10,... | collective-permute-start | bytes 786440 | tf_op jit(solution)/shard_map/ppermute | solution.py:18
  140.6 12.5 %collective-permute-start.44 = (bf16[2,64,1024]{2,1,0:T(8,128)(2,1)S(1)}, bf16[2,64,1024]{2,1,0:T(8,128)(2,1)S(1)}, u32[]{:S(2)}, u32[]{:S(2)}) collective-permute-start(bf16[2,64,1024]{2,1,0:T(8,128)(2,1)S(1)} %image_back_b.1.refs_1_.refs_0_.refs_4_), channel_id=1, source_target_pairs={{0,6},{1,7},{2,4},{3,5},{4,2},{5,3},{6,0},{7,1},{8,14},{9,15},{10,... | collective-permute-start | bytes 786440 | tf_op jit(solution)/shard_map/ppermute | solution.py:18
  143.4 11.1 %collective-permute-start.42 = (bf16[2,64,1024]{2,1,0:T(8,128)(2,1)S(1)}, bf16[2,64,1024]{2,1,0:T(8,128)(2,1)}, u32[]{:S(2)}, u32[]{:S(2)}) collective-permute-start(bf16[2,64,1024]{2,1,0:T(8,128)(2,1)S(1)} %image_back_b.1.refs_1_.refs_0_.refs_4_), channel_id=1, source_target_pairs={{0,2},{1,3},{2,0},{3,1},{4,6},{5,7},{6,4},{7,5},{8,10},{9,11},{10,... | collective-permute-start | bytes 786440 | tf_op jit(solution)/shard_map/ppermute | solution.py:18
  144.0 17.4 %collective-permute-start.49 = (bf16[2,128,1024]{2,1,0:T(8,128)(2,1)S(1)}, bf16[2,128,1024]{2,1,0:T(8,128)(2,1)S(1)}, u32[]{:S(2)}, u32[]{:S(2)}) collective-permute-start(bf16[2,128,1024]{2,1,0:T(8,128)(2,1)S(1)} %stack_text_grads.1.refs_0_.refs_3_), channel_id=1, source_target_pairs={{0,6},{1,7},{2,4},{3,5},{4,2},{5,3},{6,0},{7,1},{8,14},{9,15},{10,... | collective-permute-start | bytes 1572872 | tf_op jit(solution)/shard_map/ppermute | solution.py:18
  145.6 15.8 %collective-permute-start.48 = (bf16[2,128,1024]{2,1,0:T(8,128)(2,1)S(1)}, bf16[2,128,1024]{2,1,0:T(8,128)(2,1)S(1)}, u32[]{:S(2)}, u32[]{:S(2)}) collective-permute-start(bf16[2,128,1024]{2,1,0:T(8,128)(2,1)S(1)} %stack_text_grads.1.refs_0_.refs_3_), channel_id=1, source_target_pairs={{0,2},{1,3},{2,0},{3,1},{4,6},{5,7},{6,4},{7,5},{8,10},{9,11},{10,... | collective-permute-start | bytes 1572872 | tf_op jit(solution)/shard_map/ppermute | solution.py:18
  163.7 9.4 %collective-permute-start.53 = (bf16[4,64,768]{2,1,0:T(8,128)(2,1)S(1)}, bf16[4,64,768]{2,1,0:T(8,128)(2,1)S(1)}, u32[]{:S(2)}, u32[]{:S(2)}) collective-permute-start(bf16[4,64,768]{2,1,0:T(8,128)(2,1)S(1)} %get-tuple-element.129), channel_id=1, source_target_pairs={{0,16},{8,24},{16,0},{24,8},{32,48},{40,56},{48,32},{56,40},{64,80... | collective-permute-start | bytes 1179656 | tf_op jit(solution)/shard_map/ppermute | solution.py:18
  173.4 10.3 %collective-permute-start.58 = (bf16[2,64,512]{2,1,0:T(8,128)(2,1)S(1)}, bf16[2,64,512]{2,1,0:T(8,128)(2,1)S(1)}, u32[]{:S(2)}, u32[]{:S(2)}) collective-permute-start(bf16[2,64,512]{2,1,0:T(8,128)(2,1)S(1)} %get-tuple-element.137), channel_id=1, source_target_pairs={{0,32},{8,40},{16,48},{24,56},{32,0},{40,8},{48,16},{56,24},{64,96... | collective-permute-start | bytes 393224 | tf_op jit(solution)/shard_map/ppermute | solution.py:18
  173.8 12.2 %collective-permute-start.59 = (bf16[2,64,512]{2,1,0:T(8,128)(2,1)S(1)}, bf16[2,64,512]{2,1,0:T(8,128)(2,1)S(1)}, u32[]{:S(2)}, u32[]{:S(2)}) collective-permute-start(bf16[2,64,512]{2,1,0:T(8,128)(2,1)S(1)} %get-tuple-element.138), channel_id=1, source_target_pairs={{0,96},{8,104},{16,112},{24,120},{32,64},{40,72},{48,80},{56,88},{... | collective-permute-start | bytes 393224 | tf_op jit(solution)/shard_map/ppermute | solution.py:18
  175.3 10.7 %collective-permute-start.60 = (bf16[2,64,512]{2,1,0:T(8,128)(2,1)S(1)}, bf16[2,64,512]{2,1,0:T(8,128)(2,1)S(1)}, u32[]{:S(2)}, u32[]{:S(2)}) collective-permute-start(bf16[2,64,512]{2,1,0:T(8,128)(2,1)S(1)} %get-tuple-element.139), channel_id=1, source_target_pairs={{0,64},{8,72},{16,80},{24,88},{32,96},{40,104},{48,112},{56,120},{... | collective-permute-start | bytes 393224 | tf_op jit(solution)/shard_map/ppermute | solution.py:18
  (38 other events, 286.2 us)

commit v9 on v8

--- a/solution.py
+++ b/solution.py
@@ -508,13 +508,16 @@
     (d0,) = call("text_back", text_back, [shape(*one)], (p0, p2_got, txt_emb), after=e01_a)
     d1 = swap(d0, "mp", 1)
     (e01_b,) = call("image_back_b", back_half, [shape(*half)], (x_b, y_b, emb_b), after=d0)
-    e23_b, e67_b, e45_b = swap(e01_b, "mp", 2), swap(e01_b, "mp", 6), swap(e01_b, "mp", 4)
+    e23_b, e67_b = swap(e01_b, "mp", 2), swap(e01_b, "mp", 6)
+    e2_b, e7_b = call("cut_image_grads", cut, [shape(*own_half)] * 2, (e23_b, e67_b))
+    e4_b, e5_b = swap(e2_b, "mp", 6), swap(e7_b, "mp", 2)
+    (e45_b,) = call("stack_image_grads", stack, [shape(*half)], (e4_b, e5_b))
 
     (d01,) = call("stack_text_grads", stack, [shape(*two)], (d0, d1), after=(e01_b, e23_a, e67_a, e45_a))
     d23, d67 = swap(d01, "mp", 2), swap(d01, "mp", 6)
 
     e_all = (e01_a, e01_b, e23_a, e23_b, e67_a, e67_b, e45_a, e45_b)
-    same, other = weight_part("weight_image", column, place, e_all, 2, img_feat, d01, ORDER_COST // 4)
+    same, other = weight_part("weight_image", column, place, e_all, 2, img_feat, d01)
     d2, d7 = call("cut_text_grads", cut, [shape(*one)] * 2, (d23, d67), ORDER_COST, after=same)
     d4, d5 = swap(d2, "mp", 6), swap(d7, "mp", 2)
     image_chip = chip_weight_y("weight_image_chip", same, other)

time: 193 us -> 197 us (1.021)
  waiting for transfers between devices: 73.3 us -> 80.3 us
    ppermute x62 -> x63, waiting for transfers between devices: 73.3 us -> 80.3 us  [swap(): return lax.ppermute(value, axis, [(i, i ^ offset) for i in range(count)])]
    ppermute x62 -> x63, starting transfers between devices: 74.9 us -> 73 us  [swap(): return lax.ppermute(value, axis, [(i, i ^ offset) for i in range(count)])]
    pallas_call x39 -> x41, Pallas kernels: 28.5 us -> 28.3 us  [call(): pl.pallas_call(run, out_shape=outs, in_specs=specs, scratch_shapes=list(s...]
  transfers between devices with their start and end apart: 62 -> 63, of which waited for: 35 -> 36; matrix products, arithmetic and copies ran while one was open for 0% -> 0% of each run, Pallas kernels for 15% -> 15%
where the time goes in v9:
time: 197 us
  waiting for transfers between devices  80.3 us (41%)
  starting transfers between devices  73 us (37%)
  Pallas kernels  37.4 us (19%)
  local copies, waits for them, and re-layouts  3.87 us (2%)
  between operations  2.36 us (1%)
    ppermute x63, waiting for transfers between devices, swap(): return lax.ppermute(value, axis, [(i, i ^ offset) for i in range(count)])  80.3 us
    ppermute x63, starting transfers between devices, swap(): return lax.ppermute(value, axis, [(i, i ^ offset) for i in range(count)])  73 us
    pallas_call x41, Pallas kernels, call(): pl.pallas_call(run, out_shape=outs, in_specs=specs, scratch_shapes=list(s...  28.3 us
    pallas_call x2, Pallas kernels, pair_call(): pl.pallas_call(body, in_specs=[smem, smem] + [vmem] * len(arrays), out_sh...  9.11 us
  transfers between devices with their start and end apart: 63, of which 36 were waited for; matrix products, arithmetic and copies ran while one was open for 0% of the time, Pallas kernels for 15%

profile of v9, /device:TPU:8, one launch (start us, length us, event | category | flops | bytes accessed | tf_op | source)
XLA Modules:
  0.0 196.9 jit_solution(15272729542133403467)
XLA Ops:
  5.2 2.8 %collective-permute-start = (bf16[128,1024]{1,0:T(8,128)(2,1)S(1)}, bf16[128,1024]{1,0:T(8,128)(2,1)S(1)}, u32[]{:S(2)}, u32[]{:S(2)}) collective-permute-start(bf16[128,1024]{1,0:T(8,128)(2,1)S(1)} %get-tuple-element.78), channel_id=1, source_target_pairs={{0,6},{1,7},{2,4},{3,5},{4,2},{5,3},{6,0},{7,1},{8,14},{9,15},{10,... | collective-permute-start | bytes 786440 | tf_op jit(solution)/shard_map/ppermute | solution.py:18
  8.2 6.3 %collective-permute-done.r4 = bf16[128,1024]{1,0:T(8,128)(2,1)S(1)} collective-permute-done((bf16[128,1024]{1,0:T(8,128)(2,1)S(1)}, bf16[128,1024]{1,0:T(8,128)(2,1)S(1)}, u32[]{:S(2)}, u32[]{:S(2)}) %collective-permute-start) | collective-permute-done | bytes 262176 | tf_op jit(solution)/shard_map/ppermute | solution.py:18
  17.6 2.6 %embed_image.1 = (bf16[2,128,1024]{2,1,0:T(8,128)(2,1)S(1)}, bf16[2,128,1024]{2,1,0:T(8,128)(2,1)S(1)}, bf16[2,128,1024]{2,1,0:T(8,128)(2,1)S(1)}, bf16[128,1024]{1,0:T(8,128)(2,1)S(1)}, bf16[128,1024]{1,0:T(8,128)(2,1)S(1)}) custom-call(s32[1]{0:T(128)} %bitcast.column_ref.refs_1_, bf16[1024,768]{1,0:T(8,128)(2,1)S(1)} %copy-done.2, ...), custom_call_target="tpu_custom_call" | custom-call | flops 1610612736 | bytes 5242884 | tf_op jit(solution)/shard_map/embed_image/pallas_call | solution.py:36
  22.8 8.1 %collective-permute-done.2.t23 = bf16[2,128,1024]{2,1,0:T(8,128)(2,1)S(1)} collective-permute-done((bf16[2,128,1024]{2,1,0:T(8,128)(2,1)S(1)}, bf16[2,128,1024]{2,1,0:T(8,128)(2,1)S(1)}, u32[]{:S(2)}, u32[]{:S(2)}) %collective-permute-start.2) | collective-permute-done | bytes 524320 | tf_op jit(solution)/shard_map/ppermute | solution.py:18
  32.5 2.4 %collective-permute-start.6 = (bf16[128,1024]{1,0:T(8,128)(2,1)S(1)}, bf16[128,1024]{1,0:T(8,128)(2,1)S(1)}, u32[]{:S(2)}, u32[]{:S(2)}) collective-permute-start(bf16[128,1024]{1,0:T(8,128)(2,1)S(1)} %get-tuple-element.82.refs_0_), channel_id=1, source_target_pairs={{0,1},{1,0},{2,3},{3,2},{4,5},{5,4},{6,7},{7,6},{8,9},{9,8},{10,11... | collective-permute-start | bytes 786440 | tf_op jit(solution)/shard_map/ppermute | solution.py:18
  37.4 4.5 %collective-permute-done.6.refs_2_ = bf16[128,1024]{1,0:T(8,128)(2,1)S(1)} collective-permute-done((bf16[128,1024]{1,0:T(8,128)(2,1)S(1)}, bf16[128,1024]{1,0:T(8,128)(2,1)S(1)}, u32[]{:S(2)}, u32[]{:S(2)}) %collective-permute-start.6) | collective-permute-done | bytes 262176 | tf_op jit(solution)/shard_map/ppermute | solution.py:18
  46.3 2.4 %collective-permute-start.12 = (bf16[2,64,1024]{2,1,0:T(8,128)(2,1)S(1)}, bf16[2,64,1024]{2,1,0:T(8,128)(2,1)S(1)}, u32[]{:S(2)}, u32[]{:S(2)}) collective-permute-start(bf16[2,64,1024]{2,1,0:T(8,128)(2,1)S(1)} %image_x_a.1.refs_0_.refs_1_), channel_id=1, source_target_pairs={{0,1},{1,0},{2,3},{3,2},{4,5},{5,4},{6,7},{7,6},{8,9},{9,8},{10,11... | collective-permute-start | bytes 786440 | tf_op jit(solution)/shard_map/ppermute | solution.py:18
  50.8 4.5 %collective-permute-start.19 = (bf16[2,128,1024]{2,1,0:T(8,128)(2,1)S(1)}, bf16[2,128,1024]{2,1,0:T(8,128)(2,1)S(1)}, u32[]{:S(2)}, u32[]{:S(2)}) collective-permute-start(bf16[2,128,1024]{2,1,0:T(8,128)(2,1)S(1)} %stack_text.1.refs_0_.refs_4_), channel_id=1, source_target_pairs={{0,96},{8,104},{16,112},{24,120},{32,64},{40,72},{48,80},{56,88},{... | collective-permute-start | bytes 1572872 | tf_op jit(solution)/shard_map/ppermute | solution.py:18
  55.4 3.0 %collective-permute-start.13 = (bf16[2,64,1024]{2,1,0:T(8,128)(2,1)S(1)}, bf16[2,64,1024]{2,1,0:T(8,128)(2,1)S(1)}, u32[]{:S(2)}, u32[]{:S(2)}) collective-permute-start(bf16[2,64,1024]{2,1,0:T(8,128)(2,1)S(1)} %image_x_b.1.refs_0_.refs_1_), channel_id=1, source_target_pairs={{0,1},{1,0},{2,3},{3,2},{4,5},{5,4},{6,7},{7,6},{8,9},{9,8},{10,11... | collective-permute-start | bytes 786440 | tf_op jit(solution)/shard_map/ppermute | solution.py:18
  59.9 3.5 %collective-permute-done.13.refs_2_ = bf16[2,64,1024]{2,1,0:T(8,128)(2,1)S(1)} collective-permute-done((bf16[2,64,1024]{2,1,0:T(8,128)(2,1)S(1)}, bf16[2,64,1024]{2,1,0:T(8,128)(2,1)S(1)}, u32[]{:S(2)}, u32[]{:S(2)}) %collective-permute-start.13) | collective-permute-done | bytes 262176 | tf_op jit(solution)/shard_map/ppermute | solution.py:18
  64.5 2.3 %collective-permute-done.15.refs_2_.refs_4_ = bf16[2,64,1024]{2,1,0:T(8,128)(2,1)S(1)} collective-permute-done((bf16[2,64,1024]{2,1,0:T(8,128)(2,1)S(1)}, bf16[2,64,1024]{2,1,0:T(8,128)(2,1)S(1)}, u32[]{:S(2)}, u32[]{:S(2)}) %collective-permute-start.15) | collective-permute-done | bytes 262176 | tf_op jit(solution)/shard_map/ppermute | solution.py:18
  74.7 2.5 %collective-permute-start.22 = (bf16[64,1024]{1,0:T(8,128)(2,1)S(1)}, bf16[64,1024]{1,0:T(8,128)(2,1)S(1)}, u32[]{:S(2)}, u32[]{:S(2)}) collective-permute-start(bf16[64,1024]{1,0:T(8,128)(2,1)S(1)} %get-tuple-element.99), channel_id=1, source_target_pairs={{0,6},{1,7},{2,4},{3,5},{4,2},{5,3},{6,0},{7,1},{8,14},{9,15},{10,... | collective-permute-start | bytes 393224 | tf_op jit(solution)/shard_map/ppermute | solution.py:18
  77.1 2.8 %collective-permute-done.16.refs_0_.refs_6_ = bf16[64,1024]{1,0:T(8,128)(2,1)S(1)} collective-permute-done((bf16[64,1024]{1,0:T(8,128)(2,1)S(1)}, bf16[64,1024]{1,0:T(8,128)(2,1)S(1)}, u32[]{:S(2)}, u32[]{:S(2)}) %collective-permute-start.16) | collective-permute-done | bytes 131104 | tf_op jit(solution)/shard_map/ppermute | solution.py:18
  83.9 4.0 %pairs_even.1 = (bf16[1024,1024]{1,0:T(8,128)(2,1)S(1)}, bf16[1024,1024]{1,0:T(8,128)(2,1)S(1)}, bf16[1024,1024]{1,0:T(8,128)(2,1)S(1)}) custom-call(f32[1]{0:T(128)S(6)} %exp.3.scale_ref, f32[1]{0:T(128)S(6)} %copy.11.bias_ref, bf16[8,128,1024]{2,1,0:T(8,128)(2,1)S(1)} %collect.1.texts.refs_3_, bf16[2,64,1024]{2,1,0:T(8,128)(2,1)S(1)} %get-tuple-element.94.refs_0_, ...), custom_call_target="tpu_custom_call" | custom-call | flops 2147483648 | bytes 10485760 | tf_op jit(solution)/shard_map/pairs_even/pallas_call | solution.py:183
  87.8 5.2 %pairs_odd.1 = (bf16[1024,1024]{1,0:T(8,128)(2,1)S(1)}, bf16[8,128,1024]{2,1,0:T(8,128)(2,1)S(1)}) custom-call(f32[1]{0:T(128)S(6)} %exp.3.scale_ref, f32[1]{0:T(128)S(6)} %copy.11.bias_ref, bf16[8,128,1024]{2,1,0:T(8,128)(2,1)S(1)} %collective-permute-done.26.texts.refs_4_, bf16[1024,1024]{1,0:T(8,128)(2,1)S(1)} %get-tuple-element.102.image_all.refs_2_, ...), custom_call_target="tpu_custom_call" | custom-call | flops 4294967296 | bytes 10485760 | tf_op jit(solution)/shard_map/pairs_odd/pallas_call | solution.py:183
  96.2 2.5 %text_grads_even.1.even.refs_1_ = bf16[8,128,1024]{2,1,0:T(8,128)(2,1)S(1)} custom-call(bf16[128,1024]{1,0:T(8,128)(2,1)S(1)} %get-tuple-element.106.refs_0_, bf16[1024,1024]{1,0:T(8,128)(2,1)S(1)} %get-tuple-element.107.refs_1_, bf16[1024,1024]{1,0:T(8,128)(2,1)S(1)} %get-tuple-element.102.image_all.refs_2_), custom_call_target="tpu_custom_call" | custom-call | flops 2147483648 | bytes 6553600 | tf_op jit(solution)/shard_map/text_grads_even/pallas_call | solution.py:36
  98.9 2.1 %collective-permute-start.31 = (bf16[128,1024]{1,0:T(8,128)(2,1)S(1)}, bf16[128,1024]{1,0:T(8,128)(2,1)S(1)}, u32[]{:S(2)}, u32[]{:S(2)}) collective-permute-start(bf16[128,1024]{1,0:T(8,128)(2,1)S(1)} %get-tuple-element.113), channel_id=1, source_target_pairs={{0,32},{8,40},{16,48},{24,56},{32,0},{40,8},{48,16},{56,24},{64,96... | collective-permute-start | bytes 786440 | tf_op jit(solution)/shard_map/ppermute | solution.py:18
  101.4 3.6 %pairs_near_images.1 = (bf16[2,128,1024]{2,1,0:T(8,128)(2,1)S(1)}, bf16[2,128,1024]{2,1,0:T(8,128)(2,1)S(1)}, bf16[2,128,1024]{2,1,0:T(8,128)(2,1)S(1)}) custom-call(bf16[128,1024]{1,0:T(8,128)(2,1)S(1)} %get-tuple-element.108.refs_0_, bf16[1024,1024]{1,0:T(8,128)(2,1)S(1)} %get-tuple-element.103._.refs_1_, ...), custom_call_target="tpu_custom_call" | custom-call | flops 3221225472 | bytes 10223616 | tf_op jit(solution)/shard_map/pairs_near_images/pallas_call | solution.py:36
  107.6 2.3 %collective-permute-done.30.refs_3_ = bf16[128,1024]{1,0:T(8,128)(2,1)S(1)} collective-permute-done((bf16[128,1024]{1,0:T(8,128)(2,1)S(1)}, bf16[128,1024]{1,0:T(8,128)(2,1)S(1)}, u32[]{:S(2)}, u32[]{:S(2)}) %collective-permute-start.30) | collective-permute-done | bytes 262176 | tf_op jit(solution)/shard_map/ppermute | solution.py:18
  116.2 3.0 %collective-permute-start.38 = (bf16[2,64,1024]{2,1,0:T(8,128)(2,1)S(1)}, bf16[2,64,1024]{2,1,0:T(8,128)(2,1)S(1)}, u32[]{:S(2)}, u32[]{:S(2)}) collective-permute-start(bf16[2,64,1024]{2,1,0:T(8,128)(2,1)S(1)} %image_grads_x_a.1.refs_0_.refs_1_), channel_id=1, source_target_pairs={{0,1},{1,0},{2,3},{3,2},{4,5},{5,4},{6,7},{7,6},{8,9},{9,8},{10,11... | collective-permute-start | bytes 786440 | tf_op jit(solution)/shard_map/ppermute | solution.py:18
  126.4 2.3 %collective-permute-start.45 = (bf16[2,64,1024]{2,1,0:T(8,128)(2,1)S(1)}, bf16[2,64,1024]{2,1,0:T(8,128)(2,1)S(1)}, u32[]{:S(2)}, u32[]{:S(2)}) collective-permute-start(bf16[2,64,1024]{2,1,0:T(8,128)(2,1)S(1)} %image_back_a.1.refs_0_.refs_3_), channel_id=1, source_target_pairs={{0,4},{1,5},{2,6},{3,7},{4,0},{5,1},{6,2},{7,3},{8,12},{9,13},{10,... | collective-permute-start | bytes 786440 | tf_op jit(solution)/shard_map/ppermute | solution.py:18
  129.9 3.6 %collective-permute-done.39.refs_2_ = bf16[128,1024]{1,0:T(8,128)(2,1)S(1)} collective-permute-done((bf16[128,1024]{1,0:T(8,128)(2,1)S(1)}, bf16[128,1024]{1,0:T(8,128)(2,1)S(1)}, u32[]{:S(2)}, u32[]{:S(2)}) %collective-permute-start.39) | collective-permute-done | bytes 262176 | tf_op jit(solution)/shard_map/ppermute | solution.py:18
  135.4 3.0 %collective-permute-done.40.refs_2_ = bf16[2,64,1024]{2,1,0:T(8,128)(2,1)S(1)} collective-permute-done((bf16[2,64,1024]{2,1,0:T(8,128)(2,1)S(1)}, bf16[2,64,1024]{2,1,0:T(8,128)(2,1)S(1)}, u32[]{:S(2)}, u32[]{:S(2)}) %collective-permute-start.40) | collective-permute-done | bytes 262176 | tf_op jit(solution)/shard_map/ppermute | solution.py:18
  144.1 5.1 %collective-permute-done.44.other.refs_5_.refs_8_ = bf16[2,64,1024]{2,1,0:T(8,128)(2,1)S(1)} collective-permute-done((bf16[2,64,1024]{2,1,0:T(8,128)(2,1)S(1)}, bf16[2,64,1024]{2,1,0:T(8,128)(2,1)S(1)}, u32[]{:S(2)}, u32[]{:S(2)}) %collective-permute-start.44) | collective-permute-done | bytes 262176 | tf_op jit(solution)/shard_map/ppermute | solution.py:18
  152.0 6.8 %collective-permute-done.46.first = bf16[64,1024]{1,0:T(8,128)(2,1)S(1)} collective-permute-done((bf16[64,1024]{1,0:T(8,128)(2,1)}, bf16[64,1024]{1,0:T(8,128)(2,1)S(1)}, u32[]{:S(2)}, u32[]{:S(2)}) %collective-permute-start.46) | collective-permute-done | bytes 131104 | tf_op jit(solution)/shard_map/ppermute | solution.py:18
  161.6 2.1 %weight_image.1 = (bf16[8,64,768]{2,1,0:T(8,128)(2,1)S(1)}, bf16[8,64,768]{2,1,0:T(8,128)(2,1)S(1)}) custom-call(bf16[2,128,1024]{2,1,0:T(8,128)(2,1)S(1)} %stack_text_grads.1.refs_0_.refs_3_, s32[1]{0:T(128)} %bitcast.column_ref.refs_1_, s32[1]{0:T(128)} %bitcast.1.refs_2_, bf16[2,64,1024]{2,1,0:T(8,128)(2,1)S(1)} %image_back_a.1.refs_0_.refs_3_, ...), custom_call_target="tpu_custom_call" | custom-call | flops 1610612736 | bytes 5767176 | tf_op jit(solution)/shard_map/weight_image/pallas_call | solution.py:36
  168.3 5.5 %collective-permute-done.51.refs_3_.refs_6_ = bf16[128,1024]{1,0:T(8,128)(2,1)S(1)} collective-permute-done((bf16[128,1024]{1,0:T(8,128)(2,1)S(1)}, bf16[128,1024]{1,0:T(8,128)(2,1)S(1)}, u32[]{:S(2)}, u32[]{:S(2)}) %collective-permute-start.51) | collective-permute-done | bytes 262176 | tf_op jit(solution)/shard_map/ppermute | solution.py:18
  175.4 2.3 %collective-permute-done.54.got = bf16[4,64,768]{2,1,0:T(8,128)(2,1)S(1)} collective-permute-done((bf16[4,64,768]{2,1,0:T(8,128)(2,1)S(1)}, bf16[4,64,768]{2,1,0:T(8,128)(2,1)S(1)}, u32[]{:S(2)}, u32[]{:S(2)}) %collective-permute-start.54) | collective-permute-done | bytes 393248 | tf_op jit(solution)/shard_map/ppermute | solution.py:18
  178.7 3.2 %collective-permute-start.60 = (bf16[2,64,512]{2,1,0:T(8,128)(2,1)S(1)}, bf16[2,64,512]{2,1,0:T(8,128)(2,1)S(1)}, u32[]{:S(2)}, u32[]{:S(2)}) collective-permute-start(bf16[2,64,512]{2,1,0:T(8,128)(2,1)S(1)} %get-tuple-element.142), channel_id=1, source_target_pairs={{0,96},{8,104},{16,112},{24,120},{32,64},{40,72},{48,80},{56,88},{... | collective-permute-start | bytes 393224 | tf_op jit(solution)/shard_map/ppermute | solution.py:18
  183.3 3.4 %feature_image.1 = bf16[1024,768]{1,0:T(8,128)(2,1)} custom-call(s32[1]{0:T(128)} %bitcast.column_ref.refs_1_, bf16[2,64,1024]{2,1,0:T(8,128)(2,1)S(1)} %image_back_a.1.refs_0_.refs_3_, bf16[2,64,1024]{2,1,0:T(8,128)(2,1)S(1)} %image_back_b.1.refs_1_.refs_0_.refs_4_, bf16[2,64,1024]{2,1,0:T(8,128)(2,1)S(1)} %collective-permute-done.41.refs_2_.refs_1_.refs_5_, ...), custom_call_target="tpu_custom_call" | custom-call | flops 1610612736 | bytes 5242884 | tf_op jit(solution)/shard_map/feature_image/pallas_call | solution.py:36
  186.7 2.7 %collective-permute-start.56 = (bf16[64,768]{1,0:T(8,128)(2,1)S(1)}, bf16[64,768]{1,0:T(8,128)(2,1)S(1)}, u32[]{:S(2)}, u32[]{:S(2)}) collective-permute-start(bf16[64,768]{1,0:T(8,128)(2,1)S(1)} %get-tuple-element.136), channel_id=1, source_target_pairs={{0,96},{8,104},{16,112},{24,120},{32,64},{40,72},{48,80},{56,88},{... | collective-permute-start | bytes 294920 | tf_op jit(solution)/shard_map/ppermute | solution.py:18
  191.5 2.5 %feature_text.1 = bf16[1024,512]{1,0:T(8,128)(2,1)} custom-call(s32[1]{0:T(128)} %bitcast.column_ref.refs_1_, bf16[2,128,1024]{2,1,0:T(8,128)(2,1)S(1)} %stack_text_grads.1.refs_0_.refs_3_, bf16[2,128,1024]{2,1,0:T(8,128)(2,1)S(1)} %collective-permute-done.49.refs_1_.refs_4_, bf16[2,128,1024]{2,1,0:T(8,128)(2,1)S(1)} %collective-permute-done.50.refs_2_.refs_5_, ...), custom_call_target="tpu_custom_call" | custom-call | flops 1073741824 | bytes 4194308 | tf_op jit(solution)/shard_map/feature_text/pallas_call | solution.py:36
  (153 shorter events, 81.6 us)
Async XLA Ops:
  5.2 9.3 %collective-permute-start = (bf16[128,1024]{1,0:T(8,128)(2,1)S(1)}, bf16[128,1024]{1,0:T(8,128)(2,1)S(1)}, u32[]{:S(2)}, u32[]{:S(2)}) collective-permute-start(bf16[128,1024]{1,0:T(8,128)(2,1)S(1)} %get-tuple-element.78), channel_id=1, source_target_pairs={{0,6},{1,7},{2,4},{3,5},{4,2},{5,3},{6,0},{7,1},{8,14},{9,15},{10,... | collective-permute-start | bytes 786440 | tf_op jit(solution)/shard_map/ppermute | solution.py:18
  15.9 14.9 %collective-permute-start.2 = (bf16[2,128,1024]{2,1,0:T(8,128)(2,1)S(1)}, bf16[2,128,1024]{2,1,0:T(8,128)(2,1)S(1)}, u32[]{:S(2)}, u32[]{:S(2)}) collective-permute-start(bf16[2,128,1024]{2,1,0:T(8,128)(2,1)S(1)} %get-tuple-element.80), channel_id=1, source_target_pairs={{0,2},{1,3},{2,0},{3,1},{4,6},{5,7},{6,4},{7,5},{8,10},{9,11},{10,... | collective-permute-start | bytes 1572872 | tf_op jit(solution)/shard_map/ppermute | solution.py:18
  16.3 16.1 %collective-permute-start.3 = (bf16[2,128,1024]{2,1,0:T(8,128)(2,1)S(1)}, bf16[2,128,1024]{2,1,0:T(8,128)(2,1)S(1)}, u32[]{:S(2)}, u32[]{:S(2)}) collective-permute-start(bf16[2,128,1024]{2,1,0:T(8,128)(2,1)S(1)} %get-tuple-element.81), channel_id=1, source_target_pairs={{0,6},{1,7},{2,4},{3,5},{4,2},{5,3},{6,0},{7,1},{8,14},{9,15},{10,... | collective-permute-start | bytes 1572872 | tf_op jit(solution)/shard_map/ppermute | solution.py:18
  20.2 15.1 %collective-permute-start.4 = (bf16[128,1024]{1,0:T(8,128)(2,1)S(1)}, bf16[128,1024]{1,0:T(8,128)(2,1)S(1)}, u32[]{:S(2)}, u32[]{:S(2)}) collective-permute-start(bf16[128,1024]{1,0:T(8,128)(2,1)S(1)} %get-tuple-element.85), channel_id=1, source_target_pairs={{0,6},{1,7},{2,4},{3,5},{4,2},{5,3},{6,0},{7,1},{8,14},{9,15},{10,... | collective-permute-start | bytes 786440 | tf_op jit(solution)/shard_map/ppermute | solution.py:18
  22.2 13.2 %collective-permute-start.5 = (bf16[128,1024]{1,0:T(8,128)(2,1)S(1)}, bf16[128,1024]{1,0:T(8,128)(2,1)S(1)}, u32[]{:S(2)}, u32[]{:S(2)}) collective-permute-start(bf16[128,1024]{1,0:T(8,128)(2,1)S(1)} %get-tuple-element.86), channel_id=1, source_target_pairs={{0,2},{1,3},{2,0},{3,1},{4,6},{5,7},{6,4},{7,5},{8,10},{9,11},{10,... | collective-permute-start | bytes 786440 | tf_op jit(solution)/shard_map/ppermute | solution.py:18
  32.5 9.3 %collective-permute-start.6 = (bf16[128,1024]{1,0:T(8,128)(2,1)S(1)}, bf16[128,1024]{1,0:T(8,128)(2,1)S(1)}, u32[]{:S(2)}, u32[]{:S(2)}) collective-permute-start(bf16[128,1024]{1,0:T(8,128)(2,1)S(1)} %get-tuple-element.82.refs_0_), channel_id=1, source_target_pairs={{0,1},{1,0},{2,3},{3,2},{4,5},{5,4},{6,7},{7,6},{8,9},{9,8},{10,11... | collective-permute-start | bytes 786440 | tf_op jit(solution)/shard_map/ppermute | solution.py:18
  35.5 10.1 %collective-permute-start.8 = (bf16[2,64,1024]{2,1,0:T(8,128)(2,1)S(1)}, bf16[2,64,1024]{2,1,0:T(8,128)(2,1)S(1)}, u32[]{:S(2)}, u32[]{:S(2)}) collective-permute-start(bf16[2,64,1024]{2,1,0:T(8,128)(2,1)S(1)} %get-tuple-element.91), channel_id=1, source_target_pairs={{0,6},{1,7},{2,4},{3,5},{4,2},{5,3},{6,0},{7,1},{8,14},{9,15},{10,... | collective-permute-start | bytes 786440 | tf_op jit(solution)/shard_map/ppermute | solution.py:18
  43.0 12.3 %collective-permute-start.10 = (bf16[2,64,1024]{2,1,0:T(8,128)(2,1)S(1)}, bf16[2,64,1024]{2,1,0:T(8,128)(2,1)S(1)}, u32[]{:S(2)}, u32[]{:S(2)}) collective-permute-start(bf16[2,64,1024]{2,1,0:T(8,128)(2,1)S(1)} %get-tuple-element.92), channel_id=1, source_target_pairs={{0,2},{1,3},{2,0},{3,1},{4,6},{5,7},{6,4},{7,5},{8,10},{9,11},{10,... | collective-permute-start | bytes 786440 | tf_op jit(solution)/shard_map/ppermute | solution.py:18
  43.0 12.3 %collective-permute-start.11 = (bf16[2,64,1024]{2,1,0:T(8,128)(2,1)S(1)}, bf16[2,64,1024]{2,1,0:T(8,128)(2,1)S(1)}, u32[]{:S(2)}, u32[]{:S(2)}) collective-permute-start(bf16[2,64,1024]{2,1,0:T(8,128)(2,1)S(1)} %get-tuple-element.93), channel_id=1, source_target_pairs={{0,6},{1,7},{2,4},{3,5},{4,2},{5,3},{6,0},{7,1},{8,14},{9,15},{10,... | collective-permute-start | bytes 786440 | tf_op jit(solution)/shard_map/ppermute | solution.py:18
  46.3 12.1 %collective-permute-start.12 = (bf16[2,64,1024]{2,1,0:T(8,128)(2,1)S(1)}, bf16[2,64,1024]{2,1,0:T(8,128)(2,1)S(1)}, u32[]{:S(2)}, u32[]{:S(2)}) collective-permute-start(bf16[2,64,1024]{2,1,0:T(8,128)(2,1)S(1)} %image_x_a.1.refs_0_.refs_1_), channel_id=1, source_target_pairs={{0,1},{1,0},{2,3},{3,2},{4,5},{5,4},{6,7},{7,6},{8,9},{9,8},{10,11... | collective-permute-start | bytes 786440 | tf_op jit(solution)/shard_map/ppermute | solution.py:18
  50.8 18.2 %collective-permute-start.19 = (bf16[2,128,1024]{2,1,0:T(8,128)(2,1)S(1)}, bf16[2,128,1024]{2,1,0:T(8,128)(2,1)S(1)}, u32[]{:S(2)}, u32[]{:S(2)}) collective-permute-start(bf16[2,128,1024]{2,1,0:T(8,128)(2,1)S(1)} %stack_text.1.refs_0_.refs_4_), channel_id=1, source_target_pairs={{0,96},{8,104},{16,112},{24,120},{32,64},{40,72},{48,80},{56,88},{... | collective-permute-start | bytes 1572872 | tf_op jit(solution)/shard_map/ppermute | solution.py:18
  55.3 13.7 %collective-permute-start.18 = (bf16[2,128,1024]{2,1,0:T(8,128)(2,1)S(1)}, bf16[2,128,1024]{2,1,0:T(8,128)(2,1)S(1)}, u32[]{:S(2)}, u32[]{:S(2)}) collective-permute-start(bf16[2,128,1024]{2,1,0:T(8,128)(2,1)S(1)} %stack_text.1.refs_0_.refs_4_), channel_id=1, source_target_pairs={{0,32},{8,40},{16,48},{24,56},{32,0},{40,8},{48,16},{56,24},{64,96... | collective-permute-start | bytes 1572872 | tf_op jit(solution)/shard_map/ppermute | solution.py:18
  63.5 10.3 %collective-permute-start.21 = (bf16[2,64,1024]{2,1,0:T(8,128)(2,1)S(1)}, bf16[2,64,1024]{2,1,0:T(8,128)(2,1)S(1)}, u32[]{:S(2)}, u32[]{:S(2)}) collective-permute-start(bf16[2,64,1024]{2,1,0:T(8,128)(2,1)S(1)} %get-tuple-element.95.refs_0_.refs_1_), channel_id=1, source_target_pairs={{0,6},{1,7},{2,4},{3,5},{4,2},{5,3},{6,0},{7,1},{8,14},{9,15},{10,... | collective-permute-start | bytes 786440 | tf_op jit(solution)/shard_map/ppermute | solution.py:18
  69.0 13.1 %collective-permute-start.25 = (bf16[128,1024]{1,0:T(8,128)(2,1)S(1)}, bf16[128,1024]{1,0:T(8,128)(2,1)S(1)}, u32[]{:S(2)}, u32[]{:S(2)}) collective-permute-start(bf16[128,1024]{1,0:T(8,128)(2,1)S(1)} %get-tuple-element.101), channel_id=1, source_target_pairs={{0,32},{8,40},{16,48},{24,56},{32,0},{40,8},{48,16},{56,24},{64,96... | collective-permute-start | bytes 786440 | tf_op jit(solution)/shard_map/ppermute | solution.py:18
  71.0 11.1 %collective-permute-start.24 = (bf16[128,1024]{1,0:T(8,128)(2,1)S(1)}, bf16[128,1024]{1,0:T(8,128)(2,1)S(1)}, u32[]{:S(2)}, u32[]{:S(2)}) collective-permute-start(bf16[128,1024]{1,0:T(8,128)(2,1)S(1)} %get-tuple-element.98.refs_0_), channel_id=1, source_target_pairs={{0,96},{8,104},{16,112},{24,120},{32,64},{40,72},{48,80},{56,88},{... | collective-permute-start | bytes 786440 | tf_op jit(solution)/shard_map/ppermute | solution.py:18
  94.8 10.2 %collective-permute-start.29 = (bf16[128,1024]{1,0:T(8,128)(2,1)S(1)}, bf16[128,1024]{1,0:T(8,128)(2,1)S(1)}, u32[]{:S(2)}, u32[]{:S(2)}) collective-permute-start(bf16[128,1024]{1,0:T(8,128)(2,1)S(1)} %get-tuple-element.111), channel_id=1, source_target_pairs={{0,2},{1,3},{2,0},{3,1},{4,6},{5,7},{6,4},{7,5},{8,10},{9,11},{10,... | collective-permute-start | bytes 786440 | tf_op jit(solution)/shard_map/ppermute | solution.py:18
  94.9 10.1 %collective-permute-start.28 = (bf16[128,1024]{1,0:T(8,128)(2,1)S(1)}, bf16[128,1024]{1,0:T(8,128)(2,1)S(1)}, u32[]{:S(2)}, u32[]{:S(2)}) collective-permute-start(bf16[128,1024]{1,0:T(8,128)(2,1)S(1)} %get-tuple-element.106.refs_0_), channel_id=1, source_target_pairs={{0,6},{1,7},{2,4},{3,5},{4,2},{5,3},{6,0},{7,1},{8,14},{9,15},{10,... | collective-permute-start | bytes 786440 | tf_op jit(solution)/shard_map/ppermute | solution.py:18
  110.3 12.4 %collective-permute-start.36 = (bf16[2,128,1024]{2,1,0:T(8,128)(2,1)S(1)}, bf16[2,128,1024]{2,1,0:T(8,128)(2,1)S(1)}, u32[]{:S(2)}, u32[]{:S(2)}) collective-permute-start(bf16[2,128,1024]{2,1,0:T(8,128)(2,1)S(1)} %get-tuple-element.119), channel_id=1, source_target_pairs={{0,32},{8,40},{16,48},{24,56},{32,0},{40,8},{48,16},{56,24},{64,96... | collective-permute-start | bytes 1572872 | tf_op jit(solution)/shard_map/ppermute | solution.py:18
  110.4 13.7 %collective-permute-start.37 = (bf16[2,128,1024]{2,1,0:T(8,128)(2,1)S(1)}, bf16[2,128,1024]{2,1,0:T(8,128)(2,1)S(1)}, u32[]{:S(2)}, u32[]{:S(2)}) collective-permute-start(bf16[2,128,1024]{2,1,0:T(8,128)(2,1)S(1)} %get-tuple-element.120), channel_id=1, source_target_pairs={{0,96},{8,104},{16,112},{24,120},{32,64},{40,72},{48,80},{56,88},{... | collective-permute-start | bytes 1572872 | tf_op jit(solution)/shard_map/ppermute | solution.py:18
  116.2 9.9 %collective-permute-start.38 = (bf16[2,64,1024]{2,1,0:T(8,128)(2,1)S(1)}, bf16[2,64,1024]{2,1,0:T(8,128)(2,1)S(1)}, u32[]{:S(2)}, u32[]{:S(2)}) collective-permute-start(bf16[2,64,1024]{2,1,0:T(8,128)(2,1)S(1)} %image_grads_x_a.1.refs_0_.refs_1_), channel_id=1, source_target_pairs={{0,1},{1,0},{2,3},{3,2},{4,5},{5,4},{6,7},{7,6},{8,9},{9,8},{10,11... | collective-permute-start | bytes 786440 | tf_op jit(solution)/shard_map/ppermute | solution.py:18
  124.3 9.3 %collective-permute-start.39 = (bf16[128,1024]{1,0:T(8,128)(2,1)S(1)}, bf16[128,1024]{1,0:T(8,128)(2,1)S(1)}, u32[]{:S(2)}, u32[]{:S(2)}) collective-permute-start(bf16[128,1024]{1,0:T(8,128)(2,1)S(1)} %get-tuple-element.121.refs_0_), channel_id=1, source_target_pairs={{0,16},{8,24},{16,0},{24,8},{32,48},{40,56},{48,32},{56,40},{64,80... | collective-permute-start | bytes 786440 | tf_op jit(solution)/shard_map/ppermute | solution.py:18
  124.7 13.8 %collective-permute-start.40 = (bf16[2,64,1024]{2,1,0:T(8,128)(2,1)S(1)}, bf16[2,64,1024]{2,1,0:T(8,128)(2,1)S(1)}, u32[]{:S(2)}, u32[]{:S(2)}) collective-permute-start(bf16[2,64,1024]{2,1,0:T(8,128)(2,1)S(1)} %image_grads_x_b.1.refs_0_.refs_1_), channel_id=1, source_target_pairs={{0,1},{1,0},{2,3},{3,2},{4,5},{5,4},{6,7},{7,6},{8,9},{9,8},{10,11... | collective-permute-start | bytes 786440 | tf_op jit(solution)/shard_map/ppermute | solution.py:18
  126.4 14.3 %collective-permute-start.45 = (bf16[2,64,1024]{2,1,0:T(8,128)(2,1)S(1)}, bf16[2,64,1024]{2,1,0:T(8,128)(2,1)S(1)}, u32[]{:S(2)}, u32[]{:S(2)}) collective-permute-start(bf16[2,64,1024]{2,1,0:T(8,128)(2,1)S(1)} %image_back_a.1.refs_0_.refs_3_), channel_id=1, source_target_pairs={{0,4},{1,5},{2,6},{3,7},{4,0},{5,1},{6,2},{7,3},{8,12},{9,13},{10,... | collective-permute-start | bytes 786440 | tf_op jit(solution)/shard_map/ppermute | solution.py:18
  128.7 12.3 %collective-permute-start.43 = (bf16[2,64,1024]{2,1,0:T(8,128)(2,1)S(1)}, bf16[2,64,1024]{2,1,0:T(8,128)(2,1)S(1)}, u32[]{:S(2)}, u32[]{:S(2)}) collective-permute-start(bf16[2,64,1024]{2,1,0:T(8,128)(2,1)S(1)} %image_back_a.1.refs_0_.refs_3_), channel_id=1, source_target_pairs={{0,6},{1,7},{2,4},{3,5},{4,2},{5,3},{6,0},{7,1},{8,14},{9,15},{10,... | collective-permute-start | bytes 786440 | tf_op jit(solution)/shard_map/ppermute | solution.py:18
  129.9 11.1 %collective-permute-start.41 = (bf16[2,64,1024]{2,1,0:T(8,128)(2,1)S(1)}, bf16[2,64,1024]{2,1,0:T(8,128)(2,1)S(1)}, u32[]{:S(2)}, u32[]{:S(2)}) collective-permute-start(bf16[2,64,1024]{2,1,0:T(8,128)(2,1)S(1)} %image_back_a.1.refs_0_.refs_3_), channel_id=1, source_target_pairs={{0,2},{1,3},{2,0},{3,1},{4,6},{5,7},{6,4},{7,5},{8,10},{9,11},{10,... | collective-permute-start | bytes 786440 | tf_op jit(solution)/shard_map/ppermute | solution.py:18
  138.7 10.5 %collective-permute-start.44 = (bf16[2,64,1024]{2,1,0:T(8,128)(2,1)S(1)}, bf16[2,64,1024]{2,1,0:T(8,128)(2,1)S(1)}, u32[]{:S(2)}, u32[]{:S(2)}) collective-permute-start(bf16[2,64,1024]{2,1,0:T(8,128)(2,1)S(1)} %image_back_b.1.refs_1_.refs_0_.refs_4_), channel_id=1, source_target_pairs={{0,6},{1,7},{2,4},{3,5},{4,2},{5,3},{6,0},{7,1},{8,14},{9,15},{10,... | collective-permute-start | bytes 786440 | tf_op jit(solution)/shard_map/ppermute | solution.py:18
  141.8 22.0 %collective-permute-start.50 = (bf16[2,128,1024]{2,1,0:T(8,128)(2,1)S(1)}, bf16[2,128,1024]{2,1,0:T(8,128)(2,1)S(1)}, u32[]{:S(2)}, u32[]{:S(2)}) collective-permute-start(bf16[2,128,1024]{2,1,0:T(8,128)(2,1)S(1)} %stack_text_grads.1.refs_0_.refs_3_), channel_id=1, source_target_pairs={{0,6},{1,7},{2,4},{3,5},{4,2},{5,3},{6,0},{7,1},{8,14},{9,15},{10,... | collective-permute-start | bytes 1572872 | tf_op jit(solution)/shard_map/ppermute | solution.py:18
  143.9 19.9 %collective-permute-start.49 = (bf16[2,128,1024]{2,1,0:T(8,128)(2,1)S(1)}, bf16[2,128,1024]{2,1,0:T(8,128)(2,1)S(1)}, u32[]{:S(2)}, u32[]{:S(2)}) collective-permute-start(bf16[2,128,1024]{2,1,0:T(8,128)(2,1)S(1)} %stack_text_grads.1.refs_0_.refs_3_), channel_id=1, source_target_pairs={{0,2},{1,3},{2,0},{3,1},{4,6},{5,7},{6,4},{7,5},{8,10},{9,11},{10,... | collective-permute-start | bytes 1572872 | tf_op jit(solution)/shard_map/ppermute | solution.py:18
  163.9 10.0 %collective-permute-start.51 = (bf16[128,1024]{1,0:T(8,128)(2,1)S(1)}, bf16[128,1024]{1,0:T(8,128)(2,1)S(1)}, u32[]{:S(2)}, u32[]{:S(2)}) collective-permute-start(bf16[128,1024]{1,0:T(8,128)(2,1)S(1)} %get-tuple-element.129), channel_id=1, source_target_pairs={{0,6},{1,7},{2,4},{3,5},{4,2},{5,3},{6,0},{7,1},{8,14},{9,15},{10,... | collective-permute-start | bytes 786440 | tf_op jit(solution)/shard_map/ppermute | solution.py:18
  166.3 11.5 %collective-permute-start.54 = (bf16[4,64,768]{2,1,0:T(8,128)(2,1)S(1)}, bf16[4,64,768]{2,1,0:T(8,128)(2,1)S(1)}, u32[]{:S(2)}, u32[]{:S(2)}) collective-permute-start(bf16[4,64,768]{2,1,0:T(8,128)(2,1)S(1)} %get-tuple-element.133), channel_id=1, source_target_pairs={{0,16},{8,24},{16,0},{24,8},{32,48},{40,56},{48,32},{56,40},{64,80... | collective-permute-start | bytes 1179656 | tf_op jit(solution)/shard_map/ppermute | solution.py:18
  178.0 11.4 %collective-permute-start.59 = (bf16[2,64,512]{2,1,0:T(8,128)(2,1)S(1)}, bf16[2,64,512]{2,1,0:T(8,128)(2,1)S(1)}, u32[]{:S(2)}, u32[]{:S(2)}) collective-permute-start(bf16[2,64,512]{2,1,0:T(8,128)(2,1)S(1)} %get-tuple-element.141), channel_id=1, source_target_pairs={{0,32},{8,40},{16,48},{24,56},{32,0},{40,8},{48,16},{56,24},{64,96... | collective-permute-start | bytes 393224 | tf_op jit(solution)/shard_map/ppermute | solution.py:18
  178.7 12.0 %collective-permute-start.60 = (bf16[2,64,512]{2,1,0:T(8,128)(2,1)S(1)}, bf16[2,64,512]{2,1,0:T(8,128)(2,1)S(1)}, u32[]{:S(2)}, u32[]{:S(2)}) collective-permute-start(bf16[2,64,512]{2,1,0:T(8,128)(2,1)S(1)} %get-tuple-element.142), channel_id=1, source_target_pairs={{0,96},{8,104},{16,112},{24,120},{32,64},{40,72},{48,80},{56,88},{... | collective-permute-start | bytes 393224 | tf_op jit(solution)/shard_map/ppermute | solution.py:18
  (39 other events, 289.4 us)
